TPU v7x, 32 devices: a whole 2x2x4 slice. The times are simulated.
32 devices in a mesh: blk: 8 (over y, x, core), grp: 4 (over z).
Axes of the slice: x: 2, y: 2, z: 4, core: 2. Of those that a mesh axis runs over, the one named last changes fastest.
Arguments:
- raw_panels: bfloat16 [4, 1024, 8192], P('grp', 'blk'), may hold values from -0.4375 to 0.4375
- metric: bfloat16 [1024, 1024], replicated, may hold values from -0.1875 to 0.1875
- tile_pairs: int32 [112, 2], P('blk'), may hold values from 0 to 7, as said below
- owners: int32 [112, 1], P('blk'), may hold values from 0 to 7; in each aligned block of 14 rows (0 to 13, 14 to 27, ...) at most 3 rows name the same one
- group_mask: int32 [112, 4], P('blk', 'grp'), may hold values 0 or 1
Outputs:
- owned_tiles: float32 [8, 8, 3, 128, 128], P('blk', None, None, 'grp')
Inputs may be any that keep to these rules, and one draw needn't show every extreme that they name: `tile_pairs`: tile rows of source s (rows s * 14 to s * 14 + 13) have first entry s, the basis block held by index s of blk; the second entry differs from the first. `owners`: in each aligned block of 14 rows (one source) no owner appears more than 3 times.
All inputs are finite; a program needn't handle non-finite values. No bound on the sum of `group_mask` on one device may be relied on, other than what follows from the above.
Results may differ from a plain program's by a relative error of at most 0.0029.
Values may be sent and summed in bfloat16 or wider, within the bound.
No kernel may reach another device: no remote copies, remote signals or barrier semaphores. Data moves between devices by JAX's collectives and lax.ppermute only.
A program may use at most 128 MiB of HBM per device.

v0:
```python
import jax
import jax.numpy as jnp
from jax import lax
from jax.sharding import PartitionSpec as P

TILE = 128


def passed_along(value, axis, steps):
    count = lax.axis_size(axis)
    pairs = [(source, (source + steps) % count) for source in range(count)]
    return lax.ppermute(value, axis, pairs)


def per_device(raw_panels, metric, tile_pairs, owners, group_mask):
    raw = raw_panels[0]
    rows = raw.shape[0]
    columns = raw.shape[1]
    naux = metric.shape[0]
    occ = columns // naux
    flat = raw.reshape(rows * occ, naux)
    fitted = lax.dot_general(
        flat, metric, (((1,), (1,)), ((), ())), preferred_element_type=jnp.float32
    )
    panel = fitted.astype(jnp.bfloat16).reshape(rows, columns)
    cycle = lax.axis_size("blk")
    mine = lax.axis_index("blk")
    tile_count = tile_pairs.shape[0]
    capacity = max(2, 2 * tile_count // cycle)
    labels = jnp.arange(cycle)

    def place(total, visiting, source):
        block = lax.dot_general(
            panel, visiting, (((1,), (1,)), ((), ())), preferred_element_type=jnp.float32
        )
        return lax.dynamic_update_slice(total, block, (jnp.int32(0), source * rows))

    start = place(jnp.zeros((rows, cycle * rows), jnp.float32), panel, mine)

    def advance(step, carry):
        visiting, total = carry
        visiting = passed_along(visiting, "blk", 1)
        source = (mine - step) % cycle
        return (visiting, place(total, visiting, source))

    _, row_block = lax.fori_loop(1, cycle, advance, (panel, start))
    local_blocks = rows // TILE
    arranged = jnp.swapaxes(row_block.reshape(local_blocks, TILE, cycle * local_blocks, TILE), 1, 2)
    mu_local = tile_pairs[:, 0] - mine * local_blocks
    picked = arranged[mu_local, tile_pairs[:, 1]]
    weighted = picked * group_mask[:, 0].astype(jnp.float32)[:, None, None]
    owner_ids = owners[:, 0]
    hits = (owner_ids[:, None] == labels[None, :]).astype(jnp.int32)
    before = jnp.cumsum(hits, axis=0) - hits
    slots = jnp.sum(before * hits, axis=1)
    outgoing = (
        jnp.zeros((cycle, capacity, TILE, TILE), jnp.float32).at[owner_ids, slots].set(weighted)
    )
    arrived = lax.all_to_all(outgoing, "blk", split_axis=0, concat_axis=0, tiled=True)
    summed = lax.psum_scatter(arrived, "grp", scatter_dimension=2, tiled=True)
    return summed[None]


def solution(mesh):
    placed = (P("grp", "blk", None), P(), P("blk", None), P("blk", None), P("blk", "grp"))
    return jax.shard_map(
        per_device,
        mesh=mesh,
        in_specs=placed,
        out_specs=P("blk", None, None, "grp", None),
        check_vma=False,
    )
```

profile of v0, /device:TPU:0, one launch (start us, length us, event | category | flops | bytes accessed | tf_op | source)
XLA Modules:
  0.0 326.9 jit_solution(9457108860381942994)
XLA Ops:
  6.5 4.3 %reshape_squeeze.3 = bf16[1024,1024]{1,0:T(8,128)(2,1)} reshape(bf16[1,128,8192]{2,1,0:T(8,128)(2,1)} %param.7) | data formatting | bytes 4194304 | tf_op jit(solution)/shard_map/reshape;squeeze | solution.py:21
  10.9 5.3 %convolution_convert_fusion = bf16[1024,1024]{1,0:T(8,128)(2,1)} fusion(bf16[1024,1024]{1,0:T(8,128)(2,1)} %reshape_squeeze.3, bf16[1024,1024]{1,0:T(8,128)(2,1)S(1)} %copy-done), kind=kOutput, calls=%fused_computation.3 | convolution fusion | flops 2148532224 | bytes 6291456 | tf_op jit(solution)/shard_map/dot_general | solution.py:22
  16.1 4.2 %reshape.25 = bf16[128,8192]{1,0:T(8,128)(2,1)} reshape(bf16[1024,1024]{1,0:T(8,128)(2,1)} %convolution_convert_fusion) | data formatting | bytes 4194304 | tf_op jit(solution)/shard_map/reshape | solution.py:25
  20.3 3.1 copy.13
  23.5 2.9 convolution_dynamic-update-slice_fusion.1
  26.4 225.7 %while.17 = (s32[]{:T(128)}, bf16[128,8192]{1,0:T(8,128)(2,1)}, f32[128,1024]{1,0:T(8,128)S(1)}, bf16[128,8192]{1,0:T(8,128)(2,1)}, s32[]{:T(128)}, /*index=5*/s...) while((s32[]{:T(128)}, bf16[128,8192]{1,0:T(8,128)(2,1)}, ...), condition=%wide.region_3.4_spmd, body=%wide.region_2.3_spmd.sunk | while | flops 268435488 | bytes 25231708 | solution.py:46
  27.0 26.9 %collective-permute-done = bf16[128,8192]{1,0:T(8,128)(2,1)} collective-permute-done((bf16[128,8192]{1,0:T(8,128)(2,1)}, bf16[128,8192]{1,0:T(8,128)(2,1)}, u32[]{:S(2)}, u32[]{:S(2)}) %collective-permute-start) | collective-permute-done | bytes 2097184 | tf_op jit(solution)/shard_map/while/body/eval_jaxpr/ppermute | solution.py:12
  53.9 3.1 copy.19
  57.0 2.3 convolution_dynamic-update-slice_fusion.3
  59.4 26.6 %collective-permute-done = bf16[128,8192]{1,0:T(8,128)(2,1)} collective-permute-done((bf16[128,8192]{1,0:T(8,128)(2,1)}, bf16[128,8192]{1,0:T(8,128)(2,1)}, u32[]{:S(2)}, u32[]{:S(2)}) %collective-permute-start) | collective-permute-done | bytes 2097184 | tf_op jit(solution)/shard_map/while/body/eval_jaxpr/ppermute | solution.py:12
  86.0 3.1 copy.19
  89.1 2.3 convolution_dynamic-update-slice_fusion.3
  91.5 26.6 %collective-permute-done = bf16[128,8192]{1,0:T(8,128)(2,1)} collective-permute-done((bf16[128,8192]{1,0:T(8,128)(2,1)}, bf16[128,8192]{1,0:T(8,128)(2,1)}, u32[]{:S(2)}, u32[]{:S(2)}) %collective-permute-start) | collective-permute-done | bytes 2097184 | tf_op jit(solution)/shard_map/while/body/eval_jaxpr/ppermute | solution.py:12
  118.2 3.1 copy.19
  121.3 2.3 convolution_dynamic-update-slice_fusion.3
  123.7 26.6 %collective-permute-done = bf16[128,8192]{1,0:T(8,128)(2,1)} collective-permute-done((bf16[128,8192]{1,0:T(8,128)(2,1)}, bf16[128,8192]{1,0:T(8,128)(2,1)}, u32[]{:S(2)}, u32[]{:S(2)}) %collective-permute-start) | collective-permute-done | bytes 2097184 | tf_op jit(solution)/shard_map/while/body/eval_jaxpr/ppermute | solution.py:12
  150.3 3.1 copy.19
  153.4 2.3 convolution_dynamic-update-slice_fusion.3
  155.8 26.6 %collective-permute-done = bf16[128,8192]{1,0:T(8,128)(2,1)} collective-permute-done((bf16[128,8192]{1,0:T(8,128)(2,1)}, bf16[128,8192]{1,0:T(8,128)(2,1)}, u32[]{:S(2)}, u32[]{:S(2)}) %collective-permute-start) | collective-permute-done | bytes 2097184 | tf_op jit(solution)/shard_map/while/body/eval_jaxpr/ppermute | solution.py:12
  182.5 3.1 copy.19
  185.6 2.3 convolution_dynamic-update-slice_fusion.3
  188.0 26.6 %collective-permute-done = bf16[128,8192]{1,0:T(8,128)(2,1)} collective-permute-done((bf16[128,8192]{1,0:T(8,128)(2,1)}, bf16[128,8192]{1,0:T(8,128)(2,1)}, u32[]{:S(2)}, u32[]{:S(2)}) %collective-permute-start) | collective-permute-done | bytes 2097184 | tf_op jit(solution)/shard_map/while/body/eval_jaxpr/ppermute | solution.py:12
  214.6 3.1 copy.19
  217.7 2.3 convolution_dynamic-update-slice_fusion.3
  220.1 26.6 %collective-permute-done = bf16[128,8192]{1,0:T(8,128)(2,1)} collective-permute-done((bf16[128,8192]{1,0:T(8,128)(2,1)}, bf16[128,8192]{1,0:T(8,128)(2,1)}, u32[]{:S(2)}, u32[]{:S(2)}) %collective-permute-start) | collective-permute-done | bytes 2097184 | tf_op jit(solution)/shard_map/while/body/eval_jaxpr/ppermute | solution.py:12
  246.7 3.1 copy.19
  249.9 2.3 convolution_dynamic-update-slice_fusion.3
  253.7 1.1 broadcast_multiply_fusion
  254.8 1.3 broadcast_in_dim.6
  256.1 3.0 scatter_fusion
  259.2 25.3 %all_to_all.5 = f32[8,3,128,128]{3,2,1,0:T(8,128)} all-to-all(f32[8,3,128,128]{3,2,1,0:T(8,128)} %scatter_fusion), channel_id=1, replica_groups=mesh['blk'=8,'grp'=4] {'blk'}, dimensions={0} | all-to-all | bytes 3145728 | tf_op jit(solution)/shard_map/all_to_all | solution.py:59
  284.5 35.6 %reduce-scatter.2.cloned.1.call-done = f32[8,3,32,128]{3,2,1,0:T(8,128)} async-done(((f32[8,3,128,128]{3,2,1,0:T(8,128)}), f32[8,3,32,128]{3,2,1,0:T(8,128)}) %reduce-scatter.2.cloned.1.call-update) | async-done | bytes 393232 | tf_op jit(solution)/shard_map/reduce_scatter | solution.py:60
  (43 shorter events, 2.5 us)
Async XLA Ops:
  6.5 4.3 %copy-start = (bf16[1024,1024]{1,0:T(8,128)(2,1)S(1)}, bf16[1024,1024]{1,0:T(8,128)(2,1)}, u32[]{:S(2)}) copy-start(bf16[1024,1024]{1,0:T(8,128)(2,1)} %param.8) | copy-start | bytes 6291460
  6.5 313.5 %reduce-scatter.2.cloned.1.call-start = ((), (), s32[]{:S(2)}) async-start(), calls=%async_computation.2 | async-start | bytes 1966080 | tf_op jit(solution)/shard_map/reduce_scatter | solution.py:60
  26.4 27.4 %collective-permute-start = (bf16[128,8192]{1,0:T(8,128)(2,1)}, bf16[128,8192]{1,0:T(8,128)(2,1)}, u32[]{:S(2)}, u32[]{:S(2)}) collective-permute-start(bf16[128,8192]{1,0:T(8,128)(2,1)} %get-tuple-element.192), channel_id=1, source_target_pairs={{0,4},{4,8},{8,12},{12,16},{16,20},{20,24},{24,28},{28,0},{1,5},{5... | collective-permute-start | bytes 6291464 | tf_op jit(solution)/shard_map/while/body/eval_jaxpr/ppermute | solution.py:12
  27.0 30.0 %copy-start.1 = (bf16[128,8192]{1,0:T(8,128)(2,1)S(1)}, bf16[128,8192]{1,0:T(8,128)(2,1)}, u32[]{:S(2)}) copy-start(bf16[128,8192]{1,0:T(8,128)(2,1)} %get-tuple-element.205) | copy-start | bytes 6291460 | tf_op jit(solution)/shard_map/while
  59.3 26.7 %collective-permute-start = (bf16[128,8192]{1,0:T(8,128)(2,1)}, bf16[128,8192]{1,0:T(8,128)(2,1)}, u32[]{:S(2)}, u32[]{:S(2)}) collective-permute-start(bf16[128,8192]{1,0:T(8,128)(2,1)} %get-tuple-element.192), channel_id=1, source_target_pairs={{0,4},{4,8},{8,12},{12,16},{16,20},{20,24},{24,28},{28,0},{1,5},{5... | collective-permute-start | bytes 6291464 | tf_op jit(solution)/shard_map/while/body/eval_jaxpr/ppermute | solution.py:12
  59.4 29.7 %copy-start.1 = (bf16[128,8192]{1,0:T(8,128)(2,1)S(1)}, bf16[128,8192]{1,0:T(8,128)(2,1)}, u32[]{:S(2)}) copy-start(bf16[128,8192]{1,0:T(8,128)(2,1)} %get-tuple-element.205) | copy-start | bytes 6291460 | tf_op jit(solution)/shard_map/while
  91.4 26.7 %collective-permute-start = (bf16[128,8192]{1,0:T(8,128)(2,1)}, bf16[128,8192]{1,0:T(8,128)(2,1)}, u32[]{:S(2)}, u32[]{:S(2)}) collective-permute-start(bf16[128,8192]{1,0:T(8,128)(2,1)} %get-tuple-element.192), channel_id=1, source_target_pairs={{0,4},{4,8},{8,12},{12,16},{16,20},{20,24},{24,28},{28,0},{1,5},{5... | collective-permute-start | bytes 6291464 | tf_op jit(solution)/shard_map/while/body/eval_jaxpr/ppermute | solution.py:12
  91.5 29.7 %copy-start.1 = (bf16[128,8192]{1,0:T(8,128)(2,1)S(1)}, bf16[128,8192]{1,0:T(8,128)(2,1)}, u32[]{:S(2)}) copy-start(bf16[128,8192]{1,0:T(8,128)(2,1)} %get-tuple-element.205) | copy-start | bytes 6291460 | tf_op jit(solution)/shard_map/while
  123.6 26.7 %collective-permute-start = (bf16[128,8192]{1,0:T(8,128)(2,1)}, bf16[128,8192]{1,0:T(8,128)(2,1)}, u32[]{:S(2)}, u32[]{:S(2)}) collective-permute-start(bf16[128,8192]{1,0:T(8,128)(2,1)} %get-tuple-element.192), channel_id=1, source_target_pairs={{0,4},{4,8},{8,12},{12,16},{16,20},{20,24},{24,28},{28,0},{1,5},{5... | collective-permute-start | bytes 6291464 | tf_op jit(solution)/shard_map/while/body/eval_jaxpr/ppermute | solution.py:12
  123.7 29.7 %copy-start.1 = (bf16[128,8192]{1,0:T(8,128)(2,1)S(1)}, bf16[128,8192]{1,0:T(8,128)(2,1)}, u32[]{:S(2)}) copy-start(bf16[128,8192]{1,0:T(8,128)(2,1)} %get-tuple-element.205) | copy-start | bytes 6291460 | tf_op jit(solution)/shard_map/while
  155.7 26.7 %collective-permute-start = (bf16[128,8192]{1,0:T(8,128)(2,1)}, bf16[128,8192]{1,0:T(8,128)(2,1)}, u32[]{:S(2)}, u32[]{:S(2)}) collective-permute-start(bf16[128,8192]{1,0:T(8,128)(2,1)} %get-tuple-element.192), channel_id=1, source_target_pairs={{0,4},{4,8},{8,12},{12,16},{16,20},{20,24},{24,28},{28,0},{1,5},{5... | collective-permute-start | bytes 6291464 | tf_op jit(solution)/shard_map/while/body/eval_jaxpr/ppermute | solution.py:12
  155.8 29.7 %copy-start.1 = (bf16[128,8192]{1,0:T(8,128)(2,1)S(1)}, bf16[128,8192]{1,0:T(8,128)(2,1)}, u32[]{:S(2)}) copy-start(bf16[128,8192]{1,0:T(8,128)(2,1)} %get-tuple-element.205) | copy-start | bytes 6291460 | tf_op jit(solution)/shard_map/while
  187.9 26.7 %collective-permute-start = (bf16[128,8192]{1,0:T(8,128)(2,1)}, bf16[128,8192]{1,0:T(8,128)(2,1)}, u32[]{:S(2)}, u32[]{:S(2)}) collective-permute-start(bf16[128,8192]{1,0:T(8,128)(2,1)} %get-tuple-element.192), channel_id=1, source_target_pairs={{0,4},{4,8},{8,12},{12,16},{16,20},{20,24},{24,28},{28,0},{1,5},{5... | collective-permute-start | bytes 6291464 | tf_op jit(solution)/shard_map/while/body/eval_jaxpr/ppermute | solution.py:12
  188.0 29.7 %copy-start.1 = (bf16[128,8192]{1,0:T(8,128)(2,1)S(1)}, bf16[128,8192]{1,0:T(8,128)(2,1)}, u32[]{:S(2)}) copy-start(bf16[128,8192]{1,0:T(8,128)(2,1)} %get-tuple-element.205) | copy-start | bytes 6291460 | tf_op jit(solution)/shard_map/while
  220.0 26.7 %collective-permute-start = (bf16[128,8192]{1,0:T(8,128)(2,1)}, bf16[128,8192]{1,0:T(8,128)(2,1)}, u32[]{:S(2)}, u32[]{:S(2)}) collective-permute-start(bf16[128,8192]{1,0:T(8,128)(2,1)} %get-tuple-element.192), channel_id=1, source_target_pairs={{0,4},{4,8},{8,12},{12,16},{16,20},{20,24},{24,28},{28,0},{1,5},{5... | collective-permute-start | bytes 6291464 | tf_op jit(solution)/shard_map/while/body/eval_jaxpr/ppermute | solution.py:12
  220.1 29.7 %copy-start.1 = (bf16[128,8192]{1,0:T(8,128)(2,1)S(1)}, bf16[128,8192]{1,0:T(8,128)(2,1)}, u32[]{:S(2)}) copy-start(bf16[128,8192]{1,0:T(8,128)(2,1)} %get-tuple-element.205) | copy-start | bytes 6291460 | tf_op jit(solution)/shard_map/while
  252.2 0.7 copy-start.4
  252.2 0.7 copy-start.5
  252.2 0.7 copy-start.3
  254.8 1.4 copy-start.2
Sparse Core Ops, SparseCore 0:
  284.6 35.4 reduce-scatter.1
where the time goes:
time: 328 us; the launch traced here: 327 us
  waiting for transfers between devices  222 us (68%)
  local copies, waits for them, and re-layouts  39.1 us (12%)
  blocking collectives  25.3 us (8%)
  matrix products  24.3 us (7%)
  between operations  13.5 us (4%)
    ppermute x7, waiting for transfers between devices, passed_along(): return lax.ppermute(value, axis, pairs)  187 us
    reduce_scatter x1, waiting for transfers between devices, per_device(): summed = lax.psum_scatter(arrived, 'grp', scatter_dimension=2, tiled=True)  35.6 us
    all_to_all x1, blocking collectives, per_device(): lax.all_to_all(outgoing, 'blk', split_axis=0, concat_axis=0, tiled=True)  25.3 us
    while x21, local copies, waits for them, and re-layouts  21.7 us
    dot_general x8, matrix products, place(): lax.dot_general(panel, visiting, (((1,), (1,)), ((), ())), preferred_elem...  19 us
  transfers between devices with their start and end apart: 8, of which 8 were waited for; matrix products, arithmetic and copies ran while one was open for 0% of the time, Pallas kernels for 0%

commit v1 on v0

v1 whole, which is shorter than its diff:
```python
import jax
import jax.numpy as jnp
from jax import lax
from jax.experimental import pallas as pl
from jax.experimental.pallas import tpu as pltpu
from jax.sharding import PartitionSpec as P

TILE = 128
CORES = 2


def swapped(value, axis, distance):
    count = lax.axis_size(axis)
    return lax.ppermute(value, axis, [(source, source ^ distance) for source in range(count)])


def combine_kernel(block_ref, mask_ref, *refs):
    chunks, out_ref = refs[:-1], refs[-1]
    owners, slots = out_ref.shape[0], out_ref.shape[1]
    for owner in range(owners):
        for slot in range(slots):
            at = owner * slots + slot
            start = pl.multiple_of(block_ref[at] * TILE, TILE)
            total = jnp.zeros(out_ref.shape[2:], jnp.float32)
            for group, chunk in enumerate(chunks):
                weight = mask_ref[group, at].astype(jnp.float32)
                total = total + weight * chunk[:, pl.ds(start, TILE)].astype(jnp.float32)
            out_ref[owner, slot] = total


def combine(blocks, masks, chunks, owners, slots):
    rows = chunks[0].shape[0]
    smem = pl.BlockSpec(memory_space=pltpu.SMEM)
    vmem = pl.BlockSpec(memory_space=pltpu.VMEM)
    return pl.pallas_call(
        combine_kernel,
        out_shape=jax.ShapeDtypeStruct((owners, slots, rows, TILE), jnp.float32),
        in_specs=[smem, smem] + [vmem] * len(chunks),
        out_specs=vmem,
        compiler_params=pltpu.CompilerParams(vmem_limit_bytes=16 * 1024 * 1024),
    )(blocks, masks, *chunks)


def contract(left, right):
    return lax.dot_general(
        left, right, (((1,), (1,)), ((), ())), preferred_element_type=jnp.float32
    )


def per_device(raw_panels, metric, tile_pairs, owners, group_mask):
    raw = raw_panels[0]
    rows, columns = raw.shape
    naux = metric.shape[0]
    cycle = lax.axis_size("blk")
    groups = lax.axis_size("grp")
    chips = cycle // CORES
    width = columns // chips
    mine = lax.axis_index("blk")
    my_group = lax.axis_index("grp")
    my_chip = mine // CORES
    tile_count = tile_pairs.shape[0]
    capacity = max(2, 2 * tile_count // cycle)

    def piece(distance):
        return lax.dynamic_slice(raw, (jnp.int32(0), (my_chip ^ distance) * width), (rows, width))

    def fit(panel):
        parts = [
            contract(panel[:, at : at + naux], metric).astype(jnp.bfloat16)
            for at in range(0, width, naux)
        ]
        return jnp.concatenate(parts, axis=1)

    arrived = [piece(0)] + [
        swapped(piece(chip), "blk", CORES * chip) for chip in range(1, chips)
    ]

    owner_ids = owners[:, 0] ^ mine
    hits = (owner_ids[:, None] == jnp.arange(cycle)[None, :]).astype(jnp.int32)
    before = jnp.cumsum(hits, axis=0) - hits
    slots = jnp.sum(before * hits, axis=1)
    places = owner_ids * capacity + slots
    taken = (places[None, :] == jnp.arange(cycle * capacity)[:, None]).astype(jnp.int32)
    blocks = jnp.sum(taken * (tile_pairs[:, 1] ^ mine)[None, :], axis=1)
    own_mask = group_mask[:, 0]
    all_masks = [own_mask] + [swapped(own_mask, "grp", d) for d in range(1, groups)]
    masks = jnp.stack([jnp.sum(taken * mask[None, :], axis=1) for mask in all_masks])

    fitted = [fit(panel) for panel in arrived]
    beside = [swapped(panel, "blk", 1) for panel in fitted]
    everything = jnp.concatenate(
        [panel for pair in zip(fitted, beside, strict=True) for panel in pair], axis=0
    )
    slabs = [contract(panel, everything) for panel in fitted]

    total = slabs[0].reshape(rows, cycle, TILE)
    for chip in range(1, chips):
        came = swapped(slabs[chip].astype(jnp.bfloat16), "blk", CORES * chip)
        order = [block ^ (CORES * chip) for block in range(cycle)]
        came = came.reshape(rows, cycle, TILE)
        total = total + jnp.stack([came[:, block] for block in order], axis=1).astype(jnp.float32)
    total = total.reshape(rows, cycle * TILE)

    share = rows // groups

    def strip(distance):
        return lax.dynamic_slice(
            total, ((my_group ^ distance) * share, jnp.int32(0)), (share, cycle * TILE)
        )

    chunks = [strip(0)] + [
        swapped(strip(d).astype(jnp.bfloat16), "grp", d) for d in range(1, groups)
    ]
    outgoing = combine(blocks, masks, chunks, cycle, capacity)
    outgoing = outgoing.reshape(chips, CORES, capacity, share, TILE)
    crossed = swapped(outgoing[:, 1], "blk", 1)
    pairs = jnp.stack([outgoing[:, 0], crossed], axis=1)
    received = [pairs[0]] + [
        swapped(pairs[chip], "blk", CORES * chip) for chip in range(1, chips)
    ]
    by_distance = jnp.concatenate(received, axis=0)
    owned = jnp.take(by_distance, jnp.arange(cycle) ^ mine, axis=0)
    return owned[None]


def solution(mesh):
    placed = (P("grp", "blk", None), P(), P("blk", None), P("blk", None), P("blk", "grp"))
    return jax.shard_map(
        per_device,
        mesh=mesh,
        in_specs=placed,
        out_specs=P("blk", None, None, "grp", None),
        check_vma=False,
    )
```

time: 328 us -> 113 us (0.34)
  waiting for transfers between devices: 222 us -> 51.5 us
  local copies, waits for them, and re-layouts: 39.1 us -> 9.45 us
  blocking collectives: 25.3 us -> 0 us
  starting transfers between devices: 0.86 us -> 22.8 us
  between operations: 13.5 us -> 0.37 us
  other arithmetic: 1.27 us -> 5.89 us
    ppermute x7 -> x20, waiting for transfers between devices: 187 us -> 51.5 us  [swapped(): lax.ppermute(value, axis, [(source, source ^ distance) for source in rang...]
    reduce_scatter x1 -> x0, waiting for transfers between devices: 35.6 us -> none  [per_device(): summed = lax.psum_scatter(arrived, 'grp', scatter_dimension=2, tiled=True)]
    all_to_all x1 -> x0, blocking collectives: 25.3 us -> none  [per_device(): lax.all_to_all(outgoing, 'blk', split_axis=0, concat_axis=0, tiled=True)]
    while x22 -> x0, local copies, waits for them, and re-layouts: 21.9 us -> none
    ppermute x7 -> x20, starting transfers between devices: 0.86 us -> 22.8 us  [swapped(): lax.ppermute(value, axis, [(source, source ^ distance) for source in rang...]
    reshape x2 -> x0, local copies, waits for them, and re-layouts: 4.39 us -> none  [the longest x1 4.19 us: per_device(): panel = fitted.astype(jnp.bfloat16).reshape(rows, columns)]
    another operation x1 -> x0, local copies, waits for them, and re-layouts: 4.34 us -> none  [per_device(): flat = raw.reshape(rows * occ, naux)]
    concatenate x2 -> x5, other arithmetic: 0.02 us -> 3.97 us  [the longest x4 3.94 us: fit(): return jnp.concatenate(parts, axis=1)]
  transfers between devices with their start and end apart: 8 -> 20, of which waited for: 8 -> 14; matrix products, arithmetic and copies ran while one was open for 0% -> 19% of each run, Pallas kernels for 0% -> 0%
where the time goes in v1:
time: 113 us; the launch traced here: 112 us
  waiting for transfers between devices  51.5 us (46%)
  starting transfers between devices  22.8 us (20%)
  matrix products  21.7 us (19%)
  local copies, waits for them, and re-layouts  9.45 us (8%)
  other arithmetic  5.89 us (5%)
    ppermute x20, waiting for transfers between devices, swapped(): lax.ppermute(value, axis, [(source, source ^ distance) for source in rang...  51.5 us
    ppermute x20, starting transfers between devices, swapped(): lax.ppermute(value, axis, [(source, source ^ distance) for source in rang...  22.8 us
    dot_general x12, matrix products, contract(): lax.dot_general(left, right, (((1,), (1,)), ((), ())), preferred_element_...  21.7 us
    concatenate x4, other arithmetic, fit(): return jnp.concatenate(parts, axis=1)  3.94 us
    unnamed x27, local copies, waits for them, and re-layouts  3.8 us
    dynamic_slice x1, local copies, waits for them, and re-layouts, piece(): lax.dynamic_slice(raw, (jnp.int32(0), (my_chip ^ distance) * width), (row...  2.68 us
  transfers between devices with their start and end apart: 20, of which 14 were waited for; matrix products, arithmetic and copies ran while one was open for 19% of the time, Pallas kernels for 0%

profile of v1, /device:TPU:0, one launch (start us, length us, event | category | flops | bytes accessed | tf_op | source)
XLA Modules:
  0.0 112.4 jit_solution(10786421208084332229)
XLA Ops:
  0.0 3.0 %collective-permute-start = (s32[14]{0:T(128)}, s32[14]{0:T(128)S(1)}, u32[]{:S(2)}, u32[]{:S(2)}) collective-permute-start(s32[14]{0:T(128)} %bitcast.85), channel_id=1, source_target_pairs={{0,1},{1,0},{2,3},{3,2},{4,5},{5,4},{6,7},{7,6},{8,9},{9,8},{10,11... | collective-permute-start | bytes 176 | tf_op jit(solution)/shard_map/ppermute | solution.py:14
  3.0 2.6 %collective-permute-start.1 = (s32[14]{0:T(128)}, s32[14]{0:T(128)S(1)}, u32[]{:S(2)}, u32[]{:S(2)}) collective-permute-start(s32[14]{0:T(128)} %bitcast.86), channel_id=1, source_target_pairs={{0,2},{1,3},{2,0},{3,1},{4,6},{5,7},{6,4},{7,5},{8,10},{9,11},{10,... | collective-permute-start | bytes 176 | tf_op jit(solution)/shard_map/ppermute | solution.py:14
  5.6 2.7 %dynamic-slice_bitcast_fusion = (bf16[128,2048]{1,0:T(8,128)(2,1)}, bf16[128,2048]{1,0:T(8,128)(2,1)S(1)}, bf16[128,2048]{1,0:T(8,128)(2,1)S(1)}, bf16[128,2048]{1,0:T(8,128)(2,1)}) fusion(bf16[1,128,8192]{2,1,0:T(8,128)(2,1)} %param.5, s32[]{:T(128)S(6)} %select_n.61, s32[]{:T(128)S(6)} %select_n.59, s32[]{:T(128)S(6)} %select_n.58, s32[]{:T(128)S(6)} %select_n.60), kind=kLoop, calls=%fused_computation.25 | loop fusion | bytes 4194320 | tf_op jit(solution)/shard_map/dynamic_slice | solution.py:65
  10.0 1.1 pad_maximum_fusion
  11.1 1.7 %collective-permute-start.4 = (bf16[128,2048]{1,0:T(8,128)(2,1)S(1)}, bf16[128,2048]{1,0:T(8,128)(2,1)S(1)}, u32[]{:S(2)}, u32[]{:S(2)}) collective-permute-start(bf16[128,2048]{1,0:T(8,128)(2,1)S(1)} %get-tuple-element.11), channel_id=1, source_target_pairs={{0,8},{4,12},{8,0},{12,4},{16,24},{20,28},{24,16},{28,20},{1,9},{5... | collective-permute-start | bytes 1572872 | tf_op jit(solution)/shard_map/ppermute | solution.py:14
  13.0 12.4 %collective-permute-done.4 = bf16[128,2048]{1,0:T(8,128)(2,1)S(1)} collective-permute-done((bf16[128,2048]{1,0:T(8,128)(2,1)S(1)}, bf16[128,2048]{1,0:T(8,128)(2,1)S(1)}, u32[]{:S(2)}, u32[]{:S(2)}) %collective-permute-start.4) | collective-permute-done | bytes 524320 | tf_op jit(solution)/shard_map/ppermute | solution.py:14
  25.5 1.7 %collective-permute-start.6 = (bf16[128,2048]{1,0:T(8,128)(2,1)}, bf16[128,2048]{1,0:T(8,128)(2,1)S(1)}, u32[]{:S(2)}, u32[]{:S(2)}) collective-permute-start(bf16[128,2048]{1,0:T(8,128)(2,1)} %get-tuple-element.13), channel_id=1, source_target_pairs={{0,16},{4,20},{8,24},{12,28},{16,0},{20,4},{24,8},{28,12},{1,17},{... | collective-permute-start | bytes 1572872 | tf_op jit(solution)/shard_map/ppermute | solution.py:14
  28.0 1.5 %collective-permute-start.8 = (bf16[128,2048]{1,0:T(8,128)(2,1)}, bf16[128,2048]{1,0:T(8,128)(2,1)S(1)}, u32[]{:S(2)}, u32[]{:S(2)}) collective-permute-start(bf16[128,2048]{1,0:T(8,128)(2,1)} %get-tuple-element.10), channel_id=1, source_target_pairs={{0,24},{4,28},{8,16},{12,20},{16,8},{20,12},{24,0},{28,4},{1,25},{... | collective-permute-start | bytes 1572872 | tf_op jit(solution)/shard_map/ppermute | solution.py:14
  29.5 1.9 %constant_dynamic-update-slice_fusion.6 = bf16[1024,2048]{1,0:T(8,128)(2,1)} fusion(bf16[1024,2048]{1,0:T(8,128)(2,1)} %get-tuple-element.24, bf16[128,2048]{1,0:T(8,128)(2,1)} %collective-permute-done.3), kind=kLoop, calls=%fused_computation.61 | loop fusion | bytes 1048576
  33.1 17.3 %collective-permute-done.6 = bf16[128,2048]{1,0:T(8,128)(2,1)S(1)} collective-permute-done((bf16[128,2048]{1,0:T(8,128)(2,1)}, bf16[128,2048]{1,0:T(8,128)(2,1)S(1)}, u32[]{:S(2)}, u32[]{:S(2)}) %collective-permute-start.6) | collective-permute-done | bytes 524320 | tf_op jit(solution)/shard_map/ppermute | solution.py:14
  57.0 1.1 pad_maximum_fusion.1
  58.5 1.9 %collective-permute-done.9 = bf16[128,2048]{1,0:T(8,128)(2,1)} collective-permute-done((bf16[128,2048]{1,0:T(8,128)(2,1)}, bf16[128,2048]{1,0:T(8,128)(2,1)}, u32[]{:S(2)}, u32[]{:S(2)}) %collective-permute-start.9) | collective-permute-done | bytes 524320 | tf_op jit(solution)/shard_map/ppermute | solution.py:14
  60.3 1.9 %constant_dynamic-update-slice_fusion = bf16[1024,2048]{1,0:T(8,128)(2,1)} fusion(bf16[1024,2048]{1,0:T(8,128)(2,1)} %get-tuple-element.18, bf16[128,2048]{1,0:T(8,128)(2,1)} %collective-permute-done.9), kind=kLoop, calls=%fused_computation.55 | loop fusion | bytes 1048576 | tf_op jit(solution)/shard_map/concatenate | solution.py:91
  62.2 3.7 %convolution_convert_fusion.10 = bf16[128,1024]{1,0:T(8,128)(2,1)S(1)} fusion(bf16[1024,2048]{1,0:T(8,128)(2,1)} %constant_dynamic-update-slice_fusion, bf16[128,1024]{1,0:T(8,128)(2,1)S(1)} %convolution_convert_fusion.4, bf16[128,1024]{1,0:T(8,128)(2,1)S(1)} %convolution_convert_fusion.5), kind=kOutput, calls=%fused_computation.14 | convolution fusion | flops 538050560 | bytes 4980736 | tf_op jit(solution)/shard_map/dot_general | solution.py:45
  65.9 3.7 %convolution_convert_fusion.9 = bf16[128,1024]{1,0:T(8,128)(2,1)S(1)} fusion(bf16[1024,2048]{1,0:T(8,128)(2,1)} %constant_dynamic-update-slice_fusion, bf16[128,1024]{1,0:T(8,128)(2,1)S(1)} %convolution_convert_fusion.2, bf16[128,1024]{1,0:T(8,128)(2,1)S(1)} %convolution_convert_fusion.3), kind=kOutput, calls=%fused_computation.13 | convolution fusion | flops 538050560 | bytes 4980736 | tf_op jit(solution)/shard_map/dot_general | solution.py:45
  69.7 1.8 %collective-permute-start.10 = (bf16[128,1024]{1,0:T(8,128)(2,1)S(1)}, bf16[128,1024]{1,0:T(8,128)(2,1)S(1)}, u32[]{:S(2)}, u32[]{:S(2)}) collective-permute-start(bf16[128,1024]{1,0:T(8,128)(2,1)S(1)} %convolution_convert_fusion.10), channel_id=1, source_target_pairs={{0,8},{4,12},{8,0},{12,4},{16,24},{20,28},{24,16},{28,20},{1,9},{5... | collective-permute-start | bytes 786440 | tf_op jit(solution)/shard_map/ppermute | solution.py:14
  71.4 1.5 %collective-permute-start.11 = (bf16[128,1024]{1,0:T(8,128)(2,1)S(1)}, bf16[128,1024]{1,0:T(8,128)(2,1)S(1)}, u32[]{:S(2)}, u32[]{:S(2)}) collective-permute-start(bf16[128,1024]{1,0:T(8,128)(2,1)S(1)} %convolution_convert_fusion.9), channel_id=1, source_target_pairs={{0,16},{4,20},{8,24},{12,28},{16,0},{20,4},{24,8},{28,12},{1,17},{... | collective-permute-start | bytes 786440 | tf_op jit(solution)/shard_map/ppermute | solution.py:14
  73.0 3.7 %convolution_convert_fusion.8 = bf16[128,1024]{1,0:T(8,128)(2,1)S(1)} fusion(bf16[1024,2048]{1,0:T(8,128)(2,1)} %constant_dynamic-update-slice_fusion, bf16[128,1024]{1,0:T(8,128)(2,1)S(1)} %convolution_convert_fusion, bf16[128,1024]{1,0:T(8,128)(2,1)S(1)} %copy-done.2), kind=kOutput, calls=%fused_computation.12 | convolution fusion | flops 538050560 | bytes 4980736 | tf_op jit(solution)/shard_map/dot_general | solution.py:45
  77.0 1.2 %collective-permute-done.10 = bf16[128,1024]{1,0:T(8,128)(2,1)S(1)} collective-permute-done((bf16[128,1024]{1,0:T(8,128)(2,1)S(1)}, bf16[128,1024]{1,0:T(8,128)(2,1)S(1)}, u32[]{:S(2)}, u32[]{:S(2)}) %collective-permute-start.10) | collective-permute-done | bytes 262176 | tf_op jit(solution)/shard_map/ppermute | solution.py:14
  78.4 5.9 %collective-permute-done.11 = bf16[128,1024]{1,0:T(8,128)(2,1)S(1)} collective-permute-done((bf16[128,1024]{1,0:T(8,128)(2,1)S(1)}, bf16[128,1024]{1,0:T(8,128)(2,1)S(1)}, u32[]{:S(2)}, u32[]{:S(2)}) %collective-permute-start.11) | collective-permute-done | bytes 262176 | tf_op jit(solution)/shard_map/ppermute | solution.py:14
  84.4 1.1 collective-permute-done.12
  86.5 3.9 %fusion.1 = f32[128,1024]{1,0:T(8,128)S(1)} fusion(bf16[1024,2048]{1,0:T(8,128)(2,1)} %constant_dynamic-update-slice_fusion, f32[16,8,8,128]{3,2,1,0:T(8,128)S(1)} %bitcast.73, f32[16,8,8,128]{3,2,1,0:T(8,128)S(1)} %bitcast.71, f32[16,8,8,128]{3,2,1,0:T(8,128)S(1)} %bitcast.72, bf16[128,1024]{1,0:T(8,128)(2,1)S(1)} %copy-done.4, ...), kind=kOutput, calls=%fused_computation.3 | convolution fusion | flops 538312704 | bytes 6815744 | tf_op jit(solution)/shard_map/dot_general | solution.py:45
  91.2 3.5 %collective-permute-start.14 = (bf16[32,1024]{1,0:T(8,128)(2,1)S(1)}, bf16[32,1024]{1,0:T(8,128)(2,1)S(1)}, u32[]{:S(2)}, u32[]{:S(2)}) collective-permute-start(bf16[32,1024]{1,0:T(8,128)(2,1)S(1)} %get-tuple-element.15), channel_id=1, source_target_pairs={{0,2},{1,3},{2,0},{3,1},{4,6},{5,7},{6,4},{7,5},{8,10},{9,11},{10,... | collective-permute-start | bytes 196616 | tf_op jit(solution)/shard_map/ppermute | solution.py:14
  95.3 3.1 %collective-permute-done.14.refs_2_ = bf16[32,1024]{1,0:T(8,128)(2,1)S(1)} collective-permute-done((bf16[32,1024]{1,0:T(8,128)(2,1)S(1)}, bf16[32,1024]{1,0:T(8,128)(2,1)S(1)}, u32[]{:S(2)}, u32[]{:S(2)}) %collective-permute-start.14) | collective-permute-done | bytes 65568 | tf_op jit(solution)/shard_map/ppermute | solution.py:14
  98.4 2.4 %collective-permute-done.15.refs_3_ = bf16[32,1024]{1,0:T(8,128)(2,1)S(1)} collective-permute-done((bf16[32,1024]{1,0:T(8,128)(2,1)S(1)}, bf16[32,1024]{1,0:T(8,128)(2,1)S(1)}, u32[]{:S(2)}, u32[]{:S(2)}) %collective-permute-start.15) | collective-permute-done | bytes 65568 | tf_op jit(solution)/shard_map/ppermute | solution.py:14
  101.7 1.4 %collective-permute-done.16 = f32[4,3,32,128]{3,2,1,0:T(8,128)S(1)} collective-permute-done((f32[4,3,32,128]{3,2,1,0:T(8,128)S(1)}, f32[4,3,32,128]{3,2,1,0:T(8,128)S(1)}, u32[]{:S(2)}, u32[]{:S(2)}) %collective-permute-start.16) | collective-permute-done | bytes 196640 | tf_op jit(solution)/shard_map/ppermute | solution.py:14
  103.1 1.0 collective-permute-start.17
  104.1 1.0 collective-permute-start.18
  105.1 1.6 %collective-permute-start.19 = (f32[2,3,32,128]{3,2,1,0:T(8,128)S(1)}, f32[2,3,32,128]{3,2,1,0:T(8,128)S(1)}, u32[]{:S(2)}, u32[]{:S(2)}) collective-permute-start(f32[2,3,32,128]{3,2,1,0:T(8,128)S(1)} %get-tuple-element.27), channel_id=1, source_target_pairs={{0,24},{4,28},{8,16},{12,20},{16,8},{20,12},{24,0},{28,4},{1,25},{... | collective-permute-start | bytes 294920 | tf_op jit(solution)/shard_map/ppermute | solution.py:14
  106.7 1.6 %collective-permute-done.17 = f32[2,3,32,128]{3,2,1,0:T(8,128)S(1)} collective-permute-done((f32[2,3,32,128]{3,2,1,0:T(8,128)S(1)}, f32[2,3,32,128]{3,2,1,0:T(8,128)S(1)}, u32[]{:S(2)}, u32[]{:S(2)}) %collective-permute-start.17) | collective-permute-done | bytes 98336 | tf_op jit(solution)/shard_map/ppermute | solution.py:14
  108.3 1.1 collective-permute-done.18
  109.4 1.6 %collective-permute-done.19 = f32[2,3,32,128]{3,2,1,0:T(8,128)S(1)} collective-permute-done((f32[2,3,32,128]{3,2,1,0:T(8,128)S(1)}, f32[2,3,32,128]{3,2,1,0:T(8,128)S(1)}, u32[]{:S(2)}, u32[]{:S(2)}) %collective-permute-start.19) | collective-permute-done | bytes 98336 | tf_op jit(solution)/shard_map/ppermute | solution.py:14
  (77 shorter events, 16.6 us)
Async XLA Ops:
  0.0 8.3 %copy-start = (bf16[1024,1024]{1,0:T(8,128)(2,1)S(1)}, bf16[1024,1024]{1,0:T(8,128)(2,1)}, u32[]{:S(2)}) copy-start(bf16[1024,1024]{1,0:T(8,128)(2,1)} %param.6) | copy-start | bytes 6291460
  0.0 58.3 %collective-permute-start = (s32[14]{0:T(128)}, s32[14]{0:T(128)S(1)}, u32[]{:S(2)}, u32[]{:S(2)}) collective-permute-start(s32[14]{0:T(128)} %bitcast.85), channel_id=1, source_target_pairs={{0,1},{1,0},{2,3},{3,2},{4,5},{5,4},{6,7},{7,6},{8,9},{9,8},{10,11... | collective-permute-start | bytes 176 | tf_op jit(solution)/shard_map/ppermute | solution.py:14
  3.0 55.3 %collective-permute-start.1 = (s32[14]{0:T(128)}, s32[14]{0:T(128)S(1)}, u32[]{:S(2)}, u32[]{:S(2)}) collective-permute-start(s32[14]{0:T(128)} %bitcast.86), channel_id=1, source_target_pairs={{0,2},{1,3},{2,0},{3,1},{4,6},{5,7},{6,4},{7,5},{8,10},{9,11},{10,... | collective-permute-start | bytes 176 | tf_op jit(solution)/shard_map/ppermute | solution.py:14
  5.6 52.7 %collective-permute-start.2 = (s32[14]{0:T(128)}, s32[14]{0:T(128)S(1)}, u32[]{:S(2)}, u32[]{:S(2)}) collective-permute-start(s32[14]{0:T(128)} %bitcast.87), channel_id=1, source_target_pairs={{0,3},{1,2},{2,1},{3,0},{4,7},{5,6},{6,5},{7,4},{8,11},{9,10},{10,... | collective-permute-start | bytes 176 | tf_op jit(solution)/shard_map/ppermute | solution.py:14
  8.3 4.5 %copy-start.7 = (s32[14,1]{0,1:T(1,128)S(1)}, s32[14,1]{0,1:T(1,128)}, u32[]{:S(2)}) copy-start(s32[14,1]{0,1:T(1,128)} %param.8) | copy-start | bytes 172
  9.1 0.8 copy-start.3
  10.0 1.1 copy-start.5
  11.1 16.9 %collective-permute-start.3 = (bf16[128,2048]{1,0:T(8,128)(2,1)}, bf16[128,2048]{1,0:T(8,128)(2,1)}, u32[]{:S(2)}, u32[]{:S(2)}) collective-permute-start(bf16[128,2048]{1,0:T(8,128)(2,1)} %get-tuple-element.23), channel_id=1, source_target_pairs={{0,4},{4,0},{8,12},{12,8},{16,20},{20,16},{24,28},{28,24},{1,5},{5... | collective-permute-start | bytes 1572872 | tf_op jit(solution)/shard_map/ppermute | solution.py:14
  11.1 14.3 %collective-permute-start.4 = (bf16[128,2048]{1,0:T(8,128)(2,1)S(1)}, bf16[128,2048]{1,0:T(8,128)(2,1)S(1)}, u32[]{:S(2)}, u32[]{:S(2)}) collective-permute-start(bf16[128,2048]{1,0:T(8,128)(2,1)S(1)} %get-tuple-element.11), channel_id=1, source_target_pairs={{0,8},{4,12},{8,0},{12,4},{16,24},{20,28},{24,16},{28,20},{1,9},{5... | collective-permute-start | bytes 1572872 | tf_op jit(solution)/shard_map/ppermute | solution.py:14
  25.5 25.0 %collective-permute-start.6 = (bf16[128,2048]{1,0:T(8,128)(2,1)}, bf16[128,2048]{1,0:T(8,128)(2,1)S(1)}, u32[]{:S(2)}, u32[]{:S(2)}) collective-permute-start(bf16[128,2048]{1,0:T(8,128)(2,1)} %get-tuple-element.13), channel_id=1, source_target_pairs={{0,16},{4,20},{8,24},{12,28},{16,0},{20,4},{24,8},{28,12},{1,17},{... | collective-permute-start | bytes 1572872 | tf_op jit(solution)/shard_map/ppermute | solution.py:14
  28.0 26.3 %collective-permute-start.8 = (bf16[128,2048]{1,0:T(8,128)(2,1)}, bf16[128,2048]{1,0:T(8,128)(2,1)S(1)}, u32[]{:S(2)}, u32[]{:S(2)}) collective-permute-start(bf16[128,2048]{1,0:T(8,128)(2,1)} %get-tuple-element.10), channel_id=1, source_target_pairs={{0,24},{4,28},{8,16},{12,20},{16,8},{20,12},{24,0},{28,4},{1,25},{... | collective-permute-start | bytes 1572872 | tf_op jit(solution)/shard_map/ppermute | solution.py:14
  50.5 1.9 %collective-permute-start.5 = (bf16[128,2048]{1,0:T(8,128)(2,1)S(1)}, bf16[128,2048]{1,0:T(8,128)(2,1)S(1)}, u32[]{:S(2)}, u32[]{:S(2)}) collective-permute-start(bf16[128,2048]{1,0:T(8,128)(2,1)S(1)} %get-tuple-element.21), channel_id=1, source_target_pairs={{0,4},{4,0},{8,12},{12,8},{16,20},{20,16},{24,28},{28,24},{1,5},{5... | collective-permute-start | bytes 1572872 | tf_op jit(solution)/shard_map/ppermute | solution.py:14
  54.1 4.2 %copy-start.9 = (s32[14,2]{0,1:T(2,128)S(1)}, s32[14,2]{0,1:T(2,128)}, u32[]{:S(2)}) copy-start(s32[14,2]{0,1:T(2,128)} %param.7) | copy-start | bytes 340
  54.1 4.2 %copy-start.8 = (s32[14,1]{0,1:T(1,128)S(1)}, s32[14,1]{0,1:T(1,128)}, u32[]{:S(2)}) copy-start(s32[14,1]{0,1:T(1,128)} %param.9) | copy-start | bytes 172
  54.1 2.0 %collective-permute-start.7 = (bf16[128,2048]{1,0:T(8,128)(2,1)S(1)}, bf16[128,2048]{1,0:T(8,128)(2,1)S(1)}, u32[]{:S(2)}, u32[]{:S(2)}) collective-permute-start(bf16[128,2048]{1,0:T(8,128)(2,1)S(1)} %get-tuple-element.19), channel_id=1, source_target_pairs={{0,4},{4,0},{8,12},{12,8},{16,20},{20,16},{24,28},{28,24},{1,5},{5... | collective-permute-start | bytes 1572872 | tf_op jit(solution)/shard_map/ppermute | solution.py:14
  56.1 0.9 copy-start.1
  58.1 2.3 %collective-permute-start.9 = (bf16[128,2048]{1,0:T(8,128)(2,1)}, bf16[128,2048]{1,0:T(8,128)(2,1)}, u32[]{:S(2)}, u32[]{:S(2)}) collective-permute-start(bf16[128,2048]{1,0:T(8,128)(2,1)} %get-tuple-element.17), channel_id=1, source_target_pairs={{0,4},{4,0},{8,12},{12,8},{16,20},{20,16},{24,28},{28,24},{1,5},{5... | collective-permute-start | bytes 1572872 | tf_op jit(solution)/shard_map/ppermute | solution.py:14
  62.2 10.8 %copy-start.2 = (bf16[128,1024]{1,0:T(8,128)(2,1)S(1)}, bf16[128,1024]{1,0:T(8,128)(2,1)}, u32[]{:S(2)}) copy-start(bf16[128,1024]{1,0:T(8,128)(2,1)} %copy-done.1) | copy-start | bytes 786436
  69.6 16.9 %copy-start.4 = (bf16[128,1024]{1,0:T(8,128)(2,1)S(1)}, bf16[128,1024]{1,0:T(8,128)(2,1)}, u32[]{:S(2)}) copy-start(bf16[128,1024]{1,0:T(8,128)(2,1)} %copy-done.3) | copy-start | bytes 786436
  69.6 16.9 %copy-start.6 = (bf16[128,1024]{1,0:T(8,128)(2,1)S(1)}, bf16[128,1024]{1,0:T(8,128)(2,1)}, u32[]{:S(2)}) copy-start(bf16[128,1024]{1,0:T(8,128)(2,1)} %copy-done.5) | copy-start | bytes 786436
  69.7 8.5 %collective-permute-start.10 = (bf16[128,1024]{1,0:T(8,128)(2,1)S(1)}, bf16[128,1024]{1,0:T(8,128)(2,1)S(1)}, u32[]{:S(2)}, u32[]{:S(2)}) collective-permute-start(bf16[128,1024]{1,0:T(8,128)(2,1)S(1)} %convolution_convert_fusion.10), channel_id=1, source_target_pairs={{0,8},{4,12},{8,0},{12,4},{16,24},{20,28},{24,16},{28,20},{1,9},{5... | collective-permute-start | bytes 786440 | tf_op jit(solution)/shard_map/ppermute | solution.py:14
  71.4 12.9 %collective-permute-start.11 = (bf16[128,1024]{1,0:T(8,128)(2,1)S(1)}, bf16[128,1024]{1,0:T(8,128)(2,1)S(1)}, u32[]{:S(2)}, u32[]{:S(2)}) collective-permute-start(bf16[128,1024]{1,0:T(8,128)(2,1)S(1)} %convolution_convert_fusion.9), channel_id=1, source_target_pairs={{0,16},{4,20},{8,24},{12,28},{16,0},{20,4},{24,8},{28,12},{1,17},{... | collective-permute-start | bytes 786440 | tf_op jit(solution)/shard_map/ppermute | solution.py:14
  76.7 8.8 %collective-permute-start.12 = (bf16[128,1024]{1,0:T(8,128)(2,1)S(1)}, bf16[128,1024]{1,0:T(8,128)(2,1)S(1)}, u32[]{:S(2)}, u32[]{:S(2)}) collective-permute-start(bf16[128,1024]{1,0:T(8,128)(2,1)S(1)} %convolution_convert_fusion.8), channel_id=1, source_target_pairs={{0,24},{4,28},{8,16},{12,20},{16,8},{20,12},{24,0},{28,4},{1,25},{... | collective-permute-start | bytes 786440 | tf_op jit(solution)/shard_map/ppermute | solution.py:14
  90.5 4.8 %collective-permute-start.13 = (bf16[32,1024]{1,0:T(8,128)(2,1)S(1)}, bf16[32,1024]{1,0:T(8,128)(2,1)S(1)}, u32[]{:S(2)}, u32[]{:S(2)}) collective-permute-start(bf16[32,1024]{1,0:T(8,128)(2,1)S(1)} %get-tuple-element.16), channel_id=1, source_target_pairs={{0,1},{1,0},{2,3},{3,2},{4,5},{5,4},{6,7},{7,6},{8,9},{9,8},{10,11... | collective-permute-start | bytes 196616 | tf_op jit(solution)/shard_map/ppermute | solution.py:14
  91.2 7.1 %collective-permute-start.14 = (bf16[32,1024]{1,0:T(8,128)(2,1)S(1)}, bf16[32,1024]{1,0:T(8,128)(2,1)S(1)}, u32[]{:S(2)}, u32[]{:S(2)}) collective-permute-start(bf16[32,1024]{1,0:T(8,128)(2,1)S(1)} %get-tuple-element.15), channel_id=1, source_target_pairs={{0,2},{1,3},{2,0},{3,1},{4,6},{5,7},{6,4},{7,5},{8,10},{9,11},{10,... | collective-permute-start | bytes 196616 | tf_op jit(solution)/shard_map/ppermute | solution.py:14
  94.7 6.1 %collective-permute-start.15 = (bf16[32,1024]{1,0:T(8,128)(2,1)S(1)}, bf16[32,1024]{1,0:T(8,128)(2,1)S(1)}, u32[]{:S(2)}, u32[]{:S(2)}) collective-permute-start(bf16[32,1024]{1,0:T(8,128)(2,1)S(1)} %get-tuple-element.14), channel_id=1, source_target_pairs={{0,3},{1,2},{2,1},{3,0},{4,7},{5,6},{6,5},{7,4},{8,11},{9,10},{10,... | collective-permute-start | bytes 196616 | tf_op jit(solution)/shard_map/ppermute | solution.py:14
  101.6 1.5 %collective-permute-start.16 = (f32[4,3,32,128]{3,2,1,0:T(8,128)S(1)}, f32[4,3,32,128]{3,2,1,0:T(8,128)S(1)}, u32[]{:S(2)}, u32[]{:S(2)}) collective-permute-start(f32[4,3,32,128]{3,2,1,0:T(8,128)S(1)} %get-tuple-element.30), channel_id=1, source_target_pairs={{0,4},{4,0},{8,12},{12,8},{16,20},{20,16},{24,28},{28,24},{1,5},{5... | collective-permute-start | bytes 589832 | tf_op jit(solution)/shard_map/ppermute | solution.py:14
  103.1 5.2 %collective-permute-start.17 = (f32[2,3,32,128]{3,2,1,0:T(8,128)S(1)}, f32[2,3,32,128]{3,2,1,0:T(8,128)S(1)}, u32[]{:S(2)}, u32[]{:S(2)}) collective-permute-start(f32[2,3,32,128]{3,2,1,0:T(8,128)S(1)} %get-tuple-element.26), channel_id=1, source_target_pairs={{0,8},{4,12},{8,0},{12,4},{16,24},{20,28},{24,16},{28,20},{1,9},{5... | collective-permute-start | bytes 294920 | tf_op jit(solution)/shard_map/ppermute | solution.py:14
  104.1 5.2 %collective-permute-start.18 = (f32[2,3,32,128]{3,2,1,0:T(8,128)S(1)}, f32[2,3,32,128]{3,2,1,0:T(8,128)S(1)}, u32[]{:S(2)}, u32[]{:S(2)}) collective-permute-start(f32[2,3,32,128]{3,2,1,0:T(8,128)S(1)} %get-tuple-element.28), channel_id=1, source_target_pairs={{0,16},{4,20},{8,24},{12,28},{16,0},{20,4},{24,8},{28,12},{1,17},{... | collective-permute-start | bytes 294920 | tf_op jit(solution)/shard_map/ppermute | solution.py:14
  105.1 5.9 %collective-permute-start.19 = (f32[2,3,32,128]{3,2,1,0:T(8,128)S(1)}, f32[2,3,32,128]{3,2,1,0:T(8,128)S(1)}, u32[]{:S(2)}, u32[]{:S(2)}) collective-permute-start(f32[2,3,32,128]{3,2,1,0:T(8,128)S(1)} %get-tuple-element.27), channel_id=1, source_target_pairs={{0,24},{4,28},{8,16},{12,20},{16,8},{20,12},{24,0},{28,4},{1,25},{... | collective-permute-start | bytes 294920 | tf_op jit(solution)/shard_map/ppermute | solution.py:14

commit v2 on v0

v2 whole, which is shorter than its diff:
```python
import functools

import jax
import jax.numpy as jnp
from jax import lax
from jax.experimental import pallas as pl
from jax.experimental.pallas import tpu as pltpu
from jax.sharding import PartitionSpec as P

TILE = 128
CORES = 2
MIB = 1024 * 1024
SMEM = pl.BlockSpec(memory_space=pltpu.SMEM)
VMEM = pl.BlockSpec(memory_space=pltpu.VMEM)


def swapped(value, axis, distance):
    count = lax.axis_size(axis)
    return lax.ppermute(value, axis, [(source, source ^ distance) for source in range(count)])


def shaped(shape, dtype):
    return jax.ShapeDtypeStruct(shape, dtype)


def kept(shape, dtype):
    return pltpu.VMEM(shape, dtype)


def kernel_call(body, ins, outs, out_specs, grant, scratch=()):
    return pl.pallas_call(
        body,
        out_shape=outs,
        in_specs=ins,
        out_specs=out_specs,
        scratch_shapes=scratch,
        compiler_params=pltpu.CompilerParams(vmem_limit_bytes=grant * MIB),
    )


def contract(left, right):
    return lax.dot_general(
        left, right, (((1,), (1,)), ((), ())), preferred_element_type=jnp.float32
    )


def columns(refs, start, size):
    width = refs[0].shape[1]
    return refs[start // width][:, start % width : start % width + size]


def gram(left, right):
    size = min(left[0].shape[1], right[0].shape[1])
    whole = len(left) * left[0].shape[1]
    return sum(
        contract(columns(left, at, size), columns(right, at, size))
        for at in range(0, whole, size)
    )


def unpack(refs, counts):
    groups, at = [], 0
    for count in counts:
        groups.append(refs[at : at + count])
        at += count
    return groups


def fit_kernel(count, *refs):
    panels, metric_ref, outs = refs[:count], refs[count], refs[count + 1 :]
    naux = metric_ref.shape[0]
    rows, width = panels[0].shape
    size = outs[0].shape[1]
    starts = range(0, width, naux)
    stacked = jnp.concatenate([ref[:, at : at + naux] for ref in panels for at in starts], axis=0)
    fitted = contract(stacked, metric_ref[...]).astype(jnp.bfloat16)
    for index in range(count):
        for number, out_ref in enumerate(outs):
            at = number * size
            for start in range(at, at + size, min(size, naux)):
                top = (index * len(starts) + start // naux) * rows
                from_column = start % naux
                span = min(size, naux)
                out_ref[index * rows : (index + 1) * rows, start - at : start - at + span] = fitted[
                    top : top + rows, from_column : from_column + span
                ]


def fit(panels, metric, pieces):
    rows, width = panels[0].shape
    rows_out = rows * len(panels)
    return kernel_call(
        functools.partial(fit_kernel, len(panels)),
        [VMEM] * (len(panels) + 1),
        [kept((rows_out, width // pieces), jnp.bfloat16)] * pieces,
        [VMEM] * pieces,
        8,
    )(*panels, metric)


def place(block, chip):
    spot = ((block ^ (CORES * chip)) - 1) * TILE
    return slice(spot, spot + TILE)


def put(slabs, chip, block, tile):
    if block != CORES * chip:
        slabs[chip][:, place(block, chip)] = tile.astype(slabs[chip].dtype)


def part(value, row, column):
    return value[row * TILE : (row + 1) * TILE, column * TILE : (column + 1) * TILE]


def early_kernel(counts, *refs):
    own, own_beside, others, others_beside, slabs = unpack(refs, counts)
    count = others[0].shape[0] // TILE
    put(slabs, 0, 1, gram(own, own_beside))
    outer = gram(others, own_beside)
    across = gram(own, others)
    beside = gram(own, others_beside)
    inner = gram(others, others)
    sideways = gram(others, others_beside)
    for at in range(count):
        chip = at + 1
        put(slabs, 0, CORES * chip, part(across, 0, at))
        put(slabs, 0, CORES * chip + 1, part(beside, 0, at))
        put(slabs, chip, 0, part(across, 0, at).T)
        put(slabs, chip, 1, part(outer, at, 0))
        for other in range(count):
            put(slabs, chip, CORES * (other + 1), part(inner, at, other))
            put(slabs, chip, CORES * (other + 1) + 1, part(sideways, at, other))


def early(own, own_beside, others, others_beside):
    rows = own[0].shape[0]
    chips = others[0].shape[0] // rows + 2
    span = (CORES * chips - 1) * TILE
    given = [own, own_beside, others, others_beside]
    counts = [len(pieces) for pieces in given] + [chips - 1]
    return kernel_call(
        functools.partial(early_kernel, counts),
        [VMEM] * sum(counts[:-1]),
        [kept((rows, span), jnp.bfloat16 if chip else jnp.float32) for chip in range(chips - 1)],
        [VMEM] * (chips - 1),
        12,
    )(*[piece for pieces in given for piece in pieces])


def middle_kernel(counts, *refs):
    last, own, own_beside, others, others_beside, (out_ref,) = unpack(refs, counts)
    half = others[0].shape[0]
    out_ref[:, :TILE] = gram(last, own)
    out_ref[:, TILE : 2 * TILE] = gram(last, own_beside)
    out_ref[:, 2 * TILE : 2 * TILE + half] = gram(last, others)
    out_ref[:, 2 * TILE + half :] = gram(last, others_beside)


def middle(last, own, own_beside, others, others_beside):
    rows = last[0].shape[0]
    span = 2 * (rows + others[0].shape[0])
    given = [last, own, own_beside, others, others_beside]
    counts = [len(pieces) for pieces in given] + [1]
    return kernel_call(
        functools.partial(middle_kernel, counts),
        [VMEM] * sum(counts[:-1]),
        kept((rows, span), jnp.float32),
        VMEM,
        8,
    )(*[piece for pieces in given for piece in pieces])


def late_kernel(counts, *refs):
    last, last_beside, own, others, (middle_ref,), begun, slabs = unpack(refs, counts)
    count = others[0].shape[0] // TILE
    final = count + 1
    for chip in range(final):
        slabs[chip][:, : begun[chip].shape[1]] = begun[chip][...]
    tall = gram(others, last_beside)
    put(slabs, 0, CORES * final + 1, gram(own, last_beside))
    put(slabs, final, CORES * final + 1, gram(last, last_beside))
    for core in range(CORES):
        put(slabs, final, core, middle_ref[:, core * TILE : (core + 1) * TILE])
        for at in range(count):
            spot = (CORES + core * count + at) * TILE
            put(slabs, final, CORES * (at + 1) + core, middle_ref[:, spot : spot + TILE])
    put(slabs, 0, CORES * final, middle_ref[:, :TILE].T)
    for at in range(count):
        spot = (CORES + at) * TILE
        put(slabs, at + 1, CORES * final, middle_ref[:, spot : spot + TILE].T)
        put(slabs, at + 1, CORES * final + 1, part(tall, at, 0))


def late(last, last_beside, own, others, across, begun):
    rows = own[0].shape[0]
    chips = len(begun) + 1
    span = (CORES * chips - 1) * TILE
    given = [last, last_beside, own, others, [across], begun]
    counts = [len(pieces) for pieces in given] + [chips]
    return kernel_call(
        functools.partial(late_kernel, counts),
        [VMEM] * sum(counts[:-1]),
        [kept((rows, span), jnp.bfloat16 if chip else jnp.float32) for chip in range(chips)],
        [VMEM] * chips,
        12,
    )(*[piece for pieces in given for piece in pieces])


def strips_kernel(starts_ref, weights_ref, own_ref, *refs):
    groups = starts_ref.shape[0]
    came, strips = refs[:-groups], refs[-groups:]
    share = strips[0].shape[0]
    span = own_ref.shape[1]
    for distance, strip in enumerate(strips):
        rows = pl.ds(pl.multiple_of(starts_ref[distance], share), share)
        total = own_ref[rows, :]
        for ref in came:
            total = total + ref[rows, :].astype(jnp.float32)
        strip[:, :span] = total.astype(strip.dtype)
        strip[:, span:] = weights_ref[...].astype(strip.dtype)


def strips(own, came, starts, weights):
    groups = starts.shape[0]
    rows, span = own.shape
    share = rows // groups
    whole = span + weights.shape[1]
    return kernel_call(
        strips_kernel,
        [SMEM] + [VMEM] * (2 + len(came)),
        [shaped((share, whole), jnp.bfloat16 if at else jnp.float32) for at in range(groups)],
        [VMEM] * groups,
        8,
    )(starts, weights, own, *came)


def combine_kernel(span, block_ref, *refs):
    chunks, outs = refs[:-CORES], refs[-CORES:]
    chips, slots, share = outs[0].shape[:3]
    weights = [chunk[:, span:].astype(jnp.float32) for chunk in chunks]
    for chip in range(chips):
        for core, out_ref in enumerate(outs):
            for slot in range(slots):
                at = (chip * CORES + core) * slots + slot
                start = pl.multiple_of(block_ref[at] * TILE, TILE)
                row, lanes = at % share, at // share * TILE
                total = jnp.zeros((share, TILE), jnp.float32)
                for chunk, weight in zip(chunks, weights, strict=True):
                    scale = weight[row : row + 1, lanes : lanes + TILE]
                    total = total + scale * chunk[:, pl.ds(start, TILE)].astype(jnp.float32)
                out_ref[chip, slot] = total


def combine(blocks, chunks, span, chips, slots):
    share = chunks[0].shape[0]
    return kernel_call(
        functools.partial(combine_kernel, span),
        [SMEM] + [VMEM] * len(chunks),
        [shaped((chips, slots, share, TILE), jnp.float32)] * CORES,
        [VMEM] * CORES,
        8,
    )(blocks, *chunks)


def settle_kernel(mine_ref, *refs):
    pieces, out_ref = refs[:-1], refs[-1]
    mine = mine_ref[0]
    for chip, piece in enumerate(pieces):
        for core in range(CORES):
            out_ref[mine ^ (chip * CORES + core)] = piece[core]


def settle(mine, pieces):
    shape = (CORES * len(pieces), *pieces[0].shape[1:])
    return kernel_call(
        settle_kernel,
        [SMEM] + [VMEM] * len(pieces),
        shaped(shape, jnp.float32),
        VMEM,
        8,
    )(mine, *pieces)


def per_device(raw_panels, metric, tile_pairs, owners, group_mask):
    raw = raw_panels[0]
    rows, columns = raw.shape
    cycle = lax.axis_size("blk")
    groups = lax.axis_size("grp")
    chips = cycle // CORES
    width = columns // chips
    mine = lax.axis_index("blk")
    my_group = lax.axis_index("grp")
    tile_count = tile_pairs.shape[0]
    capacity = max(2, 2 * tile_count // cycle)
    final = chips - 1
    share = rows // groups

    def piece(source, chip):
        start = ((mine // CORES) ^ chip) * width
        return lax.dynamic_slice(source, (jnp.int32(0), start), (rows, width))

    def beside(pieces):
        return [swapped(piece, "blk", 1) for piece in pieces]

    pieces = [piece(raw, chip) for chip in range(1, final)]
    arrived = [swapped(value, "blk", CORES * (at + 1)) for at, value in enumerate(pieces)]
    raw = lax.optimization_barrier((raw, *pieces))[0]
    own = fit([piece(raw, 0)], metric, 2)
    own_beside = beside(own)
    last_piece = lax.optimization_barrier((piece(raw, final), *own_beside))[0]
    last = swapped(last_piece, "blk", CORES * final)

    others = fit(arrived, metric, 4)
    others_beside = beside(others)
    begun = early(own, own_beside, others, others_beside)

    own_mask, pairs, owner_ids = lax.optimization_barrier(
        (group_mask[:, 0], tile_pairs, owners[:, 0], *own)
    )[:3]
    owner_ids = owner_ids ^ mine
    hits = (owner_ids[:, None] == jnp.arange(cycle)[None, :]).astype(jnp.int32)
    before = jnp.cumsum(hits, axis=0) - hits
    slots = jnp.sum(before * hits, axis=1)
    places = owner_ids * capacity + slots
    taken = (places[None, :] == jnp.arange(cycle * capacity)[:, None]).astype(jnp.int32)
    blocks = jnp.maximum(jnp.sum(taken * (pairs[:, 1] ^ mine)[None, :], axis=1) - 1, 0)
    weights = jnp.sum(taken * own_mask[None, :], axis=1).astype(jnp.float32)
    tall = -(-weights.shape[0] // share) * share
    weights = jnp.pad(weights, (0, tall - weights.shape[0])).reshape(-1, share).T
    weights = jnp.repeat(weights, TILE, axis=1)

    last, blocks, weights = lax.optimization_barrier((last, blocks, weights, *begun))[:3]
    last_fitted = fit([last], metric, 2)
    last_beside = beside(last_fitted)
    across = middle(last_fitted, own, own_beside, others, others_beside)
    slabs = late(last_fitted, last_beside, own, others, across, begun)

    came = [swapped(slabs[chip], "blk", CORES * chip) for chip in range(1, chips)]
    strip_starts = (my_group ^ jnp.arange(groups, dtype=jnp.int32)) * share
    own_strips = strips(slabs[0], came, strip_starts, weights)
    chunks = [own_strips[0]] + [swapped(own_strips[d], "grp", d) for d in range(1, groups)]

    straight, crossing = combine(blocks, chunks, slabs[0].shape[1], chips, capacity)
    crossed = swapped(crossing, "blk", 1)
    paired = jnp.stack([straight, crossed], axis=1)
    received = [paired[0]] + [
        swapped(paired[chip], "blk", CORES * chip) for chip in range(1, chips)
    ]
    return settle(mine[None], received)[None]


def solution(mesh):
    placed = (P("grp", "blk", None), P(), P("blk", None), P("blk", None), P("blk", "grp"))
    return jax.shard_map(
        per_device,
        mesh=mesh,
        in_specs=placed,
        out_specs=P("blk", None, None, "grp", None),
        check_vma=False,
    )
```

time: 328 us -> 69.8 us (0.21)
  waiting for transfers between devices: 222 us -> 36.4 us
  local copies, waits for them, and re-layouts: 39.1 us -> 4.68 us
  blocking collectives: 25.3 us -> 0 us
  matrix products: 24.3 us -> 0 us
  starting transfers between devices: 0.86 us -> 18.3 us
  between operations: 13.5 us -> 0.15 us
  Pallas kernels: 0 us -> 9.72 us
    ppermute x7 -> x21, waiting for transfers between devices: 187 us -> 36.4 us  [swapped(): lax.ppermute(value, axis, [(source, source ^ distance) for source in rang...]
    reduce_scatter x1 -> x0, waiting for transfers between devices: 35.6 us -> none  [per_device(): summed = lax.psum_scatter(arrived, 'grp', scatter_dimension=2, tiled=True)]
    all_to_all x1 -> x0, blocking collectives: 25.3 us -> none  [per_device(): lax.all_to_all(outgoing, 'blk', split_axis=0, concat_axis=0, tiled=True)]
    dot_general x9 -> x0, matrix products: 24.3 us -> none  [the longest x8 19 us: place(): lax.dot_general(panel, visiting, (((1,), (1,)), ((), ())), preferred_elem...]
    while x22 -> x0, local copies, waits for them, and re-layouts: 21.9 us -> none
    ppermute x7 -> x21, starting transfers between devices: 0.86 us -> 18.3 us  [swapped(): lax.ppermute(value, axis, [(source, source ^ distance) for source in rang...]
    pallas_call x0 -> x9, Pallas kernels: none -> 9.72 us  [the longest x3 3.96 us: fit(): kernel_call(functools.partial(fit_kernel, len(panels)), [VMEM] * (len(pan...]
    dynamic_slice x0 -> x2, local copies, waits for them, and re-layouts: none -> 4.59 us  [piece(): return lax.dynamic_slice(source, (jnp.int32(0), start), (rows, width))]
  transfers between devices with their start and end apart: 8 -> 21, of which waited for: 8 -> 19; matrix products, arithmetic and copies ran while one was open for 0% -> 4% of each run, Pallas kernels for 0% -> 9%
where the time goes in v2:
time: 69.8 us; the launch traced here: 69.6 us
  waiting for transfers between devices  36.4 us (52%)
  starting transfers between devices  18.3 us (26%)
  Pallas kernels  9.72 us (14%)
  local copies, waits for them, and re-layouts  4.68 us (7%)
    ppermute x21, waiting for transfers between devices, swapped(): lax.ppermute(value, axis, [(source, source ^ distance) for source in rang...  36.4 us
    ppermute x21, starting transfers between devices, swapped(): lax.ppermute(value, axis, [(source, source ^ distance) for source in rang...  18.3 us
    dynamic_slice x2, local copies, waits for them, and re-layouts, piece(): return lax.dynamic_slice(source, (jnp.int32(0), start), (rows, width))  4.59 us
    pallas_call x3, Pallas kernels, fit(): kernel_call(functools.partial(fit_kernel, len(panels)), [VMEM] * (len(pan...  3.96 us
    pallas_call x1, Pallas kernels, early(): kernel_call(functools.partial(early_kernel, counts), [VMEM] * sum(counts[...  1.79 us
  transfers between devices with their start and end apart: 21, of which 19 were waited for; matrix products, arithmetic and copies ran while one was open for 4% of the time, Pallas kernels for 9%

profile of v2, /device:TPU:0, one launch (start us, length us, event | category | flops | bytes accessed | tf_op | source)
XLA Modules:
  0.0 69.6 jit_solution(17082856629279873375)
XLA Ops:
  0.0 2.5 %dynamic-slice_bitcast_fusion = (bf16[128,2048]{1,0:T(8,128)(2,1)}, bf16[128,2048]{1,0:T(8,128)(2,1)}) fusion(bf16[1,128,8192]{2,1,0:T(8,128)(2,1)} %param.5, s32[]{:T(128)S(6)} %select_n.22, s32[]{:T(128)S(6)} %select_n.21), kind=kLoop, calls=%fused_computation.6 | loop fusion | bytes 2097160 | tf_op jit(solution)/shard_map/dynamic_slice | solution.py:300
  2.5 3.0 %collective-permute-start.4 = (bf16[128,2048]{1,0:T(8,128)(2,1)}, bf16[128,2048]{1,0:T(8,128)(2,1)}, u32[]{:S(2)}, u32[]{:S(2)}) collective-permute-start(bf16[128,2048]{1,0:T(8,128)(2,1)} %get-tuple-element.67), channel_id=1, source_target_pairs={{0,16},{4,20},{8,24},{12,28},{16,0},{20,4},{24,8},{28,12},{1,17},{... | collective-permute-start | bytes 1572872 | tf_op jit(solution)/shard_map/ppermute | solution.py:19
  5.4 1.5 %collective-permute-start.3 = (bf16[128,2048]{1,0:T(8,128)(2,1)}, bf16[128,2048]{1,0:T(8,128)(2,1)}, u32[]{:S(2)}, u32[]{:S(2)}) collective-permute-start(bf16[128,2048]{1,0:T(8,128)(2,1)} %get-tuple-element.68), channel_id=1, source_target_pairs={{0,8},{4,12},{8,0},{12,4},{16,24},{20,28},{24,16},{28,20},{1,9},{5... | collective-permute-start | bytes 1572872 | tf_op jit(solution)/shard_map/ppermute | solution.py:19
  6.9 2.1 %constant_dynamic-slice_fusion = (bf16[128,2048]{1,0:T(8,128)(2,1)S(1)}, bf16[128,2048]{1,0:T(8,128)(2,1)}) fusion(bf16[128,8192]{1,0:T(8,128)(2,1)} %bitcast.22, s32[]{:T(128)S(6)} %select_n.24, s32[]{:T(128)S(6)} %select_n.23), kind=kLoop, calls=%fused_computation.22 | loop fusion | bytes 2097160 | tf_op jit(solution)/shard_map/dynamic_slice | solution.py:300
  9.1 0.7 %shard_map.55 = (bf16[128,1024]{1,0:T(8,128)(2,1)S(1)}, bf16[128,1024]{1,0:T(8,128)(2,1)S(1)}) custom-call(bf16[128,2048]{1,0:T(8,128)(2,1)S(1)} %get-tuple-element.65.refs_0_, bf16[1024,1024]{1,0:T(8,128)(2,1)S(1)} %copy-done), custom_call_target="tpu_custom_call" | custom-call | tf_op jit(solution)/shard_map/pallas_call | solution.py:92
  10.6 0.8 %collective-permute-done.refs_2_.refs_4_ = bf16[128,1024]{1,0:T(8,128)(2,1)S(1)} collective-permute-done((bf16[128,1024]{1,0:T(8,128)(2,1)S(1)}, bf16[128,1024]{1,0:T(8,128)(2,1)S(1)}, u32[]{:S(2)}, u32[]{:S(2)}) %collective-permute-start) | collective-permute-done | bytes 262176 | tf_op jit(solution)/shard_map/ppermute | solution.py:19
  11.8 5.9 %collective-permute-done.4.refs_1_ = bf16[128,2048]{1,0:T(8,128)(2,1)} collective-permute-done((bf16[128,2048]{1,0:T(8,128)(2,1)}, bf16[128,2048]{1,0:T(8,128)(2,1)}, u32[]{:S(2)}, u32[]{:S(2)}) %collective-permute-start.4) | collective-permute-done | bytes 524320 | tf_op jit(solution)/shard_map/ppermute | solution.py:19
  17.7 2.9 %collective-permute-done.3.refs_0_ = bf16[128,2048]{1,0:T(8,128)(2,1)} collective-permute-done((bf16[128,2048]{1,0:T(8,128)(2,1)}, bf16[128,2048]{1,0:T(8,128)(2,1)}, u32[]{:S(2)}, u32[]{:S(2)}) %collective-permute-start.3) | collective-permute-done | bytes 524320 | tf_op jit(solution)/shard_map/ppermute | solution.py:19
  20.6 2.5 %shard_map.56 = (bf16[256,512]{1,0:T(8,128)(2,1)S(1)}, bf16[256,512]{1,0:T(8,128)(2,1)S(1)}, bf16[256,512]{1,0:T(8,128)(2,1)S(1)}, bf16[256,512]{1,0:T(8,128)(2,1)S(1)}) custom-call(bf16[128,2048]{1,0:T(8,128)(2,1)} %collective-permute-done.3.refs_0_, bf16[128,2048]{1,0:T(8,128)(2,1)} %collective-permute-done.4.refs_1_, bf16[1024,1024]{1,0:T(8,128)(2,1)S(1)} %copy-done), custom_call_target="tpu_custom_call" | custom-call | tf_op jit(solution)/shard_map/pallas_call | solution.py:92
  25.8 1.8 %shard_map.57 = (f32[128,896]{1,0:T(8,128)S(1)}, bf16[128,896]{1,0:T(8,128)(2,1)S(1)}, bf16[128,896]{1,0:T(8,128)(2,1)S(1)}) custom-call(bf16[128,1024]{1,0:T(8,128)(2,1)S(1)} %get-tuple-element.35.refs_0_.refs_2_.refs_4_, bf16[128,1024]{1,0:T(8,128)(2,1)S(1)} %get-tuple-element.36.refs_1_.refs_3_.refs_5_, ...), custom_call_target="tpu_custom_call" | custom-call | tf_op jit(solution)/shard_map/pallas_call | solution.py:141
  27.6 2.4 %collective-permute-done.2.refs_0_ = bf16[128,2048]{1,0:T(8,128)(2,1)S(1)} collective-permute-done((bf16[128,2048]{1,0:T(8,128)(2,1)}, bf16[128,2048]{1,0:T(8,128)(2,1)S(1)}, u32[]{:S(2)}, u32[]{:S(2)}) %collective-permute-start.2) | collective-permute-done | bytes 524320 | tf_op jit(solution)/shard_map/ppermute | solution.py:19
  30.1 0.7 %shard_map.58 = (bf16[128,1024]{1,0:T(8,128)(2,1)S(1)}, bf16[128,1024]{1,0:T(8,128)(2,1)S(1)}) custom-call(bf16[128,2048]{1,0:T(8,128)(2,1)S(1)} %collective-permute-done.2.refs_0_, bf16[1024,1024]{1,0:T(8,128)(2,1)S(1)} %copy-done), custom_call_target="tpu_custom_call" | custom-call | tf_op jit(solution)/shard_map/pallas_call | solution.py:92
  31.4 1.1 %shard_map.59.refs_10_ = f32[128,768]{1,0:T(8,128)S(1)} custom-call(bf16[128,1024]{1,0:T(8,128)(2,1)S(1)} %get-tuple-element.51.refs_0_, bf16[128,1024]{1,0:T(8,128)(2,1)S(1)} %get-tuple-element.52.refs_1_, bf16[128,1024]{1,0:T(8,128)(2,1)S(1)} %get-tuple-element.35.refs_0_.refs_2_.refs_4_, bf16[128,1024]{1,0:T(8,128)(2,1)S(1)} %get-tuple-element.36.refs_1_.refs_3_.refs_5_, ...), custom_call_target="tpu_custom_call" | custom-call | tf_op jit(solution)/shard_map/pallas_call | solution.py:164
  32.8 0.7 %shard_map.60 = (f32[128,896]{1,0:T(8,128)S(1)}, bf16[128,896]{1,0:T(8,128)(2,1)S(1)}, bf16[128,896]{1,0:T(8,128)(2,1)S(1)}, bf16[128,896]{1,0:T(8,128)(2,1)S(1)}) custom-call(bf16[128,1024]{1,0:T(8,128)(2,1)S(1)} %get-tuple-element.51.refs_0_, bf16[128,1024]{1,0:T(8,128)(2,1)S(1)} %get-tuple-element.52.refs_1_, ...), custom_call_target="tpu_custom_call" | custom-call | tf_op jit(solution)/shard_map/pallas_call | solution.py:200
  33.5 1.8 %collective-permute-start.11 = (bf16[128,896]{1,0:T(8,128)(2,1)S(1)}, bf16[128,896]{1,0:T(8,128)(2,1)S(1)}, u32[]{:S(2)}, u32[]{:S(2)}) collective-permute-start(bf16[128,896]{1,0:T(8,128)(2,1)S(1)} %get-tuple-element.54), channel_id=1, source_target_pairs={{0,8},{4,12},{8,0},{12,4},{16,24},{20,28},{24,16},{28,20},{1,9},{5... | collective-permute-start | bytes 688136 | tf_op jit(solution)/shard_map/ppermute | solution.py:19
  35.3 1.5 %collective-permute-start.12 = (bf16[128,896]{1,0:T(8,128)(2,1)S(1)}, bf16[128,896]{1,0:T(8,128)(2,1)S(1)}, u32[]{:S(2)}, u32[]{:S(2)}) collective-permute-start(bf16[128,896]{1,0:T(8,128)(2,1)S(1)} %get-tuple-element.55), channel_id=1, source_target_pairs={{0,16},{4,20},{8,24},{12,28},{16,0},{20,4},{24,8},{28,12},{1,17},{... | collective-permute-start | bytes 688136 | tf_op jit(solution)/shard_map/ppermute | solution.py:19
  37.1 5.0 %collective-permute-done.11.refs_0_ = bf16[128,896]{1,0:T(8,128)(2,1)S(1)} collective-permute-done((bf16[128,896]{1,0:T(8,128)(2,1)S(1)}, bf16[128,896]{1,0:T(8,128)(2,1)S(1)}, u32[]{:S(2)}, u32[]{:S(2)}) %collective-permute-start.11) | collective-permute-done | bytes 229408 | tf_op jit(solution)/shard_map/ppermute | solution.py:19
  42.0 5.5 %collective-permute-done.12.refs_1_ = bf16[128,896]{1,0:T(8,128)(2,1)S(1)} collective-permute-done((bf16[128,896]{1,0:T(8,128)(2,1)S(1)}, bf16[128,896]{1,0:T(8,128)(2,1)S(1)}, u32[]{:S(2)}, u32[]{:S(2)}) %collective-permute-start.12) | collective-permute-done | bytes 229408 | tf_op jit(solution)/shard_map/ppermute | solution.py:19
  47.6 0.7 shard_map.61
  48.2 1.6 %collective-permute-start.14 = (bf16[32,1024]{1,0:T(8,128)(2,1)S(1)}, bf16[32,1024]{1,0:T(8,128)(2,1)S(1)}, u32[]{:S(2)}, u32[]{:S(2)}) collective-permute-start(bf16[32,1024]{1,0:T(8,128)(2,1)S(1)} %get-tuple-element.58), channel_id=1, source_target_pairs={{0,1},{1,0},{2,3},{3,2},{4,5},{5,4},{6,7},{7,6},{8,9},{9,8},{10,11... | collective-permute-start | bytes 196616 | tf_op jit(solution)/shard_map/ppermute | solution.py:19
  49.9 2.6 %collective-permute-start.15 = (bf16[32,1024]{1,0:T(8,128)(2,1)S(1)}, bf16[32,1024]{1,0:T(8,128)(2,1)S(1)}, u32[]{:S(2)}, u32[]{:S(2)}) collective-permute-start(bf16[32,1024]{1,0:T(8,128)(2,1)S(1)} %get-tuple-element.59), channel_id=1, source_target_pairs={{0,2},{1,3},{2,0},{3,1},{4,6},{5,7},{6,4},{7,5},{8,10},{9,11},{10,... | collective-permute-start | bytes 196616 | tf_op jit(solution)/shard_map/ppermute | solution.py:19
  52.7 0.5 collective-permute-done.14.refs_1_
  53.2 3.3 %collective-permute-done.15.refs_2_ = bf16[32,1024]{1,0:T(8,128)(2,1)S(1)} collective-permute-done((bf16[32,1024]{1,0:T(8,128)(2,1)S(1)}, bf16[32,1024]{1,0:T(8,128)(2,1)S(1)}, u32[]{:S(2)}, u32[]{:S(2)}) %collective-permute-start.15) | collective-permute-done | bytes 65568 | tf_op jit(solution)/shard_map/ppermute | solution.py:19
  56.4 2.1 %collective-permute-done.16.refs_3_ = bf16[32,1024]{1,0:T(8,128)(2,1)S(1)} collective-permute-done((bf16[32,1024]{1,0:T(8,128)(2,1)S(1)}, bf16[32,1024]{1,0:T(8,128)(2,1)S(1)}, u32[]{:S(2)}, u32[]{:S(2)}) %collective-permute-start.16) | collective-permute-done | bytes 65568 | tf_op jit(solution)/shard_map/ppermute | solution.py:19
  58.5 0.8 %shard_map.62 = (f32[4,3,32,128]{3,2,1,0:T(8,128)S(1)}, f32[4,3,32,128]{3,2,1,0:T(8,128)S(1)}) custom-call(s32[24]{0:T(128)S(1)} %add_maximum_fusion.block_ref, f32[32,1024]{1,0:T(8,128)S(1)} %get-tuple-element.57.refs_0_, bf16[32,1024]{1,0:T(8,128)(2,1)S(1)} %collective-permute-done.14.refs_1_, bf16[32,1024]{1,0:T(8,128)(2,1)S(1)} %collective-permute-done.15.refs_2_, ...), custom_call_target="tpu_custom_call" | custom-call | tf_op jit(solution)/shard_map/pallas_call | solution.py:256
  59.3 1.4 %collective-permute-done.17 = f32[4,3,32,128]{3,2,1,0:T(8,128)S(1)} collective-permute-done((f32[4,3,32,128]{3,2,1,0:T(8,128)S(1)}, f32[4,3,32,128]{3,2,1,0:T(8,128)S(1)}, u32[]{:S(2)}, u32[]{:S(2)}) %collective-permute-start.17) | collective-permute-done | bytes 196640 | tf_op jit(solution)/shard_map/ppermute | solution.py:19
  60.8 1.5 %collective-permute-start.20 = (f32[2,3,32,128]{3,2,1,0:T(8,128)S(1)}, f32[2,3,32,128]{3,2,1,0:T(8,128)S(1)}, u32[]{:S(2)}, u32[]{:S(2)}) collective-permute-start(f32[2,3,32,128]{3,2,1,0:T(8,128)S(1)} %get-tuple-element.69), channel_id=1, source_target_pairs={{0,24},{4,28},{8,16},{12,20},{16,8},{20,12},{24,0},{28,4},{1,25},{... | collective-permute-start | bytes 294920 | tf_op jit(solution)/shard_map/ppermute | solution.py:19
  62.4 1.5 %collective-permute-start.18 = (f32[2,3,32,128]{3,2,1,0:T(8,128)S(1)}, f32[2,3,32,128]{3,2,1,0:T(8,128)S(1)}, u32[]{:S(2)}, u32[]{:S(2)}) collective-permute-start(f32[2,3,32,128]{3,2,1,0:T(8,128)S(1)} %get-tuple-element.71), channel_id=1, source_target_pairs={{0,8},{4,12},{8,0},{12,4},{16,24},{20,28},{24,16},{28,20},{1,9},{5... | collective-permute-start | bytes 294920 | tf_op jit(solution)/shard_map/ppermute | solution.py:19
  63.9 0.5 collective-permute-start.19
  64.4 3.1 %collective-permute-done.20.refs_3_ = f32[2,3,32,128]{3,2,1,0:T(8,128)S(1)} collective-permute-done((f32[2,3,32,128]{3,2,1,0:T(8,128)S(1)}, f32[2,3,32,128]{3,2,1,0:T(8,128)S(1)}, u32[]{:S(2)}, u32[]{:S(2)}) %collective-permute-start.20) | collective-permute-done | bytes 98336 | tf_op jit(solution)/shard_map/ppermute | solution.py:19
  67.4 1.4 %collective-permute-done.18.refs_1_ = f32[2,3,32,128]{3,2,1,0:T(8,128)S(1)} collective-permute-done((f32[2,3,32,128]{3,2,1,0:T(8,128)S(1)}, f32[2,3,32,128]{3,2,1,0:T(8,128)S(1)}, u32[]{:S(2)}, u32[]{:S(2)}) %collective-permute-start.18) | collective-permute-done | bytes 98336 | tf_op jit(solution)/shard_map/ppermute | solution.py:19
  68.8 0.8 %shard_map.63 = f32[8,3,32,128]{3,2,1,0:T(8,128)} custom-call(s32[1]{0:T(128)} %bitcast.mine_ref, f32[2,3,32,128]{3,2,1,0:T(8,128)S(1)} %get-tuple-element.70.refs_0_, f32[2,3,32,128]{3,2,1,0:T(8,128)S(1)} %collective-permute-done.18.refs_1_, f32[2,3,32,128]{3,2,1,0:T(8,128)S(1)} %collective-permute-done.19.refs_2_, ...), custom_call_target="tpu_custom_call" | custom-call | tf_op jit(solution)/shard_map/pallas_call | solution.py:275
  (42 shorter events, 5.4 us)
Async XLA Ops:
  0.0 9.1 %copy-start = (bf16[1024,1024]{1,0:T(8,128)(2,1)S(1)}, bf16[1024,1024]{1,0:T(8,128)(2,1)}, u32[]{:S(2)}) copy-start(bf16[1024,1024]{1,0:T(8,128)(2,1)} %refs_1_.3) | copy-start | bytes 6291460
  2.5 15.2 %collective-permute-start.4 = (bf16[128,2048]{1,0:T(8,128)(2,1)}, bf16[128,2048]{1,0:T(8,128)(2,1)}, u32[]{:S(2)}, u32[]{:S(2)}) collective-permute-start(bf16[128,2048]{1,0:T(8,128)(2,1)} %get-tuple-element.67), channel_id=1, source_target_pairs={{0,16},{4,20},{8,24},{12,28},{16,0},{20,4},{24,8},{28,12},{1,17},{... | collective-permute-start | bytes 1572872 | tf_op jit(solution)/shard_map/ppermute | solution.py:19
  5.4 15.2 %collective-permute-start.3 = (bf16[128,2048]{1,0:T(8,128)(2,1)}, bf16[128,2048]{1,0:T(8,128)(2,1)}, u32[]{:S(2)}, u32[]{:S(2)}) collective-permute-start(bf16[128,2048]{1,0:T(8,128)(2,1)} %get-tuple-element.68), channel_id=1, source_target_pairs={{0,8},{4,12},{8,0},{12,4},{16,24},{20,28},{24,16},{28,20},{1,9},{5... | collective-permute-start | bytes 1572872 | tf_op jit(solution)/shard_map/ppermute | solution.py:19
  6.9 3.5 %copy-start.2 = (s32[14,1]{0,1:T(1,128)S(1)}, s32[14,1]{0,1:T(1,128)}, u32[]{:S(2)}) copy-start(s32[14,1]{0,1:T(1,128)} %param.8) | copy-start | bytes 172
  6.9 3.7 %copy-start.3 = (s32[14,2]{0,1:T(2,128)S(1)}, s32[14,2]{0,1:T(2,128)}, u32[]{:S(2)}) copy-start(s32[14,2]{0,1:T(2,128)} %param.7) | copy-start | bytes 340
  9.8 14.4 %copy-start.1 = (s32[14,1]{0,1:T(1,128)S(1)}, s32[14,1]{0,1:T(1,128)}, u32[]{:S(2)}) copy-start(s32[14,1]{0,1:T(1,128)} %param.9) | copy-start | bytes 172
  9.8 1.6 %collective-permute-start = (bf16[128,1024]{1,0:T(8,128)(2,1)S(1)}, bf16[128,1024]{1,0:T(8,128)(2,1)S(1)}, u32[]{:S(2)}, u32[]{:S(2)}) collective-permute-start(bf16[128,1024]{1,0:T(8,128)(2,1)S(1)} %get-tuple-element.35.refs_0_.refs_2_.refs_4_), channel_id=1, source_target_pairs={{0,4},{4,0},{8,12},{12,8},{16,20},{20,16},{24,28},{28,24},{1,5},{5... | collective-permute-start | bytes 786440 | tf_op jit(solution)/shard_map/ppermute | solution.py:19
  9.9 1.9 %collective-permute-start.1 = (bf16[128,1024]{1,0:T(8,128)(2,1)S(1)}, bf16[128,1024]{1,0:T(8,128)(2,1)S(1)}, u32[]{:S(2)}, u32[]{:S(2)}) collective-permute-start(bf16[128,1024]{1,0:T(8,128)(2,1)S(1)} %get-tuple-element.36.refs_1_.refs_3_.refs_5_), channel_id=1, source_target_pairs={{0,4},{4,0},{8,12},{12,8},{16,20},{20,16},{24,28},{28,24},{1,5},{5... | collective-permute-start | bytes 786440 | tf_op jit(solution)/shard_map/ppermute | solution.py:19
  11.8 18.2 %collective-permute-start.2 = (bf16[128,2048]{1,0:T(8,128)(2,1)}, bf16[128,2048]{1,0:T(8,128)(2,1)S(1)}, u32[]{:S(2)}, u32[]{:S(2)}) collective-permute-start(bf16[128,2048]{1,0:T(8,128)(2,1)} %get-tuple-element.37), channel_id=1, source_target_pairs={{0,24},{4,28},{8,16},{12,20},{16,8},{20,12},{24,0},{28,4},{1,25},{... | collective-permute-start | bytes 1572872 | tf_op jit(solution)/shard_map/ppermute | solution.py:19
  23.1 1.6 %collective-permute-start.5 = (bf16[256,512]{1,0:T(8,128)(2,1)S(1)}, bf16[256,512]{1,0:T(8,128)(2,1)S(1)}, u32[]{:S(2)}, u32[]{:S(2)}) collective-permute-start(bf16[256,512]{1,0:T(8,128)(2,1)S(1)} %get-tuple-element.41.refs_4_.refs_6_), channel_id=1, source_target_pairs={{0,4},{4,0},{8,12},{12,8},{16,20},{20,16},{24,28},{28,24},{1,5},{5... | collective-permute-start | bytes 786440 | tf_op jit(solution)/shard_map/ppermute | solution.py:19
  23.2 1.9 %collective-permute-start.6 = (bf16[256,512]{1,0:T(8,128)(2,1)S(1)}, bf16[256,512]{1,0:T(8,128)(2,1)S(1)}, u32[]{:S(2)}, u32[]{:S(2)}) collective-permute-start(bf16[256,512]{1,0:T(8,128)(2,1)S(1)} %get-tuple-element.42.refs_5_.refs_7_), channel_id=1, source_target_pairs={{0,4},{4,0},{8,12},{12,8},{16,20},{20,16},{24,28},{28,24},{1,5},{5... | collective-permute-start | bytes 786440 | tf_op jit(solution)/shard_map/ppermute | solution.py:19
  23.7 1.8 %collective-permute-start.7 = (bf16[256,512]{1,0:T(8,128)(2,1)S(1)}, bf16[256,512]{1,0:T(8,128)(2,1)S(1)}, u32[]{:S(2)}, u32[]{:S(2)}) collective-permute-start(bf16[256,512]{1,0:T(8,128)(2,1)S(1)} %get-tuple-element.43.refs_6_.refs_8_), channel_id=1, source_target_pairs={{0,4},{4,0},{8,12},{12,8},{16,20},{20,16},{24,28},{28,24},{1,5},{5... | collective-permute-start | bytes 786440 | tf_op jit(solution)/shard_map/ppermute | solution.py:19
  23.7 2.1 %collective-permute-start.8 = (bf16[256,512]{1,0:T(8,128)(2,1)S(1)}, bf16[256,512]{1,0:T(8,128)(2,1)S(1)}, u32[]{:S(2)}, u32[]{:S(2)}) collective-permute-start(bf16[256,512]{1,0:T(8,128)(2,1)S(1)} %get-tuple-element.44.refs_7_.refs_9_), channel_id=1, source_target_pairs={{0,4},{4,0},{8,12},{12,8},{16,20},{20,16},{24,28},{28,24},{1,5},{5... | collective-permute-start | bytes 786440 | tf_op jit(solution)/shard_map/ppermute | solution.py:19
  30.8 1.7 %collective-permute-start.9 = (bf16[128,1024]{1,0:T(8,128)(2,1)S(1)}, bf16[128,1024]{1,0:T(8,128)(2,1)S(1)}, u32[]{:S(2)}, u32[]{:S(2)}) collective-permute-start(bf16[128,1024]{1,0:T(8,128)(2,1)S(1)} %get-tuple-element.51.refs_0_), channel_id=1, source_target_pairs={{0,4},{4,0},{8,12},{12,8},{16,20},{20,16},{24,28},{28,24},{1,5},{5... | collective-permute-start | bytes 786440 | tf_op jit(solution)/shard_map/ppermute | solution.py:19
  30.9 1.9 %collective-permute-start.10 = (bf16[128,1024]{1,0:T(8,128)(2,1)S(1)}, bf16[128,1024]{1,0:T(8,128)(2,1)S(1)}, u32[]{:S(2)}, u32[]{:S(2)}) collective-permute-start(bf16[128,1024]{1,0:T(8,128)(2,1)S(1)} %get-tuple-element.52.refs_1_), channel_id=1, source_target_pairs={{0,4},{4,0},{8,12},{12,8},{16,20},{20,16},{24,28},{28,24},{1,5},{5... | collective-permute-start | bytes 786440 | tf_op jit(solution)/shard_map/ppermute | solution.py:19
  33.5 8.5 %collective-permute-start.11 = (bf16[128,896]{1,0:T(8,128)(2,1)S(1)}, bf16[128,896]{1,0:T(8,128)(2,1)S(1)}, u32[]{:S(2)}, u32[]{:S(2)}) collective-permute-start(bf16[128,896]{1,0:T(8,128)(2,1)S(1)} %get-tuple-element.54), channel_id=1, source_target_pairs={{0,8},{4,12},{8,0},{12,4},{16,24},{20,28},{24,16},{28,20},{1,9},{5... | collective-permute-start | bytes 688136 | tf_op jit(solution)/shard_map/ppermute | solution.py:19
  35.3 12.3 %collective-permute-start.12 = (bf16[128,896]{1,0:T(8,128)(2,1)S(1)}, bf16[128,896]{1,0:T(8,128)(2,1)S(1)}, u32[]{:S(2)}, u32[]{:S(2)}) collective-permute-start(bf16[128,896]{1,0:T(8,128)(2,1)S(1)} %get-tuple-element.55), channel_id=1, source_target_pairs={{0,16},{4,20},{8,24},{12,28},{16,0},{20,4},{24,8},{28,12},{1,17},{... | collective-permute-start | bytes 688136 | tf_op jit(solution)/shard_map/ppermute | solution.py:19
  36.8 10.8 %collective-permute-start.13 = (bf16[128,896]{1,0:T(8,128)(2,1)S(1)}, bf16[128,896]{1,0:T(8,128)(2,1)S(1)}, u32[]{:S(2)}, u32[]{:S(2)}) collective-permute-start(bf16[128,896]{1,0:T(8,128)(2,1)S(1)} %get-tuple-element.56), channel_id=1, source_target_pairs={{0,24},{4,28},{8,16},{12,20},{16,8},{20,12},{24,0},{28,4},{1,25},{... | collective-permute-start | bytes 688136 | tf_op jit(solution)/shard_map/ppermute | solution.py:19
  48.2 5.0 %collective-permute-start.14 = (bf16[32,1024]{1,0:T(8,128)(2,1)S(1)}, bf16[32,1024]{1,0:T(8,128)(2,1)S(1)}, u32[]{:S(2)}, u32[]{:S(2)}) collective-permute-start(bf16[32,1024]{1,0:T(8,128)(2,1)S(1)} %get-tuple-element.58), channel_id=1, source_target_pairs={{0,1},{1,0},{2,3},{3,2},{4,5},{5,4},{6,7},{7,6},{8,9},{9,8},{10,11... | collective-permute-start | bytes 196616 | tf_op jit(solution)/shard_map/ppermute | solution.py:19
  49.9 6.6 %collective-permute-start.15 = (bf16[32,1024]{1,0:T(8,128)(2,1)S(1)}, bf16[32,1024]{1,0:T(8,128)(2,1)S(1)}, u32[]{:S(2)}, u32[]{:S(2)}) collective-permute-start(bf16[32,1024]{1,0:T(8,128)(2,1)S(1)} %get-tuple-element.59), channel_id=1, source_target_pairs={{0,2},{1,3},{2,0},{3,1},{4,6},{5,7},{6,4},{7,5},{8,10},{9,11},{10,... | collective-permute-start | bytes 196616 | tf_op jit(solution)/shard_map/ppermute | solution.py:19
  52.4 6.1 %collective-permute-start.16 = (bf16[32,1024]{1,0:T(8,128)(2,1)S(1)}, bf16[32,1024]{1,0:T(8,128)(2,1)S(1)}, u32[]{:S(2)}, u32[]{:S(2)}) collective-permute-start(bf16[32,1024]{1,0:T(8,128)(2,1)S(1)} %get-tuple-element.60), channel_id=1, source_target_pairs={{0,3},{1,2},{2,1},{3,0},{4,7},{5,6},{6,5},{7,4},{8,11},{9,10},{10,... | collective-permute-start | bytes 196616 | tf_op jit(solution)/shard_map/ppermute | solution.py:19
  59.3 1.5 %collective-permute-start.17 = (f32[4,3,32,128]{3,2,1,0:T(8,128)S(1)}, f32[4,3,32,128]{3,2,1,0:T(8,128)S(1)}, u32[]{:S(2)}, u32[]{:S(2)}) collective-permute-start(f32[4,3,32,128]{3,2,1,0:T(8,128)S(1)} %get-tuple-element.62), channel_id=1, source_target_pairs={{0,4},{4,0},{8,12},{12,8},{16,20},{20,16},{24,28},{28,24},{1,5},{5... | collective-permute-start | bytes 589832 | tf_op jit(solution)/shard_map/ppermute | solution.py:19
  60.8 6.6 %collective-permute-start.20 = (f32[2,3,32,128]{3,2,1,0:T(8,128)S(1)}, f32[2,3,32,128]{3,2,1,0:T(8,128)S(1)}, u32[]{:S(2)}, u32[]{:S(2)}) collective-permute-start(f32[2,3,32,128]{3,2,1,0:T(8,128)S(1)} %get-tuple-element.69), channel_id=1, source_target_pairs={{0,24},{4,28},{8,16},{12,20},{16,8},{20,12},{24,0},{28,4},{1,25},{... | collective-permute-start | bytes 294920 | tf_op jit(solution)/shard_map/ppermute | solution.py:19
  62.4 6.4 %collective-permute-start.18 = (f32[2,3,32,128]{3,2,1,0:T(8,128)S(1)}, f32[2,3,32,128]{3,2,1,0:T(8,128)S(1)}, u32[]{:S(2)}, u32[]{:S(2)}) collective-permute-start(f32[2,3,32,128]{3,2,1,0:T(8,128)S(1)} %get-tuple-element.71), channel_id=1, source_target_pairs={{0,8},{4,12},{8,0},{12,4},{16,24},{20,28},{24,16},{28,20},{1,9},{5... | collective-permute-start | bytes 294920 | tf_op jit(solution)/shard_map/ppermute | solution.py:19
  63.9 5.0 %collective-permute-start.19 = (f32[2,3,32,128]{3,2,1,0:T(8,128)S(1)}, f32[2,3,32,128]{3,2,1,0:T(8,128)S(1)}, u32[]{:S(2)}, u32[]{:S(2)}) collective-permute-start(f32[2,3,32,128]{3,2,1,0:T(8,128)S(1)} %get-tuple-element.72), channel_id=1, source_target_pairs={{0,16},{4,20},{8,24},{12,28},{16,0},{20,4},{24,8},{28,12},{1,17},{... | collective-permute-start | bytes 294920 | tf_op jit(solution)/shard_map/ppermute | solution.py:19

commit v3 on v2

--- a/solution.py
+++ b/solution.py
@@ -12,6 +12,8 @@
 MIB = 1024 * 1024
 SMEM = pl.BlockSpec(memory_space=pltpu.SMEM)
 VMEM = pl.BlockSpec(memory_space=pltpu.VMEM)
+HBM = pl.BlockSpec(memory_space=pltpu.HBM)
+ANY = pl.BlockSpec(memory_space=pl.ANY)
 
 
 def swapped(value, axis, distance):
@@ -66,36 +68,104 @@
     return groups
 
 
-def fit_kernel(count, *refs):
-    panels, metric_ref, outs = refs[:count], refs[count], refs[count + 1 :]
-    naux = metric_ref.shape[0]
+def write_fitted(panels, metric, outs):
+    naux = metric.shape[0]
     rows, width = panels[0].shape
     size = outs[0].shape[1]
+    span = min(size, naux)
     starts = range(0, width, naux)
     stacked = jnp.concatenate([ref[:, at : at + naux] for ref in panels for at in starts], axis=0)
-    fitted = contract(stacked, metric_ref[...]).astype(jnp.bfloat16)
-    for index in range(count):
-        for number, out_ref in enumerate(outs):
-            at = number * size
-            for start in range(at, at + size, min(size, naux)):
-                top = (index * len(starts) + start // naux) * rows
-                from_column = start % naux
-                span = min(size, naux)
-                out_ref[index * rows : (index + 1) * rows, start - at : start - at + span] = fitted[
-                    top : top + rows, from_column : from_column + span
-                ]
-
-
-def fit(panels, metric, pieces):
+    fitted = contract(stacked, metric).astype(jnp.bfloat16)
+    for index in range(len(panels)):
+        for at in range(0, width, span):
+            top = (index * len(starts) + at // naux) * rows
+            left = at % naux
+            outs[at // size][index * rows : (index + 1) * rows, at % size : at % size + span] = (
+                fitted[top : top + rows, left : left + span]
+            )
+
+
+def fit_kernel(count, pieces, *refs):
+    outs = refs[-pieces:]
+    write_fitted(refs[:count][::-1], refs[count][...], outs)
+    below = outs[0].shape[0] - count * refs[0].shape[0]
+    if below:
+        for ref, out_ref in zip(refs[count + 1 : count + 1 + pieces], outs, strict=True):
+            out_ref[out_ref.shape[0] - below :] = ref[...]
+
+
+def fit(panels, metric, pieces, below=(), before=()):
     rows, width = panels[0].shape
-    rows_out = rows * len(panels)
-    return kernel_call(
-        functools.partial(fit_kernel, len(panels)),
-        [VMEM] * (len(panels) + 1),
+    rows_out = rows * len(panels) + (below[0].shape[0] if below else 0)
+    return kernel_call(
+        functools.partial(fit_kernel, len(panels), pieces),
+        [VMEM] * (len(panels) + 1 + len(below)) + [ANY] * len(before),
         [kept((rows_out, width // pieces), jnp.bfloat16)] * pieces,
         [VMEM] * pieces,
         8,
-    )(*panels, metric)
+    )(*panels[::-1], metric, *below, *before)
+
+
+def copy_all(pairs, arrived):
+    copies = [
+        pltpu.make_async_copy(source, target, arrived.at[at])
+        for at, (source, target) in enumerate(pairs)
+    ]
+    for copy in copies:
+        copy.start()
+    for copy in copies:
+        copy.wait()
+
+
+def column_block(raw_ref, start_ref, at, width):
+    return raw_ref.at[:, pl.ds(pl.multiple_of(start_ref[at], width), width)]
+
+
+def cut_kernel(count, starts_ref, raw_ref, *refs):
+    pieces, token_ref, arrived = refs[-count - 2 : -2], refs[-2], refs[-1]
+    width = pieces[0].shape[1]
+    copy_all(
+        [(column_block(raw_ref, starts_ref, at, width), piece) for at, piece in enumerate(pieces)],
+        arrived,
+    )
+    token_ref[0] = jnp.int32(0)
+
+
+def cut(raw, starts, width, *before):
+    rows = raw.shape[0]
+    count = len(starts)
+    *pieces, token = kernel_call(
+        functools.partial(cut_kernel, count),
+        [SMEM, HBM] + [ANY] * len(before),
+        [kept((rows, width), raw.dtype)] * count + [shaped((1,), jnp.int32)],
+        [VMEM] * count + [SMEM],
+        4,
+        [pltpu.SemaphoreType.DMA((count,))],
+    )(jnp.stack(starts), raw, *before)
+    return pieces, token
+
+
+def first_fit_kernel(token_ref, starts_ref, raw_ref, metric_ref, *refs):
+    held_ref, outs, (own_ref, arrived) = refs[0], refs[1:-2], refs[-2:]
+    width = own_ref.shape[1]
+    copy_all(
+        [(column_block(raw_ref, starts_ref, 0, width), own_ref), (metric_ref, held_ref)], arrived
+    )
+    write_fitted([own_ref], held_ref[...], outs)
+
+
+def first_fit(token, raw, metric, start, width, pieces):
+    rows = raw.shape[0]
+    held, *fitted = kernel_call(
+        first_fit_kernel,
+        [SMEM, SMEM, HBM, HBM],
+        [kept(metric.shape, metric.dtype)]
+        + [kept((rows, width // pieces), jnp.bfloat16)] * pieces,
+        [VMEM] * (pieces + 1),
+        8,
+        [pltpu.VMEM((rows, width), raw.dtype), pltpu.SemaphoreType.DMA((2,))],
+    )(token, start[None], raw, pltpu.with_memory_space_constraint(metric, pltpu.HBM))
+    return held, fitted
 
 
 def place(block, chip):
@@ -235,20 +305,25 @@
 
 
 def combine_kernel(span, block_ref, *refs):
-    chunks, outs = refs[:-CORES], refs[-CORES:]
-    chips, slots, share = outs[0].shape[:3]
+    chunks, (home_ref, straight_ref, crossing_ref) = refs[:-3], refs[-3:]
+    slots, share = home_ref.shape[:2]
     weights = [chunk[:, span:].astype(jnp.float32) for chunk in chunks]
-    for chip in range(chips):
-        for core, out_ref in enumerate(outs):
-            for slot in range(slots):
-                at = (chip * CORES + core) * slots + slot
-                start = pl.multiple_of(block_ref[at] * TILE, TILE)
-                row, lanes = at % share, at // share * TILE
-                total = jnp.zeros((share, TILE), jnp.float32)
-                for chunk, weight in zip(chunks, weights, strict=True):
-                    scale = weight[row : row + 1, lanes : lanes + TILE]
-                    total = total + scale * chunk[:, pl.ds(start, TILE)].astype(jnp.float32)
-                out_ref[chip, slot] = total
+    for owner in range(crossing_ref.shape[0] * CORES):
+        chip, core = owner // CORES, owner % CORES
+        for slot in range(slots):
+            at = owner * slots + slot
+            start = pl.multiple_of(block_ref[at] * TILE, TILE)
+            row, lanes = at % share, at // share * TILE
+            total = jnp.zeros((share, TILE), jnp.float32)
+            for chunk, weight in zip(chunks, weights, strict=True):
+                scale = weight[row : row + 1, lanes : lanes + TILE]
+                total = total + scale * chunk[:, pl.ds(start, TILE)].astype(jnp.float32)
+            if owner == 0:
+                home_ref[slot] = total
+            elif core == 0:
+                straight_ref[chip - 1, slot] = total.astype(jnp.bfloat16)
+            else:
+                crossing_ref[chip, slot] = total.astype(jnp.bfloat16)
 
 
 def combine(blocks, chunks, span, chips, slots):
@@ -256,33 +331,38 @@
     return kernel_call(
         functools.partial(combine_kernel, span),
         [SMEM] + [VMEM] * len(chunks),
-        [shaped((chips, slots, share, TILE), jnp.float32)] * CORES,
-        [VMEM] * CORES,
+        [
+            shaped((slots, share, TILE), jnp.float32),
+            shaped((chips - 1, slots, share, TILE), jnp.bfloat16),
+            shaped((chips, slots, share, TILE), jnp.bfloat16),
+        ],
+        [VMEM] * 3,
         8,
     )(blocks, *chunks)
 
 
-def settle_kernel(mine_ref, *refs):
-    pieces, out_ref = refs[:-1], refs[-1]
+def settle_kernel(mine_ref, home_ref, beside_ref, *refs):
+    came, out_ref = refs[:-1], refs[-1]
     mine = mine_ref[0]
-    for chip, piece in enumerate(pieces):
+    out_ref[mine] = home_ref[...]
+    out_ref[mine ^ 1] = beside_ref[...].astype(jnp.float32)
+    for at, piece in enumerate(came):
         for core in range(CORES):
-            out_ref[mine ^ (chip * CORES + core)] = piece[core]
-
-
-def settle(mine, pieces):
-    shape = (CORES * len(pieces), *pieces[0].shape[1:])
+            out_ref[mine ^ ((at + 1) * CORES + core)] = piece[core].astype(jnp.float32)
+
+
+def settle(mine, home, from_beside, came):
     return kernel_call(
         settle_kernel,
-        [SMEM] + [VMEM] * len(pieces),
-        shaped(shape, jnp.float32),
+        [SMEM] + [VMEM] * (2 + len(came)),
+        shaped((CORES * (len(came) + 1), *home.shape), jnp.float32),
         VMEM,
         8,
-    )(mine, *pieces)
+    )(mine, home, from_beside, *came)
 
 
 def per_device(raw_panels, metric, tile_pairs, owners, group_mask):
-    raw = raw_panels[0]
+    raw = pltpu.with_memory_space_constraint(raw_panels[0], pltpu.HBM)
     rows, columns = raw.shape
     cycle = lax.axis_size("blk")
     groups = lax.axis_size("grp")
@@ -295,27 +375,19 @@
     final = chips - 1
     share = rows // groups
 
-    def piece(source, chip):
-        start = ((mine // CORES) ^ chip) * width
-        return lax.dynamic_slice(source, (jnp.int32(0), start), (rows, width))
-
     def beside(pieces):
         return [swapped(piece, "blk", 1) for piece in pieces]
 
-    pieces = [piece(raw, chip) for chip in range(1, final)]
-    arrived = [swapped(value, "blk", CORES * (at + 1)) for at, value in enumerate(pieces)]
-    raw = lax.optimization_barrier((raw, *pieces))[0]
-    own = fit([piece(raw, 0)], metric, 2)
+    starts = [((mine // CORES) ^ chip) * width for chip in range(chips)]
+    pieces, token = cut(raw, starts[1:final], width)
+    arrived = [swapped(piece, "blk", CORES * (at + 1)) for at, piece in enumerate(pieces)]
+    metric, own = first_fit(token, raw, metric, starts[0], width, 2)
     own_beside = beside(own)
-    last_piece = lax.optimization_barrier((piece(raw, final), *own_beside))[0]
+    (last_piece,), token = cut(raw, starts[final:], width, *own_beside)
     last = swapped(last_piece, "blk", CORES * final)
 
-    others = fit(arrived, metric, 4)
-    others_beside = beside(others)
-    begun = early(own, own_beside, others, others_beside)
-
     own_mask, pairs, owner_ids = lax.optimization_barrier(
-        (group_mask[:, 0], tile_pairs, owners[:, 0], *own)
+        (group_mask[:, 0], tile_pairs, owners[:, 0], token)
     )[:3]
     owner_ids = owner_ids ^ mine
     hits = (owner_ids[:, None] == jnp.arange(cycle)[None, :]).astype(jnp.int32)
@@ -329,8 +401,11 @@
     weights = jnp.pad(weights, (0, tall - weights.shape[0])).reshape(-1, share).T
     weights = jnp.repeat(weights, TILE, axis=1)
 
-    last, blocks, weights = lax.optimization_barrier((last, blocks, weights, *begun))[:3]
-    last_fitted = fit([last], metric, 2)
+    others = fit(arrived, metric, 4)
+    others_beside = beside(others)
+    begun = early(own, own_beside, others, others_beside)
+
+    last_fitted = fit([last], metric, 2, (), (blocks, weights, begun[0]))
     last_beside = beside(last_fitted)
     across = middle(last_fitted, own, own_beside, others, others_beside)
     slabs = late(last_fitted, last_beside, own, others, across, begun)
@@ -340,13 +415,13 @@
     own_strips = strips(slabs[0], came, strip_starts, weights)
     chunks = [own_strips[0]] + [swapped(own_strips[d], "grp", d) for d in range(1, groups)]
 
-    straight, crossing = combine(blocks, chunks, slabs[0].shape[1], chips, capacity)
+    home, straight, crossing = combine(blocks, chunks, slabs[0].shape[1], chips, capacity)
     crossed = swapped(crossing, "blk", 1)
-    paired = jnp.stack([straight, crossed], axis=1)
-    received = [paired[0]] + [
-        swapped(paired[chip], "blk", CORES * chip) for chip in range(1, chips)
+    paired = jnp.stack([straight, crossed[1:]], axis=1)
+    received = [
+        swapped(paired[chip - 1], "blk", CORES * chip) for chip in range(1, chips)
     ]
-    return settle(mine[None], received)[None]
+    return settle(mine[None], home, crossed[0], received)[None]
 
 
 def solution(mesh):

time: 69.8 us -> 69.3 us (level)
  Pallas kernels: 9.72 us -> 16.5 us
  local copies, waits for them, and re-layouts: 4.68 us -> 0.1 us
  waiting for transfers between devices: 36.4 us -> 33.3 us
    pallas_call x4 -> x6, Pallas kernels: 4.73 us -> 11.5 us  [the longest x2 4.33 us: cut(): kernel_call(functools.partial(cut_kernel, count), [SMEM, HBM] + [ANY] * l...]
    dynamic_slice x2 -> x0, local copies, waits for them, and re-layouts: 4.59 us -> none  [piece(): return lax.dynamic_slice(source, (jnp.int32(0), start), (rows, width))]
    ppermute x21, waiting for transfers between devices: 36.4 us -> 33.3 us  [swapped(): lax.ppermute(value, axis, [(source, source ^ distance) for source in rang...]
  transfers between devices with their start and end apart: 21 -> 21, of which waited for: 19 -> 19; matrix products, arithmetic and copies ran while one was open for 4% -> 0% of each run, Pallas kernels for 9% -> 15%
where the time goes in v3:
time: 69.3 us; the launch traced here: 69 us
  waiting for transfers between devices  33.3 us (48%)
  starting transfers between devices  18.5 us (27%)
  Pallas kernels  16.5 us (24%)
    ppermute x21, waiting for transfers between devices, swapped(): lax.ppermute(value, axis, [(source, source ^ distance) for source in rang...  33.3 us
    ppermute x21, starting transfers between devices, swapped(): lax.ppermute(value, axis, [(source, source ^ distance) for source in rang...  18.5 us
    pallas_call x2, Pallas kernels, cut(): kernel_call(functools.partial(cut_kernel, count), [SMEM, HBM] + [ANY] * l...  4.33 us
    pallas_call x2, Pallas kernels, fit(): kernel_call(functools.partial(fit_kernel, len(panels), pieces), [VMEM] *...  3.22 us
    pallas_call x1, Pallas kernels, first_fit(): kernel_call(first_fit_kernel, [SMEM, SMEM, HBM, HBM], [kept(metric.shape,...  3.2 us
    pallas_call x1, Pallas kernels, early(): kernel_call(functools.partial(early_kernel, counts), [VMEM] * sum(counts[...  1.79 us
  transfers between devices with their start and end apart: 21, of which 19 were waited for; matrix products, arithmetic and copies ran while one was open for 0% of the time, Pallas kernels for 15%

profile of v3, /device:TPU:0, one launch (start us, length us, event | category | flops | bytes accessed | tf_op | source)
XLA Modules:
  0.0 69.0 jit_solution(3025383001617351415)
XLA Ops:
  0.1 2.8 %shard_map.55 = (bf16[128,2048]{1,0:T(8,128)(2,1)}, bf16[128,2048]{1,0:T(8,128)(2,1)}, s32[1]{0:T(128)}) custom-call(s32[2]{0:T(128)S(1)} %pad_add_fusion.starts_ref, bf16[128,8192]{1,0:T(8,128)(2,1)} %bitcast.23), custom_call_target="tpu_custom_call" | custom-call | tf_op jit(solution)/shard_map/pallas_call | solution.py:137
  2.8 3.0 %collective-permute-start.3 = (bf16[128,2048]{1,0:T(8,128)(2,1)}, bf16[128,2048]{1,0:T(8,128)(2,1)}, u32[]{:S(2)}, u32[]{:S(2)}) collective-permute-start(bf16[128,2048]{1,0:T(8,128)(2,1)} %get-tuple-element.43), channel_id=1, source_target_pairs={{0,16},{4,20},{8,24},{12,28},{16,0},{20,4},{24,8},{28,12},{1,17},{... | collective-permute-start | bytes 1572872 | tf_op jit(solution)/shard_map/ppermute | solution.py:21
  5.9 1.5 %collective-permute-start.4 = (bf16[128,2048]{1,0:T(8,128)(2,1)}, bf16[128,2048]{1,0:T(8,128)(2,1)}, u32[]{:S(2)}, u32[]{:S(2)}) collective-permute-start(bf16[128,2048]{1,0:T(8,128)(2,1)} %get-tuple-element.44), channel_id=1, source_target_pairs={{0,8},{4,12},{8,0},{12,4},{16,24},{20,28},{24,16},{28,20},{1,9},{5... | collective-permute-start | bytes 1572872 | tf_op jit(solution)/shard_map/ppermute | solution.py:21
  7.4 3.2 %shard_map.56 = (bf16[1024,1024]{1,0:T(8,128)(2,1)S(1)}, bf16[128,1024]{1,0:T(8,128)(2,1)S(1)}, bf16[128,1024]{1,0:T(8,128)(2,1)S(1)}) custom-call(s32[1]{0:T(128)} %get-tuple-element.38.token_ref, s32[1]{0:T(128)} %bitcast.8.starts_ref, bf16[128,8192]{1,0:T(8,128)(2,1)} %bitcast.24, bf16[1024,1024]{1,0:T(8,128)(2,1)} %metric_ref.1), custom_call_target="tpu_custom_call" | custom-call | tf_op jit(solution)/shard_map/pallas_call | solution.py:159
  11.4 0.8 %collective-permute-done.refs_0_.refs_2_.refs_4_ = bf16[128,1024]{1,0:T(8,128)(2,1)S(1)} collective-permute-done((bf16[128,1024]{1,0:T(8,128)(2,1)S(1)}, bf16[128,1024]{1,0:T(8,128)(2,1)S(1)}, u32[]{:S(2)}, u32[]{:S(2)}) %collective-permute-start) | collective-permute-done | bytes 262176 | tf_op jit(solution)/shard_map/ppermute | solution.py:21
  12.6 1.6 %shard_map.57 = (bf16[128,2048]{1,0:T(8,128)(2,1)S(1)}, s32[1]{0:T(128)}) custom-call(s32[1]{0:T(128)} %bitcast.4.starts_ref, bf16[128,8192]{1,0:T(8,128)(2,1)} %bitcast.25, bf16[128,1024]{1,0:T(8,128)(2,1)S(1)} %collective-permute-done.refs_0_.refs_2_.refs_4_, bf16[128,1024]{1,0:T(8,128)(2,1)S(1)} %collective-permute-done.1.refs_1_.refs_3_.refs_5_), custom_call_target="tpu_custom_call" | custom-call | tf_op jit(solution)/shard_map/pallas_call | solution.py:137
  14.3 3.8 %collective-permute-done.3.refs_0_ = bf16[128,2048]{1,0:T(8,128)(2,1)} collective-permute-done((bf16[128,2048]{1,0:T(8,128)(2,1)}, bf16[128,2048]{1,0:T(8,128)(2,1)}, u32[]{:S(2)}, u32[]{:S(2)}) %collective-permute-start.3) | collective-permute-done | bytes 524320 | tf_op jit(solution)/shard_map/ppermute | solution.py:21
  18.1 2.9 %collective-permute-done.4.refs_1_ = bf16[128,2048]{1,0:T(8,128)(2,1)} collective-permute-done((bf16[128,2048]{1,0:T(8,128)(2,1)}, bf16[128,2048]{1,0:T(8,128)(2,1)}, u32[]{:S(2)}, u32[]{:S(2)}) %collective-permute-start.4) | collective-permute-done | bytes 524320 | tf_op jit(solution)/shard_map/ppermute | solution.py:21
  21.0 2.5 %shard_map.58 = (bf16[256,512]{1,0:T(8,128)(2,1)S(1)}, bf16[256,512]{1,0:T(8,128)(2,1)S(1)}, bf16[256,512]{1,0:T(8,128)(2,1)S(1)}, bf16[256,512]{1,0:T(8,128)(2,1)S(1)}) custom-call(bf16[128,2048]{1,0:T(8,128)(2,1)} %collective-permute-done.3.refs_0_, bf16[128,2048]{1,0:T(8,128)(2,1)} %collective-permute-done.4.refs_1_, ...), custom_call_target="tpu_custom_call" | custom-call | tf_op jit(solution)/shard_map/pallas_call | solution.py:100
  26.3 1.8 %shard_map.59 = (f32[128,896]{1,0:T(8,128)S(1)}, bf16[128,896]{1,0:T(8,128)(2,1)S(1)}, bf16[128,896]{1,0:T(8,128)(2,1)S(1)}) custom-call(bf16[128,1024]{1,0:T(8,128)(2,1)S(1)} %get-tuple-element.39.refs_0_.refs_2_.refs_4_, bf16[128,1024]{1,0:T(8,128)(2,1)S(1)} %get-tuple-element.40.refs_1_.refs_3_.refs_5_, ...), custom_call_target="tpu_custom_call" | custom-call | tf_op jit(solution)/shard_map/pallas_call | solution.py:211
  28.1 2.5 %collective-permute-done.2.refs_0_ = bf16[128,2048]{1,0:T(8,128)(2,1)S(1)} collective-permute-done((bf16[128,2048]{1,0:T(8,128)(2,1)S(1)}, bf16[128,2048]{1,0:T(8,128)(2,1)S(1)}, u32[]{:S(2)}, u32[]{:S(2)}) %collective-permute-start.2) | collective-permute-done | bytes 524320 | tf_op jit(solution)/shard_map/ppermute | solution.py:21
  30.6 0.7 %shard_map.60 = (bf16[128,1024]{1,0:T(8,128)(2,1)S(1)}, bf16[128,1024]{1,0:T(8,128)(2,1)S(1)}) custom-call(bf16[128,2048]{1,0:T(8,128)(2,1)S(1)} %collective-permute-done.2.refs_0_, bf16[1024,1024]{1,0:T(8,128)(2,1)S(1)} %get-tuple-element.42.refs_2_.refs_1_, s32[24]{0:T(128)S(1)} %add_maximum_fusion.refs_2_.block_ref, ...), custom_call_target="tpu_custom_call" | custom-call | tf_op jit(solution)/shard_map/pallas_call | solution.py:100
  31.9 1.1 %shard_map.61.refs_10_ = f32[128,768]{1,0:T(8,128)S(1)} custom-call(bf16[128,1024]{1,0:T(8,128)(2,1)S(1)} %get-tuple-element.50.refs_0_, bf16[128,1024]{1,0:T(8,128)(2,1)S(1)} %get-tuple-element.51.refs_1_, bf16[128,1024]{1,0:T(8,128)(2,1)S(1)} %get-tuple-element.39.refs_0_.refs_2_.refs_4_, bf16[128,1024]{1,0:T(8,128)(2,1)S(1)} %get-tuple-element.40.refs_1_.refs_3_.refs_5_, ...), custom_call_target="tpu_custom_call" | custom-call | tf_op jit(solution)/shard_map/pallas_call | solution.py:234
  33.3 0.7 %shard_map.62 = (f32[128,896]{1,0:T(8,128)S(1)}, bf16[128,896]{1,0:T(8,128)(2,1)S(1)}, bf16[128,896]{1,0:T(8,128)(2,1)S(1)}, bf16[128,896]{1,0:T(8,128)(2,1)S(1)}) custom-call(bf16[128,1024]{1,0:T(8,128)(2,1)S(1)} %get-tuple-element.50.refs_0_, bf16[128,1024]{1,0:T(8,128)(2,1)S(1)} %get-tuple-element.51.refs_1_, ...), custom_call_target="tpu_custom_call" | custom-call | tf_op jit(solution)/shard_map/pallas_call | solution.py:270
  34.0 1.7 %collective-permute-start.11 = (bf16[128,896]{1,0:T(8,128)(2,1)S(1)}, bf16[128,896]{1,0:T(8,128)(2,1)S(1)}, u32[]{:S(2)}, u32[]{:S(2)}) collective-permute-start(bf16[128,896]{1,0:T(8,128)(2,1)S(1)} %get-tuple-element.55), channel_id=1, source_target_pairs={{0,8},{4,12},{8,0},{12,4},{16,24},{20,28},{24,16},{28,20},{1,9},{5... | collective-permute-start | bytes 688136 | tf_op jit(solution)/shard_map/ppermute | solution.py:21
  35.7 1.5 %collective-permute-start.12 = (bf16[128,896]{1,0:T(8,128)(2,1)S(1)}, bf16[128,896]{1,0:T(8,128)(2,1)S(1)}, u32[]{:S(2)}, u32[]{:S(2)}) collective-permute-start(bf16[128,896]{1,0:T(8,128)(2,1)S(1)} %get-tuple-element.56), channel_id=1, source_target_pairs={{0,16},{4,20},{8,24},{12,28},{16,0},{20,4},{24,8},{28,12},{1,17},{... | collective-permute-start | bytes 688136 | tf_op jit(solution)/shard_map/ppermute | solution.py:21
  37.6 5.0 %collective-permute-done.11.refs_0_ = bf16[128,896]{1,0:T(8,128)(2,1)S(1)} collective-permute-done((bf16[128,896]{1,0:T(8,128)(2,1)S(1)}, bf16[128,896]{1,0:T(8,128)(2,1)S(1)}, u32[]{:S(2)}, u32[]{:S(2)}) %collective-permute-start.11) | collective-permute-done | bytes 229408 | tf_op jit(solution)/shard_map/ppermute | solution.py:21
  42.5 5.5 %collective-permute-done.12.refs_1_ = bf16[128,896]{1,0:T(8,128)(2,1)S(1)} collective-permute-done((bf16[128,896]{1,0:T(8,128)(2,1)S(1)}, bf16[128,896]{1,0:T(8,128)(2,1)S(1)}, u32[]{:S(2)}, u32[]{:S(2)}) %collective-permute-start.12) | collective-permute-done | bytes 229408 | tf_op jit(solution)/shard_map/ppermute | solution.py:21
  48.0 0.7 shard_map.63
  48.7 1.6 %collective-permute-start.14 = (bf16[32,1024]{1,0:T(8,128)(2,1)S(1)}, bf16[32,1024]{1,0:T(8,128)(2,1)S(1)}, u32[]{:S(2)}, u32[]{:S(2)}) collective-permute-start(bf16[32,1024]{1,0:T(8,128)(2,1)S(1)} %get-tuple-element.59), channel_id=1, source_target_pairs={{0,1},{1,0},{2,3},{3,2},{4,5},{5,4},{6,7},{7,6},{8,9},{9,8},{10,11... | collective-permute-start | bytes 196616 | tf_op jit(solution)/shard_map/ppermute | solution.py:21
  50.3 2.6 %collective-permute-start.15 = (bf16[32,1024]{1,0:T(8,128)(2,1)S(1)}, bf16[32,1024]{1,0:T(8,128)(2,1)S(1)}, u32[]{:S(2)}, u32[]{:S(2)}) collective-permute-start(bf16[32,1024]{1,0:T(8,128)(2,1)S(1)} %get-tuple-element.60), channel_id=1, source_target_pairs={{0,2},{1,3},{2,0},{3,1},{4,6},{5,7},{6,4},{7,5},{8,10},{9,11},{10,... | collective-permute-start | bytes 196616 | tf_op jit(solution)/shard_map/ppermute | solution.py:21
  53.1 0.5 collective-permute-done.14.refs_1_
  53.6 3.3 %collective-permute-done.15.refs_2_ = bf16[32,1024]{1,0:T(8,128)(2,1)S(1)} collective-permute-done((bf16[32,1024]{1,0:T(8,128)(2,1)S(1)}, bf16[32,1024]{1,0:T(8,128)(2,1)S(1)}, u32[]{:S(2)}, u32[]{:S(2)}) %collective-permute-start.15) | collective-permute-done | bytes 65568 | tf_op jit(solution)/shard_map/ppermute | solution.py:21
  56.9 2.1 %collective-permute-done.16.refs_3_ = bf16[32,1024]{1,0:T(8,128)(2,1)S(1)} collective-permute-done((bf16[32,1024]{1,0:T(8,128)(2,1)S(1)}, bf16[32,1024]{1,0:T(8,128)(2,1)S(1)}, u32[]{:S(2)}, u32[]{:S(2)}) %collective-permute-start.16) | collective-permute-done | bytes 65568 | tf_op jit(solution)/shard_map/ppermute | solution.py:21
  59.0 0.8 %shard_map.64 = (f32[3,32,128]{2,1,0:T(8,128)S(1)}, bf16[3,3,32,128]{3,2,1,0:T(8,128)(2,1)S(1)}, bf16[4,3,32,128]{3,2,1,0:T(8,128)(2,1)S(1)}) custom-call(s32[24]{0:T(128)S(1)} %add_maximum_fusion.refs_2_.block_ref, f32[32,1024]{1,0:T(8,128)S(1)} %get-tuple-element.58.refs_0_, bf16[32,1024]{1,0:T(8,128)(2,1)S(1)} %collective-permute-done.14.refs_1_, ...), custom_call_target="tpu_custom_call" | custom-call | tf_op jit(solution)/shard_map/pallas_call | solution.py:331
  59.8 1.3 %collective-permute-done.17 = bf16[4,3,32,128]{3,2,1,0:T(8,128)(2,1)S(1)} collective-permute-done((bf16[4,3,32,128]{3,2,1,0:T(8,128)(2,1)S(1)}, bf16[4,3,32,128]{3,2,1,0:T(8,128)(2,1)S(1)}, u32[]{:S(2)}, u32[]{:S(2)}) %collective-permute-start.17) | collective-permute-done | bytes 98336 | tf_op jit(solution)/shard_map/ppermute | solution.py:21
  61.1 1.5 %collective-permute-start.20 = (bf16[2,3,32,128]{3,2,1,0:T(8,128)(2,1)S(1)}, bf16[2,3,32,128]{3,2,1,0:T(8,128)(2,1)S(1)}, u32[]{:S(2)}, u32[]{:S(2)}) collective-permute-start(bf16[2,3,32,128]{3,2,1,0:T(8,128)(2,1)S(1)} %get-tuple-element.67), channel_id=1, source_target_pairs={{0,24},{4,28},{8,16},{12,20},{16,8},{20,12},{24,0},{28,4},{1,25},{... | collective-permute-start | bytes 147464 | tf_op jit(solution)/shard_map/ppermute | solution.py:21
  62.7 1.5 %collective-permute-start.18 = (bf16[2,3,32,128]{3,2,1,0:T(8,128)(2,1)S(1)}, bf16[2,3,32,128]{3,2,1,0:T(8,128)(2,1)S(1)}, u32[]{:S(2)}, u32[]{:S(2)}) collective-permute-start(bf16[2,3,32,128]{3,2,1,0:T(8,128)(2,1)S(1)} %get-tuple-element.68), channel_id=1, source_target_pairs={{0,8},{4,12},{8,0},{12,4},{16,24},{20,28},{24,16},{28,20},{1,9},{5... | collective-permute-start | bytes 147464 | tf_op jit(solution)/shard_map/ppermute | solution.py:21
  64.2 0.5 collective-permute-start.19
  64.7 1.9 %collective-permute-done.20.refs_2_ = bf16[2,3,32,128]{3,2,1,0:T(8,128)(2,1)S(1)} collective-permute-done((bf16[2,3,32,128]{3,2,1,0:T(8,128)(2,1)S(1)}, bf16[2,3,32,128]{3,2,1,0:T(8,128)(2,1)S(1)}, u32[]{:S(2)}, u32[]{:S(2)}) %collective-permute-start.20) | collective-permute-done | bytes 49184 | tf_op jit(solution)/shard_map/ppermute | solution.py:21
  67.0 1.3 %collective-permute-done.19.refs_1_ = bf16[2,3,32,128]{3,2,1,0:T(8,128)(2,1)S(1)} collective-permute-done((bf16[2,3,32,128]{3,2,1,0:T(8,128)(2,1)S(1)}, bf16[2,3,32,128]{3,2,1,0:T(8,128)(2,1)S(1)}, u32[]{:S(2)}, u32[]{:S(2)}) %collective-permute-start.19) | collective-permute-done | bytes 49184 | tf_op jit(solution)/shard_map/ppermute | solution.py:21
  68.2 0.8 %shard_map.65 = f32[8,3,32,128]{3,2,1,0:T(8,128)} custom-call(s32[1]{0:T(128)} %bitcast.mine_ref, f32[3,32,128]{2,1,0:T(8,128)S(1)} %get-tuple-element.62.home_ref, bf16[3,32,128]{2,1,0:T(8,128)(2,1)S(1)} %slice_bitcast_fusion.1.beside_ref, bf16[2,3,32,128]{3,2,1,0:T(8,128)(2,1)S(1)} %collective-permute-done.18.refs_0_, ...), custom_call_target="tpu_custom_call" | custom-call | tf_op jit(solution)/shard_map/pallas_call | solution.py:355
  (43 shorter events, 6.1 us)
Async XLA Ops:
  2.8 15.3 %collective-permute-start.3 = (bf16[128,2048]{1,0:T(8,128)(2,1)}, bf16[128,2048]{1,0:T(8,128)(2,1)}, u32[]{:S(2)}, u32[]{:S(2)}) collective-permute-start(bf16[128,2048]{1,0:T(8,128)(2,1)} %get-tuple-element.43), channel_id=1, source_target_pairs={{0,16},{4,20},{8,24},{12,28},{16,0},{20,4},{24,8},{28,12},{1,17},{... | collective-permute-start | bytes 1572872 | tf_op jit(solution)/shard_map/ppermute | solution.py:21
  5.9 15.2 %collective-permute-start.4 = (bf16[128,2048]{1,0:T(8,128)(2,1)}, bf16[128,2048]{1,0:T(8,128)(2,1)}, u32[]{:S(2)}, u32[]{:S(2)}) collective-permute-start(bf16[128,2048]{1,0:T(8,128)(2,1)} %get-tuple-element.44), channel_id=1, source_target_pairs={{0,8},{4,12},{8,0},{12,4},{16,24},{20,28},{24,16},{28,20},{1,9},{5... | collective-permute-start | bytes 1572872 | tf_op jit(solution)/shard_map/ppermute | solution.py:21
  7.4 3.8 %copy-start.1 = (s32[14,1]{0,1:T(1,128)S(1)}, s32[14,1]{0,1:T(1,128)}, u32[]{:S(2)}) copy-start(s32[14,1]{0,1:T(1,128)} %param.8) | copy-start | bytes 172
  7.4 4.0 %copy-start.2 = (s32[14,2]{0,1:T(2,128)S(1)}, s32[14,2]{0,1:T(2,128)}, u32[]{:S(2)}) copy-start(s32[14,2]{0,1:T(2,128)} %param.7) | copy-start | bytes 340
  10.6 1.6 %collective-permute-start = (bf16[128,1024]{1,0:T(8,128)(2,1)S(1)}, bf16[128,1024]{1,0:T(8,128)(2,1)S(1)}, u32[]{:S(2)}, u32[]{:S(2)}) collective-permute-start(bf16[128,1024]{1,0:T(8,128)(2,1)S(1)} %get-tuple-element.39.refs_0_.refs_2_.refs_4_), channel_id=1, source_target_pairs={{0,4},{4,0},{8,12},{12,8},{16,20},{20,16},{24,28},{28,24},{1,5},{5... | collective-permute-start | bytes 786440 | tf_op jit(solution)/shard_map/ppermute | solution.py:21
  10.7 1.9 %collective-permute-start.1 = (bf16[128,1024]{1,0:T(8,128)(2,1)S(1)}, bf16[128,1024]{1,0:T(8,128)(2,1)S(1)}, u32[]{:S(2)}, u32[]{:S(2)}) collective-permute-start(bf16[128,1024]{1,0:T(8,128)(2,1)S(1)} %get-tuple-element.40.refs_1_.refs_3_.refs_5_), channel_id=1, source_target_pairs={{0,4},{4,0},{8,12},{12,8},{16,20},{20,16},{24,28},{28,24},{1,5},{5... | collective-permute-start | bytes 786440 | tf_op jit(solution)/shard_map/ppermute | solution.py:21
  14.1 10.5 %copy-start = (s32[14,1]{0,1:T(1,128)S(1)}, s32[14,1]{0,1:T(1,128)}, u32[]{:S(2)}) copy-start(s32[14,1]{0,1:T(1,128)} %param.9) | copy-start | bytes 172
  14.1 16.4 %collective-permute-start.2 = (bf16[128,2048]{1,0:T(8,128)(2,1)S(1)}, bf16[128,2048]{1,0:T(8,128)(2,1)S(1)}, u32[]{:S(2)}, u32[]{:S(2)}) collective-permute-start(bf16[128,2048]{1,0:T(8,128)(2,1)S(1)} %get-tuple-element.41), channel_id=1, source_target_pairs={{0,24},{4,28},{8,16},{12,20},{16,8},{20,12},{24,0},{28,4},{1,25},{... | collective-permute-start | bytes 1572872 | tf_op jit(solution)/shard_map/ppermute | solution.py:21
  23.5 1.6 %collective-permute-start.5 = (bf16[256,512]{1,0:T(8,128)(2,1)S(1)}, bf16[256,512]{1,0:T(8,128)(2,1)S(1)}, u32[]{:S(2)}, u32[]{:S(2)}) collective-permute-start(bf16[256,512]{1,0:T(8,128)(2,1)S(1)} %get-tuple-element.45.refs_4_.refs_6_), channel_id=1, source_target_pairs={{0,4},{4,0},{8,12},{12,8},{16,20},{20,16},{24,28},{28,24},{1,5},{5... | collective-permute-start | bytes 786440 | tf_op jit(solution)/shard_map/ppermute | solution.py:21
  23.6 1.9 %collective-permute-start.6 = (bf16[256,512]{1,0:T(8,128)(2,1)S(1)}, bf16[256,512]{1,0:T(8,128)(2,1)S(1)}, u32[]{:S(2)}, u32[]{:S(2)}) collective-permute-start(bf16[256,512]{1,0:T(8,128)(2,1)S(1)} %get-tuple-element.46.refs_5_.refs_7_), channel_id=1, source_target_pairs={{0,4},{4,0},{8,12},{12,8},{16,20},{20,16},{24,28},{28,24},{1,5},{5... | collective-permute-start | bytes 786440 | tf_op jit(solution)/shard_map/ppermute | solution.py:21
  24.1 1.8 %collective-permute-start.7 = (bf16[256,512]{1,0:T(8,128)(2,1)S(1)}, bf16[256,512]{1,0:T(8,128)(2,1)S(1)}, u32[]{:S(2)}, u32[]{:S(2)}) collective-permute-start(bf16[256,512]{1,0:T(8,128)(2,1)S(1)} %get-tuple-element.47.refs_6_.refs_8_), channel_id=1, source_target_pairs={{0,4},{4,0},{8,12},{12,8},{16,20},{20,16},{24,28},{28,24},{1,5},{5... | collective-permute-start | bytes 786440 | tf_op jit(solution)/shard_map/ppermute | solution.py:21
  24.2 2.1 %collective-permute-start.8 = (bf16[256,512]{1,0:T(8,128)(2,1)S(1)}, bf16[256,512]{1,0:T(8,128)(2,1)S(1)}, u32[]{:S(2)}, u32[]{:S(2)}) collective-permute-start(bf16[256,512]{1,0:T(8,128)(2,1)S(1)} %get-tuple-element.48.refs_7_.refs_9_), channel_id=1, source_target_pairs={{0,4},{4,0},{8,12},{12,8},{16,20},{20,16},{24,28},{28,24},{1,5},{5... | collective-permute-start | bytes 786440 | tf_op jit(solution)/shard_map/ppermute | solution.py:21
  31.3 1.7 %collective-permute-start.9 = (bf16[128,1024]{1,0:T(8,128)(2,1)S(1)}, bf16[128,1024]{1,0:T(8,128)(2,1)S(1)}, u32[]{:S(2)}, u32[]{:S(2)}) collective-permute-start(bf16[128,1024]{1,0:T(8,128)(2,1)S(1)} %get-tuple-element.50.refs_0_), channel_id=1, source_target_pairs={{0,4},{4,0},{8,12},{12,8},{16,20},{20,16},{24,28},{28,24},{1,5},{5... | collective-permute-start | bytes 786440 | tf_op jit(solution)/shard_map/ppermute | solution.py:21
  31.4 1.9 %collective-permute-start.10 = (bf16[128,1024]{1,0:T(8,128)(2,1)S(1)}, bf16[128,1024]{1,0:T(8,128)(2,1)S(1)}, u32[]{:S(2)}, u32[]{:S(2)}) collective-permute-start(bf16[128,1024]{1,0:T(8,128)(2,1)S(1)} %get-tuple-element.51.refs_1_), channel_id=1, source_target_pairs={{0,4},{4,0},{8,12},{12,8},{16,20},{20,16},{24,28},{28,24},{1,5},{5... | collective-permute-start | bytes 786440 | tf_op jit(solution)/shard_map/ppermute | solution.py:21
  34.0 8.5 %collective-permute-start.11 = (bf16[128,896]{1,0:T(8,128)(2,1)S(1)}, bf16[128,896]{1,0:T(8,128)(2,1)S(1)}, u32[]{:S(2)}, u32[]{:S(2)}) collective-permute-start(bf16[128,896]{1,0:T(8,128)(2,1)S(1)} %get-tuple-element.55), channel_id=1, source_target_pairs={{0,8},{4,12},{8,0},{12,4},{16,24},{20,28},{24,16},{28,20},{1,9},{5... | collective-permute-start | bytes 688136 | tf_op jit(solution)/shard_map/ppermute | solution.py:21
  35.7 12.3 %collective-permute-start.12 = (bf16[128,896]{1,0:T(8,128)(2,1)S(1)}, bf16[128,896]{1,0:T(8,128)(2,1)S(1)}, u32[]{:S(2)}, u32[]{:S(2)}) collective-permute-start(bf16[128,896]{1,0:T(8,128)(2,1)S(1)} %get-tuple-element.56), channel_id=1, source_target_pairs={{0,16},{4,20},{8,24},{12,28},{16,0},{20,4},{24,8},{28,12},{1,17},{... | collective-permute-start | bytes 688136 | tf_op jit(solution)/shard_map/ppermute | solution.py:21
  37.2 10.8 %collective-permute-start.13 = (bf16[128,896]{1,0:T(8,128)(2,1)S(1)}, bf16[128,896]{1,0:T(8,128)(2,1)S(1)}, u32[]{:S(2)}, u32[]{:S(2)}) collective-permute-start(bf16[128,896]{1,0:T(8,128)(2,1)S(1)} %get-tuple-element.57), channel_id=1, source_target_pairs={{0,24},{4,28},{8,16},{12,20},{16,8},{20,12},{24,0},{28,4},{1,25},{... | collective-permute-start | bytes 688136 | tf_op jit(solution)/shard_map/ppermute | solution.py:21
  48.7 5.0 %collective-permute-start.14 = (bf16[32,1024]{1,0:T(8,128)(2,1)S(1)}, bf16[32,1024]{1,0:T(8,128)(2,1)S(1)}, u32[]{:S(2)}, u32[]{:S(2)}) collective-permute-start(bf16[32,1024]{1,0:T(8,128)(2,1)S(1)} %get-tuple-element.59), channel_id=1, source_target_pairs={{0,1},{1,0},{2,3},{3,2},{4,5},{5,4},{6,7},{7,6},{8,9},{9,8},{10,11... | collective-permute-start | bytes 196616 | tf_op jit(solution)/shard_map/ppermute | solution.py:21
  50.3 6.6 %collective-permute-start.15 = (bf16[32,1024]{1,0:T(8,128)(2,1)S(1)}, bf16[32,1024]{1,0:T(8,128)(2,1)S(1)}, u32[]{:S(2)}, u32[]{:S(2)}) collective-permute-start(bf16[32,1024]{1,0:T(8,128)(2,1)S(1)} %get-tuple-element.60), channel_id=1, source_target_pairs={{0,2},{1,3},{2,0},{3,1},{4,6},{5,7},{6,4},{7,5},{8,10},{9,11},{10,... | collective-permute-start | bytes 196616 | tf_op jit(solution)/shard_map/ppermute | solution.py:21
  52.9 6.1 %collective-permute-start.16 = (bf16[32,1024]{1,0:T(8,128)(2,1)S(1)}, bf16[32,1024]{1,0:T(8,128)(2,1)S(1)}, u32[]{:S(2)}, u32[]{:S(2)}) collective-permute-start(bf16[32,1024]{1,0:T(8,128)(2,1)S(1)} %get-tuple-element.61), channel_id=1, source_target_pairs={{0,3},{1,2},{2,1},{3,0},{4,7},{5,6},{6,5},{7,4},{8,11},{9,10},{10,... | collective-permute-start | bytes 196616 | tf_op jit(solution)/shard_map/ppermute | solution.py:21
  59.7 1.4 %collective-permute-start.17 = (bf16[4,3,32,128]{3,2,1,0:T(8,128)(2,1)S(1)}, bf16[4,3,32,128]{3,2,1,0:T(8,128)(2,1)S(1)}, u32[]{:S(2)}, u32[]{:S(2)}) collective-permute-start(bf16[4,3,32,128]{3,2,1,0:T(8,128)(2,1)S(1)} %get-tuple-element.63), channel_id=1, source_target_pairs={{0,4},{4,0},{8,12},{12,8},{16,20},{20,16},{24,28},{28,24},{1,5},{5... | collective-permute-start | bytes 294920 | tf_op jit(solution)/shard_map/ppermute | solution.py:21
  61.1 5.5 %collective-permute-start.20 = (bf16[2,3,32,128]{3,2,1,0:T(8,128)(2,1)S(1)}, bf16[2,3,32,128]{3,2,1,0:T(8,128)(2,1)S(1)}, u32[]{:S(2)}, u32[]{:S(2)}) collective-permute-start(bf16[2,3,32,128]{3,2,1,0:T(8,128)(2,1)S(1)} %get-tuple-element.67), channel_id=1, source_target_pairs={{0,24},{4,28},{8,16},{12,20},{16,8},{20,12},{24,0},{28,4},{1,25},{... | collective-permute-start | bytes 147464 | tf_op jit(solution)/shard_map/ppermute | solution.py:21
  62.7 4.3 %collective-permute-start.18 = (bf16[2,3,32,128]{3,2,1,0:T(8,128)(2,1)S(1)}, bf16[2,3,32,128]{3,2,1,0:T(8,128)(2,1)S(1)}, u32[]{:S(2)}, u32[]{:S(2)}) collective-permute-start(bf16[2,3,32,128]{3,2,1,0:T(8,128)(2,1)S(1)} %get-tuple-element.68), channel_id=1, source_target_pairs={{0,8},{4,12},{8,0},{12,4},{16,24},{20,28},{24,16},{28,20},{1,9},{5... | collective-permute-start | bytes 147464 | tf_op jit(solution)/shard_map/ppermute | solution.py:21
  64.2 4.1 %collective-permute-start.19 = (bf16[2,3,32,128]{3,2,1,0:T(8,128)(2,1)S(1)}, bf16[2,3,32,128]{3,2,1,0:T(8,128)(2,1)S(1)}, u32[]{:S(2)}, u32[]{:S(2)}) collective-permute-start(bf16[2,3,32,128]{3,2,1,0:T(8,128)(2,1)S(1)} %get-tuple-element.69), channel_id=1, source_target_pairs={{0,16},{4,20},{8,24},{12,28},{16,0},{20,4},{24,8},{28,12},{1,17},{... | collective-permute-start | bytes 147464 | tf_op jit(solution)/shard_map/ppermute | solution.py:21

commit v4 on v3

--- a/solution.py
+++ b/solution.py
@@ -10,6 +10,8 @@
 TILE = 128
 CORES = 2
 MIB = 1024 * 1024
+MIDDLE_WEIGHT = 60 * 10**8
+HOME_WEIGHT = 12 * 10**8
 SMEM = pl.BlockSpec(memory_space=pltpu.SMEM)
 VMEM = pl.BlockSpec(memory_space=pltpu.VMEM)
 HBM = pl.BlockSpec(memory_space=pltpu.HBM)
@@ -29,7 +31,7 @@
     return pltpu.VMEM(shape, dtype)
 
 
-def kernel_call(body, ins, outs, out_specs, grant, scratch=()):
+def kernel_call(body, ins, outs, out_specs, grant, scratch=(), weight=None):
     return pl.pallas_call(
         body,
         out_shape=outs,
@@ -37,6 +39,8 @@
         out_specs=out_specs,
         scratch_shapes=scratch,
         compiler_params=pltpu.CompilerParams(vmem_limit_bytes=grant * MIB),
+        cost_estimate=weight
+        and pl.CostEstimate(flops=weight, bytes_accessed=MIB, transcendentals=0),
     )
 
 
@@ -168,51 +172,57 @@
     return held, fitted
 
 
+def spot(number):
+    return slice(number * TILE, (number + 1) * TILE)
+
+
 def place(block, chip):
-    spot = ((block ^ (CORES * chip)) - 1) * TILE
-    return slice(spot, spot + TILE)
-
-
-def put(slabs, chip, block, tile):
-    if block != CORES * chip:
-        slabs[chip][:, place(block, chip)] = tile.astype(slabs[chip].dtype)
+    return (block ^ (CORES * chip)) - 1
+
+
+def early_blocks(chip, final):
+    return [block for block in range(CORES * final) if block != CORES * chip]
 
 
 def part(value, row, column):
-    return value[row * TILE : (row + 1) * TILE, column * TILE : (column + 1) * TILE]
+    return value[spot(row), spot(column)]
 
 
 def early_kernel(counts, *refs):
     own, own_beside, others, others_beside, slabs = unpack(refs, counts)
+    final = len(slabs)
     count = others[0].shape[0] // TILE
-    put(slabs, 0, 1, gram(own, own_beside))
-    outer = gram(others, own_beside)
     across = gram(own, others)
     beside = gram(own, others_beside)
+    outer = gram(others, own_beside)
     inner = gram(others, others)
     sideways = gram(others, others_beside)
+    tiles = {(0, 1): gram(own, own_beside)}
     for at in range(count):
         chip = at + 1
-        put(slabs, 0, CORES * chip, part(across, 0, at))
-        put(slabs, 0, CORES * chip + 1, part(beside, 0, at))
-        put(slabs, chip, 0, part(across, 0, at).T)
-        put(slabs, chip, 1, part(outer, at, 0))
+        tiles[0, CORES * chip] = part(across, 0, at)
+        tiles[0, CORES * chip + 1] = part(beside, 0, at)
+        tiles[chip, 0] = part(across, 0, at).T
+        tiles[chip, 1] = part(outer, at, 0)
         for other in range(count):
-            put(slabs, chip, CORES * (other + 1), part(inner, at, other))
-            put(slabs, chip, CORES * (other + 1) + 1, part(sideways, at, other))
+            tiles[chip, CORES * (other + 1)] = part(inner, at, other)
+            tiles[chip, CORES * (other + 1) + 1] = part(sideways, at, other)
+    for chip, slab in enumerate(slabs):
+        for at, block in enumerate(early_blocks(chip, final)):
+            where = place(block, chip) if chip == 0 else at
+            slab[:, spot(where)] = tiles[chip, block].astype(slab.dtype)
 
 
 def early(own, own_beside, others, others_beside):
-    rows = own[0].shape[0]
-    chips = others[0].shape[0] // rows + 2
-    span = (CORES * chips - 1) * TILE
+    final = others[0].shape[0] // TILE + 1
+    span = (CORES * final - 1) * TILE
     given = [own, own_beside, others, others_beside]
-    counts = [len(pieces) for pieces in given] + [chips - 1]
+    counts = [len(pieces) for pieces in given] + [final]
     return kernel_call(
         functools.partial(early_kernel, counts),
         [VMEM] * sum(counts[:-1]),
-        [kept((rows, span), jnp.bfloat16 if chip else jnp.float32) for chip in range(chips - 1)],
-        [VMEM] * (chips - 1),
+        [kept((TILE, span), jnp.bfloat16 if chip else jnp.float32) for chip in range(final)],
+        [VMEM] * final,
         12,
     )(*[piece for pieces in given for piece in pieces])
 
@@ -237,57 +247,92 @@
         kept((rows, span), jnp.float32),
         VMEM,
         8,
+        weight=MIDDLE_WEIGHT,
     )(*[piece for pieces in given for piece in pieces])
 
 
 def late_kernel(counts, *refs):
-    last, last_beside, own, others, (middle_ref,), begun, slabs = unpack(refs, counts)
-    count = others[0].shape[0] // TILE
-    final = count + 1
+    last, last_beside, own, others, (middle_ref,), slabs, (side_ref,) = unpack(refs, counts)
+    final = len(slabs)
+    last_slab = slabs[-1]
+    tall = gram(others, last_beside)
+    side_ref[...] = gram(own, last_beside)
+    tile = gram(last, last_beside)
+    last_slab[:, spot(place(CORES * final + 1, final))] = tile.astype(jnp.bfloat16)
     for chip in range(final):
-        slabs[chip][:, : begun[chip].shape[1]] = begun[chip][...]
-    tall = gram(others, last_beside)
-    put(slabs, 0, CORES * final + 1, gram(own, last_beside))
-    put(slabs, final, CORES * final + 1, gram(last, last_beside))
-    for core in range(CORES):
-        put(slabs, final, core, middle_ref[:, core * TILE : (core + 1) * TILE])
-        for at in range(count):
-            spot = (CORES + core * count + at) * TILE
-            put(slabs, final, CORES * (at + 1) + core, middle_ref[:, spot : spot + TILE])
-    put(slabs, 0, CORES * final, middle_ref[:, :TILE].T)
-    for at in range(count):
-        spot = (CORES + at) * TILE
-        put(slabs, at + 1, CORES * final, middle_ref[:, spot : spot + TILE].T)
-        put(slabs, at + 1, CORES * final + 1, part(tall, at, 0))
-
-
-def late(last, last_beside, own, others, across, begun):
-    rows = own[0].shape[0]
-    chips = len(begun) + 1
-    span = (CORES * chips - 1) * TILE
-    given = [last, last_beside, own, others, [across], begun]
-    counts = [len(pieces) for pieces in given] + [chips]
+        straight = middle_ref[:, spot(chip + 1 if chip else 0)]
+        sideways = middle_ref[:, spot(chip + final if chip else 1)]
+        last_slab[:, spot(place(CORES * chip, final))] = straight.astype(jnp.bfloat16)
+        last_slab[:, spot(place(CORES * chip + 1, final))] = sideways.astype(jnp.bfloat16)
+        if chip:
+            slabs[chip - 1][:, spot(0)] = straight.T.astype(jnp.bfloat16)
+            slabs[chip - 1][:, spot(1)] = part(tall, chip - 1, 0).astype(jnp.bfloat16)
+
+
+def late(last, last_beside, own, others, across):
+    final = others[0].shape[0] // TILE + 1
+    span = (CORES * final + 1) * TILE
+    given = [last, last_beside, own, others, [across]]
+    counts = [len(pieces) for pieces in given] + [final, 1]
     return kernel_call(
         functools.partial(late_kernel, counts),
-        [VMEM] * sum(counts[:-1]),
-        [kept((rows, span), jnp.bfloat16 if chip else jnp.float32) for chip in range(chips)],
-        [VMEM] * chips,
+        [VMEM] * sum(counts[:-2]),
+        [kept((TILE, CORES * TILE), jnp.bfloat16)] * (final - 1)
+        + [kept((TILE, span), jnp.bfloat16), kept((TILE, TILE), jnp.float32)],
+        [VMEM] * (final + 1),
         12,
     )(*[piece for pieces in given for piece in pieces])
 
 
+def home_kernel(counts, *refs):
+    (middle_ref, side_ref, begun), came, (own_slab,) = unpack(refs, counts)
+    final = len(came) + 1
+
+    def with_early(tile, block):
+        for at, ref in enumerate(came):
+            seen = block ^ (CORES * (at + 1))
+            blocks = early_blocks(at + 1, final)
+            if seen in blocks:
+                tile = tile + ref[:, spot(blocks.index(seen))].astype(jnp.float32)
+        own_slab[:, spot(place(block, 0))] = tile
+
+    for block in early_blocks(0, final):
+        with_early(begun[:, spot(place(block, 0))], block)
+    with_early(middle_ref[:, spot(0)].T, CORES * final)
+    with_early(side_ref[...], CORES * final + 1)
+
+
+def home_slab(across, side, begun, came):
+    span = (CORES * (len(came) + 2) - 1) * TILE
+    given = [[across, side, begun], came]
+    counts = [len(pieces) for pieces in given] + [1]
+    return kernel_call(
+        functools.partial(home_kernel, counts),
+        [VMEM] * sum(counts[:-1]),
+        kept((TILE, span), jnp.float32),
+        VMEM,
+        8,
+        weight=HOME_WEIGHT,
+    )(*[piece for pieces in given for piece in pieces])
+
+
 def strips_kernel(starts_ref, weights_ref, own_ref, *refs):
     groups = starts_ref.shape[0]
-    came, strips = refs[:-groups], refs[-groups:]
+    (last_came, *came), strips = refs[:-groups], refs[-groups:]
+    final = len(came) + 1
     share = strips[0].shape[0]
     span = own_ref.shape[1]
     for distance, strip in enumerate(strips):
         rows = pl.ds(pl.multiple_of(starts_ref[distance], share), share)
-        total = own_ref[rows, :]
-        for ref in came:
-            total = total + ref[rows, :].astype(jnp.float32)
-        strip[:, :span] = total.astype(strip.dtype)
         strip[:, span:] = weights_ref[...].astype(strip.dtype)
+        for number in range(span // TILE):
+            total = own_ref[rows, spot(number)]
+            total = total + last_came[rows, spot(number)].astype(jnp.float32)
+            for at, ref in enumerate(came):
+                core = ((number + 1) ^ (CORES * (at + 1))) - CORES * final
+                if core in range(CORES):
+                    total = total + ref[rows, spot(core)].astype(jnp.float32)
+            strip[:, spot(number)] = total.astype(strip.dtype)
 
 
 def strips(own, came, starts, weights):
@@ -404,18 +449,21 @@
     others = fit(arrived, metric, 4)
     others_beside = beside(others)
     begun = early(own, own_beside, others, others_beside)
+    came_early = [swapped(begun[chip], "blk", CORES * chip) for chip in range(1, final)]
 
     last_fitted = fit([last], metric, 2, (), (blocks, weights, begun[0]))
     last_beside = beside(last_fitted)
     across = middle(last_fitted, own, own_beside, others, others_beside)
-    slabs = late(last_fitted, last_beside, own, others, across, begun)
-
-    came = [swapped(slabs[chip], "blk", CORES * chip) for chip in range(1, chips)]
+    *slabs, side = late(last_fitted, last_beside, own, others, across)
+    came = [
+        swapped(slabs[chip - 1], "blk", CORES * chip) for chip in (final, *range(1, final))
+    ]
+    own_slab = home_slab(across, side, begun[0], came_early)
     strip_starts = (my_group ^ jnp.arange(groups, dtype=jnp.int32)) * share
-    own_strips = strips(slabs[0], came, strip_starts, weights)
+    own_strips = strips(own_slab, came, strip_starts, weights)
     chunks = [own_strips[0]] + [swapped(own_strips[d], "grp", d) for d in range(1, groups)]
 
-    home, straight, crossing = combine(blocks, chunks, slabs[0].shape[1], chips, capacity)
+    home, straight, crossing = combine(blocks, [chunks[-1], *chunks[1:-1], chunks[0]], own_slab.shape[1], chips, capacity)
     crossed = swapped(crossing, "blk", 1)
     paired = jnp.stack([straight, crossed[1:]], axis=1)
     received = [

time: 69.3 us -> 64.6 us (0.932)
  waiting for transfers between devices: 33.3 us -> 25 us
  starting transfers between devices: 18.5 us -> 20.5 us
  Pallas kernels: 16.5 us -> 18.2 us
    ppermute x21 -> x23, waiting for transfers between devices: 33.3 us -> 25 us  [swapped(): lax.ppermute(value, axis, [(source, source ^ distance) for source in rang...]
    ppermute x21 -> x23, starting transfers between devices: 18.5 us -> 20.5 us  [swapped(): lax.ppermute(value, axis, [(source, source ^ distance) for source in rang...]
    pallas_call x0 -> x1, Pallas kernels: none -> 1.13 us  [home_slab(): kernel_call(functools.partial(home_kernel, counts), [VMEM] * sum(counts[:...]
  transfers between devices with their start and end apart: 21 -> 23, of which waited for: 19 -> 17; matrix products, arithmetic and copies ran while one was open for 0% -> 1% of each run, Pallas kernels for 15% -> 21%
where the time goes in v4:
time: 64.6 us; the launch traced here: 64.4 us
  waiting for transfers between devices  25 us (39%)
  starting transfers between devices  20.5 us (32%)
  Pallas kernels  18.2 us (28%)
    ppermute x23, waiting for transfers between devices, swapped(): lax.ppermute(value, axis, [(source, source ^ distance) for source in rang...  25 us
    ppermute x23, starting transfers between devices, swapped(): lax.ppermute(value, axis, [(source, source ^ distance) for source in rang...  20.5 us
    pallas_call x2, Pallas kernels, cut(): kernel_call(functools.partial(cut_kernel, count), [SMEM, HBM] + [ANY] * l...  4.34 us
    pallas_call x2, Pallas kernels, fit(): kernel_call(functools.partial(fit_kernel, len(panels), pieces), [VMEM] *...  3.22 us
    pallas_call x1, Pallas kernels, first_fit(): kernel_call(first_fit_kernel, [SMEM, SMEM, HBM, HBM], [kept(metric.shape,...  3.2 us
    pallas_call x1, Pallas kernels, early(): kernel_call(functools.partial(early_kernel, counts), [VMEM] * sum(counts[...  2.41 us
  transfers between devices with their start and end apart: 23, of which 17 were waited for; matrix products, arithmetic and copies ran while one was open for 1% of the time, Pallas kernels for 21%

profile of v4, /device:TPU:0, one launch (start us, length us, event | category | flops | bytes accessed | tf_op | source)
XLA Modules:
  0.0 64.4 jit_solution(4790807135312478447)
XLA Ops:
  0.1 2.8 %shard_map.55 = (bf16[128,2048]{1,0:T(8,128)(2,1)}, bf16[128,2048]{1,0:T(8,128)(2,1)}, s32[1]{0:T(128)}) custom-call(s32[2]{0:T(128)S(1)} %pad_add_fusion.starts_ref, bf16[128,8192]{1,0:T(8,128)(2,1)} %bitcast.23), custom_call_target="tpu_custom_call" | custom-call | tf_op jit(solution)/shard_map/pallas_call | solution.py:141
  2.9 3.0 %collective-permute-start.3 = (bf16[128,2048]{1,0:T(8,128)(2,1)}, bf16[128,2048]{1,0:T(8,128)(2,1)}, u32[]{:S(2)}, u32[]{:S(2)}) collective-permute-start(bf16[128,2048]{1,0:T(8,128)(2,1)} %get-tuple-element.43), channel_id=1, source_target_pairs={{0,16},{4,20},{8,24},{12,28},{16,0},{20,4},{24,8},{28,12},{1,17},{... | collective-permute-start | bytes 1572872 | tf_op jit(solution)/shard_map/ppermute | solution.py:23
  5.9 1.5 %collective-permute-start.4 = (bf16[128,2048]{1,0:T(8,128)(2,1)}, bf16[128,2048]{1,0:T(8,128)(2,1)}, u32[]{:S(2)}, u32[]{:S(2)}) collective-permute-start(bf16[128,2048]{1,0:T(8,128)(2,1)} %get-tuple-element.44), channel_id=1, source_target_pairs={{0,8},{4,12},{8,0},{12,4},{16,24},{20,28},{24,16},{28,20},{1,9},{5... | collective-permute-start | bytes 1572872 | tf_op jit(solution)/shard_map/ppermute | solution.py:23
  7.4 3.2 %shard_map.56 = (bf16[1024,1024]{1,0:T(8,128)(2,1)S(1)}, bf16[128,1024]{1,0:T(8,128)(2,1)S(1)}, bf16[128,1024]{1,0:T(8,128)(2,1)S(1)}) custom-call(s32[1]{0:T(128)} %get-tuple-element.38.token_ref, s32[1]{0:T(128)} %bitcast.8.starts_ref, bf16[128,8192]{1,0:T(8,128)(2,1)} %bitcast.24, bf16[1024,1024]{1,0:T(8,128)(2,1)} %metric_ref.1), custom_call_target="tpu_custom_call" | custom-call | tf_op jit(solution)/shard_map/pallas_call | solution.py:163
  11.4 0.8 %collective-permute-done.refs_0_.refs_2_.refs_4_ = bf16[128,1024]{1,0:T(8,128)(2,1)S(1)} collective-permute-done((bf16[128,1024]{1,0:T(8,128)(2,1)S(1)}, bf16[128,1024]{1,0:T(8,128)(2,1)S(1)}, u32[]{:S(2)}, u32[]{:S(2)}) %collective-permute-start) | collective-permute-done | bytes 262176 | tf_op jit(solution)/shard_map/ppermute | solution.py:23
  12.6 1.6 %shard_map.57 = (bf16[128,2048]{1,0:T(8,128)(2,1)S(1)}, s32[1]{0:T(128)}) custom-call(s32[1]{0:T(128)} %bitcast.4.starts_ref, bf16[128,8192]{1,0:T(8,128)(2,1)} %bitcast.25, bf16[128,1024]{1,0:T(8,128)(2,1)S(1)} %collective-permute-done.refs_0_.refs_2_.refs_4_, bf16[128,1024]{1,0:T(8,128)(2,1)S(1)} %collective-permute-done.1.refs_1_.refs_3_.refs_5_), custom_call_target="tpu_custom_call" | custom-call | tf_op jit(solution)/shard_map/pallas_call | solution.py:141
  14.3 3.8 %collective-permute-done.3.refs_0_ = bf16[128,2048]{1,0:T(8,128)(2,1)} collective-permute-done((bf16[128,2048]{1,0:T(8,128)(2,1)}, bf16[128,2048]{1,0:T(8,128)(2,1)}, u32[]{:S(2)}, u32[]{:S(2)}) %collective-permute-start.3) | collective-permute-done | bytes 524320 | tf_op jit(solution)/shard_map/ppermute | solution.py:23
  18.1 2.9 %collective-permute-done.4.refs_1_ = bf16[128,2048]{1,0:T(8,128)(2,1)} collective-permute-done((bf16[128,2048]{1,0:T(8,128)(2,1)}, bf16[128,2048]{1,0:T(8,128)(2,1)}, u32[]{:S(2)}, u32[]{:S(2)}) %collective-permute-start.4) | collective-permute-done | bytes 524320 | tf_op jit(solution)/shard_map/ppermute | solution.py:23
  21.1 2.5 %shard_map.58 = (bf16[256,512]{1,0:T(8,128)(2,1)S(1)}, bf16[256,512]{1,0:T(8,128)(2,1)S(1)}, bf16[256,512]{1,0:T(8,128)(2,1)S(1)}, bf16[256,512]{1,0:T(8,128)(2,1)S(1)}) custom-call(bf16[128,2048]{1,0:T(8,128)(2,1)} %collective-permute-done.3.refs_0_, bf16[128,2048]{1,0:T(8,128)(2,1)} %collective-permute-done.4.refs_1_, ...), custom_call_target="tpu_custom_call" | custom-call | tf_op jit(solution)/shard_map/pallas_call | solution.py:104
  26.3 2.4 %shard_map.59 = (f32[128,640]{1,0:T(8,128)S(1)}, bf16[128,640]{1,0:T(8,128)(2,1)}, bf16[128,640]{1,0:T(8,128)(2,1)}) custom-call(bf16[128,1024]{1,0:T(8,128)(2,1)S(1)} %get-tuple-element.39.refs_0_.refs_2_.refs_4_, bf16[128,1024]{1,0:T(8,128)(2,1)S(1)} %get-tuple-element.40.refs_1_.refs_3_.refs_5_, ...), custom_call_target="tpu_custom_call" | custom-call | tf_op jit(solution)/shard_map/pallas_call | solution.py:221
  28.7 1.5 %collective-permute-start.11 = (bf16[128,640]{1,0:T(8,128)(2,1)}, bf16[128,640]{1,0:T(8,128)(2,1)}, u32[]{:S(2)}, u32[]{:S(2)}) collective-permute-start(bf16[128,640]{1,0:T(8,128)(2,1)} %get-tuple-element.53), channel_id=1, source_target_pairs={{0,8},{4,12},{8,0},{12,4},{16,24},{20,28},{24,16},{28,20},{1,9},{5... | collective-permute-start | bytes 491528 | tf_op jit(solution)/shard_map/ppermute | solution.py:23
  30.8 0.7 %shard_map.60 = (bf16[128,1024]{1,0:T(8,128)(2,1)S(1)}, bf16[128,1024]{1,0:T(8,128)(2,1)S(1)}) custom-call(bf16[128,2048]{1,0:T(8,128)(2,1)S(1)} %collective-permute-done.2.refs_0_, bf16[1024,1024]{1,0:T(8,128)(2,1)S(1)} %get-tuple-element.42.refs_2_.refs_1_, s32[24]{0:T(128)S(1)} %add_maximum_fusion.refs_2_.block_ref, ...), custom_call_target="tpu_custom_call" | custom-call | tf_op jit(solution)/shard_map/pallas_call | solution.py:104
  32.1 1.1 %shard_map.61.refs_10_.refs_0_ = f32[128,768]{1,0:T(8,128)S(1)} custom-call(bf16[128,1024]{1,0:T(8,128)(2,1)S(1)} %get-tuple-element.50.refs_0_, bf16[128,1024]{1,0:T(8,128)(2,1)S(1)} %get-tuple-element.51.refs_1_, bf16[128,1024]{1,0:T(8,128)(2,1)S(1)} %get-tuple-element.39.refs_0_.refs_2_.refs_4_, ...), custom_call_target="tpu_custom_call" | custom-call | flops 6000000000 | bytes 1048576 | tf_op jit(solution)/shard_map/pallas_call | solution.py:244
  33.5 0.7 %shard_map.62 = (bf16[128,256]{1,0:T(8,128)(2,1)S(1)}, bf16[128,256]{1,0:T(8,128)(2,1)S(1)}, bf16[128,896]{1,0:T(8,128)(2,1)S(1)}, f32[128,128]{1,0:T(8,128)S(1)}) custom-call(bf16[128,1024]{1,0:T(8,128)(2,1)S(1)} %get-tuple-element.50.refs_0_, bf16[128,1024]{1,0:T(8,128)(2,1)S(1)} %get-tuple-element.51.refs_1_, ...), custom_call_target="tpu_custom_call" | custom-call | tf_op jit(solution)/shard_map/pallas_call | solution.py:277
  34.2 2.5 %collective-permute-start.13 = (bf16[128,896]{1,0:T(8,128)(2,1)S(1)}, bf16[128,896]{1,0:T(8,128)(2,1)S(1)}, u32[]{:S(2)}, u32[]{:S(2)}) collective-permute-start(bf16[128,896]{1,0:T(8,128)(2,1)S(1)} %get-tuple-element.55), channel_id=1, source_target_pairs={{0,24},{4,28},{8,16},{12,20},{16,8},{20,12},{24,0},{28,4},{1,25},{... | collective-permute-start | bytes 688136 | tf_op jit(solution)/shard_map/ppermute | solution.py:23
  36.7 0.6 collective-permute-start.14
  37.8 1.1 %shard_map.63.own_ref = f32[128,896]{1,0:T(8,128)S(1)} custom-call(f32[128,768]{1,0:T(8,128)S(1)} %shard_map.61.refs_10_.refs_0_, f32[128,128]{1,0:T(8,128)S(1)} %get-tuple-element.52.refs_1_, f32[128,640]{1,0:T(8,128)S(1)} %get-tuple-element.49.refs_4_.refs_2_, bf16[128,640]{1,0:T(8,128)(2,1)} %collective-permute-done.11.refs_3_, ...), custom_call_target="tpu_custom_call" | custom-call | flops 1200000000 | bytes 1048576 | tf_op jit(solution)/shard_map/pallas_call | solution.py:309
  38.9 5.4 %collective-permute-done.14.refs_1_ = bf16[128,256]{1,0:T(8,128)(2,1)S(1)} collective-permute-done((bf16[128,256]{1,0:T(8,128)(2,1)S(1)}, bf16[128,256]{1,0:T(8,128)(2,1)S(1)}, u32[]{:S(2)}, u32[]{:S(2)}) %collective-permute-start.14) | collective-permute-done | bytes 65568 | tf_op jit(solution)/shard_map/ppermute | solution.py:23
  44.3 0.6 shard_map.64
  44.9 3.7 %collective-permute-start.16 = (bf16[32,1024]{1,0:T(8,128)(2,1)S(1)}, bf16[32,1024]{1,0:T(8,128)(2,1)S(1)}, u32[]{:S(2)}, u32[]{:S(2)}) collective-permute-start(bf16[32,1024]{1,0:T(8,128)(2,1)S(1)} %get-tuple-element.58), channel_id=1, source_target_pairs={{0,3},{1,2},{2,1},{3,0},{4,7},{5,6},{6,5},{7,4},{8,11},{9,10},{10,... | collective-permute-start | bytes 196616 | tf_op jit(solution)/shard_map/ppermute | solution.py:23
  48.6 0.8 %collective-permute-start.18 = (bf16[32,1024]{1,0:T(8,128)(2,1)S(1)}, bf16[32,1024]{1,0:T(8,128)(2,1)S(1)}, u32[]{:S(2)}, u32[]{:S(2)}) collective-permute-start(bf16[32,1024]{1,0:T(8,128)(2,1)S(1)} %get-tuple-element.60), channel_id=1, source_target_pairs={{0,2},{1,3},{2,0},{3,1},{4,6},{5,7},{6,4},{7,5},{8,10},{9,11},{10,... | collective-permute-start | bytes 196616 | tf_op jit(solution)/shard_map/ppermute | solution.py:23
  49.4 2.2 %collective-permute-done.16.refs_0_ = bf16[32,1024]{1,0:T(8,128)(2,1)S(1)} collective-permute-done((bf16[32,1024]{1,0:T(8,128)(2,1)S(1)}, bf16[32,1024]{1,0:T(8,128)(2,1)S(1)}, u32[]{:S(2)}, u32[]{:S(2)}) %collective-permute-start.16) | collective-permute-done | bytes 65568 | tf_op jit(solution)/shard_map/ppermute | solution.py:23
  51.6 1.9 %collective-permute-done.17.refs_1_ = bf16[32,1024]{1,0:T(8,128)(2,1)S(1)} collective-permute-done((bf16[32,1024]{1,0:T(8,128)(2,1)S(1)}, bf16[32,1024]{1,0:T(8,128)(2,1)S(1)}, u32[]{:S(2)}, u32[]{:S(2)}) %collective-permute-start.17) | collective-permute-done | bytes 65568 | tf_op jit(solution)/shard_map/ppermute | solution.py:23
  53.4 0.9 %collective-permute-done.18.refs_2_ = bf16[32,1024]{1,0:T(8,128)(2,1)S(1)} collective-permute-done((bf16[32,1024]{1,0:T(8,128)(2,1)S(1)}, bf16[32,1024]{1,0:T(8,128)(2,1)S(1)}, u32[]{:S(2)}, u32[]{:S(2)}) %collective-permute-start.18) | collective-permute-done | bytes 65568 | tf_op jit(solution)/shard_map/ppermute | solution.py:23
  54.3 0.8 %shard_map.65 = (f32[3,32,128]{2,1,0:T(8,128)S(1)}, bf16[3,3,32,128]{3,2,1,0:T(8,128)(2,1)S(1)}, bf16[4,3,32,128]{3,2,1,0:T(8,128)(2,1)S(1)}) custom-call(s32[24]{0:T(128)S(1)} %add_maximum_fusion.refs_2_.block_ref, bf16[32,1024]{1,0:T(8,128)(2,1)S(1)} %collective-permute-done.16.refs_0_, bf16[32,1024]{1,0:T(8,128)(2,1)S(1)} %collective-permute-done.17.refs_1_, ...), custom_call_target="tpu_custom_call" | custom-call | tf_op jit(solution)/shard_map/pallas_call | solution.py:376
  55.2 1.3 %collective-permute-done.19 = bf16[4,3,32,128]{3,2,1,0:T(8,128)(2,1)S(1)} collective-permute-done((bf16[4,3,32,128]{3,2,1,0:T(8,128)(2,1)S(1)}, bf16[4,3,32,128]{3,2,1,0:T(8,128)(2,1)S(1)}, u32[]{:S(2)}, u32[]{:S(2)}) %collective-permute-start.19) | collective-permute-done | bytes 98336 | tf_op jit(solution)/shard_map/ppermute | solution.py:23
  56.5 2.5 %collective-permute-start.22 = (bf16[2,3,32,128]{3,2,1,0:T(8,128)(2,1)S(1)}, bf16[2,3,32,128]{3,2,1,0:T(8,128)(2,1)S(1)}, u32[]{:S(2)}, u32[]{:S(2)}) collective-permute-start(bf16[2,3,32,128]{3,2,1,0:T(8,128)(2,1)S(1)} %get-tuple-element.67), channel_id=1, source_target_pairs={{0,24},{4,28},{8,16},{12,20},{16,8},{20,12},{24,0},{28,4},{1,25},{... | collective-permute-start | bytes 147464 | tf_op jit(solution)/shard_map/ppermute | solution.py:23
  58.9 0.6 collective-permute-start.20
  60.0 1.7 %collective-permute-done.22.refs_2_ = bf16[2,3,32,128]{3,2,1,0:T(8,128)(2,1)S(1)} collective-permute-done((bf16[2,3,32,128]{3,2,1,0:T(8,128)(2,1)S(1)}, bf16[2,3,32,128]{3,2,1,0:T(8,128)(2,1)S(1)}, u32[]{:S(2)}, u32[]{:S(2)}) %collective-permute-start.22) | collective-permute-done | bytes 49184 | tf_op jit(solution)/shard_map/ppermute | solution.py:23
  61.8 1.3 %collective-permute-done.20.refs_0_ = bf16[2,3,32,128]{3,2,1,0:T(8,128)(2,1)S(1)} collective-permute-done((bf16[2,3,32,128]{3,2,1,0:T(8,128)(2,1)S(1)}, bf16[2,3,32,128]{3,2,1,0:T(8,128)(2,1)S(1)}, u32[]{:S(2)}, u32[]{:S(2)}) %collective-permute-start.20) | collective-permute-done | bytes 49184 | tf_op jit(solution)/shard_map/ppermute | solution.py:23
  63.0 0.6 collective-permute-done.21.refs_1_
  63.6 0.8 %shard_map.66 = f32[8,3,32,128]{3,2,1,0:T(8,128)} custom-call(s32[1]{0:T(128)} %bitcast.mine_ref, f32[3,32,128]{2,1,0:T(8,128)S(1)} %get-tuple-element.62.home_ref, bf16[3,32,128]{2,1,0:T(8,128)(2,1)S(1)} %slice_bitcast_fusion.1.beside_ref, bf16[2,3,32,128]{3,2,1,0:T(8,128)(2,1)S(1)} %collective-permute-done.20.refs_0_, ...), custom_call_target="tpu_custom_call" | custom-call | tf_op jit(solution)/shard_map/pallas_call | solution.py:400
  (48 shorter events, 6.6 us)
Async XLA Ops:
  2.9 15.3 %collective-permute-start.3 = (bf16[128,2048]{1,0:T(8,128)(2,1)}, bf16[128,2048]{1,0:T(8,128)(2,1)}, u32[]{:S(2)}, u32[]{:S(2)}) collective-permute-start(bf16[128,2048]{1,0:T(8,128)(2,1)} %get-tuple-element.43), channel_id=1, source_target_pairs={{0,16},{4,20},{8,24},{12,28},{16,0},{20,4},{24,8},{28,12},{1,17},{... | collective-permute-start | bytes 1572872 | tf_op jit(solution)/shard_map/ppermute | solution.py:23
  5.9 15.2 %collective-permute-start.4 = (bf16[128,2048]{1,0:T(8,128)(2,1)}, bf16[128,2048]{1,0:T(8,128)(2,1)}, u32[]{:S(2)}, u32[]{:S(2)}) collective-permute-start(bf16[128,2048]{1,0:T(8,128)(2,1)} %get-tuple-element.44), channel_id=1, source_target_pairs={{0,8},{4,12},{8,0},{12,4},{16,24},{20,28},{24,16},{28,20},{1,9},{5... | collective-permute-start | bytes 1572872 | tf_op jit(solution)/shard_map/ppermute | solution.py:23
  7.4 3.8 %copy-start.1 = (s32[14,1]{0,1:T(1,128)S(1)}, s32[14,1]{0,1:T(1,128)}, u32[]{:S(2)}) copy-start(s32[14,1]{0,1:T(1,128)} %param.8) | copy-start | bytes 172
  7.4 4.0 %copy-start.2 = (s32[14,2]{0,1:T(2,128)S(1)}, s32[14,2]{0,1:T(2,128)}, u32[]{:S(2)}) copy-start(s32[14,2]{0,1:T(2,128)} %param.7) | copy-start | bytes 340
  10.6 1.6 %collective-permute-start = (bf16[128,1024]{1,0:T(8,128)(2,1)S(1)}, bf16[128,1024]{1,0:T(8,128)(2,1)S(1)}, u32[]{:S(2)}, u32[]{:S(2)}) collective-permute-start(bf16[128,1024]{1,0:T(8,128)(2,1)S(1)} %get-tuple-element.39.refs_0_.refs_2_.refs_4_), channel_id=1, source_target_pairs={{0,4},{4,0},{8,12},{12,8},{16,20},{20,16},{24,28},{28,24},{1,5},{5... | collective-permute-start | bytes 786440 | tf_op jit(solution)/shard_map/ppermute | solution.py:23
  10.7 1.9 %collective-permute-start.1 = (bf16[128,1024]{1,0:T(8,128)(2,1)S(1)}, bf16[128,1024]{1,0:T(8,128)(2,1)S(1)}, u32[]{:S(2)}, u32[]{:S(2)}) collective-permute-start(bf16[128,1024]{1,0:T(8,128)(2,1)S(1)} %get-tuple-element.40.refs_1_.refs_3_.refs_5_), channel_id=1, source_target_pairs={{0,4},{4,0},{8,12},{12,8},{16,20},{20,16},{24,28},{28,24},{1,5},{5... | collective-permute-start | bytes 786440 | tf_op jit(solution)/shard_map/ppermute | solution.py:23
  14.1 10.5 %copy-start = (s32[14,1]{0,1:T(1,128)S(1)}, s32[14,1]{0,1:T(1,128)}, u32[]{:S(2)}) copy-start(s32[14,1]{0,1:T(1,128)} %param.9) | copy-start | bytes 172
  14.2 16.5 %collective-permute-start.2 = (bf16[128,2048]{1,0:T(8,128)(2,1)S(1)}, bf16[128,2048]{1,0:T(8,128)(2,1)S(1)}, u32[]{:S(2)}, u32[]{:S(2)}) collective-permute-start(bf16[128,2048]{1,0:T(8,128)(2,1)S(1)} %get-tuple-element.41), channel_id=1, source_target_pairs={{0,24},{4,28},{8,16},{12,20},{16,8},{20,12},{24,0},{28,4},{1,25},{... | collective-permute-start | bytes 1572872 | tf_op jit(solution)/shard_map/ppermute | solution.py:23
  23.5 1.6 %collective-permute-start.5 = (bf16[256,512]{1,0:T(8,128)(2,1)S(1)}, bf16[256,512]{1,0:T(8,128)(2,1)S(1)}, u32[]{:S(2)}, u32[]{:S(2)}) collective-permute-start(bf16[256,512]{1,0:T(8,128)(2,1)S(1)} %get-tuple-element.45.refs_4_.refs_6_), channel_id=1, source_target_pairs={{0,4},{4,0},{8,12},{12,8},{16,20},{20,16},{24,28},{28,24},{1,5},{5... | collective-permute-start | bytes 786440 | tf_op jit(solution)/shard_map/ppermute | solution.py:23
  23.6 1.9 %collective-permute-start.6 = (bf16[256,512]{1,0:T(8,128)(2,1)S(1)}, bf16[256,512]{1,0:T(8,128)(2,1)S(1)}, u32[]{:S(2)}, u32[]{:S(2)}) collective-permute-start(bf16[256,512]{1,0:T(8,128)(2,1)S(1)} %get-tuple-element.46.refs_5_.refs_7_), channel_id=1, source_target_pairs={{0,4},{4,0},{8,12},{12,8},{16,20},{20,16},{24,28},{28,24},{1,5},{5... | collective-permute-start | bytes 786440 | tf_op jit(solution)/shard_map/ppermute | solution.py:23
  24.1 1.8 %collective-permute-start.7 = (bf16[256,512]{1,0:T(8,128)(2,1)S(1)}, bf16[256,512]{1,0:T(8,128)(2,1)S(1)}, u32[]{:S(2)}, u32[]{:S(2)}) collective-permute-start(bf16[256,512]{1,0:T(8,128)(2,1)S(1)} %get-tuple-element.47.refs_6_.refs_8_), channel_id=1, source_target_pairs={{0,4},{4,0},{8,12},{12,8},{16,20},{20,16},{24,28},{28,24},{1,5},{5... | collective-permute-start | bytes 786440 | tf_op jit(solution)/shard_map/ppermute | solution.py:23
  24.2 2.1 %collective-permute-start.8 = (bf16[256,512]{1,0:T(8,128)(2,1)S(1)}, bf16[256,512]{1,0:T(8,128)(2,1)S(1)}, u32[]{:S(2)}, u32[]{:S(2)}) collective-permute-start(bf16[256,512]{1,0:T(8,128)(2,1)S(1)} %get-tuple-element.48.refs_7_.refs_9_), channel_id=1, source_target_pairs={{0,4},{4,0},{8,12},{12,8},{16,20},{20,16},{24,28},{28,24},{1,5},{5... | collective-permute-start | bytes 786440 | tf_op jit(solution)/shard_map/ppermute | solution.py:23
  28.7 9.1 %collective-permute-start.11 = (bf16[128,640]{1,0:T(8,128)(2,1)}, bf16[128,640]{1,0:T(8,128)(2,1)}, u32[]{:S(2)}, u32[]{:S(2)}) collective-permute-start(bf16[128,640]{1,0:T(8,128)(2,1)} %get-tuple-element.53), channel_id=1, source_target_pairs={{0,8},{4,12},{8,0},{12,4},{16,24},{20,28},{24,16},{28,20},{1,9},{5... | collective-permute-start | bytes 491528 | tf_op jit(solution)/shard_map/ppermute | solution.py:23
  30.2 7.6 %collective-permute-start.12 = (bf16[128,640]{1,0:T(8,128)(2,1)}, bf16[128,640]{1,0:T(8,128)(2,1)}, u32[]{:S(2)}, u32[]{:S(2)}) collective-permute-start(bf16[128,640]{1,0:T(8,128)(2,1)} %get-tuple-element.54), channel_id=1, source_target_pairs={{0,16},{4,20},{8,24},{12,28},{16,0},{20,4},{24,8},{28,12},{1,17},{... | collective-permute-start | bytes 491528 | tf_op jit(solution)/shard_map/ppermute | solution.py:23
  31.5 1.7 %collective-permute-start.9 = (bf16[128,1024]{1,0:T(8,128)(2,1)S(1)}, bf16[128,1024]{1,0:T(8,128)(2,1)S(1)}, u32[]{:S(2)}, u32[]{:S(2)}) collective-permute-start(bf16[128,1024]{1,0:T(8,128)(2,1)S(1)} %get-tuple-element.50.refs_0_), channel_id=1, source_target_pairs={{0,4},{4,0},{8,12},{12,8},{16,20},{20,16},{24,28},{28,24},{1,5},{5... | collective-permute-start | bytes 786440 | tf_op jit(solution)/shard_map/ppermute | solution.py:23
  31.6 1.9 %collective-permute-start.10 = (bf16[128,1024]{1,0:T(8,128)(2,1)S(1)}, bf16[128,1024]{1,0:T(8,128)(2,1)S(1)}, u32[]{:S(2)}, u32[]{:S(2)}) collective-permute-start(bf16[128,1024]{1,0:T(8,128)(2,1)S(1)} %get-tuple-element.51.refs_1_), channel_id=1, source_target_pairs={{0,4},{4,0},{8,12},{12,8},{16,20},{20,16},{24,28},{28,24},{1,5},{5... | collective-permute-start | bytes 786440 | tf_op jit(solution)/shard_map/ppermute | solution.py:23
  34.2 10.1 %collective-permute-start.13 = (bf16[128,896]{1,0:T(8,128)(2,1)S(1)}, bf16[128,896]{1,0:T(8,128)(2,1)S(1)}, u32[]{:S(2)}, u32[]{:S(2)}) collective-permute-start(bf16[128,896]{1,0:T(8,128)(2,1)S(1)} %get-tuple-element.55), channel_id=1, source_target_pairs={{0,24},{4,28},{8,16},{12,20},{16,8},{20,12},{24,0},{28,4},{1,25},{... | collective-permute-start | bytes 688136 | tf_op jit(solution)/shard_map/ppermute | solution.py:23
  36.7 7.6 %collective-permute-start.14 = (bf16[128,256]{1,0:T(8,128)(2,1)S(1)}, bf16[128,256]{1,0:T(8,128)(2,1)S(1)}, u32[]{:S(2)}, u32[]{:S(2)}) collective-permute-start(bf16[128,256]{1,0:T(8,128)(2,1)S(1)} %get-tuple-element.56), channel_id=1, source_target_pairs={{0,8},{4,12},{8,0},{12,4},{16,24},{20,28},{24,16},{28,20},{1,9},{5... | collective-permute-start | bytes 196616 | tf_op jit(solution)/shard_map/ppermute | solution.py:23
  37.2 7.1 %collective-permute-start.15 = (bf16[128,256]{1,0:T(8,128)(2,1)S(1)}, bf16[128,256]{1,0:T(8,128)(2,1)S(1)}, u32[]{:S(2)}, u32[]{:S(2)}) collective-permute-start(bf16[128,256]{1,0:T(8,128)(2,1)S(1)} %get-tuple-element.57), channel_id=1, source_target_pairs={{0,16},{4,20},{8,24},{12,28},{16,0},{20,4},{24,8},{28,12},{1,17},{... | collective-permute-start | bytes 196616 | tf_op jit(solution)/shard_map/ppermute | solution.py:23
  44.9 6.6 %collective-permute-start.16 = (bf16[32,1024]{1,0:T(8,128)(2,1)S(1)}, bf16[32,1024]{1,0:T(8,128)(2,1)S(1)}, u32[]{:S(2)}, u32[]{:S(2)}) collective-permute-start(bf16[32,1024]{1,0:T(8,128)(2,1)S(1)} %get-tuple-element.58), channel_id=1, source_target_pairs={{0,3},{1,2},{2,1},{3,0},{4,7},{5,6},{6,5},{7,4},{8,11},{9,10},{10,... | collective-permute-start | bytes 196616 | tf_op jit(solution)/shard_map/ppermute | solution.py:23
  48.6 4.8 %collective-permute-start.17 = (bf16[32,1024]{1,0:T(8,128)(2,1)S(1)}, bf16[32,1024]{1,0:T(8,128)(2,1)S(1)}, u32[]{:S(2)}, u32[]{:S(2)}) collective-permute-start(bf16[32,1024]{1,0:T(8,128)(2,1)S(1)} %get-tuple-element.59), channel_id=1, source_target_pairs={{0,1},{1,0},{2,3},{3,2},{4,5},{5,4},{6,7},{7,6},{8,9},{9,8},{10,11... | collective-permute-start | bytes 196616 | tf_op jit(solution)/shard_map/ppermute | solution.py:23
  48.6 5.7 %collective-permute-start.18 = (bf16[32,1024]{1,0:T(8,128)(2,1)S(1)}, bf16[32,1024]{1,0:T(8,128)(2,1)S(1)}, u32[]{:S(2)}, u32[]{:S(2)}) collective-permute-start(bf16[32,1024]{1,0:T(8,128)(2,1)S(1)} %get-tuple-element.60), channel_id=1, source_target_pairs={{0,2},{1,3},{2,0},{3,1},{4,6},{5,7},{6,4},{7,5},{8,10},{9,11},{10,... | collective-permute-start | bytes 196616 | tf_op jit(solution)/shard_map/ppermute | solution.py:23
  55.1 1.4 %collective-permute-start.19 = (bf16[4,3,32,128]{3,2,1,0:T(8,128)(2,1)S(1)}, bf16[4,3,32,128]{3,2,1,0:T(8,128)(2,1)S(1)}, u32[]{:S(2)}, u32[]{:S(2)}) collective-permute-start(bf16[4,3,32,128]{3,2,1,0:T(8,128)(2,1)S(1)} %get-tuple-element.63), channel_id=1, source_target_pairs={{0,4},{4,0},{8,12},{12,8},{16,20},{20,16},{24,28},{28,24},{1,5},{5... | collective-permute-start | bytes 294920 | tf_op jit(solution)/shard_map/ppermute | solution.py:23
  56.5 5.3 %collective-permute-start.22 = (bf16[2,3,32,128]{3,2,1,0:T(8,128)(2,1)S(1)}, bf16[2,3,32,128]{3,2,1,0:T(8,128)(2,1)S(1)}, u32[]{:S(2)}, u32[]{:S(2)}) collective-permute-start(bf16[2,3,32,128]{3,2,1,0:T(8,128)(2,1)S(1)} %get-tuple-element.67), channel_id=1, source_target_pairs={{0,24},{4,28},{8,16},{12,20},{16,8},{20,12},{24,0},{28,4},{1,25},{... | collective-permute-start | bytes 147464 | tf_op jit(solution)/shard_map/ppermute | solution.py:23
  58.9 4.1 %collective-permute-start.20 = (bf16[2,3,32,128]{3,2,1,0:T(8,128)(2,1)S(1)}, bf16[2,3,32,128]{3,2,1,0:T(8,128)(2,1)S(1)}, u32[]{:S(2)}, u32[]{:S(2)}) collective-permute-start(bf16[2,3,32,128]{3,2,1,0:T(8,128)(2,1)S(1)} %get-tuple-element.68), channel_id=1, source_target_pairs={{0,8},{4,12},{8,0},{12,4},{16,24},{20,28},{24,16},{28,20},{1,9},{5... | collective-permute-start | bytes 147464 | tf_op jit(solution)/shard_map/ppermute | solution.py:23
  59.5 4.1 %collective-permute-start.21 = (bf16[2,3,32,128]{3,2,1,0:T(8,128)(2,1)S(1)}, bf16[2,3,32,128]{3,2,1,0:T(8,128)(2,1)S(1)}, u32[]{:S(2)}, u32[]{:S(2)}) collective-permute-start(bf16[2,3,32,128]{3,2,1,0:T(8,128)(2,1)S(1)} %get-tuple-element.69), channel_id=1, source_target_pairs={{0,16},{4,20},{8,24},{12,28},{16,0},{20,4},{24,8},{28,12},{1,17},{... | collective-permute-start | bytes 147464 | tf_op jit(solution)/shard_map/ppermute | solution.py:23

commit v5 on v4

--- a/solution.py
+++ b/solution.py
@@ -11,6 +11,7 @@
 CORES = 2
 MIB = 1024 * 1024
 MIDDLE_WEIGHT = 60 * 10**8
+LATE_WEIGHT = 5 * 10**9
 HOME_WEIGHT = 12 * 10**8
 SMEM = pl.BlockSpec(memory_space=pltpu.SMEM)
 VMEM = pl.BlockSpec(memory_space=pltpu.VMEM)
@@ -91,7 +92,7 @@
 
 def fit_kernel(count, pieces, *refs):
     outs = refs[-pieces:]
-    write_fitted(refs[:count][::-1], refs[count][...], outs)
+    write_fitted(refs[:count], refs[count][...], outs)
     below = outs[0].shape[0] - count * refs[0].shape[0]
     if below:
         for ref, out_ref in zip(refs[count + 1 : count + 1 + pieces], outs, strict=True):
@@ -107,7 +108,7 @@
         [kept((rows_out, width // pieces), jnp.bfloat16)] * pieces,
         [VMEM] * pieces,
         8,
-    )(*panels[::-1], metric, *below, *before)
+    )(*panels, metric, *below, *before)
 
 
 def copy_all(pairs, arrived):
@@ -149,7 +150,7 @@
     return pieces, token
 
 
-def first_fit_kernel(token_ref, starts_ref, raw_ref, metric_ref, *refs):
+def first_fit_kernel(starts_ref, raw_ref, metric_ref, *refs):
     held_ref, outs, (own_ref, arrived) = refs[0], refs[1:-2], refs[-2:]
     width = own_ref.shape[1]
     copy_all(
@@ -158,17 +159,17 @@
     write_fitted([own_ref], held_ref[...], outs)
 
 
-def first_fit(token, raw, metric, start, width, pieces):
+def first_fit(raw, metric, start, width, pieces):
     rows = raw.shape[0]
     held, *fitted = kernel_call(
         first_fit_kernel,
-        [SMEM, SMEM, HBM, HBM],
+        [SMEM, HBM, HBM],
         [kept(metric.shape, metric.dtype)]
         + [kept((rows, width // pieces), jnp.bfloat16)] * pieces,
         [VMEM] * (pieces + 1),
         8,
         [pltpu.VMEM((rows, width), raw.dtype), pltpu.SemaphoreType.DMA((2,))],
-    )(token, start[None], raw, pltpu.with_memory_space_constraint(metric, pltpu.HBM))
+    )(start[None], raw, pltpu.with_memory_space_constraint(metric, pltpu.HBM))
     return held, fitted
 
 
@@ -251,36 +252,50 @@
     )(*[piece for pieces in given for piece in pieces])
 
 
-def late_kernel(counts, *refs):
-    last, last_beside, own, others, (middle_ref,), slabs, (side_ref,) = unpack(refs, counts)
-    final = len(slabs)
-    last_slab = slabs[-1]
-    tall = gram(others, last_beside)
-    side_ref[...] = gram(own, last_beside)
+def last_slab_kernel(counts, *refs):
+    last, last_beside, (middle_ref,), (slab,) = unpack(refs, counts)
+    final = middle_ref.shape[1] // (CORES * TILE)
     tile = gram(last, last_beside)
-    last_slab[:, spot(place(CORES * final + 1, final))] = tile.astype(jnp.bfloat16)
+    slab[:, spot(place(CORES * final + 1, final))] = tile.astype(jnp.bfloat16)
     for chip in range(final):
         straight = middle_ref[:, spot(chip + 1 if chip else 0)]
         sideways = middle_ref[:, spot(chip + final if chip else 1)]
-        last_slab[:, spot(place(CORES * chip, final))] = straight.astype(jnp.bfloat16)
-        last_slab[:, spot(place(CORES * chip + 1, final))] = sideways.astype(jnp.bfloat16)
-        if chip:
-            slabs[chip - 1][:, spot(0)] = straight.T.astype(jnp.bfloat16)
-            slabs[chip - 1][:, spot(1)] = part(tall, chip - 1, 0).astype(jnp.bfloat16)
-
-
-def late(last, last_beside, own, others, across):
-    final = others[0].shape[0] // TILE + 1
-    span = (CORES * final + 1) * TILE
-    given = [last, last_beside, own, others, [across]]
-    counts = [len(pieces) for pieces in given] + [final, 1]
+        slab[:, spot(place(CORES * chip, final))] = straight.astype(jnp.bfloat16)
+        slab[:, spot(place(CORES * chip + 1, final))] = sideways.astype(jnp.bfloat16)
+
+
+def last_chip_slab(last, last_beside, across):
+    given = [last, last_beside, [across]]
+    counts = [len(pieces) for pieces in given] + [1]
+    return kernel_call(
+        functools.partial(last_slab_kernel, counts),
+        [VMEM] * sum(counts[:-1]),
+        kept((TILE, across.shape[1] + TILE), jnp.bfloat16),
+        VMEM,
+        8,
+    )(*[piece for pieces in given for piece in pieces])
+
+
+def late_kernel(counts, *refs):
+    last_beside, own, others, (middle_ref,), slabs, (side_ref,) = unpack(refs, counts)
+    tall = gram(others, last_beside)
+    side_ref[...] = gram(own, last_beside)
+    for at, slab in enumerate(slabs):
+        slab[:, spot(0)] = middle_ref[:, spot(at + 2)].T.astype(jnp.bfloat16)
+        slab[:, spot(1)] = part(tall, at, 0).astype(jnp.bfloat16)
+
+
+def late(last_beside, own, others, across):
+    chips = others[0].shape[0] // TILE
+    given = [last_beside, own, others, [across]]
+    counts = [len(pieces) for pieces in given] + [chips, 1]
     return kernel_call(
         functools.partial(late_kernel, counts),
         [VMEM] * sum(counts[:-2]),
-        [kept((TILE, CORES * TILE), jnp.bfloat16)] * (final - 1)
-        + [kept((TILE, span), jnp.bfloat16), kept((TILE, TILE), jnp.float32)],
-        [VMEM] * (final + 1),
-        12,
+        [kept((TILE, CORES * TILE), jnp.bfloat16)] * chips + [kept((TILE, TILE), jnp.float32)],
+        [VMEM] * (chips + 1),
+        8,
+        weight=LATE_WEIGHT,
     )(*[piece for pieces in given for piece in pieces])
 
 
@@ -316,14 +331,14 @@
     )(*[piece for pieces in given for piece in pieces])
 
 
-def strips_kernel(starts_ref, weights_ref, own_ref, *refs):
-    groups = starts_ref.shape[0]
+def strips_kernel(groups, weights_ref, own_ref, *refs):
+    my_group = lax.axis_index("grp")
     (last_came, *came), strips = refs[:-groups], refs[-groups:]
     final = len(came) + 1
     share = strips[0].shape[0]
     span = own_ref.shape[1]
     for distance, strip in enumerate(strips):
-        rows = pl.ds(pl.multiple_of(starts_ref[distance], share), share)
+        rows = pl.ds(pl.multiple_of((my_group ^ distance) * share, share), share)
         strip[:, span:] = weights_ref[...].astype(strip.dtype)
         for number in range(span // TILE):
             total = own_ref[rows, spot(number)]
@@ -335,75 +350,79 @@
             strip[:, spot(number)] = total.astype(strip.dtype)
 
 
-def strips(own, came, starts, weights):
-    groups = starts.shape[0]
+def strips(own, came, groups, weights):
     rows, span = own.shape
     share = rows // groups
     whole = span + weights.shape[1]
     return kernel_call(
-        strips_kernel,
-        [SMEM] + [VMEM] * (2 + len(came)),
+        functools.partial(strips_kernel, groups),
+        [VMEM] * (2 + len(came)),
         [shaped((share, whole), jnp.bfloat16 if at else jnp.float32) for at in range(groups)],
         [VMEM] * groups,
         8,
-    )(starts, weights, own, *came)
-
-
-def combine_kernel(span, block_ref, *refs):
-    chunks, (home_ref, straight_ref, crossing_ref) = refs[:-3], refs[-3:]
-    slots, share = home_ref.shape[:2]
+    )(weights, own, *came)
+
+
+def combine_kernel(owners, span, block_ref, *refs):
+    chunks, outs = refs[: -len(owners)], refs[-len(owners) :]
+    slots, share = outs[0].shape[1:3]
     weights = [chunk[:, span:].astype(jnp.float32) for chunk in chunks]
-    for owner in range(crossing_ref.shape[0] * CORES):
-        chip, core = owner // CORES, owner % CORES
-        for slot in range(slots):
-            at = owner * slots + slot
-            start = pl.multiple_of(block_ref[at] * TILE, TILE)
-            row, lanes = at % share, at // share * TILE
-            total = jnp.zeros((share, TILE), jnp.float32)
-            for chunk, weight in zip(chunks, weights, strict=True):
-                scale = weight[row : row + 1, lanes : lanes + TILE]
-                total = total + scale * chunk[:, pl.ds(start, TILE)].astype(jnp.float32)
-            if owner == 0:
-                home_ref[slot] = total
-            elif core == 0:
-                straight_ref[chip - 1, slot] = total.astype(jnp.bfloat16)
-            else:
-                crossing_ref[chip, slot] = total.astype(jnp.bfloat16)
-
-
-def combine(blocks, chunks, span, chips, slots):
+    for out_ref, held in zip(outs, owners, strict=True):
+        for number, owner in enumerate(held):
+            for slot in range(slots):
+                at = owner * slots + slot
+                start = pl.multiple_of(block_ref[at] * TILE, TILE)
+                row, lanes = at % share, at // share * TILE
+                total = jnp.zeros((share, TILE), jnp.float32)
+                for chunk, weight in zip(chunks, weights, strict=True):
+                    scale = weight[row : row + 1, lanes : lanes + TILE]
+                    total = total + scale * chunk[:, pl.ds(start, TILE)].astype(jnp.float32)
+                out_ref[number, slot] = total.astype(out_ref.dtype)
+
+
+def combine(owners, blocks, chunks, span, slots):
     share = chunks[0].shape[0]
     return kernel_call(
-        functools.partial(combine_kernel, span),
+        functools.partial(combine_kernel, owners, span),
         [SMEM] + [VMEM] * len(chunks),
         [
-            shaped((slots, share, TILE), jnp.float32),
-            shaped((chips - 1, slots, share, TILE), jnp.bfloat16),
-            shaped((chips, slots, share, TILE), jnp.bfloat16),
+            shaped((len(held), slots, share, TILE), jnp.bfloat16 if any(held) else jnp.float32)
+            for held in owners
         ],
-        [VMEM] * 3,
+        [VMEM] * len(owners),
         8,
     )(blocks, *chunks)
 
 
-def settle_kernel(mine_ref, home_ref, beside_ref, *refs):
+def scalars_kernel(values_ref, out_ref):
+    for at in range(values_ref.shape[0]):
+        out_ref[at] = values_ref[at]
+
+
+def scalars(values):
+    return kernel_call(
+        scalars_kernel, [SMEM], pltpu.SMEM(values.shape, values.dtype), SMEM, 1
+    )(values)
+
+
+def settle_kernel(order, home_ref, beside_ref, *refs):
     came, out_ref = refs[:-1], refs[-1]
-    mine = mine_ref[0]
+    mine = lax.axis_index("blk")
     out_ref[mine] = home_ref[...]
     out_ref[mine ^ 1] = beside_ref[...].astype(jnp.float32)
-    for at, piece in enumerate(came):
+    for chip, piece in zip(order, came, strict=True):
         for core in range(CORES):
-            out_ref[mine ^ ((at + 1) * CORES + core)] = piece[core].astype(jnp.float32)
-
-
-def settle(mine, home, from_beside, came):
-    return kernel_call(
-        settle_kernel,
-        [SMEM] + [VMEM] * (2 + len(came)),
+            out_ref[mine ^ (chip * CORES + core)] = piece[core].astype(jnp.float32)
+
+
+def settle(home, from_beside, came, order):
+    return kernel_call(
+        functools.partial(settle_kernel, order),
+        [VMEM] * (2 + len(came)),
         shaped((CORES * (len(came) + 1), *home.shape), jnp.float32),
         VMEM,
         8,
-    )(mine, home, from_beside, *came)
+    )(home, from_beside, *came)
 
 
 def per_device(raw_panels, metric, tile_pairs, owners, group_mask):
@@ -414,7 +433,6 @@
     chips = cycle // CORES
     width = columns // chips
     mine = lax.axis_index("blk")
-    my_group = lax.axis_index("grp")
     tile_count = tile_pairs.shape[0]
     capacity = max(2, 2 * tile_count // cycle)
     final = chips - 1
@@ -424,9 +442,12 @@
         return [swapped(piece, "blk", 1) for piece in pieces]
 
     starts = [((mine // CORES) ^ chip) * width for chip in range(chips)]
-    pieces, token = cut(raw, starts[1:final], width)
+    pieces = [
+        lax.dynamic_slice(raw_panels[0], (jnp.int32(0), starts[chip]), (rows, width))
+        for chip in range(1, final)
+    ]
     arrived = [swapped(piece, "blk", CORES * (at + 1)) for at, piece in enumerate(pieces)]
-    metric, own = first_fit(token, raw, metric, starts[0], width, 2)
+    metric, own = first_fit(raw, metric, starts[0], width, 1)
     own_beside = beside(own)
     (last_piece,), token = cut(raw, starts[final:], width, *own_beside)
     last = swapped(last_piece, "blk", CORES * final)
@@ -440,7 +461,7 @@
     slots = jnp.sum(before * hits, axis=1)
     places = owner_ids * capacity + slots
     taken = (places[None, :] == jnp.arange(cycle * capacity)[:, None]).astype(jnp.int32)
-    blocks = jnp.maximum(jnp.sum(taken * (pairs[:, 1] ^ mine)[None, :], axis=1) - 1, 0)
+    blocks = scalars(jnp.maximum(jnp.sum(taken * (pairs[:, 1] ^ mine)[None, :], axis=1) - 1, 0))
     weights = jnp.sum(taken * own_mask[None, :], axis=1).astype(jnp.float32)
     tall = -(-weights.shape[0] // share) * share
     weights = jnp.pad(weights, (0, tall - weights.shape[0])).reshape(-1, share).T
@@ -454,22 +475,25 @@
     last_fitted = fit([last], metric, 2, (), (blocks, weights, begun[0]))
     last_beside = beside(last_fitted)
     across = middle(last_fitted, own, own_beside, others, others_beside)
-    *slabs, side = late(last_fitted, last_beside, own, others, across)
-    came = [
-        swapped(slabs[chip - 1], "blk", CORES * chip) for chip in (final, *range(1, final))
+    last_slab = last_chip_slab(last_fitted, last_beside, across)
+    *slabs, side = late(last_beside, own, others, across)
+    came = [swapped(last_slab, "blk", CORES * final)] + [
+        swapped(slabs[chip - 1], "blk", CORES * chip) for chip in range(1, final)
     ]
     own_slab = home_slab(across, side, begun[0], came_early)
-    strip_starts = (my_group ^ jnp.arange(groups, dtype=jnp.int32)) * share
-    own_strips = strips(own_slab, came, strip_starts, weights)
+    own_strips = strips(own_slab, came, groups, weights)
     chunks = [own_strips[0]] + [swapped(own_strips[d], "grp", d) for d in range(1, groups)]
 
-    home, straight, crossing = combine(blocks, [chunks[-1], *chunks[1:-1], chunks[0]], own_slab.shape[1], chips, capacity)
+    chunks = [*chunks[2:], chunks[1], chunks[0]]
+    span = own_slab.shape[1]
+    (crossing,) = combine([range(1, cycle, CORES)], blocks, chunks, span, capacity)
     crossed = swapped(crossing, "blk", 1)
+    own_owners = [range(1), range(CORES, cycle, CORES)]
+    home, straight = combine(own_owners, blocks, chunks, span, capacity)
     paired = jnp.stack([straight, crossed[1:]], axis=1)
-    received = [
-        swapped(paired[chip - 1], "blk", CORES * chip) for chip in range(1, chips)
-    ]
-    return settle(mine[None], home, crossed[0], received)[None]
+    order = (final, *range(1, final))
+    received = [swapped(paired[chip - 1], "blk", CORES * chip) for chip in order]
+    return settle(home[0], crossed[0], received, order)[None]
 
 
 def solution(mesh):

time: 64.6 us -> 62 us (0.960)
  Pallas kernels: 18.2 us -> 12.8 us
  local copies, waits for them, and re-layouts: 0.1 us -> 2.4 us
  waiting for transfers between devices: 25 us -> 26.3 us
  starting transfers between devices: 20.5 us -> 19.8 us
    pallas_call x2 -> x1, Pallas kernels: 4.34 us -> 1.57 us  [cut(): kernel_call(functools.partial(cut_kernel, count), [SMEM, HBM] + [ANY] * l...]
    dynamic_slice x0 -> x1, local copies, waits for them, and re-layouts: none -> 2.3 us  [per_device(): lax.dynamic_slice(raw_panels[0], (jnp.int32(0), starts[chip]), (rows, wid...]
    ppermute x23 -> x22, waiting for transfers between devices: 25 us -> 26.3 us  [swapped(): lax.ppermute(value, axis, [(source, source ^ distance) for source in rang...]
    pallas_call x1, Pallas kernels: 1.13 us -> 0.11 us  [home_slab(): kernel_call(functools.partial(home_kernel, counts), [VMEM] * sum(counts[:...]
    pallas_call x4 -> x7, Pallas kernels: 5.35 us -> 4.49 us  [the longest x1 2.55 us: first_fit(): kernel_call(first_fit_kernel, [SMEM, HBM, HBM], [kept(metric.shape, metri...]
    ppermute x23 -> x22, starting transfers between devices: 20.5 us -> 19.8 us  [swapped(): lax.ppermute(value, axis, [(source, source ^ distance) for source in rang...]
    pallas_call x1, Pallas kernels: 2.41 us -> 1.73 us  [early(): kernel_call(functools.partial(early_kernel, counts), [VMEM] * sum(counts[...]
  transfers between devices with their start and end apart: 23 -> 22, of which waited for: 17 -> 16; matrix products, arithmetic and copies ran while one was open for 1% -> 1% of each run, Pallas kernels for 21% -> 19%
where the time goes in v5:
time: 62 us; the launch traced here: 61.8 us
  waiting for transfers between devices  26.3 us (42%)
  starting transfers between devices  19.8 us (32%)
  Pallas kernels  12.8 us (21%)
  local copies, waits for them, and re-layouts  2.4 us (4%)
    ppermute x22, waiting for transfers between devices, swapped(): lax.ppermute(value, axis, [(source, source ^ distance) for source in rang...  26.3 us
    ppermute x22, starting transfers between devices, swapped(): lax.ppermute(value, axis, [(source, source ^ distance) for source in rang...  19.8 us
    pallas_call x2, Pallas kernels, fit(): kernel_call(functools.partial(fit_kernel, len(panels), pieces), [VMEM] *...  3.22 us
    pallas_call x1, Pallas kernels, first_fit(): kernel_call(first_fit_kernel, [SMEM, HBM, HBM], [kept(metric.shape, metri...  2.55 us
    dynamic_slice x1, local copies, waits for them, and re-layouts, per_device(): lax.dynamic_slice(raw_panels[0], (jnp.int32(0), starts[chip]), (rows, wid...  2.3 us
    pallas_call x1, Pallas kernels, early(): kernel_call(functools.partial(early_kernel, counts), [VMEM] * sum(counts[...  1.73 us
    pallas_call x1, Pallas kernels, cut(): kernel_call(functools.partial(cut_kernel, count), [SMEM, HBM] + [ANY] * l...  1.57 us
  transfers between devices with their start and end apart: 22, of which 16 were waited for; matrix products, arithmetic and copies ran while one was open for 1% of the time, Pallas kernels for 19%

profile of v5, /device:TPU:0, one launch (start us, length us, event | category | flops | bytes accessed | tf_op | source)
XLA Modules:
  0.0 61.8 jit_solution(8330760874195505717)
XLA Ops:
  0.0 2.3 %dynamic-slice_bitcast_fusion = (bf16[128,2048]{1,0:T(8,128)(2,1)}, bf16[128,2048]{1,0:T(8,128)(2,1)}) fusion(bf16[1,128,8192]{2,1,0:T(8,128)(2,1)} %param.5, s32[]{:T(128)S(6)} %select_n.16, s32[]{:T(128)S(6)} %select_n.15), kind=kLoop, calls=%fused_computation | loop fusion | bytes 2097160 | tf_op jit(solution)/shard_map/dynamic_slice | solution.py:446
  2.3 3.0 %collective-permute-start.3 = (bf16[128,2048]{1,0:T(8,128)(2,1)}, bf16[128,2048]{1,0:T(8,128)(2,1)}, u32[]{:S(2)}, u32[]{:S(2)}) collective-permute-start(bf16[128,2048]{1,0:T(8,128)(2,1)} %get-tuple-element.55), channel_id=1, source_target_pairs={{0,16},{4,20},{8,24},{12,28},{16,0},{20,4},{24,8},{28,12},{1,17},{... | collective-permute-start | bytes 1572872 | tf_op jit(solution)/shard_map/ppermute | solution.py:24
  5.3 1.5 %collective-permute-start.2 = (bf16[128,2048]{1,0:T(8,128)(2,1)}, bf16[128,2048]{1,0:T(8,128)(2,1)}, u32[]{:S(2)}, u32[]{:S(2)}) collective-permute-start(bf16[128,2048]{1,0:T(8,128)(2,1)} %get-tuple-element.56), channel_id=1, source_target_pairs={{0,8},{4,12},{8,0},{12,4},{16,24},{20,28},{24,16},{28,20},{1,9},{5... | collective-permute-start | bytes 1572872 | tf_op jit(solution)/shard_map/ppermute | solution.py:24
  6.8 2.5 %shard_map.56 = (bf16[1024,1024]{1,0:T(8,128)(2,1)S(1)}, bf16[128,2048]{1,0:T(8,128)(2,1)S(1)}) custom-call(s32[1]{0:T(128)} %bitcast.5.starts_ref, bf16[128,8192]{1,0:T(8,128)(2,1)} %bitcast.26, bf16[1024,1024]{1,0:T(8,128)(2,1)} %metric_ref.1), custom_call_target="tpu_custom_call" | custom-call | tf_op jit(solution)/shard_map/pallas_call | solution.py:164
  9.6 1.7 %collective-permute-done.refs_0_.refs_1_.refs_3_ = bf16[128,2048]{1,0:T(8,128)(2,1)S(1)} collective-permute-done((bf16[128,2048]{1,0:T(8,128)(2,1)S(1)}, bf16[128,2048]{1,0:T(8,128)(2,1)S(1)}, u32[]{:S(2)}, u32[]{:S(2)}) %collective-permute-start) | collective-permute-done | bytes 524320 | tf_op jit(solution)/shard_map/ppermute | solution.py:24
  11.3 1.6 %shard_map.57 = (bf16[128,2048]{1,0:T(8,128)(2,1)S(1)}, s32[1]{0:T(128)}) custom-call(s32[1]{0:T(128)} %bitcast.3.starts_ref, bf16[128,8192]{1,0:T(8,128)(2,1)} %bitcast.27, bf16[128,2048]{1,0:T(8,128)(2,1)S(1)} %collective-permute-done.refs_0_.refs_1_.refs_3_), custom_call_target="tpu_custom_call" | custom-call | tf_op jit(solution)/shard_map/pallas_call | solution.py:142
  13.0 4.5 %collective-permute-done.3.refs_1_ = bf16[128,2048]{1,0:T(8,128)(2,1)} collective-permute-done((bf16[128,2048]{1,0:T(8,128)(2,1)}, bf16[128,2048]{1,0:T(8,128)(2,1)}, u32[]{:S(2)}, u32[]{:S(2)}) %collective-permute-start.3) | collective-permute-done | bytes 524320 | tf_op jit(solution)/shard_map/ppermute | solution.py:24
  17.5 2.9 %collective-permute-done.2.refs_0_ = bf16[128,2048]{1,0:T(8,128)(2,1)} collective-permute-done((bf16[128,2048]{1,0:T(8,128)(2,1)}, bf16[128,2048]{1,0:T(8,128)(2,1)}, u32[]{:S(2)}, u32[]{:S(2)}) %collective-permute-start.2) | collective-permute-done | bytes 524320 | tf_op jit(solution)/shard_map/ppermute | solution.py:24
  20.4 2.5 %shard_map.58 = (bf16[256,512]{1,0:T(8,128)(2,1)S(1)}, bf16[256,512]{1,0:T(8,128)(2,1)S(1)}, bf16[256,512]{1,0:T(8,128)(2,1)S(1)}, bf16[256,512]{1,0:T(8,128)(2,1)S(1)}) custom-call(bf16[128,2048]{1,0:T(8,128)(2,1)} %collective-permute-done.2.refs_0_, bf16[128,2048]{1,0:T(8,128)(2,1)} %collective-permute-done.3.refs_1_, ...), custom_call_target="tpu_custom_call" | custom-call | tf_op jit(solution)/shard_map/pallas_call | solution.py:105
  23.0 0.5 collective-permute-start.5
  24.1 0.6 shard_map.55.refs_2_.block_ref
  25.6 1.7 %shard_map.59 = (f32[128,640]{1,0:T(8,128)S(1)}, bf16[128,640]{1,0:T(8,128)(2,1)S(1)}, bf16[128,640]{1,0:T(8,128)(2,1)S(1)}) custom-call(bf16[128,2048]{1,0:T(8,128)(2,1)S(1)} %get-tuple-element.32.refs_0_.refs_2_, bf16[128,2048]{1,0:T(8,128)(2,1)S(1)} %collective-permute-done.refs_0_.refs_1_.refs_3_, ...), custom_call_target="tpu_custom_call" | custom-call | tf_op jit(solution)/shard_map/pallas_call | solution.py:222
  27.4 1.6 %collective-permute-start.10 = (bf16[128,640]{1,0:T(8,128)(2,1)S(1)}, bf16[128,640]{1,0:T(8,128)(2,1)S(1)}, u32[]{:S(2)}, u32[]{:S(2)}) collective-permute-start(bf16[128,640]{1,0:T(8,128)(2,1)S(1)} %get-tuple-element.43), channel_id=1, source_target_pairs={{0,8},{4,12},{8,0},{12,4},{16,24},{20,28},{24,16},{28,20},{1,9},{5... | collective-permute-start | bytes 491528 | tf_op jit(solution)/shard_map/ppermute | solution.py:24
  28.9 0.5 collective-permute-start.11
  29.9 0.7 %shard_map.60 = (bf16[128,1024]{1,0:T(8,128)(2,1)S(1)}, bf16[128,1024]{1,0:T(8,128)(2,1)S(1)}) custom-call(bf16[128,2048]{1,0:T(8,128)(2,1)S(1)} %collective-permute-done.1.refs_0_, bf16[1024,1024]{1,0:T(8,128)(2,1)S(1)} %get-tuple-element.34.refs_2_.refs_1_, s32[24]{0:T(128)S(4)} %shard_map.55.refs_2_.block_ref, f32[32,128]{1,0:T(8,128)S(1)} %reshape.15.refs_3_.weights_ref, ...), custom_call_target="tpu_custom_call" | custom-call | tf_op jit(solution)/shard_map/pallas_call | solution.py:105
  30.7 0.5 collective-permute-start.9
  31.2 1.1 %shard_map.61.refs_7_.refs_0_.refs_4_ = f32[128,768]{1,0:T(8,128)S(1)} custom-call(bf16[128,1024]{1,0:T(8,128)(2,1)S(1)} %get-tuple-element.40.refs_0_, bf16[128,1024]{1,0:T(8,128)(2,1)S(1)} %get-tuple-element.41.refs_1_, bf16[128,2048]{1,0:T(8,128)(2,1)S(1)} %get-tuple-element.32.refs_0_.refs_2_, ...), custom_call_target="tpu_custom_call" | custom-call | flops 6000000000 | bytes 1048576 | tf_op jit(solution)/shard_map/pallas_call | solution.py:245
  32.9 2.8 %collective-permute-start.12 = (bf16[128,896]{1,0:T(8,128)(2,1)S(1)}, bf16[128,896]{1,0:T(8,128)(2,1)S(1)}, u32[]{:S(2)}, u32[]{:S(2)}) collective-permute-start(bf16[128,896]{1,0:T(8,128)(2,1)S(1)} %shard_map.64), channel_id=1, source_target_pairs={{0,24},{4,28},{8,16},{12,20},{16,8},{20,12},{24,0},{28,4},{1,25},{... | collective-permute-start | bytes 688136 | tf_op jit(solution)/shard_map/ppermute | solution.py:24
  35.7 0.6 shard_map.62
  36.3 0.5 collective-permute-start.13
  37.2 6.0 %collective-permute-done.13.refs_1_ = bf16[128,256]{1,0:T(8,128)(2,1)S(1)} collective-permute-done((bf16[128,256]{1,0:T(8,128)(2,1)S(1)}, bf16[128,256]{1,0:T(8,128)(2,1)S(1)}, u32[]{:S(2)}, u32[]{:S(2)}) %collective-permute-start.13) | collective-permute-done | bytes 65568 | tf_op jit(solution)/shard_map/ppermute | solution.py:24
  43.3 2.7 %collective-permute-start.15 = (bf16[32,1024]{1,0:T(8,128)(2,1)S(1)}, bf16[32,1024]{1,0:T(8,128)(2,1)S(1)}, u32[]{:S(2)}, u32[]{:S(2)}) collective-permute-start(bf16[32,1024]{1,0:T(8,128)(2,1)S(1)} %get-tuple-element.47), channel_id=1, source_target_pairs={{0,2},{1,3},{2,0},{3,1},{4,6},{5,7},{6,4},{7,5},{8,10},{9,11},{10,... | collective-permute-start | bytes 196616 | tf_op jit(solution)/shard_map/ppermute | solution.py:24
  46.0 1.3 %collective-permute-start.16 = (bf16[32,1024]{1,0:T(8,128)(2,1)S(1)}, bf16[32,1024]{1,0:T(8,128)(2,1)S(1)}, u32[]{:S(2)}, u32[]{:S(2)}) collective-permute-start(bf16[32,1024]{1,0:T(8,128)(2,1)S(1)} %get-tuple-element.48), channel_id=1, source_target_pairs={{0,3},{1,2},{2,1},{3,0},{4,7},{5,6},{6,5},{7,4},{8,11},{9,10},{10,... | collective-permute-start | bytes 196616 | tf_op jit(solution)/shard_map/ppermute | solution.py:24
  47.6 3.4 %collective-permute-done.15.refs_0_ = bf16[32,1024]{1,0:T(8,128)(2,1)S(1)} collective-permute-done((bf16[32,1024]{1,0:T(8,128)(2,1)S(1)}, bf16[32,1024]{1,0:T(8,128)(2,1)S(1)}, u32[]{:S(2)}, u32[]{:S(2)}) %collective-permute-start.15) | collective-permute-done | bytes 65568 | tf_op jit(solution)/shard_map/ppermute | solution.py:24
  50.9 1.4 %collective-permute-done.16.refs_1_ = bf16[32,1024]{1,0:T(8,128)(2,1)S(1)} collective-permute-done((bf16[32,1024]{1,0:T(8,128)(2,1)S(1)}, bf16[32,1024]{1,0:T(8,128)(2,1)S(1)}, u32[]{:S(2)}, u32[]{:S(2)}) %collective-permute-start.16) | collective-permute-done | bytes 65568 | tf_op jit(solution)/shard_map/ppermute | solution.py:24
  52.8 1.2 %collective-permute-done.18 = bf16[4,3,32,128]{3,2,1,0:T(8,128)(2,1)S(1)} collective-permute-done((bf16[4,3,32,128]{3,2,1,0:T(8,128)(2,1)S(1)}, bf16[4,3,32,128]{3,2,1,0:T(8,128)(2,1)S(1)}, u32[]{:S(2)}, u32[]{:S(2)}) %collective-permute-start.18) | collective-permute-done | bytes 98336 | tf_op jit(solution)/shard_map/ppermute | solution.py:24
  54.0 1.6 %collective-permute-start.21 = (bf16[2,3,32,128]{3,2,1,0:T(8,128)(2,1)S(1)}, bf16[2,3,32,128]{3,2,1,0:T(8,128)(2,1)S(1)}, u32[]{:S(2)}, u32[]{:S(2)}) collective-permute-start(bf16[2,3,32,128]{3,2,1,0:T(8,128)(2,1)S(1)} %get-tuple-element.57), channel_id=1, source_target_pairs={{0,16},{4,20},{8,24},{12,28},{16,0},{20,4},{24,8},{28,12},{1,17},{... | collective-permute-start | bytes 147464 | tf_op jit(solution)/shard_map/ppermute | solution.py:24
  55.6 1.3 %collective-permute-start.19 = (bf16[2,3,32,128]{3,2,1,0:T(8,128)(2,1)S(1)}, bf16[2,3,32,128]{3,2,1,0:T(8,128)(2,1)S(1)}, u32[]{:S(2)}, u32[]{:S(2)}) collective-permute-start(bf16[2,3,32,128]{3,2,1,0:T(8,128)(2,1)S(1)} %get-tuple-element.58), channel_id=1, source_target_pairs={{0,24},{4,28},{8,16},{12,20},{16,8},{20,12},{24,0},{28,4},{1,25},{... | collective-permute-start | bytes 147464 | tf_op jit(solution)/shard_map/ppermute | solution.py:24
  56.9 0.6 collective-permute-start.20
  57.5 0.6 collective-permute-done.21.refs_2_
  58.1 2.8 %collective-permute-done.19.refs_0_ = bf16[2,3,32,128]{3,2,1,0:T(8,128)(2,1)S(1)} collective-permute-done((bf16[2,3,32,128]{3,2,1,0:T(8,128)(2,1)S(1)}, bf16[2,3,32,128]{3,2,1,0:T(8,128)(2,1)S(1)}, u32[]{:S(2)}, u32[]{:S(2)}) %collective-permute-start.19) | collective-permute-done | bytes 49184 | tf_op jit(solution)/shard_map/ppermute | solution.py:24
  61.0 0.8 %shard_map.68 = f32[8,3,32,128]{3,2,1,0:T(8,128)} custom-call(f32[3,32,128]{2,1,0:T(8,128)S(1)} %bitcast.25, bf16[3,32,128]{2,1,0:T(8,128)(2,1)S(1)} %slice_bitcast_fusion.1.beside_ref, bf16[2,3,32,128]{3,2,1,0:T(8,128)(2,1)S(1)} %collective-permute-done.19.refs_0_, bf16[2,3,32,128]{3,2,1,0:T(8,128)(2,1)S(1)} %collective-permute-done.20.refs_1_, ...), custom_call_target="tpu_custom_call" | custom-call | tf_op jit(solution)/shard_map/pallas_call | solution.py:419
  (47 shorter events, 4.4 us)
Async XLA Ops:
  2.3 15.2 %collective-permute-start.3 = (bf16[128,2048]{1,0:T(8,128)(2,1)}, bf16[128,2048]{1,0:T(8,128)(2,1)}, u32[]{:S(2)}, u32[]{:S(2)}) collective-permute-start(bf16[128,2048]{1,0:T(8,128)(2,1)} %get-tuple-element.55), channel_id=1, source_target_pairs={{0,16},{4,20},{8,24},{12,28},{16,0},{20,4},{24,8},{28,12},{1,17},{... | collective-permute-start | bytes 1572872 | tf_op jit(solution)/shard_map/ppermute | solution.py:24
  5.3 15.2 %collective-permute-start.2 = (bf16[128,2048]{1,0:T(8,128)(2,1)}, bf16[128,2048]{1,0:T(8,128)(2,1)}, u32[]{:S(2)}, u32[]{:S(2)}) collective-permute-start(bf16[128,2048]{1,0:T(8,128)(2,1)} %get-tuple-element.56), channel_id=1, source_target_pairs={{0,8},{4,12},{8,0},{12,4},{16,24},{20,28},{24,16},{28,20},{1,9},{5... | collective-permute-start | bytes 1572872 | tf_op jit(solution)/shard_map/ppermute | solution.py:24
  6.8 2.6 %copy-start.1 = (s32[14,1]{0,1:T(1,128)S(1)}, s32[14,1]{0,1:T(1,128)}, u32[]{:S(2)}) copy-start(s32[14,1]{0,1:T(1,128)} %param.8) | copy-start | bytes 172
  6.8 2.9 %copy-start.2 = (s32[14,2]{0,1:T(2,128)S(1)}, s32[14,2]{0,1:T(2,128)}, u32[]{:S(2)}) copy-start(s32[14,2]{0,1:T(2,128)} %param.7) | copy-start | bytes 340
  9.3 2.0 %collective-permute-start = (bf16[128,2048]{1,0:T(8,128)(2,1)S(1)}, bf16[128,2048]{1,0:T(8,128)(2,1)S(1)}, u32[]{:S(2)}, u32[]{:S(2)}) collective-permute-start(bf16[128,2048]{1,0:T(8,128)(2,1)S(1)} %get-tuple-element.32.refs_0_.refs_2_), channel_id=1, source_target_pairs={{0,4},{4,0},{8,12},{12,8},{16,20},{20,16},{24,28},{28,24},{1,5},{5... | collective-permute-start | bytes 1572872 | tf_op jit(solution)/shard_map/ppermute | solution.py:24
  12.9 11.1 %copy-start = (s32[14,1]{0,1:T(1,128)S(1)}, s32[14,1]{0,1:T(1,128)}, u32[]{:S(2)}) copy-start(s32[14,1]{0,1:T(1,128)} %param.9) | copy-start | bytes 172
  12.9 16.9 %collective-permute-start.1 = (bf16[128,2048]{1,0:T(8,128)(2,1)S(1)}, bf16[128,2048]{1,0:T(8,128)(2,1)S(1)}, u32[]{:S(2)}, u32[]{:S(2)}) collective-permute-start(bf16[128,2048]{1,0:T(8,128)(2,1)S(1)} %get-tuple-element.33), channel_id=1, source_target_pairs={{0,24},{4,28},{8,16},{12,20},{16,8},{20,12},{24,0},{28,4},{1,25},{... | collective-permute-start | bytes 1572872 | tf_op jit(solution)/shard_map/ppermute | solution.py:24
  22.9 1.8 %collective-permute-start.4 = (bf16[256,512]{1,0:T(8,128)(2,1)S(1)}, bf16[256,512]{1,0:T(8,128)(2,1)S(1)}, u32[]{:S(2)}, u32[]{:S(2)}) collective-permute-start(bf16[256,512]{1,0:T(8,128)(2,1)S(1)} %get-tuple-element.35.refs_2_.refs_4_.refs_3_), channel_id=1, source_target_pairs={{0,4},{4,0},{8,12},{12,8},{16,20},{20,16},{24,28},{28,24},{1,5},{5... | collective-permute-start | bytes 786440 | tf_op jit(solution)/shard_map/ppermute | solution.py:24
  23.0 1.9 %collective-permute-start.5 = (bf16[256,512]{1,0:T(8,128)(2,1)S(1)}, bf16[256,512]{1,0:T(8,128)(2,1)S(1)}, u32[]{:S(2)}, u32[]{:S(2)}) collective-permute-start(bf16[256,512]{1,0:T(8,128)(2,1)S(1)} %get-tuple-element.36.refs_3_.refs_5_.refs_4_), channel_id=1, source_target_pairs={{0,4},{4,0},{8,12},{12,8},{16,20},{20,16},{24,28},{28,24},{1,5},{5... | collective-permute-start | bytes 786440 | tf_op jit(solution)/shard_map/ppermute | solution.py:24
  23.5 1.8 %collective-permute-start.6 = (bf16[256,512]{1,0:T(8,128)(2,1)S(1)}, bf16[256,512]{1,0:T(8,128)(2,1)S(1)}, u32[]{:S(2)}, u32[]{:S(2)}) collective-permute-start(bf16[256,512]{1,0:T(8,128)(2,1)S(1)} %get-tuple-element.37.refs_4_.refs_6_.refs_5_), channel_id=1, source_target_pairs={{0,4},{4,0},{8,12},{12,8},{16,20},{20,16},{24,28},{28,24},{1,5},{5... | collective-permute-start | bytes 786440 | tf_op jit(solution)/shard_map/ppermute | solution.py:24
  23.6 2.1 %collective-permute-start.7 = (bf16[256,512]{1,0:T(8,128)(2,1)S(1)}, bf16[256,512]{1,0:T(8,128)(2,1)S(1)}, u32[]{:S(2)}, u32[]{:S(2)}) collective-permute-start(bf16[256,512]{1,0:T(8,128)(2,1)S(1)} %get-tuple-element.38.refs_5_.refs_7_.refs_6_), channel_id=1, source_target_pairs={{0,4},{4,0},{8,12},{12,8},{16,20},{20,16},{24,28},{28,24},{1,5},{5... | collective-permute-start | bytes 786440 | tf_op jit(solution)/shard_map/ppermute | solution.py:24
  27.4 9.7 %collective-permute-start.10 = (bf16[128,640]{1,0:T(8,128)(2,1)S(1)}, bf16[128,640]{1,0:T(8,128)(2,1)S(1)}, u32[]{:S(2)}, u32[]{:S(2)}) collective-permute-start(bf16[128,640]{1,0:T(8,128)(2,1)S(1)} %get-tuple-element.43), channel_id=1, source_target_pairs={{0,8},{4,12},{8,0},{12,4},{16,24},{20,28},{24,16},{28,20},{1,9},{5... | collective-permute-start | bytes 491528 | tf_op jit(solution)/shard_map/ppermute | solution.py:24
  28.9 8.2 %collective-permute-start.11 = (bf16[128,640]{1,0:T(8,128)(2,1)S(1)}, bf16[128,640]{1,0:T(8,128)(2,1)S(1)}, u32[]{:S(2)}, u32[]{:S(2)}) collective-permute-start(bf16[128,640]{1,0:T(8,128)(2,1)S(1)} %get-tuple-element.44), channel_id=1, source_target_pairs={{0,16},{4,20},{8,24},{12,28},{16,0},{20,4},{24,8},{28,12},{1,17},{... | collective-permute-start | bytes 491528 | tf_op jit(solution)/shard_map/ppermute | solution.py:24
  30.6 1.7 %collective-permute-start.8 = (bf16[128,1024]{1,0:T(8,128)(2,1)S(1)}, bf16[128,1024]{1,0:T(8,128)(2,1)S(1)}, u32[]{:S(2)}, u32[]{:S(2)}) collective-permute-start(bf16[128,1024]{1,0:T(8,128)(2,1)S(1)} %get-tuple-element.40.refs_0_), channel_id=1, source_target_pairs={{0,4},{4,0},{8,12},{12,8},{16,20},{20,16},{24,28},{28,24},{1,5},{5... | collective-permute-start | bytes 786440 | tf_op jit(solution)/shard_map/ppermute | solution.py:24
  30.7 1.9 %collective-permute-start.9 = (bf16[128,1024]{1,0:T(8,128)(2,1)S(1)}, bf16[128,1024]{1,0:T(8,128)(2,1)S(1)}, u32[]{:S(2)}, u32[]{:S(2)}) collective-permute-start(bf16[128,1024]{1,0:T(8,128)(2,1)S(1)} %get-tuple-element.41.refs_1_), channel_id=1, source_target_pairs={{0,4},{4,0},{8,12},{12,8},{16,20},{20,16},{24,28},{28,24},{1,5},{5... | collective-permute-start | bytes 786440 | tf_op jit(solution)/shard_map/ppermute | solution.py:24
  32.9 10.3 %collective-permute-start.12 = (bf16[128,896]{1,0:T(8,128)(2,1)S(1)}, bf16[128,896]{1,0:T(8,128)(2,1)S(1)}, u32[]{:S(2)}, u32[]{:S(2)}) collective-permute-start(bf16[128,896]{1,0:T(8,128)(2,1)S(1)} %shard_map.64), channel_id=1, source_target_pairs={{0,24},{4,28},{8,16},{12,20},{16,8},{20,12},{24,0},{28,4},{1,25},{... | collective-permute-start | bytes 688136 | tf_op jit(solution)/shard_map/ppermute | solution.py:24
  36.3 6.9 %collective-permute-start.13 = (bf16[128,256]{1,0:T(8,128)(2,1)S(1)}, bf16[128,256]{1,0:T(8,128)(2,1)S(1)}, u32[]{:S(2)}, u32[]{:S(2)}) collective-permute-start(bf16[128,256]{1,0:T(8,128)(2,1)S(1)} %get-tuple-element.45), channel_id=1, source_target_pairs={{0,8},{4,12},{8,0},{12,4},{16,24},{20,28},{24,16},{28,20},{1,9},{5... | collective-permute-start | bytes 196616 | tf_op jit(solution)/shard_map/ppermute | solution.py:24
  36.8 6.4 %collective-permute-start.14 = (bf16[128,256]{1,0:T(8,128)(2,1)S(1)}, bf16[128,256]{1,0:T(8,128)(2,1)S(1)}, u32[]{:S(2)}, u32[]{:S(2)}) collective-permute-start(bf16[128,256]{1,0:T(8,128)(2,1)S(1)} %get-tuple-element.46), channel_id=1, source_target_pairs={{0,16},{4,20},{8,24},{12,28},{16,0},{20,4},{24,8},{28,12},{1,17},{... | collective-permute-start | bytes 196616 | tf_op jit(solution)/shard_map/ppermute | solution.py:24
  43.3 7.6 %collective-permute-start.15 = (bf16[32,1024]{1,0:T(8,128)(2,1)S(1)}, bf16[32,1024]{1,0:T(8,128)(2,1)S(1)}, u32[]{:S(2)}, u32[]{:S(2)}) collective-permute-start(bf16[32,1024]{1,0:T(8,128)(2,1)S(1)} %get-tuple-element.47), channel_id=1, source_target_pairs={{0,2},{1,3},{2,0},{3,1},{4,6},{5,7},{6,4},{7,5},{8,10},{9,11},{10,... | collective-permute-start | bytes 196616 | tf_op jit(solution)/shard_map/ppermute | solution.py:24
  46.0 6.3 %collective-permute-start.16 = (bf16[32,1024]{1,0:T(8,128)(2,1)S(1)}, bf16[32,1024]{1,0:T(8,128)(2,1)S(1)}, u32[]{:S(2)}, u32[]{:S(2)}) collective-permute-start(bf16[32,1024]{1,0:T(8,128)(2,1)S(1)} %get-tuple-element.48), channel_id=1, source_target_pairs={{0,3},{1,2},{2,1},{3,0},{4,7},{5,6},{6,5},{7,4},{8,11},{9,10},{10,... | collective-permute-start | bytes 196616 | tf_op jit(solution)/shard_map/ppermute | solution.py:24
  47.3 5.1 %collective-permute-start.17 = (bf16[32,1024]{1,0:T(8,128)(2,1)S(1)}, bf16[32,1024]{1,0:T(8,128)(2,1)S(1)}, u32[]{:S(2)}, u32[]{:S(2)}) collective-permute-start(bf16[32,1024]{1,0:T(8,128)(2,1)S(1)} %get-tuple-element.49), channel_id=1, source_target_pairs={{0,1},{1,0},{2,3},{3,2},{4,5},{5,4},{6,7},{7,6},{8,9},{9,8},{10,11... | collective-permute-start | bytes 196616 | tf_op jit(solution)/shard_map/ppermute | solution.py:24
  52.6 1.4 %collective-permute-start.18 = (bf16[4,3,32,128]{3,2,1,0:T(8,128)(2,1)S(1)}, bf16[4,3,32,128]{3,2,1,0:T(8,128)(2,1)S(1)}, u32[]{:S(2)}, u32[]{:S(2)}) collective-permute-start(bf16[4,3,32,128]{3,2,1,0:T(8,128)(2,1)S(1)} %shard_map.67), channel_id=1, source_target_pairs={{0,4},{4,0},{8,12},{12,8},{16,20},{20,16},{24,28},{28,24},{1,5},{5... | collective-permute-start | bytes 294920 | tf_op jit(solution)/shard_map/ppermute | solution.py:24
  54.0 4.2 %collective-permute-start.21 = (bf16[2,3,32,128]{3,2,1,0:T(8,128)(2,1)S(1)}, bf16[2,3,32,128]{3,2,1,0:T(8,128)(2,1)S(1)}, u32[]{:S(2)}, u32[]{:S(2)}) collective-permute-start(bf16[2,3,32,128]{3,2,1,0:T(8,128)(2,1)S(1)} %get-tuple-element.57), channel_id=1, source_target_pairs={{0,16},{4,20},{8,24},{12,28},{16,0},{20,4},{24,8},{28,12},{1,17},{... | collective-permute-start | bytes 147464 | tf_op jit(solution)/shard_map/ppermute | solution.py:24
  55.6 5.3 %collective-permute-start.19 = (bf16[2,3,32,128]{3,2,1,0:T(8,128)(2,1)S(1)}, bf16[2,3,32,128]{3,2,1,0:T(8,128)(2,1)S(1)}, u32[]{:S(2)}, u32[]{:S(2)}) collective-permute-start(bf16[2,3,32,128]{3,2,1,0:T(8,128)(2,1)S(1)} %get-tuple-element.58), channel_id=1, source_target_pairs={{0,24},{4,28},{8,16},{12,20},{16,8},{20,12},{24,0},{28,4},{1,25},{... | collective-permute-start | bytes 147464 | tf_op jit(solution)/shard_map/ppermute | solution.py:24
  56.9 4.1 %collective-permute-start.20 = (bf16[2,3,32,128]{3,2,1,0:T(8,128)(2,1)S(1)}, bf16[2,3,32,128]{3,2,1,0:T(8,128)(2,1)S(1)}, u32[]{:S(2)}, u32[]{:S(2)}) collective-permute-start(bf16[2,3,32,128]{3,2,1,0:T(8,128)(2,1)S(1)} %get-tuple-element.59), channel_id=1, source_target_pairs={{0,8},{4,12},{8,0},{12,4},{16,24},{20,28},{24,16},{28,20},{1,9},{5... | collective-permute-start | bytes 147464 | tf_op jit(solution)/shard_map/ppermute | solution.py:24

commit v6 on v5

--- a/solution.py
+++ b/solution.py
@@ -229,71 +229,58 @@
 
 
 def middle_kernel(counts, *refs):
-    last, own, own_beside, others, others_beside, (out_ref,) = unpack(refs, counts)
-    half = others[0].shape[0]
-    out_ref[:, :TILE] = gram(last, own)
-    out_ref[:, TILE : 2 * TILE] = gram(last, own_beside)
-    out_ref[:, 2 * TILE : 2 * TILE + half] = gram(last, others)
-    out_ref[:, 2 * TILE + half :] = gram(last, others_beside)
+    last, own, own_beside, others, others_beside, (slab, straight_ref) = unpack(refs, counts)
+    final = straight_ref.shape[1] // TILE
+    straight = [gram(last, own)]
+    sideways = [gram(last, own_beside)]
+    wide = gram(last, others)
+    straight += [part(wide, 0, at) for at in range(final - 1)]
+    wide = gram(last, others_beside)
+    sideways += [part(wide, 0, at) for at in range(final - 1)]
+    for chip in range(final):
+        straight_ref[:, spot(chip)] = straight[chip]
+        slab[:, spot(CORES * chip)] = straight[chip].astype(slab.dtype)
+        slab[:, spot(CORES * chip + 1)] = sideways[chip].astype(slab.dtype)
 
 
 def middle(last, own, own_beside, others, others_beside):
-    rows = last[0].shape[0]
-    span = 2 * (rows + others[0].shape[0])
+    final = others[0].shape[0] // TILE + 1
     given = [last, own, own_beside, others, others_beside]
-    counts = [len(pieces) for pieces in given] + [1]
+    counts = [len(pieces) for pieces in given] + [2]
     return kernel_call(
         functools.partial(middle_kernel, counts),
         [VMEM] * sum(counts[:-1]),
-        kept((rows, span), jnp.float32),
-        VMEM,
+        [
+            kept((TILE, CORES * final * TILE), jnp.bfloat16),
+            kept((TILE, final * TILE), jnp.float32),
+        ],
+        [VMEM] * 2,
         8,
         weight=MIDDLE_WEIGHT,
     )(*[piece for pieces in given for piece in pieces])
 
 
-def last_slab_kernel(counts, *refs):
-    last, last_beside, (middle_ref,), (slab,) = unpack(refs, counts)
-    final = middle_ref.shape[1] // (CORES * TILE)
-    tile = gram(last, last_beside)
-    slab[:, spot(place(CORES * final + 1, final))] = tile.astype(jnp.bfloat16)
-    for chip in range(final):
-        straight = middle_ref[:, spot(chip + 1 if chip else 0)]
-        sideways = middle_ref[:, spot(chip + final if chip else 1)]
-        slab[:, spot(place(CORES * chip, final))] = straight.astype(jnp.bfloat16)
-        slab[:, spot(place(CORES * chip + 1, final))] = sideways.astype(jnp.bfloat16)
-
-
-def last_chip_slab(last, last_beside, across):
-    given = [last, last_beside, [across]]
-    counts = [len(pieces) for pieces in given] + [1]
-    return kernel_call(
-        functools.partial(last_slab_kernel, counts),
-        [VMEM] * sum(counts[:-1]),
-        kept((TILE, across.shape[1] + TILE), jnp.bfloat16),
-        VMEM,
-        8,
-    )(*[piece for pieces in given for piece in pieces])
-
-
 def late_kernel(counts, *refs):
-    last_beside, own, others, (middle_ref,), slabs, (side_ref,) = unpack(refs, counts)
+    last, last_beside, own, others, (straight_ref,), slabs, (side_ref,) = unpack(refs, counts)
     tall = gram(others, last_beside)
     side_ref[...] = gram(own, last_beside)
+    *slabs, corner = slabs
+    corner[...] = gram(last, last_beside).astype(corner.dtype)
     for at, slab in enumerate(slabs):
-        slab[:, spot(0)] = middle_ref[:, spot(at + 2)].T.astype(jnp.bfloat16)
-        slab[:, spot(1)] = part(tall, at, 0).astype(jnp.bfloat16)
-
-
-def late(last_beside, own, others, across):
+        slab[:, spot(0)] = straight_ref[:, spot(at + 1)].T.astype(slab.dtype)
+        slab[:, spot(1)] = part(tall, at, 0).astype(slab.dtype)
+
+
+def late(last, last_beside, own, others, straight):
     chips = others[0].shape[0] // TILE
-    given = [last_beside, own, others, [across]]
-    counts = [len(pieces) for pieces in given] + [chips, 1]
+    given = [last, last_beside, own, others, [straight]]
+    counts = [len(pieces) for pieces in given] + [chips + 1, 1]
     return kernel_call(
         functools.partial(late_kernel, counts),
         [VMEM] * sum(counts[:-2]),
-        [kept((TILE, CORES * TILE), jnp.bfloat16)] * chips + [kept((TILE, TILE), jnp.float32)],
-        [VMEM] * (chips + 1),
+        [kept((TILE, CORES * TILE), jnp.bfloat16)] * chips
+        + [kept((TILE, TILE), jnp.bfloat16), kept((TILE, TILE), jnp.float32)],
+        [VMEM] * (chips + 2),
         8,
         weight=LATE_WEIGHT,
     )(*[piece for pieces in given for piece in pieces])
@@ -333,7 +320,7 @@
 
 def strips_kernel(groups, weights_ref, own_ref, *refs):
     my_group = lax.axis_index("grp")
-    (last_came, *came), strips = refs[:-groups], refs[-groups:]
+    (last_came, corner, *came), strips = refs[:-groups], refs[-groups:]
     final = len(came) + 1
     share = strips[0].shape[0]
     span = own_ref.shape[1]
@@ -342,7 +329,11 @@
         strip[:, span:] = weights_ref[...].astype(strip.dtype)
         for number in range(span // TILE):
             total = own_ref[rows, spot(number)]
-            total = total + last_came[rows, spot(number)].astype(jnp.float32)
+            block = (number + 1) ^ (CORES * final)
+            if block < CORES * final:
+                total = total + last_came[rows, spot(block)].astype(jnp.float32)
+            else:
+                total = total + corner[rows, :].astype(jnp.float32)
             for at, ref in enumerate(came):
                 core = ((number + 1) ^ (CORES * (at + 1))) - CORES * final
                 if core in range(CORES):
@@ -474,13 +465,12 @@
 
     last_fitted = fit([last], metric, 2, (), (blocks, weights, begun[0]))
     last_beside = beside(last_fitted)
-    across = middle(last_fitted, own, own_beside, others, others_beside)
-    last_slab = last_chip_slab(last_fitted, last_beside, across)
-    *slabs, side = late(last_beside, own, others, across)
-    came = [swapped(last_slab, "blk", CORES * final)] + [
+    last_slab, straight = middle(last_fitted, own, own_beside, others, others_beside)
+    *slabs, corner, side = late(last_fitted, last_beside, own, others, straight)
+    came = [swapped(value, "blk", CORES * final) for value in (last_slab, corner)] + [
         swapped(slabs[chip - 1], "blk", CORES * chip) for chip in range(1, final)
     ]
-    own_slab = home_slab(across, side, begun[0], came_early)
+    own_slab = home_slab(straight, side, begun[0], came_early)
     own_strips = strips(own_slab, came, groups, weights)
     chunks = [own_strips[0]] + [swapped(own_strips[d], "grp", d) for d in range(1, groups)]
 

time: 62 us -> 61.4 us (level)
  waiting for transfers between devices: 26.3 us -> 23.1 us
  starting transfers between devices: 19.8 us -> 22.5 us
    ppermute x22 -> x23, waiting for transfers between devices: 26.3 us -> 23.1 us  [swapped(): lax.ppermute(value, axis, [(source, source ^ distance) for source in rang...]
    ppermute x22 -> x23, starting transfers between devices: 19.8 us -> 22.5 us  [swapped(): lax.ppermute(value, axis, [(source, source ^ distance) for source in rang...]
  transfers between devices with their start and end apart: 22 -> 23, of which waited for: 16 -> 17; matrix products, arithmetic and copies ran while one was open for 1% -> 1% of each run, Pallas kernels for 19% -> 19%
where the time goes in v6:
time: 61.4 us; the launch traced here: 61.2 us
  waiting for transfers between devices  23.1 us (38%)
  starting transfers between devices  22.5 us (37%)
  Pallas kernels  12.6 us (21%)
  local copies, waits for them, and re-layouts  2.42 us (4%)
    ppermute x23, waiting for transfers between devices, swapped(): lax.ppermute(value, axis, [(source, source ^ distance) for source in rang...  23.1 us
    ppermute x23, starting transfers between devices, swapped(): lax.ppermute(value, axis, [(source, source ^ distance) for source in rang...  22.5 us
    pallas_call x2, Pallas kernels, fit(): kernel_call(functools.partial(fit_kernel, len(panels), pieces), [VMEM] *...  3.22 us
    pallas_call x1, Pallas kernels, first_fit(): kernel_call(first_fit_kernel, [SMEM, HBM, HBM], [kept(metric.shape, metri...  2.55 us
    dynamic_slice x1, local copies, waits for them, and re-layouts, per_device(): lax.dynamic_slice(raw_panels[0], (jnp.int32(0), starts[chip]), (rows, wid...  2.33 us
    pallas_call x1, Pallas kernels, early(): kernel_call(functools.partial(early_kernel, counts), [VMEM] * sum(counts[...  1.74 us
    pallas_call x1, Pallas kernels, cut(): kernel_call(functools.partial(cut_kernel, count), [SMEM, HBM] + [ANY] * l...  1.57 us
  transfers between devices with their start and end apart: 23, of which 17 were waited for; matrix products, arithmetic and copies ran while one was open for 1% of the time, Pallas kernels for 19%

profile of v6, /device:TPU:0, one launch (start us, length us, event | category | flops | bytes accessed | tf_op | source)
XLA Modules:
  0.0 61.2 jit_solution(16221367563240769180)
XLA Ops:
  0.0 2.3 %dynamic-slice_bitcast_fusion = (bf16[128,2048]{1,0:T(8,128)(2,1)}, bf16[128,2048]{1,0:T(8,128)(2,1)}) fusion(bf16[1,128,8192]{2,1,0:T(8,128)(2,1)} %param.5, s32[]{:T(128)S(6)} %select_n.16, s32[]{:T(128)S(6)} %select_n.15), kind=kLoop, calls=%fused_computation | loop fusion | bytes 2097160 | tf_op jit(solution)/shard_map/dynamic_slice | solution.py:437
  2.3 3.0 %collective-permute-start.3 = (bf16[128,2048]{1,0:T(8,128)(2,1)}, bf16[128,2048]{1,0:T(8,128)(2,1)}, u32[]{:S(2)}, u32[]{:S(2)}) collective-permute-start(bf16[128,2048]{1,0:T(8,128)(2,1)} %get-tuple-element.61), channel_id=1, source_target_pairs={{0,16},{4,20},{8,24},{12,28},{16,0},{20,4},{24,8},{28,12},{1,17},{... | collective-permute-start | bytes 1572872 | tf_op jit(solution)/shard_map/ppermute | solution.py:24
  5.3 1.5 %collective-permute-start.2 = (bf16[128,2048]{1,0:T(8,128)(2,1)}, bf16[128,2048]{1,0:T(8,128)(2,1)}, u32[]{:S(2)}, u32[]{:S(2)}) collective-permute-start(bf16[128,2048]{1,0:T(8,128)(2,1)} %get-tuple-element.62), channel_id=1, source_target_pairs={{0,8},{4,12},{8,0},{12,4},{16,24},{20,28},{24,16},{28,20},{1,9},{5... | collective-permute-start | bytes 1572872 | tf_op jit(solution)/shard_map/ppermute | solution.py:24
  6.8 2.5 %shard_map.56 = (bf16[1024,1024]{1,0:T(8,128)(2,1)S(1)}, bf16[128,2048]{1,0:T(8,128)(2,1)S(1)}) custom-call(s32[1]{0:T(128)} %bitcast.5.starts_ref, bf16[128,8192]{1,0:T(8,128)(2,1)} %bitcast.26, bf16[1024,1024]{1,0:T(8,128)(2,1)} %metric_ref.1), custom_call_target="tpu_custom_call" | custom-call | tf_op jit(solution)/shard_map/pallas_call | solution.py:164
  9.7 1.7 %collective-permute-done.refs_0_.refs_1_.refs_3_ = bf16[128,2048]{1,0:T(8,128)(2,1)S(1)} collective-permute-done((bf16[128,2048]{1,0:T(8,128)(2,1)S(1)}, bf16[128,2048]{1,0:T(8,128)(2,1)S(1)}, u32[]{:S(2)}, u32[]{:S(2)}) %collective-permute-start) | collective-permute-done | bytes 524320 | tf_op jit(solution)/shard_map/ppermute | solution.py:24
  11.3 1.6 %shard_map.57 = (bf16[128,2048]{1,0:T(8,128)(2,1)S(1)}, s32[1]{0:T(128)}) custom-call(s32[1]{0:T(128)} %bitcast.3.starts_ref, bf16[128,8192]{1,0:T(8,128)(2,1)} %bitcast.27, bf16[128,2048]{1,0:T(8,128)(2,1)S(1)} %collective-permute-done.refs_0_.refs_1_.refs_3_), custom_call_target="tpu_custom_call" | custom-call | tf_op jit(solution)/shard_map/pallas_call | solution.py:142
  13.0 4.5 %collective-permute-done.3.refs_1_ = bf16[128,2048]{1,0:T(8,128)(2,1)} collective-permute-done((bf16[128,2048]{1,0:T(8,128)(2,1)}, bf16[128,2048]{1,0:T(8,128)(2,1)}, u32[]{:S(2)}, u32[]{:S(2)}) %collective-permute-start.3) | collective-permute-done | bytes 524320 | tf_op jit(solution)/shard_map/ppermute | solution.py:24
  17.5 2.9 %collective-permute-done.2.refs_0_ = bf16[128,2048]{1,0:T(8,128)(2,1)} collective-permute-done((bf16[128,2048]{1,0:T(8,128)(2,1)}, bf16[128,2048]{1,0:T(8,128)(2,1)}, u32[]{:S(2)}, u32[]{:S(2)}) %collective-permute-start.2) | collective-permute-done | bytes 524320 | tf_op jit(solution)/shard_map/ppermute | solution.py:24
  20.5 2.5 %shard_map.58 = (bf16[256,512]{1,0:T(8,128)(2,1)S(1)}, bf16[256,512]{1,0:T(8,128)(2,1)S(1)}, bf16[256,512]{1,0:T(8,128)(2,1)S(1)}, bf16[256,512]{1,0:T(8,128)(2,1)S(1)}) custom-call(bf16[128,2048]{1,0:T(8,128)(2,1)} %collective-permute-done.2.refs_0_, bf16[128,2048]{1,0:T(8,128)(2,1)} %collective-permute-done.3.refs_1_, ...), custom_call_target="tpu_custom_call" | custom-call | tf_op jit(solution)/shard_map/pallas_call | solution.py:105
  24.1 0.6 shard_map.55.refs_2_.block_ref
  25.7 1.7 %shard_map.59 = (f32[128,640]{1,0:T(8,128)S(1)}, bf16[128,640]{1,0:T(8,128)(2,1)S(1)}, bf16[128,640]{1,0:T(8,128)(2,1)S(1)}) custom-call(bf16[128,2048]{1,0:T(8,128)(2,1)S(1)} %get-tuple-element.35.refs_0_.refs_2_.refs_4_, bf16[128,2048]{1,0:T(8,128)(2,1)S(1)} %collective-permute-done.refs_0_.refs_1_.refs_3_, ...), custom_call_target="tpu_custom_call" | custom-call | tf_op jit(solution)/shard_map/pallas_call | solution.py:222
  27.4 1.6 %collective-permute-start.10 = (bf16[128,640]{1,0:T(8,128)(2,1)S(1)}, bf16[128,640]{1,0:T(8,128)(2,1)S(1)}, u32[]{:S(2)}, u32[]{:S(2)}) collective-permute-start(bf16[128,640]{1,0:T(8,128)(2,1)S(1)} %get-tuple-element.47), channel_id=1, source_target_pairs={{0,8},{4,12},{8,0},{12,4},{16,24},{20,28},{24,16},{28,20},{1,9},{5... | collective-permute-start | bytes 491528 | tf_op jit(solution)/shard_map/ppermute | solution.py:24
  29.9 0.7 %shard_map.60 = (bf16[128,1024]{1,0:T(8,128)(2,1)S(1)}, bf16[128,1024]{1,0:T(8,128)(2,1)S(1)}) custom-call(bf16[128,2048]{1,0:T(8,128)(2,1)S(1)} %collective-permute-done.1.refs_0_, bf16[1024,1024]{1,0:T(8,128)(2,1)S(1)} %get-tuple-element.37.refs_2_.refs_1_, s32[24]{0:T(128)S(4)} %shard_map.55.refs_2_.block_ref, f32[32,128]{1,0:T(8,128)S(1)} %reshape.15.refs_3_.weights_ref, ...), custom_call_target="tpu_custom_call" | custom-call | tf_op jit(solution)/shard_map/pallas_call | solution.py:105
  31.2 1.1 %shard_map.61 = (bf16[128,768]{1,0:T(8,128)(2,1)S(1)}, f32[128,384]{1,0:T(8,128)S(1)}) custom-call(bf16[128,1024]{1,0:T(8,128)(2,1)S(1)} %get-tuple-element.43.refs_0_, bf16[128,1024]{1,0:T(8,128)(2,1)S(1)} %get-tuple-element.44.refs_1_, bf16[128,2048]{1,0:T(8,128)(2,1)S(1)} %get-tuple-element.35.refs_0_.refs_2_.refs_4_, ...), custom_call_target="tpu_custom_call" | custom-call | flops 6000000000 | bytes 1048576 | tf_op jit(solution)/shard_map/pallas_call | solution.py:250
  32.3 2.8 %collective-permute-start.12 = (bf16[128,768]{1,0:T(8,128)(2,1)S(1)}, bf16[128,768]{1,0:T(8,128)(2,1)S(1)}, u32[]{:S(2)}, u32[]{:S(2)}) collective-permute-start(bf16[128,768]{1,0:T(8,128)(2,1)S(1)} %get-tuple-element.49), channel_id=1, source_target_pairs={{0,24},{4,28},{8,16},{12,20},{16,8},{20,12},{24,0},{28,4},{1,25},{... | collective-permute-start | bytes 589832 | tf_op jit(solution)/shard_map/ppermute | solution.py:24
  35.2 0.7 %shard_map.62 = (bf16[128,256]{1,0:T(8,128)(2,1)S(1)}, bf16[128,256]{1,0:T(8,128)(2,1)S(1)}, bf16[128,128]{1,0:T(8,128)(2,1)S(1)}, f32[128,128]{1,0:T(8,128)S(1)}) custom-call(bf16[128,1024]{1,0:T(8,128)(2,1)S(1)} %get-tuple-element.43.refs_0_, bf16[128,1024]{1,0:T(8,128)(2,1)S(1)} %get-tuple-element.44.refs_1_, ...), custom_call_target="tpu_custom_call" | custom-call | flops 5000000000 | bytes 1048576 | tf_op jit(solution)/shard_map/pallas_call | solution.py:278
  36.2 1.7 %collective-permute-start.14 = (bf16[128,256]{1,0:T(8,128)(2,1)S(1)}, bf16[128,256]{1,0:T(8,128)(2,1)S(1)}, u32[]{:S(2)}, u32[]{:S(2)}) collective-permute-start(bf16[128,256]{1,0:T(8,128)(2,1)S(1)} %get-tuple-element.51), channel_id=1, source_target_pairs={{0,8},{4,12},{8,0},{12,4},{16,24},{20,28},{24,16},{28,20},{1,9},{5... | collective-permute-start | bytes 196616 | tf_op jit(solution)/shard_map/ppermute | solution.py:24
  37.8 1.6 %collective-permute-start.15 = (bf16[128,256]{1,0:T(8,128)(2,1)S(1)}, bf16[128,256]{1,0:T(8,128)(2,1)S(1)}, u32[]{:S(2)}, u32[]{:S(2)}) collective-permute-start(bf16[128,256]{1,0:T(8,128)(2,1)S(1)} %get-tuple-element.52), channel_id=1, source_target_pairs={{0,16},{4,20},{8,24},{12,28},{16,0},{20,4},{24,8},{28,12},{1,17},{... | collective-permute-start | bytes 196616 | tf_op jit(solution)/shard_map/ppermute | solution.py:24
  39.5 1.5 %collective-permute-done.12.refs_0_ = bf16[128,768]{1,0:T(8,128)(2,1)S(1)} collective-permute-done((bf16[128,768]{1,0:T(8,128)(2,1)S(1)}, bf16[128,768]{1,0:T(8,128)(2,1)S(1)}, u32[]{:S(2)}, u32[]{:S(2)}) %collective-permute-start.12) | collective-permute-done | bytes 196640 | tf_op jit(solution)/shard_map/ppermute | solution.py:24
  41.1 0.7 %collective-permute-done.13.refs_1_ = bf16[128,128]{1,0:T(8,128)(2,1)S(1)} collective-permute-done((bf16[128,128]{1,0:T(8,128)(2,1)S(1)}, bf16[128,128]{1,0:T(8,128)(2,1)S(1)}, u32[]{:S(2)}, u32[]{:S(2)}) %collective-permute-start.13) | collective-permute-done | bytes 32800 | tf_op jit(solution)/shard_map/ppermute | solution.py:24
  41.7 0.9 %collective-permute-done.14.refs_2_ = bf16[128,256]{1,0:T(8,128)(2,1)S(1)} collective-permute-done((bf16[128,256]{1,0:T(8,128)(2,1)S(1)}, bf16[128,256]{1,0:T(8,128)(2,1)S(1)}, u32[]{:S(2)}, u32[]{:S(2)}) %collective-permute-start.14) | collective-permute-done | bytes 65568 | tf_op jit(solution)/shard_map/ppermute | solution.py:24
  42.7 2.7 %collective-permute-start.16 = (bf16[32,1024]{1,0:T(8,128)(2,1)S(1)}, bf16[32,1024]{1,0:T(8,128)(2,1)S(1)}, u32[]{:S(2)}, u32[]{:S(2)}) collective-permute-start(bf16[32,1024]{1,0:T(8,128)(2,1)S(1)} %get-tuple-element.53), channel_id=1, source_target_pairs={{0,2},{1,3},{2,0},{3,1},{4,6},{5,7},{6,4},{7,5},{8,10},{9,11},{10,... | collective-permute-start | bytes 196616 | tf_op jit(solution)/shard_map/ppermute | solution.py:24
  45.3 1.4 %collective-permute-start.17 = (bf16[32,1024]{1,0:T(8,128)(2,1)S(1)}, bf16[32,1024]{1,0:T(8,128)(2,1)S(1)}, u32[]{:S(2)}, u32[]{:S(2)}) collective-permute-start(bf16[32,1024]{1,0:T(8,128)(2,1)S(1)} %get-tuple-element.54), channel_id=1, source_target_pairs={{0,3},{1,2},{2,1},{3,0},{4,7},{5,6},{6,5},{7,4},{8,11},{9,10},{10,... | collective-permute-start | bytes 196616 | tf_op jit(solution)/shard_map/ppermute | solution.py:24
  46.9 1.1 %collective-permute-done.16.refs_0_ = bf16[32,1024]{1,0:T(8,128)(2,1)S(1)} collective-permute-done((bf16[32,1024]{1,0:T(8,128)(2,1)S(1)}, bf16[32,1024]{1,0:T(8,128)(2,1)S(1)}, u32[]{:S(2)}, u32[]{:S(2)}) %collective-permute-start.16) | collective-permute-done | bytes 65568 | tf_op jit(solution)/shard_map/ppermute | solution.py:24
  48.0 3.5 %collective-permute-done.17.refs_1_ = bf16[32,1024]{1,0:T(8,128)(2,1)S(1)} collective-permute-done((bf16[32,1024]{1,0:T(8,128)(2,1)S(1)}, bf16[32,1024]{1,0:T(8,128)(2,1)S(1)}, u32[]{:S(2)}, u32[]{:S(2)}) %collective-permute-start.17) | collective-permute-done | bytes 65568 | tf_op jit(solution)/shard_map/ppermute | solution.py:24
  51.9 1.2 %collective-permute-done.19 = bf16[4,3,32,128]{3,2,1,0:T(8,128)(2,1)S(1)} collective-permute-done((bf16[4,3,32,128]{3,2,1,0:T(8,128)(2,1)S(1)}, bf16[4,3,32,128]{3,2,1,0:T(8,128)(2,1)S(1)}, u32[]{:S(2)}, u32[]{:S(2)}) %collective-permute-start.19) | collective-permute-done | bytes 98336 | tf_op jit(solution)/shard_map/ppermute | solution.py:24
  53.1 1.5 %collective-permute-start.22 = (bf16[2,3,32,128]{3,2,1,0:T(8,128)(2,1)S(1)}, bf16[2,3,32,128]{3,2,1,0:T(8,128)(2,1)S(1)}, u32[]{:S(2)}, u32[]{:S(2)}) collective-permute-start(bf16[2,3,32,128]{3,2,1,0:T(8,128)(2,1)S(1)} %get-tuple-element.63), channel_id=1, source_target_pairs={{0,16},{4,20},{8,24},{12,28},{16,0},{20,4},{24,8},{28,12},{1,17},{... | collective-permute-start | bytes 147464 | tf_op jit(solution)/shard_map/ppermute | solution.py:24
  54.7 1.6 %collective-permute-start.20 = (bf16[2,3,32,128]{3,2,1,0:T(8,128)(2,1)S(1)}, bf16[2,3,32,128]{3,2,1,0:T(8,128)(2,1)S(1)}, u32[]{:S(2)}, u32[]{:S(2)}) collective-permute-start(bf16[2,3,32,128]{3,2,1,0:T(8,128)(2,1)S(1)} %get-tuple-element.64), channel_id=1, source_target_pairs={{0,24},{4,28},{8,16},{12,20},{16,8},{20,12},{24,0},{28,4},{1,25},{... | collective-permute-start | bytes 147464 | tf_op jit(solution)/shard_map/ppermute | solution.py:24
  56.7 0.6 collective-permute-done.22.refs_2_
  57.3 2.4 %collective-permute-done.20.refs_0_ = bf16[2,3,32,128]{3,2,1,0:T(8,128)(2,1)S(1)} collective-permute-done((bf16[2,3,32,128]{3,2,1,0:T(8,128)(2,1)S(1)}, bf16[2,3,32,128]{3,2,1,0:T(8,128)(2,1)S(1)}, u32[]{:S(2)}, u32[]{:S(2)}) %collective-permute-start.20) | collective-permute-done | bytes 49184 | tf_op jit(solution)/shard_map/ppermute | solution.py:24
  59.7 0.7 %collective-permute-done.21.refs_1_ = bf16[2,3,32,128]{3,2,1,0:T(8,128)(2,1)S(1)} collective-permute-done((bf16[2,3,32,128]{3,2,1,0:T(8,128)(2,1)S(1)}, bf16[2,3,32,128]{3,2,1,0:T(8,128)(2,1)S(1)}, u32[]{:S(2)}, u32[]{:S(2)}) %collective-permute-start.21) | collective-permute-done | bytes 49184 | tf_op jit(solution)/shard_map/ppermute | solution.py:24
  60.4 0.8 %shard_map.67 = f32[8,3,32,128]{3,2,1,0:T(8,128)} custom-call(f32[3,32,128]{2,1,0:T(8,128)S(1)} %bitcast.25, bf16[3,32,128]{2,1,0:T(8,128)(2,1)S(1)} %slice_bitcast_fusion.1.beside_ref, bf16[2,3,32,128]{3,2,1,0:T(8,128)(2,1)S(1)} %collective-permute-done.20.refs_0_, bf16[2,3,32,128]{3,2,1,0:T(8,128)(2,1)S(1)} %collective-permute-done.21.refs_1_, ...), custom_call_target="tpu_custom_call" | custom-call | tf_op jit(solution)/shard_map/pallas_call | solution.py:410
  (48 shorter events, 5.5 us)
Async XLA Ops:
  2.3 15.2 %collective-permute-start.3 = (bf16[128,2048]{1,0:T(8,128)(2,1)}, bf16[128,2048]{1,0:T(8,128)(2,1)}, u32[]{:S(2)}, u32[]{:S(2)}) collective-permute-start(bf16[128,2048]{1,0:T(8,128)(2,1)} %get-tuple-element.61), channel_id=1, source_target_pairs={{0,16},{4,20},{8,24},{12,28},{16,0},{20,4},{24,8},{28,12},{1,17},{... | collective-permute-start | bytes 1572872 | tf_op jit(solution)/shard_map/ppermute | solution.py:24
  5.3 15.2 %collective-permute-start.2 = (bf16[128,2048]{1,0:T(8,128)(2,1)}, bf16[128,2048]{1,0:T(8,128)(2,1)}, u32[]{:S(2)}, u32[]{:S(2)}) collective-permute-start(bf16[128,2048]{1,0:T(8,128)(2,1)} %get-tuple-element.62), channel_id=1, source_target_pairs={{0,8},{4,12},{8,0},{12,4},{16,24},{20,28},{24,16},{28,20},{1,9},{5... | collective-permute-start | bytes 1572872 | tf_op jit(solution)/shard_map/ppermute | solution.py:24
  6.8 2.6 %copy-start.1 = (s32[14,1]{0,1:T(1,128)S(1)}, s32[14,1]{0,1:T(1,128)}, u32[]{:S(2)}) copy-start(s32[14,1]{0,1:T(1,128)} %param.8) | copy-start | bytes 172
  6.8 2.9 %copy-start.2 = (s32[14,2]{0,1:T(2,128)S(1)}, s32[14,2]{0,1:T(2,128)}, u32[]{:S(2)}) copy-start(s32[14,2]{0,1:T(2,128)} %param.7) | copy-start | bytes 340
  9.3 2.0 %collective-permute-start = (bf16[128,2048]{1,0:T(8,128)(2,1)S(1)}, bf16[128,2048]{1,0:T(8,128)(2,1)S(1)}, u32[]{:S(2)}, u32[]{:S(2)}) collective-permute-start(bf16[128,2048]{1,0:T(8,128)(2,1)S(1)} %get-tuple-element.35.refs_0_.refs_2_.refs_4_), channel_id=1, source_target_pairs={{0,4},{4,0},{8,12},{12,8},{16,20},{20,16},{24,28},{28,24},{1,5},{5... | collective-permute-start | bytes 1572872 | tf_op jit(solution)/shard_map/ppermute | solution.py:24
  12.9 11.1 %copy-start = (s32[14,1]{0,1:T(1,128)S(1)}, s32[14,1]{0,1:T(1,128)}, u32[]{:S(2)}) copy-start(s32[14,1]{0,1:T(1,128)} %param.9) | copy-start | bytes 172
  12.9 16.9 %collective-permute-start.1 = (bf16[128,2048]{1,0:T(8,128)(2,1)S(1)}, bf16[128,2048]{1,0:T(8,128)(2,1)S(1)}, u32[]{:S(2)}, u32[]{:S(2)}) collective-permute-start(bf16[128,2048]{1,0:T(8,128)(2,1)S(1)} %get-tuple-element.36), channel_id=1, source_target_pairs={{0,24},{4,28},{8,16},{12,20},{16,8},{20,12},{24,0},{28,4},{1,25},{... | collective-permute-start | bytes 1572872 | tf_op jit(solution)/shard_map/ppermute | solution.py:24
  22.9 1.8 %collective-permute-start.4 = (bf16[256,512]{1,0:T(8,128)(2,1)S(1)}, bf16[256,512]{1,0:T(8,128)(2,1)S(1)}, u32[]{:S(2)}, u32[]{:S(2)}) collective-permute-start(bf16[256,512]{1,0:T(8,128)(2,1)S(1)} %get-tuple-element.38.refs_2_.refs_4_.refs_5_), channel_id=1, source_target_pairs={{0,4},{4,0},{8,12},{12,8},{16,20},{20,16},{24,28},{28,24},{1,5},{5... | collective-permute-start | bytes 786440 | tf_op jit(solution)/shard_map/ppermute | solution.py:24
  23.0 1.9 %collective-permute-start.5 = (bf16[256,512]{1,0:T(8,128)(2,1)S(1)}, bf16[256,512]{1,0:T(8,128)(2,1)S(1)}, u32[]{:S(2)}, u32[]{:S(2)}) collective-permute-start(bf16[256,512]{1,0:T(8,128)(2,1)S(1)} %get-tuple-element.39.refs_3_.refs_5_.refs_6_), channel_id=1, source_target_pairs={{0,4},{4,0},{8,12},{12,8},{16,20},{20,16},{24,28},{28,24},{1,5},{5... | collective-permute-start | bytes 786440 | tf_op jit(solution)/shard_map/ppermute | solution.py:24
  23.5 1.8 %collective-permute-start.6 = (bf16[256,512]{1,0:T(8,128)(2,1)S(1)}, bf16[256,512]{1,0:T(8,128)(2,1)S(1)}, u32[]{:S(2)}, u32[]{:S(2)}) collective-permute-start(bf16[256,512]{1,0:T(8,128)(2,1)S(1)} %get-tuple-element.40.refs_4_.refs_6_.refs_7_), channel_id=1, source_target_pairs={{0,4},{4,0},{8,12},{12,8},{16,20},{20,16},{24,28},{28,24},{1,5},{5... | collective-permute-start | bytes 786440 | tf_op jit(solution)/shard_map/ppermute | solution.py:24
  23.6 2.1 %collective-permute-start.7 = (bf16[256,512]{1,0:T(8,128)(2,1)S(1)}, bf16[256,512]{1,0:T(8,128)(2,1)S(1)}, u32[]{:S(2)}, u32[]{:S(2)}) collective-permute-start(bf16[256,512]{1,0:T(8,128)(2,1)S(1)} %get-tuple-element.41.refs_5_.refs_7_.refs_8_), channel_id=1, source_target_pairs={{0,4},{4,0},{8,12},{12,8},{16,20},{20,16},{24,28},{28,24},{1,5},{5... | collective-permute-start | bytes 786440 | tf_op jit(solution)/shard_map/ppermute | solution.py:24
  27.4 10.4 %collective-permute-start.10 = (bf16[128,640]{1,0:T(8,128)(2,1)S(1)}, bf16[128,640]{1,0:T(8,128)(2,1)S(1)}, u32[]{:S(2)}, u32[]{:S(2)}) collective-permute-start(bf16[128,640]{1,0:T(8,128)(2,1)S(1)} %get-tuple-element.47), channel_id=1, source_target_pairs={{0,8},{4,12},{8,0},{12,4},{16,24},{20,28},{24,16},{28,20},{1,9},{5... | collective-permute-start | bytes 491528 | tf_op jit(solution)/shard_map/ppermute | solution.py:24
  29.0 10.5 %collective-permute-start.11 = (bf16[128,640]{1,0:T(8,128)(2,1)S(1)}, bf16[128,640]{1,0:T(8,128)(2,1)S(1)}, u32[]{:S(2)}, u32[]{:S(2)}) collective-permute-start(bf16[128,640]{1,0:T(8,128)(2,1)S(1)} %get-tuple-element.48), channel_id=1, source_target_pairs={{0,16},{4,20},{8,24},{12,28},{16,0},{20,4},{24,8},{28,12},{1,17},{... | collective-permute-start | bytes 491528 | tf_op jit(solution)/shard_map/ppermute | solution.py:24
  30.7 4.5 %collective-permute-start.8 = (bf16[128,1024]{1,0:T(8,128)(2,1)S(1)}, bf16[128,1024]{1,0:T(8,128)(2,1)S(1)}, u32[]{:S(2)}, u32[]{:S(2)}) collective-permute-start(bf16[128,1024]{1,0:T(8,128)(2,1)S(1)} %get-tuple-element.43.refs_0_), channel_id=1, source_target_pairs={{0,4},{4,0},{8,12},{12,8},{16,20},{20,16},{24,28},{28,24},{1,5},{5... | collective-permute-start | bytes 786440 | tf_op jit(solution)/shard_map/ppermute | solution.py:24
  30.7 4.4 %collective-permute-start.9 = (bf16[128,1024]{1,0:T(8,128)(2,1)S(1)}, bf16[128,1024]{1,0:T(8,128)(2,1)S(1)}, u32[]{:S(2)}, u32[]{:S(2)}) collective-permute-start(bf16[128,1024]{1,0:T(8,128)(2,1)S(1)} %get-tuple-element.44.refs_1_), channel_id=1, source_target_pairs={{0,4},{4,0},{8,12},{12,8},{16,20},{20,16},{24,28},{28,24},{1,5},{5... | collective-permute-start | bytes 786440 | tf_op jit(solution)/shard_map/ppermute | solution.py:24
  32.3 8.7 %collective-permute-start.12 = (bf16[128,768]{1,0:T(8,128)(2,1)S(1)}, bf16[128,768]{1,0:T(8,128)(2,1)S(1)}, u32[]{:S(2)}, u32[]{:S(2)}) collective-permute-start(bf16[128,768]{1,0:T(8,128)(2,1)S(1)} %get-tuple-element.49), channel_id=1, source_target_pairs={{0,24},{4,28},{8,16},{12,20},{16,8},{20,12},{24,0},{28,4},{1,25},{... | collective-permute-start | bytes 589832 | tf_op jit(solution)/shard_map/ppermute | solution.py:24
  35.9 5.8 %collective-permute-start.13 = (bf16[128,128]{1,0:T(8,128)(2,1)S(1)}, bf16[128,128]{1,0:T(8,128)(2,1)S(1)}, u32[]{:S(2)}, u32[]{:S(2)}) collective-permute-start(bf16[128,128]{1,0:T(8,128)(2,1)S(1)} %get-tuple-element.50), channel_id=1, source_target_pairs={{0,24},{4,28},{8,16},{12,20},{16,8},{20,12},{24,0},{28,4},{1,25},{... | collective-permute-start | bytes 98312 | tf_op jit(solution)/shard_map/ppermute | solution.py:24
  36.2 6.4 %collective-permute-start.14 = (bf16[128,256]{1,0:T(8,128)(2,1)S(1)}, bf16[128,256]{1,0:T(8,128)(2,1)S(1)}, u32[]{:S(2)}, u32[]{:S(2)}) collective-permute-start(bf16[128,256]{1,0:T(8,128)(2,1)S(1)} %get-tuple-element.51), channel_id=1, source_target_pairs={{0,8},{4,12},{8,0},{12,4},{16,24},{20,28},{24,16},{28,20},{1,9},{5... | collective-permute-start | bytes 196616 | tf_op jit(solution)/shard_map/ppermute | solution.py:24
  37.8 4.7 %collective-permute-start.15 = (bf16[128,256]{1,0:T(8,128)(2,1)S(1)}, bf16[128,256]{1,0:T(8,128)(2,1)S(1)}, u32[]{:S(2)}, u32[]{:S(2)}) collective-permute-start(bf16[128,256]{1,0:T(8,128)(2,1)S(1)} %get-tuple-element.52), channel_id=1, source_target_pairs={{0,16},{4,20},{8,24},{12,28},{16,0},{20,4},{24,8},{28,12},{1,17},{... | collective-permute-start | bytes 196616 | tf_op jit(solution)/shard_map/ppermute | solution.py:24
  42.7 5.4 %collective-permute-start.16 = (bf16[32,1024]{1,0:T(8,128)(2,1)S(1)}, bf16[32,1024]{1,0:T(8,128)(2,1)S(1)}, u32[]{:S(2)}, u32[]{:S(2)}) collective-permute-start(bf16[32,1024]{1,0:T(8,128)(2,1)S(1)} %get-tuple-element.53), channel_id=1, source_target_pairs={{0,2},{1,3},{2,0},{3,1},{4,6},{5,7},{6,4},{7,5},{8,10},{9,11},{10,... | collective-permute-start | bytes 196616 | tf_op jit(solution)/shard_map/ppermute | solution.py:24
  45.3 6.2 %collective-permute-start.17 = (bf16[32,1024]{1,0:T(8,128)(2,1)S(1)}, bf16[32,1024]{1,0:T(8,128)(2,1)S(1)}, u32[]{:S(2)}, u32[]{:S(2)}) collective-permute-start(bf16[32,1024]{1,0:T(8,128)(2,1)S(1)} %get-tuple-element.54), channel_id=1, source_target_pairs={{0,3},{1,2},{2,1},{3,0},{4,7},{5,6},{6,5},{7,4},{8,11},{9,10},{10,... | collective-permute-start | bytes 196616 | tf_op jit(solution)/shard_map/ppermute | solution.py:24
  46.7 5.0 %collective-permute-start.18 = (bf16[32,1024]{1,0:T(8,128)(2,1)S(1)}, bf16[32,1024]{1,0:T(8,128)(2,1)S(1)}, u32[]{:S(2)}, u32[]{:S(2)}) collective-permute-start(bf16[32,1024]{1,0:T(8,128)(2,1)S(1)} %get-tuple-element.55), channel_id=1, source_target_pairs={{0,1},{1,0},{2,3},{3,2},{4,5},{5,4},{6,7},{7,6},{8,9},{9,8},{10,11... | collective-permute-start | bytes 196616 | tf_op jit(solution)/shard_map/ppermute | solution.py:24
  51.7 1.4 %collective-permute-start.19 = (bf16[4,3,32,128]{3,2,1,0:T(8,128)(2,1)S(1)}, bf16[4,3,32,128]{3,2,1,0:T(8,128)(2,1)S(1)}, u32[]{:S(2)}, u32[]{:S(2)}) collective-permute-start(bf16[4,3,32,128]{3,2,1,0:T(8,128)(2,1)S(1)} %shard_map.66), channel_id=1, source_target_pairs={{0,4},{4,0},{8,12},{12,8},{16,20},{20,16},{24,28},{28,24},{1,5},{5... | collective-permute-start | bytes 294920 | tf_op jit(solution)/shard_map/ppermute | solution.py:24
  53.1 4.2 %collective-permute-start.22 = (bf16[2,3,32,128]{3,2,1,0:T(8,128)(2,1)S(1)}, bf16[2,3,32,128]{3,2,1,0:T(8,128)(2,1)S(1)}, u32[]{:S(2)}, u32[]{:S(2)}) collective-permute-start(bf16[2,3,32,128]{3,2,1,0:T(8,128)(2,1)S(1)} %get-tuple-element.63), channel_id=1, source_target_pairs={{0,16},{4,20},{8,24},{12,28},{16,0},{20,4},{24,8},{28,12},{1,17},{... | collective-permute-start | bytes 147464 | tf_op jit(solution)/shard_map/ppermute | solution.py:24
  54.7 5.1 %collective-permute-start.20 = (bf16[2,3,32,128]{3,2,1,0:T(8,128)(2,1)S(1)}, bf16[2,3,32,128]{3,2,1,0:T(8,128)(2,1)S(1)}, u32[]{:S(2)}, u32[]{:S(2)}) collective-permute-start(bf16[2,3,32,128]{3,2,1,0:T(8,128)(2,1)S(1)} %get-tuple-element.64), channel_id=1, source_target_pairs={{0,24},{4,28},{8,16},{12,20},{16,8},{20,12},{24,0},{28,4},{1,25},{... | collective-permute-start | bytes 147464 | tf_op jit(solution)/shard_map/ppermute | solution.py:24
  56.3 4.1 %collective-permute-start.21 = (bf16[2,3,32,128]{3,2,1,0:T(8,128)(2,1)S(1)}, bf16[2,3,32,128]{3,2,1,0:T(8,128)(2,1)S(1)}, u32[]{:S(2)}, u32[]{:S(2)}) collective-permute-start(bf16[2,3,32,128]{3,2,1,0:T(8,128)(2,1)S(1)} %get-tuple-element.65), channel_id=1, source_target_pairs={{0,8},{4,12},{8,0},{12,4},{16,24},{20,28},{24,16},{28,20},{1,9},{5... | collective-permute-start | bytes 147464 | tf_op jit(solution)/shard_map/ppermute | solution.py:24

commit v7 on v6

--- a/solution.py
+++ b/solution.py
@@ -10,7 +10,7 @@
 TILE = 128
 CORES = 2
 MIB = 1024 * 1024
-MIDDLE_WEIGHT = 60 * 10**8
+MIDDLE_WEIGHT = 160 * 10**8
 LATE_WEIGHT = 5 * 10**9
 HOME_WEIGHT = 12 * 10**8
 SMEM = pl.BlockSpec(memory_space=pltpu.SMEM)
@@ -463,7 +463,7 @@
     begun = early(own, own_beside, others, others_beside)
     came_early = [swapped(begun[chip], "blk", CORES * chip) for chip in range(1, final)]
 
-    last_fitted = fit([last], metric, 2, (), (blocks, weights, begun[0]))
+    last_fitted = fit([last], metric, 1, (), (blocks, weights, begun[0]))
     last_beside = beside(last_fitted)
     last_slab, straight = middle(last_fitted, own, own_beside, others, others_beside)
     *slabs, corner, side = late(last_fitted, last_beside, own, others, straight)

time: 61.4 us -> 61.3 us (level)
    ppermute x23 -> x22, starting transfers between devices: 22.5 us -> 22 us  [swapped(): lax.ppermute(value, axis, [(source, source ^ distance) for source in rang...]
    ppermute x23 -> x22, waiting for transfers between devices: 23.1 us -> 23.5 us  [swapped(): lax.ppermute(value, axis, [(source, source ^ distance) for source in rang...]
  transfers between devices with their start and end apart: 23 -> 22, of which waited for: 17 -> 17; matrix products, arithmetic and copies ran while one was open for 1% -> 1% of each run, Pallas kernels for 19% -> 19%
where the time goes in v7:
time: 61.3 us; the launch traced here: 61.1 us
  waiting for transfers between devices  23.5 us (38%)
  starting transfers between devices  22 us (36%)
  Pallas kernels  12.6 us (21%)
  local copies, waits for them, and re-layouts  2.4 us (4%)
    ppermute x22, waiting for transfers between devices, swapped(): lax.ppermute(value, axis, [(source, source ^ distance) for source in rang...  23.5 us
    ppermute x22, starting transfers between devices, swapped(): lax.ppermute(value, axis, [(source, source ^ distance) for source in rang...  22 us
    pallas_call x2, Pallas kernels, fit(): kernel_call(functools.partial(fit_kernel, len(panels), pieces), [VMEM] *...  3.22 us
    pallas_call x1, Pallas kernels, first_fit(): kernel_call(first_fit_kernel, [SMEM, HBM, HBM], [kept(metric.shape, metri...  2.55 us
    dynamic_slice x1, local copies, waits for them, and re-layouts, per_device(): lax.dynamic_slice(raw_panels[0], (jnp.int32(0), starts[chip]), (rows, wid...  2.3 us
    pallas_call x1, Pallas kernels, early(): kernel_call(functools.partial(early_kernel, counts), [VMEM] * sum(counts[...  1.73 us
    pallas_call x1, Pallas kernels, cut(): kernel_call(functools.partial(cut_kernel, count), [SMEM, HBM] + [ANY] * l...  1.57 us
  transfers between devices with their start and end apart: 22, of which 17 were waited for; matrix products, arithmetic and copies ran while one was open for 1% of the time, Pallas kernels for 19%

profile of v7, /device:TPU:0, one launch (start us, length us, event | category | flops | bytes accessed | tf_op | source)
XLA Modules:
  0.0 61.1 jit_solution(6942392843027183794)
XLA Ops:
  0.0 2.3 %dynamic-slice_bitcast_fusion = (bf16[128,2048]{1,0:T(8,128)(2,1)}, bf16[128,2048]{1,0:T(8,128)(2,1)}) fusion(bf16[1,128,8192]{2,1,0:T(8,128)(2,1)} %param.5, s32[]{:T(128)S(6)} %select_n.16, s32[]{:T(128)S(6)} %select_n.15), kind=kLoop, calls=%fused_computation | loop fusion | bytes 2097160 | tf_op jit(solution)/shard_map/dynamic_slice | solution.py:437
  2.3 3.0 %collective-permute-start.3 = (bf16[128,2048]{1,0:T(8,128)(2,1)}, bf16[128,2048]{1,0:T(8,128)(2,1)}, u32[]{:S(2)}, u32[]{:S(2)}) collective-permute-start(bf16[128,2048]{1,0:T(8,128)(2,1)} %get-tuple-element.57), channel_id=1, source_target_pairs={{0,16},{4,20},{8,24},{12,28},{16,0},{20,4},{24,8},{28,12},{1,17},{... | collective-permute-start | bytes 1572872 | tf_op jit(solution)/shard_map/ppermute | solution.py:24
  5.3 1.5 %collective-permute-start.2 = (bf16[128,2048]{1,0:T(8,128)(2,1)}, bf16[128,2048]{1,0:T(8,128)(2,1)}, u32[]{:S(2)}, u32[]{:S(2)}) collective-permute-start(bf16[128,2048]{1,0:T(8,128)(2,1)} %get-tuple-element.58), channel_id=1, source_target_pairs={{0,8},{4,12},{8,0},{12,4},{16,24},{20,28},{24,16},{28,20},{1,9},{5... | collective-permute-start | bytes 1572872 | tf_op jit(solution)/shard_map/ppermute | solution.py:24
  6.8 2.5 %shard_map.56 = (bf16[1024,1024]{1,0:T(8,128)(2,1)S(1)}, bf16[128,2048]{1,0:T(8,128)(2,1)S(1)}) custom-call(s32[1]{0:T(128)} %bitcast.5.starts_ref, bf16[128,8192]{1,0:T(8,128)(2,1)} %bitcast.26, bf16[1024,1024]{1,0:T(8,128)(2,1)} %metric_ref.1), custom_call_target="tpu_custom_call" | custom-call | tf_op jit(solution)/shard_map/pallas_call | solution.py:164
  9.6 1.7 %collective-permute-done.refs_0_.refs_1_.refs_2_ = bf16[128,2048]{1,0:T(8,128)(2,1)S(1)} collective-permute-done((bf16[128,2048]{1,0:T(8,128)(2,1)S(1)}, bf16[128,2048]{1,0:T(8,128)(2,1)S(1)}, u32[]{:S(2)}, u32[]{:S(2)}) %collective-permute-start) | collective-permute-done | bytes 524320 | tf_op jit(solution)/shard_map/ppermute | solution.py:24
  11.3 1.6 %shard_map.57 = (bf16[128,2048]{1,0:T(8,128)(2,1)S(1)}, s32[1]{0:T(128)}) custom-call(s32[1]{0:T(128)} %bitcast.3.starts_ref, bf16[128,8192]{1,0:T(8,128)(2,1)} %bitcast.27, bf16[128,2048]{1,0:T(8,128)(2,1)S(1)} %collective-permute-done.refs_0_.refs_1_.refs_2_), custom_call_target="tpu_custom_call" | custom-call | tf_op jit(solution)/shard_map/pallas_call | solution.py:142
  13.0 4.5 %collective-permute-done.3.refs_1_ = bf16[128,2048]{1,0:T(8,128)(2,1)} collective-permute-done((bf16[128,2048]{1,0:T(8,128)(2,1)}, bf16[128,2048]{1,0:T(8,128)(2,1)}, u32[]{:S(2)}, u32[]{:S(2)}) %collective-permute-start.3) | collective-permute-done | bytes 524320 | tf_op jit(solution)/shard_map/ppermute | solution.py:24
  17.5 2.9 %collective-permute-done.2.refs_0_ = bf16[128,2048]{1,0:T(8,128)(2,1)} collective-permute-done((bf16[128,2048]{1,0:T(8,128)(2,1)}, bf16[128,2048]{1,0:T(8,128)(2,1)}, u32[]{:S(2)}, u32[]{:S(2)}) %collective-permute-start.2) | collective-permute-done | bytes 524320 | tf_op jit(solution)/shard_map/ppermute | solution.py:24
  20.4 2.5 %shard_map.58 = (bf16[256,512]{1,0:T(8,128)(2,1)S(1)}, bf16[256,512]{1,0:T(8,128)(2,1)S(1)}, bf16[256,512]{1,0:T(8,128)(2,1)S(1)}, bf16[256,512]{1,0:T(8,128)(2,1)S(1)}) custom-call(bf16[128,2048]{1,0:T(8,128)(2,1)} %collective-permute-done.2.refs_0_, bf16[128,2048]{1,0:T(8,128)(2,1)} %collective-permute-done.3.refs_1_, ...), custom_call_target="tpu_custom_call" | custom-call | tf_op jit(solution)/shard_map/pallas_call | solution.py:105
  25.6 1.7 %shard_map.59 = (f32[128,640]{1,0:T(8,128)S(1)}, bf16[128,640]{1,0:T(8,128)(2,1)S(1)}, bf16[128,640]{1,0:T(8,128)(2,1)S(1)}) custom-call(bf16[128,2048]{1,0:T(8,128)(2,1)S(1)} %get-tuple-element.33.refs_0_.refs_1_.refs_2_, bf16[128,2048]{1,0:T(8,128)(2,1)S(1)} %collective-permute-done.refs_0_.refs_1_.refs_2_, ...), custom_call_target="tpu_custom_call" | custom-call | tf_op jit(solution)/shard_map/pallas_call | solution.py:222
  27.4 1.6 %collective-permute-start.9 = (bf16[128,640]{1,0:T(8,128)(2,1)S(1)}, bf16[128,640]{1,0:T(8,128)(2,1)S(1)}, u32[]{:S(2)}, u32[]{:S(2)}) collective-permute-start(bf16[128,640]{1,0:T(8,128)(2,1)S(1)} %get-tuple-element.43), channel_id=1, source_target_pairs={{0,8},{4,12},{8,0},{12,4},{16,24},{20,28},{24,16},{28,20},{1,9},{5... | collective-permute-start | bytes 491528 | tf_op jit(solution)/shard_map/ppermute | solution.py:24
  29.9 0.7 %shard_map.60.refs_0_ = bf16[128,2048]{1,0:T(8,128)(2,1)S(1)} custom-call(bf16[128,2048]{1,0:T(8,128)(2,1)S(1)} %collective-permute-done.1.refs_0_, bf16[1024,1024]{1,0:T(8,128)(2,1)S(1)} %get-tuple-element.35.refs_2_.refs_1_, s32[24]{0:T(128)S(4)} %shard_map.55.refs_2_.block_ref, f32[32,128]{1,0:T(8,128)S(1)} %reshape.15.refs_3_.weights_ref, ...), custom_call_target="tpu_custom_call" | custom-call | tf_op jit(solution)/shard_map/pallas_call | solution.py:105
  30.7 1.1 %shard_map.61 = (bf16[128,768]{1,0:T(8,128)(2,1)S(1)}, f32[128,384]{1,0:T(8,128)S(1)}) custom-call(bf16[128,2048]{1,0:T(8,128)(2,1)S(1)} %shard_map.60.refs_0_, bf16[128,2048]{1,0:T(8,128)(2,1)S(1)} %get-tuple-element.33.refs_0_.refs_1_.refs_2_, bf16[128,2048]{1,0:T(8,128)(2,1)S(1)} %collective-permute-done.refs_0_.refs_1_.refs_2_, ...), custom_call_target="tpu_custom_call" | custom-call | flops 16000000000 | bytes 1048576 | tf_op jit(solution)/shard_map/pallas_call | solution.py:250
  31.8 2.8 %collective-permute-start.11 = (bf16[128,768]{1,0:T(8,128)(2,1)S(1)}, bf16[128,768]{1,0:T(8,128)(2,1)S(1)}, u32[]{:S(2)}, u32[]{:S(2)}) collective-permute-start(bf16[128,768]{1,0:T(8,128)(2,1)S(1)} %get-tuple-element.45), channel_id=1, source_target_pairs={{0,24},{4,28},{8,16},{12,20},{16,8},{20,12},{24,0},{28,4},{1,25},{... | collective-permute-start | bytes 589832 | tf_op jit(solution)/shard_map/ppermute | solution.py:24
  34.6 0.7 %shard_map.62 = (bf16[128,256]{1,0:T(8,128)(2,1)S(1)}, bf16[128,256]{1,0:T(8,128)(2,1)S(1)}, bf16[128,128]{1,0:T(8,128)(2,1)S(1)}, f32[128,128]{1,0:T(8,128)S(1)}) custom-call(bf16[128,2048]{1,0:T(8,128)(2,1)S(1)} %shard_map.60.refs_0_, bf16[128,2048]{1,0:T(8,128)(2,1)S(1)} %collective-permute-done.8.refs_1_, ...), custom_call_target="tpu_custom_call" | custom-call | flops 5000000000 | bytes 1048576 | tf_op jit(solution)/shard_map/pallas_call | solution.py:278
  35.3 0.8 %collective-permute-start.12 = (bf16[128,128]{1,0:T(8,128)(2,1)S(1)}, bf16[128,128]{1,0:T(8,128)(2,1)S(1)}, u32[]{:S(2)}, u32[]{:S(2)}) collective-permute-start(bf16[128,128]{1,0:T(8,128)(2,1)S(1)} %get-tuple-element.46), channel_id=1, source_target_pairs={{0,24},{4,28},{8,16},{12,20},{16,8},{20,12},{24,0},{28,4},{1,25},{... | collective-permute-start | bytes 98312 | tf_op jit(solution)/shard_map/ppermute | solution.py:24
  36.1 1.2 %collective-permute-start.13 = (bf16[128,256]{1,0:T(8,128)(2,1)S(1)}, bf16[128,256]{1,0:T(8,128)(2,1)S(1)}, u32[]{:S(2)}, u32[]{:S(2)}) collective-permute-start(bf16[128,256]{1,0:T(8,128)(2,1)S(1)} %get-tuple-element.47), channel_id=1, source_target_pairs={{0,8},{4,12},{8,0},{12,4},{16,24},{20,28},{24,16},{28,20},{1,9},{5... | collective-permute-start | bytes 196616 | tf_op jit(solution)/shard_map/ppermute | solution.py:24
  37.3 1.6 %collective-permute-start.14 = (bf16[128,256]{1,0:T(8,128)(2,1)S(1)}, bf16[128,256]{1,0:T(8,128)(2,1)S(1)}, u32[]{:S(2)}, u32[]{:S(2)}) collective-permute-start(bf16[128,256]{1,0:T(8,128)(2,1)S(1)} %get-tuple-element.48), channel_id=1, source_target_pairs={{0,16},{4,20},{8,24},{12,28},{16,0},{20,4},{24,8},{28,12},{1,17},{... | collective-permute-start | bytes 196616 | tf_op jit(solution)/shard_map/ppermute | solution.py:24
  39.0 1.6 %collective-permute-done.11.refs_0_ = bf16[128,768]{1,0:T(8,128)(2,1)S(1)} collective-permute-done((bf16[128,768]{1,0:T(8,128)(2,1)S(1)}, bf16[128,768]{1,0:T(8,128)(2,1)S(1)}, u32[]{:S(2)}, u32[]{:S(2)}) %collective-permute-start.11) | collective-permute-done | bytes 196640 | tf_op jit(solution)/shard_map/ppermute | solution.py:24
  40.6 0.6 collective-permute-done.12.refs_1_
  41.2 1.3 %collective-permute-done.13.refs_2_ = bf16[128,256]{1,0:T(8,128)(2,1)S(1)} collective-permute-done((bf16[128,256]{1,0:T(8,128)(2,1)S(1)}, bf16[128,256]{1,0:T(8,128)(2,1)S(1)}, u32[]{:S(2)}, u32[]{:S(2)}) %collective-permute-start.13) | collective-permute-done | bytes 65568 | tf_op jit(solution)/shard_map/ppermute | solution.py:24
  42.6 2.7 %collective-permute-start.15 = (bf16[32,1024]{1,0:T(8,128)(2,1)S(1)}, bf16[32,1024]{1,0:T(8,128)(2,1)S(1)}, u32[]{:S(2)}, u32[]{:S(2)}) collective-permute-start(bf16[32,1024]{1,0:T(8,128)(2,1)S(1)} %get-tuple-element.49), channel_id=1, source_target_pairs={{0,2},{1,3},{2,0},{3,1},{4,6},{5,7},{6,4},{7,5},{8,10},{9,11},{10,... | collective-permute-start | bytes 196616 | tf_op jit(solution)/shard_map/ppermute | solution.py:24
  45.2 1.3 %collective-permute-start.16 = (bf16[32,1024]{1,0:T(8,128)(2,1)S(1)}, bf16[32,1024]{1,0:T(8,128)(2,1)S(1)}, u32[]{:S(2)}, u32[]{:S(2)}) collective-permute-start(bf16[32,1024]{1,0:T(8,128)(2,1)S(1)} %get-tuple-element.50), channel_id=1, source_target_pairs={{0,3},{1,2},{2,1},{3,0},{4,7},{5,6},{6,5},{7,4},{8,11},{9,10},{10,... | collective-permute-start | bytes 196616 | tf_op jit(solution)/shard_map/ppermute | solution.py:24
  46.8 3.4 %collective-permute-done.15.refs_0_ = bf16[32,1024]{1,0:T(8,128)(2,1)S(1)} collective-permute-done((bf16[32,1024]{1,0:T(8,128)(2,1)S(1)}, bf16[32,1024]{1,0:T(8,128)(2,1)S(1)}, u32[]{:S(2)}, u32[]{:S(2)}) %collective-permute-start.15) | collective-permute-done | bytes 65568 | tf_op jit(solution)/shard_map/ppermute | solution.py:24
  50.2 1.3 %collective-permute-done.16.refs_1_ = bf16[32,1024]{1,0:T(8,128)(2,1)S(1)} collective-permute-done((bf16[32,1024]{1,0:T(8,128)(2,1)S(1)}, bf16[32,1024]{1,0:T(8,128)(2,1)S(1)}, u32[]{:S(2)}, u32[]{:S(2)}) %collective-permute-start.16) | collective-permute-done | bytes 65568 | tf_op jit(solution)/shard_map/ppermute | solution.py:24
  52.0 1.2 %collective-permute-done.18 = bf16[4,3,32,128]{3,2,1,0:T(8,128)(2,1)S(1)} collective-permute-done((bf16[4,3,32,128]{3,2,1,0:T(8,128)(2,1)S(1)}, bf16[4,3,32,128]{3,2,1,0:T(8,128)(2,1)S(1)}, u32[]{:S(2)}, u32[]{:S(2)}) %collective-permute-start.18) | collective-permute-done | bytes 98336 | tf_op jit(solution)/shard_map/ppermute | solution.py:24
  53.2 1.6 %collective-permute-start.21 = (bf16[2,3,32,128]{3,2,1,0:T(8,128)(2,1)S(1)}, bf16[2,3,32,128]{3,2,1,0:T(8,128)(2,1)S(1)}, u32[]{:S(2)}, u32[]{:S(2)}) collective-permute-start(bf16[2,3,32,128]{3,2,1,0:T(8,128)(2,1)S(1)} %get-tuple-element.59), channel_id=1, source_target_pairs={{0,16},{4,20},{8,24},{12,28},{16,0},{20,4},{24,8},{28,12},{1,17},{... | collective-permute-start | bytes 147464 | tf_op jit(solution)/shard_map/ppermute | solution.py:24
  54.8 1.4 %collective-permute-start.19 = (bf16[2,3,32,128]{3,2,1,0:T(8,128)(2,1)S(1)}, bf16[2,3,32,128]{3,2,1,0:T(8,128)(2,1)S(1)}, u32[]{:S(2)}, u32[]{:S(2)}) collective-permute-start(bf16[2,3,32,128]{3,2,1,0:T(8,128)(2,1)S(1)} %get-tuple-element.60), channel_id=1, source_target_pairs={{0,24},{4,28},{8,16},{12,20},{16,8},{20,12},{24,0},{28,4},{1,25},{... | collective-permute-start | bytes 147464 | tf_op jit(solution)/shard_map/ppermute | solution.py:24
  56.2 0.6 collective-permute-start.20
  56.8 0.6 collective-permute-done.21.refs_2_
  57.4 2.7 %collective-permute-done.19.refs_0_ = bf16[2,3,32,128]{3,2,1,0:T(8,128)(2,1)S(1)} collective-permute-done((bf16[2,3,32,128]{3,2,1,0:T(8,128)(2,1)S(1)}, bf16[2,3,32,128]{3,2,1,0:T(8,128)(2,1)S(1)}, u32[]{:S(2)}, u32[]{:S(2)}) %collective-permute-start.19) | collective-permute-done | bytes 49184 | tf_op jit(solution)/shard_map/ppermute | solution.py:24
  60.3 0.8 %shard_map.67 = f32[8,3,32,128]{3,2,1,0:T(8,128)} custom-call(f32[3,32,128]{2,1,0:T(8,128)S(1)} %bitcast.25, bf16[3,32,128]{2,1,0:T(8,128)(2,1)S(1)} %slice_bitcast_fusion.1.beside_ref, bf16[2,3,32,128]{3,2,1,0:T(8,128)(2,1)S(1)} %collective-permute-done.19.refs_0_, bf16[2,3,32,128]{3,2,1,0:T(8,128)(2,1)S(1)} %collective-permute-done.20.refs_1_, ...), custom_call_target="tpu_custom_call" | custom-call | tf_op jit(solution)/shard_map/pallas_call | solution.py:410
  (46 shorter events, 5.2 us)
Async XLA Ops:
  2.3 15.2 %collective-permute-start.3 = (bf16[128,2048]{1,0:T(8,128)(2,1)}, bf16[128,2048]{1,0:T(8,128)(2,1)}, u32[]{:S(2)}, u32[]{:S(2)}) collective-permute-start(bf16[128,2048]{1,0:T(8,128)(2,1)} %get-tuple-element.57), channel_id=1, source_target_pairs={{0,16},{4,20},{8,24},{12,28},{16,0},{20,4},{24,8},{28,12},{1,17},{... | collective-permute-start | bytes 1572872 | tf_op jit(solution)/shard_map/ppermute | solution.py:24
  5.3 15.2 %collective-permute-start.2 = (bf16[128,2048]{1,0:T(8,128)(2,1)}, bf16[128,2048]{1,0:T(8,128)(2,1)}, u32[]{:S(2)}, u32[]{:S(2)}) collective-permute-start(bf16[128,2048]{1,0:T(8,128)(2,1)} %get-tuple-element.58), channel_id=1, source_target_pairs={{0,8},{4,12},{8,0},{12,4},{16,24},{20,28},{24,16},{28,20},{1,9},{5... | collective-permute-start | bytes 1572872 | tf_op jit(solution)/shard_map/ppermute | solution.py:24
  6.8 2.6 %copy-start.1 = (s32[14,1]{0,1:T(1,128)S(1)}, s32[14,1]{0,1:T(1,128)}, u32[]{:S(2)}) copy-start(s32[14,1]{0,1:T(1,128)} %param.8) | copy-start | bytes 172
  6.8 2.9 %copy-start.2 = (s32[14,2]{0,1:T(2,128)S(1)}, s32[14,2]{0,1:T(2,128)}, u32[]{:S(2)}) copy-start(s32[14,2]{0,1:T(2,128)} %param.7) | copy-start | bytes 340
  9.3 2.0 %collective-permute-start = (bf16[128,2048]{1,0:T(8,128)(2,1)S(1)}, bf16[128,2048]{1,0:T(8,128)(2,1)S(1)}, u32[]{:S(2)}, u32[]{:S(2)}) collective-permute-start(bf16[128,2048]{1,0:T(8,128)(2,1)S(1)} %get-tuple-element.33.refs_0_.refs_1_.refs_2_), channel_id=1, source_target_pairs={{0,4},{4,0},{8,12},{12,8},{16,20},{20,16},{24,28},{28,24},{1,5},{5... | collective-permute-start | bytes 1572872 | tf_op jit(solution)/shard_map/ppermute | solution.py:24
  12.9 11.1 %copy-start = (s32[14,1]{0,1:T(1,128)S(1)}, s32[14,1]{0,1:T(1,128)}, u32[]{:S(2)}) copy-start(s32[14,1]{0,1:T(1,128)} %param.9) | copy-start | bytes 172
  12.9 16.9 %collective-permute-start.1 = (bf16[128,2048]{1,0:T(8,128)(2,1)S(1)}, bf16[128,2048]{1,0:T(8,128)(2,1)S(1)}, u32[]{:S(2)}, u32[]{:S(2)}) collective-permute-start(bf16[128,2048]{1,0:T(8,128)(2,1)S(1)} %get-tuple-element.34), channel_id=1, source_target_pairs={{0,24},{4,28},{8,16},{12,20},{16,8},{20,12},{24,0},{28,4},{1,25},{... | collective-permute-start | bytes 1572872 | tf_op jit(solution)/shard_map/ppermute | solution.py:24
  22.9 1.8 %collective-permute-start.4 = (bf16[256,512]{1,0:T(8,128)(2,1)S(1)}, bf16[256,512]{1,0:T(8,128)(2,1)S(1)}, u32[]{:S(2)}, u32[]{:S(2)}) collective-permute-start(bf16[256,512]{1,0:T(8,128)(2,1)S(1)} %get-tuple-element.36.refs_2_.refs_3_), channel_id=1, source_target_pairs={{0,4},{4,0},{8,12},{12,8},{16,20},{20,16},{24,28},{28,24},{1,5},{5... | collective-permute-start | bytes 786440 | tf_op jit(solution)/shard_map/ppermute | solution.py:24
  23.0 1.9 %collective-permute-start.5 = (bf16[256,512]{1,0:T(8,128)(2,1)S(1)}, bf16[256,512]{1,0:T(8,128)(2,1)S(1)}, u32[]{:S(2)}, u32[]{:S(2)}) collective-permute-start(bf16[256,512]{1,0:T(8,128)(2,1)S(1)} %get-tuple-element.37.refs_3_.refs_4_), channel_id=1, source_target_pairs={{0,4},{4,0},{8,12},{12,8},{16,20},{20,16},{24,28},{28,24},{1,5},{5... | collective-permute-start | bytes 786440 | tf_op jit(solution)/shard_map/ppermute | solution.py:24
  23.5 1.8 %collective-permute-start.6 = (bf16[256,512]{1,0:T(8,128)(2,1)S(1)}, bf16[256,512]{1,0:T(8,128)(2,1)S(1)}, u32[]{:S(2)}, u32[]{:S(2)}) collective-permute-start(bf16[256,512]{1,0:T(8,128)(2,1)S(1)} %get-tuple-element.38.refs_4_.refs_5_), channel_id=1, source_target_pairs={{0,4},{4,0},{8,12},{12,8},{16,20},{20,16},{24,28},{28,24},{1,5},{5... | collective-permute-start | bytes 786440 | tf_op jit(solution)/shard_map/ppermute | solution.py:24
  23.6 2.1 %collective-permute-start.7 = (bf16[256,512]{1,0:T(8,128)(2,1)S(1)}, bf16[256,512]{1,0:T(8,128)(2,1)S(1)}, u32[]{:S(2)}, u32[]{:S(2)}) collective-permute-start(bf16[256,512]{1,0:T(8,128)(2,1)S(1)} %get-tuple-element.39.refs_5_.refs_6_), channel_id=1, source_target_pairs={{0,4},{4,0},{8,12},{12,8},{16,20},{20,16},{24,28},{28,24},{1,5},{5... | collective-permute-start | bytes 786440 | tf_op jit(solution)/shard_map/ppermute | solution.py:24
  27.4 9.9 %collective-permute-start.9 = (bf16[128,640]{1,0:T(8,128)(2,1)S(1)}, bf16[128,640]{1,0:T(8,128)(2,1)S(1)}, u32[]{:S(2)}, u32[]{:S(2)}) collective-permute-start(bf16[128,640]{1,0:T(8,128)(2,1)S(1)} %get-tuple-element.43), channel_id=1, source_target_pairs={{0,8},{4,12},{8,0},{12,4},{16,24},{20,28},{24,16},{28,20},{1,9},{5... | collective-permute-start | bytes 491528 | tf_op jit(solution)/shard_map/ppermute | solution.py:24
  28.9 10.0 %collective-permute-start.10 = (bf16[128,640]{1,0:T(8,128)(2,1)S(1)}, bf16[128,640]{1,0:T(8,128)(2,1)S(1)}, u32[]{:S(2)}, u32[]{:S(2)}) collective-permute-start(bf16[128,640]{1,0:T(8,128)(2,1)S(1)} %get-tuple-element.44), channel_id=1, source_target_pairs={{0,16},{4,20},{8,24},{12,28},{16,0},{20,4},{24,8},{28,12},{1,17},{... | collective-permute-start | bytes 491528 | tf_op jit(solution)/shard_map/ppermute | solution.py:24
  30.6 4.0 %collective-permute-start.8 = (bf16[128,2048]{1,0:T(8,128)(2,1)S(1)}, bf16[128,2048]{1,0:T(8,128)(2,1)S(1)}, u32[]{:S(2)}, u32[]{:S(2)}) collective-permute-start(bf16[128,2048]{1,0:T(8,128)(2,1)S(1)} %shard_map.60.refs_0_), channel_id=1, source_target_pairs={{0,4},{4,0},{8,12},{12,8},{16,20},{20,16},{24,28},{28,24},{1,5},{5... | collective-permute-start | bytes 1572872 | tf_op jit(solution)/shard_map/ppermute | solution.py:24
  31.8 8.7 %collective-permute-start.11 = (bf16[128,768]{1,0:T(8,128)(2,1)S(1)}, bf16[128,768]{1,0:T(8,128)(2,1)S(1)}, u32[]{:S(2)}, u32[]{:S(2)}) collective-permute-start(bf16[128,768]{1,0:T(8,128)(2,1)S(1)} %get-tuple-element.45), channel_id=1, source_target_pairs={{0,24},{4,28},{8,16},{12,20},{16,8},{20,12},{24,0},{28,4},{1,25},{... | collective-permute-start | bytes 589832 | tf_op jit(solution)/shard_map/ppermute | solution.py:24
  35.3 5.8 %collective-permute-start.12 = (bf16[128,128]{1,0:T(8,128)(2,1)S(1)}, bf16[128,128]{1,0:T(8,128)(2,1)S(1)}, u32[]{:S(2)}, u32[]{:S(2)}) collective-permute-start(bf16[128,128]{1,0:T(8,128)(2,1)S(1)} %get-tuple-element.46), channel_id=1, source_target_pairs={{0,24},{4,28},{8,16},{12,20},{16,8},{20,12},{24,0},{28,4},{1,25},{... | collective-permute-start | bytes 98312 | tf_op jit(solution)/shard_map/ppermute | solution.py:24
  36.1 6.3 %collective-permute-start.13 = (bf16[128,256]{1,0:T(8,128)(2,1)S(1)}, bf16[128,256]{1,0:T(8,128)(2,1)S(1)}, u32[]{:S(2)}, u32[]{:S(2)}) collective-permute-start(bf16[128,256]{1,0:T(8,128)(2,1)S(1)} %get-tuple-element.47), channel_id=1, source_target_pairs={{0,8},{4,12},{8,0},{12,4},{16,24},{20,28},{24,16},{28,20},{1,9},{5... | collective-permute-start | bytes 196616 | tf_op jit(solution)/shard_map/ppermute | solution.py:24
  37.3 5.2 %collective-permute-start.14 = (bf16[128,256]{1,0:T(8,128)(2,1)S(1)}, bf16[128,256]{1,0:T(8,128)(2,1)S(1)}, u32[]{:S(2)}, u32[]{:S(2)}) collective-permute-start(bf16[128,256]{1,0:T(8,128)(2,1)S(1)} %get-tuple-element.48), channel_id=1, source_target_pairs={{0,16},{4,20},{8,24},{12,28},{16,0},{20,4},{24,8},{28,12},{1,17},{... | collective-permute-start | bytes 196616 | tf_op jit(solution)/shard_map/ppermute | solution.py:24
  42.6 7.7 %collective-permute-start.15 = (bf16[32,1024]{1,0:T(8,128)(2,1)S(1)}, bf16[32,1024]{1,0:T(8,128)(2,1)S(1)}, u32[]{:S(2)}, u32[]{:S(2)}) collective-permute-start(bf16[32,1024]{1,0:T(8,128)(2,1)S(1)} %get-tuple-element.49), channel_id=1, source_target_pairs={{0,2},{1,3},{2,0},{3,1},{4,6},{5,7},{6,4},{7,5},{8,10},{9,11},{10,... | collective-permute-start | bytes 196616 | tf_op jit(solution)/shard_map/ppermute | solution.py:24
  45.2 6.3 %collective-permute-start.16 = (bf16[32,1024]{1,0:T(8,128)(2,1)S(1)}, bf16[32,1024]{1,0:T(8,128)(2,1)S(1)}, u32[]{:S(2)}, u32[]{:S(2)}) collective-permute-start(bf16[32,1024]{1,0:T(8,128)(2,1)S(1)} %get-tuple-element.50), channel_id=1, source_target_pairs={{0,3},{1,2},{2,1},{3,0},{4,7},{5,6},{6,5},{7,4},{8,11},{9,10},{10,... | collective-permute-start | bytes 196616 | tf_op jit(solution)/shard_map/ppermute | solution.py:24
  46.6 5.2 %collective-permute-start.17 = (bf16[32,1024]{1,0:T(8,128)(2,1)S(1)}, bf16[32,1024]{1,0:T(8,128)(2,1)S(1)}, u32[]{:S(2)}, u32[]{:S(2)}) collective-permute-start(bf16[32,1024]{1,0:T(8,128)(2,1)S(1)} %get-tuple-element.51), channel_id=1, source_target_pairs={{0,1},{1,0},{2,3},{3,2},{4,5},{5,4},{6,7},{7,6},{8,9},{9,8},{10,11... | collective-permute-start | bytes 196616 | tf_op jit(solution)/shard_map/ppermute | solution.py:24
  51.8 1.4 %collective-permute-start.18 = (bf16[4,3,32,128]{3,2,1,0:T(8,128)(2,1)S(1)}, bf16[4,3,32,128]{3,2,1,0:T(8,128)(2,1)S(1)}, u32[]{:S(2)}, u32[]{:S(2)}) collective-permute-start(bf16[4,3,32,128]{3,2,1,0:T(8,128)(2,1)S(1)} %shard_map.66), channel_id=1, source_target_pairs={{0,4},{4,0},{8,12},{12,8},{16,20},{20,16},{24,28},{28,24},{1,5},{5... | collective-permute-start | bytes 294920 | tf_op jit(solution)/shard_map/ppermute | solution.py:24
  53.2 4.2 %collective-permute-start.21 = (bf16[2,3,32,128]{3,2,1,0:T(8,128)(2,1)S(1)}, bf16[2,3,32,128]{3,2,1,0:T(8,128)(2,1)S(1)}, u32[]{:S(2)}, u32[]{:S(2)}) collective-permute-start(bf16[2,3,32,128]{3,2,1,0:T(8,128)(2,1)S(1)} %get-tuple-element.59), channel_id=1, source_target_pairs={{0,16},{4,20},{8,24},{12,28},{16,0},{20,4},{24,8},{28,12},{1,17},{... | collective-permute-start | bytes 147464 | tf_op jit(solution)/shard_map/ppermute | solution.py:24
  54.8 5.3 %collective-permute-start.19 = (bf16[2,3,32,128]{3,2,1,0:T(8,128)(2,1)S(1)}, bf16[2,3,32,128]{3,2,1,0:T(8,128)(2,1)S(1)}, u32[]{:S(2)}, u32[]{:S(2)}) collective-permute-start(bf16[2,3,32,128]{3,2,1,0:T(8,128)(2,1)S(1)} %get-tuple-element.60), channel_id=1, source_target_pairs={{0,24},{4,28},{8,16},{12,20},{16,8},{20,12},{24,0},{28,4},{1,25},{... | collective-permute-start | bytes 147464 | tf_op jit(solution)/shard_map/ppermute | solution.py:24
  56.2 4.1 %collective-permute-start.20 = (bf16[2,3,32,128]{3,2,1,0:T(8,128)(2,1)S(1)}, bf16[2,3,32,128]{3,2,1,0:T(8,128)(2,1)S(1)}, u32[]{:S(2)}, u32[]{:S(2)}) collective-permute-start(bf16[2,3,32,128]{3,2,1,0:T(8,128)(2,1)S(1)} %get-tuple-element.61), channel_id=1, source_target_pairs={{0,8},{4,12},{8,0},{12,4},{16,24},{20,28},{24,16},{28,20},{1,9},{5... | collective-permute-start | bytes 147464 | tf_op jit(solution)/shard_map/ppermute | solution.py:24

commit v8 on v7

--- a/solution.py
+++ b/solution.py
@@ -322,11 +322,11 @@
     my_group = lax.axis_index("grp")
     (last_came, corner, *came), strips = refs[:-groups], refs[-groups:]
     final = len(came) + 1
-    share = strips[0].shape[0]
+    share = own_ref.shape[0] // groups
     span = own_ref.shape[1]
     for distance, strip in enumerate(strips):
         rows = pl.ds(pl.multiple_of((my_group ^ distance) * share, share), share)
-        strip[:, span:] = weights_ref[...].astype(strip.dtype)
+        strip[span // TILE * share :, :] = weights_ref[...].astype(strip.dtype)
         for number in range(span // TILE):
             total = own_ref[rows, spot(number)]
             block = (number + 1) ^ (CORES * final)
@@ -338,17 +338,17 @@
                 core = ((number + 1) ^ (CORES * (at + 1))) - CORES * final
                 if core in range(CORES):
                     total = total + ref[rows, spot(core)].astype(jnp.float32)
-            strip[:, spot(number)] = total.astype(strip.dtype)
+            strip[number * share : (number + 1) * share, :] = total.astype(strip.dtype)
 
 
 def strips(own, came, groups, weights):
     rows, span = own.shape
     share = rows // groups
-    whole = span + weights.shape[1]
+    whole = span // TILE * share + weights.shape[0]
     return kernel_call(
         functools.partial(strips_kernel, groups),
         [VMEM] * (2 + len(came)),
-        [shaped((share, whole), jnp.bfloat16 if at else jnp.float32) for at in range(groups)],
+        [shaped((whole, TILE), jnp.bfloat16 if at else jnp.float32) for at in range(groups)],
         [VMEM] * groups,
         8,
     )(weights, own, *came)
@@ -357,22 +357,19 @@
 def combine_kernel(owners, span, block_ref, *refs):
     chunks, outs = refs[: -len(owners)], refs[-len(owners) :]
     slots, share = outs[0].shape[1:3]
-    weights = [chunk[:, span:].astype(jnp.float32) for chunk in chunks]
+    weights = [chunk[span // TILE * share :, :].astype(jnp.float32) for chunk in chunks]
     for out_ref, held in zip(outs, owners, strict=True):
         for number, owner in enumerate(held):
             for slot in range(slots):
                 at = owner * slots + slot
-                start = pl.multiple_of(block_ref[at] * TILE, TILE)
-                row, lanes = at % share, at // share * TILE
+                rows = pl.ds(pl.multiple_of(block_ref[at] * share, share), share)
                 total = jnp.zeros((share, TILE), jnp.float32)
                 for chunk, weight in zip(chunks, weights, strict=True):
-                    scale = weight[row : row + 1, lanes : lanes + TILE]
-                    total = total + scale * chunk[:, pl.ds(start, TILE)].astype(jnp.float32)
+                    total = total + weight[:1, at : at + 1] * chunk[rows, :].astype(jnp.float32)
                 out_ref[number, slot] = total.astype(out_ref.dtype)
 
 
-def combine(owners, blocks, chunks, span, slots):
-    share = chunks[0].shape[0]
+def combine(owners, blocks, chunks, span, share, slots):
     return kernel_call(
         functools.partial(combine_kernel, owners, span),
         [SMEM] + [VMEM] * len(chunks),
@@ -454,9 +451,7 @@
     taken = (places[None, :] == jnp.arange(cycle * capacity)[:, None]).astype(jnp.int32)
     blocks = scalars(jnp.maximum(jnp.sum(taken * (pairs[:, 1] ^ mine)[None, :], axis=1) - 1, 0))
     weights = jnp.sum(taken * own_mask[None, :], axis=1).astype(jnp.float32)
-    tall = -(-weights.shape[0] // share) * share
-    weights = jnp.pad(weights, (0, tall - weights.shape[0])).reshape(-1, share).T
-    weights = jnp.repeat(weights, TILE, axis=1)
+    weights = jnp.pad(weights[None], ((0, 15), (0, TILE - weights.shape[0])))
 
     others = fit(arrived, metric, 4)
     others_beside = beside(others)
@@ -476,10 +471,10 @@
 
     chunks = [*chunks[2:], chunks[1], chunks[0]]
     span = own_slab.shape[1]
-    (crossing,) = combine([range(1, cycle, CORES)], blocks, chunks, span, capacity)
+    (crossing,) = combine([range(1, cycle, CORES)], blocks, chunks, span, share, capacity)
     crossed = swapped(crossing, "blk", 1)
     own_owners = [range(1), range(CORES, cycle, CORES)]
-    home, straight = combine(own_owners, blocks, chunks, span, capacity)
+    home, straight = combine(own_owners, blocks, chunks, span, share, capacity)
     paired = jnp.stack([straight, crossed[1:]], axis=1)
     order = (final, *range(1, final))
     received = [swapped(paired[chip - 1], "blk", CORES * chip) for chip in order]

time: 61.3 us -> 61.2 us (level)
  no operation moved by 1% of the time
where the time goes in v8:
time: 61.2 us; the launch traced here: 60.9 us
  waiting for transfers between devices  23.3 us (38%)
  starting transfers between devices  22 us (36%)
  Pallas kernels  12.7 us (21%)
  local copies, waits for them, and re-layouts  2.33 us (4%)
    ppermute x22, waiting for transfers between devices, swapped(): lax.ppermute(value, axis, [(source, source ^ distance) for source in rang...  23.3 us
    ppermute x22, starting transfers between devices, swapped(): lax.ppermute(value, axis, [(source, source ^ distance) for source in rang...  22 us
    pallas_call x2, Pallas kernels, fit(): kernel_call(functools.partial(fit_kernel, len(panels), pieces), [VMEM] *...  3.22 us
    pallas_call x1, Pallas kernels, first_fit(): kernel_call(first_fit_kernel, [SMEM, HBM, HBM], [kept(metric.shape, metri...  2.55 us
    dynamic_slice x1, local copies, waits for them, and re-layouts, per_device(): lax.dynamic_slice(raw_panels[0], (jnp.int32(0), starts[chip]), (rows, wid...  2.3 us
    pallas_call x1, Pallas kernels, early(): kernel_call(functools.partial(early_kernel, counts), [VMEM] * sum(counts[...  1.73 us
    pallas_call x1, Pallas kernels, cut(): kernel_call(functools.partial(cut_kernel, count), [SMEM, HBM] + [ANY] * l...  1.57 us
  transfers between devices with their start and end apart: 22, of which 17 were waited for; matrix products, arithmetic and copies ran while one was open for 1% of the time, Pallas kernels for 19%

profile of v8, /device:TPU:0, one launch (start us, length us, event | category | flops | bytes accessed | tf_op | source)
XLA Modules:
  0.0 60.9 jit_solution(2178016337041975782)
XLA Ops:
  0.0 2.3 %dynamic-slice_bitcast_fusion = (bf16[128,2048]{1,0:T(8,128)(2,1)}, bf16[128,2048]{1,0:T(8,128)(2,1)}) fusion(bf16[1,128,8192]{2,1,0:T(8,128)(2,1)} %param.5, s32[]{:T(128)S(6)} %select_n.16, s32[]{:T(128)S(6)} %select_n.15), kind=kLoop, calls=%fused_computation | loop fusion | bytes 2097160 | tf_op jit(solution)/shard_map/dynamic_slice | solution.py:434
  2.3 3.0 %collective-permute-start.3 = (bf16[128,2048]{1,0:T(8,128)(2,1)}, bf16[128,2048]{1,0:T(8,128)(2,1)}, u32[]{:S(2)}, u32[]{:S(2)}) collective-permute-start(bf16[128,2048]{1,0:T(8,128)(2,1)} %get-tuple-element.57), channel_id=1, source_target_pairs={{0,16},{4,20},{8,24},{12,28},{16,0},{20,4},{24,8},{28,12},{1,17},{... | collective-permute-start | bytes 1572872 | tf_op jit(solution)/shard_map/ppermute | solution.py:24
  5.3 1.5 %collective-permute-start.2 = (bf16[128,2048]{1,0:T(8,128)(2,1)}, bf16[128,2048]{1,0:T(8,128)(2,1)}, u32[]{:S(2)}, u32[]{:S(2)}) collective-permute-start(bf16[128,2048]{1,0:T(8,128)(2,1)} %get-tuple-element.58), channel_id=1, source_target_pairs={{0,8},{4,12},{8,0},{12,4},{16,24},{20,28},{24,16},{28,20},{1,9},{5... | collective-permute-start | bytes 1572872 | tf_op jit(solution)/shard_map/ppermute | solution.py:24
  6.8 2.5 %shard_map.56 = (bf16[1024,1024]{1,0:T(8,128)(2,1)S(1)}, bf16[128,2048]{1,0:T(8,128)(2,1)S(1)}) custom-call(s32[1]{0:T(128)} %bitcast.6.starts_ref, bf16[128,8192]{1,0:T(8,128)(2,1)} %bitcast.28, bf16[1024,1024]{1,0:T(8,128)(2,1)} %metric_ref.1), custom_call_target="tpu_custom_call" | custom-call | tf_op jit(solution)/shard_map/pallas_call | solution.py:164
  9.7 1.6 %collective-permute-done.refs_0_.refs_1_.refs_2_ = bf16[128,2048]{1,0:T(8,128)(2,1)S(1)} collective-permute-done((bf16[128,2048]{1,0:T(8,128)(2,1)S(1)}, bf16[128,2048]{1,0:T(8,128)(2,1)S(1)}, u32[]{:S(2)}, u32[]{:S(2)}) %collective-permute-start) | collective-permute-done | bytes 524320 | tf_op jit(solution)/shard_map/ppermute | solution.py:24
  11.3 1.6 %shard_map.57 = (bf16[128,2048]{1,0:T(8,128)(2,1)S(1)}, s32[1]{0:T(128)}) custom-call(s32[1]{0:T(128)} %bitcast.4.starts_ref, bf16[128,8192]{1,0:T(8,128)(2,1)} %bitcast.29, bf16[128,2048]{1,0:T(8,128)(2,1)S(1)} %collective-permute-done.refs_0_.refs_1_.refs_2_), custom_call_target="tpu_custom_call" | custom-call | tf_op jit(solution)/shard_map/pallas_call | solution.py:142
  13.1 4.4 %collective-permute-done.3.refs_1_ = bf16[128,2048]{1,0:T(8,128)(2,1)} collective-permute-done((bf16[128,2048]{1,0:T(8,128)(2,1)}, bf16[128,2048]{1,0:T(8,128)(2,1)}, u32[]{:S(2)}, u32[]{:S(2)}) %collective-permute-start.3) | collective-permute-done | bytes 524320 | tf_op jit(solution)/shard_map/ppermute | solution.py:24
  17.5 2.9 %collective-permute-done.2.refs_0_ = bf16[128,2048]{1,0:T(8,128)(2,1)} collective-permute-done((bf16[128,2048]{1,0:T(8,128)(2,1)}, bf16[128,2048]{1,0:T(8,128)(2,1)}, u32[]{:S(2)}, u32[]{:S(2)}) %collective-permute-start.2) | collective-permute-done | bytes 524320 | tf_op jit(solution)/shard_map/ppermute | solution.py:24
  20.4 2.5 %shard_map.58 = (bf16[256,512]{1,0:T(8,128)(2,1)S(1)}, bf16[256,512]{1,0:T(8,128)(2,1)S(1)}, bf16[256,512]{1,0:T(8,128)(2,1)S(1)}, bf16[256,512]{1,0:T(8,128)(2,1)S(1)}) custom-call(bf16[128,2048]{1,0:T(8,128)(2,1)} %collective-permute-done.2.refs_0_, bf16[128,2048]{1,0:T(8,128)(2,1)} %collective-permute-done.3.refs_1_, ...), custom_call_target="tpu_custom_call" | custom-call | tf_op jit(solution)/shard_map/pallas_call | solution.py:105
  24.0 0.6 shard_map.55.refs_2_.block_ref
  25.6 1.7 %shard_map.59 = (f32[128,640]{1,0:T(8,128)S(1)}, bf16[128,640]{1,0:T(8,128)(2,1)S(1)}, bf16[128,640]{1,0:T(8,128)(2,1)S(1)}) custom-call(bf16[128,2048]{1,0:T(8,128)(2,1)S(1)} %get-tuple-element.33.refs_0_.refs_1_.refs_2_, bf16[128,2048]{1,0:T(8,128)(2,1)S(1)} %collective-permute-done.refs_0_.refs_1_.refs_2_, ...), custom_call_target="tpu_custom_call" | custom-call | tf_op jit(solution)/shard_map/pallas_call | solution.py:222
  27.4 1.6 %collective-permute-start.9 = (bf16[128,640]{1,0:T(8,128)(2,1)S(1)}, bf16[128,640]{1,0:T(8,128)(2,1)S(1)}, u32[]{:S(2)}, u32[]{:S(2)}) collective-permute-start(bf16[128,640]{1,0:T(8,128)(2,1)S(1)} %get-tuple-element.43), channel_id=1, source_target_pairs={{0,8},{4,12},{8,0},{12,4},{16,24},{20,28},{24,16},{28,20},{1,9},{5... | collective-permute-start | bytes 491528 | tf_op jit(solution)/shard_map/ppermute | solution.py:24
  29.8 0.7 %shard_map.60.refs_0_ = bf16[128,2048]{1,0:T(8,128)(2,1)S(1)} custom-call(bf16[128,2048]{1,0:T(8,128)(2,1)S(1)} %collective-permute-done.1.refs_0_, bf16[1024,1024]{1,0:T(8,128)(2,1)S(1)} %get-tuple-element.35.refs_2_.refs_1_, s32[24]{0:T(128)S(4)} %shard_map.55.refs_2_.block_ref, f32[16,128]{1,0:T(8,128)S(1)} %pad.4.refs_3_.weights_ref, ...), custom_call_target="tpu_custom_call" | custom-call | tf_op jit(solution)/shard_map/pallas_call | solution.py:105
  30.6 1.1 %shard_map.61 = (bf16[128,768]{1,0:T(8,128)(2,1)S(1)}, f32[128,384]{1,0:T(8,128)S(1)}) custom-call(bf16[128,2048]{1,0:T(8,128)(2,1)S(1)} %shard_map.60.refs_0_, bf16[128,2048]{1,0:T(8,128)(2,1)S(1)} %get-tuple-element.33.refs_0_.refs_1_.refs_2_, bf16[128,2048]{1,0:T(8,128)(2,1)S(1)} %collective-permute-done.refs_0_.refs_1_.refs_2_, ...), custom_call_target="tpu_custom_call" | custom-call | flops 16000000000 | bytes 1048576 | tf_op jit(solution)/shard_map/pallas_call | solution.py:250
  31.8 2.8 %collective-permute-start.11 = (bf16[128,768]{1,0:T(8,128)(2,1)S(1)}, bf16[128,768]{1,0:T(8,128)(2,1)S(1)}, u32[]{:S(2)}, u32[]{:S(2)}) collective-permute-start(bf16[128,768]{1,0:T(8,128)(2,1)S(1)} %get-tuple-element.45), channel_id=1, source_target_pairs={{0,24},{4,28},{8,16},{12,20},{16,8},{20,12},{24,0},{28,4},{1,25},{... | collective-permute-start | bytes 589832 | tf_op jit(solution)/shard_map/ppermute | solution.py:24
  34.6 0.7 %shard_map.62 = (bf16[128,256]{1,0:T(8,128)(2,1)S(1)}, bf16[128,256]{1,0:T(8,128)(2,1)S(1)}, bf16[128,128]{1,0:T(8,128)(2,1)S(1)}, f32[128,128]{1,0:T(8,128)S(1)}) custom-call(bf16[128,2048]{1,0:T(8,128)(2,1)S(1)} %shard_map.60.refs_0_, bf16[128,2048]{1,0:T(8,128)(2,1)S(1)} %collective-permute-done.8.refs_1_, ...), custom_call_target="tpu_custom_call" | custom-call | flops 5000000000 | bytes 1048576 | tf_op jit(solution)/shard_map/pallas_call | solution.py:278
  35.3 0.8 %collective-permute-start.12 = (bf16[128,128]{1,0:T(8,128)(2,1)S(1)}, bf16[128,128]{1,0:T(8,128)(2,1)S(1)}, u32[]{:S(2)}, u32[]{:S(2)}) collective-permute-start(bf16[128,128]{1,0:T(8,128)(2,1)S(1)} %get-tuple-element.46), channel_id=1, source_target_pairs={{0,24},{4,28},{8,16},{12,20},{16,8},{20,12},{24,0},{28,4},{1,25},{... | collective-permute-start | bytes 98312 | tf_op jit(solution)/shard_map/ppermute | solution.py:24
  36.1 1.2 %collective-permute-start.13 = (bf16[128,256]{1,0:T(8,128)(2,1)S(1)}, bf16[128,256]{1,0:T(8,128)(2,1)S(1)}, u32[]{:S(2)}, u32[]{:S(2)}) collective-permute-start(bf16[128,256]{1,0:T(8,128)(2,1)S(1)} %get-tuple-element.47), channel_id=1, source_target_pairs={{0,8},{4,12},{8,0},{12,4},{16,24},{20,28},{24,16},{28,20},{1,9},{5... | collective-permute-start | bytes 196616 | tf_op jit(solution)/shard_map/ppermute | solution.py:24
  37.2 1.6 %collective-permute-start.14 = (bf16[128,256]{1,0:T(8,128)(2,1)S(1)}, bf16[128,256]{1,0:T(8,128)(2,1)S(1)}, u32[]{:S(2)}, u32[]{:S(2)}) collective-permute-start(bf16[128,256]{1,0:T(8,128)(2,1)S(1)} %get-tuple-element.48), channel_id=1, source_target_pairs={{0,16},{4,20},{8,24},{12,28},{16,0},{20,4},{24,8},{28,12},{1,17},{... | collective-permute-start | bytes 196616 | tf_op jit(solution)/shard_map/ppermute | solution.py:24
  38.9 1.5 %collective-permute-done.11.refs_0_ = bf16[128,768]{1,0:T(8,128)(2,1)S(1)} collective-permute-done((bf16[128,768]{1,0:T(8,128)(2,1)S(1)}, bf16[128,768]{1,0:T(8,128)(2,1)S(1)}, u32[]{:S(2)}, u32[]{:S(2)}) %collective-permute-start.11) | collective-permute-done | bytes 196640 | tf_op jit(solution)/shard_map/ppermute | solution.py:24
  40.5 0.6 collective-permute-done.12.refs_1_
  41.1 1.3 %collective-permute-done.13.refs_2_ = bf16[128,256]{1,0:T(8,128)(2,1)S(1)} collective-permute-done((bf16[128,256]{1,0:T(8,128)(2,1)S(1)}, bf16[128,256]{1,0:T(8,128)(2,1)S(1)}, u32[]{:S(2)}, u32[]{:S(2)}) %collective-permute-start.13) | collective-permute-done | bytes 65568 | tf_op jit(solution)/shard_map/ppermute | solution.py:24
  42.5 2.7 %collective-permute-start.15 = (bf16[240,128]{1,0:T(8,128)(2,1)S(1)}, bf16[240,128]{1,0:T(8,128)(2,1)S(1)}, u32[]{:S(2)}, u32[]{:S(2)}) collective-permute-start(bf16[240,128]{1,0:T(8,128)(2,1)S(1)} %get-tuple-element.49), channel_id=1, source_target_pairs={{0,2},{1,3},{2,0},{3,1},{4,6},{5,7},{6,4},{7,5},{8,10},{9,11},{10,... | collective-permute-start | bytes 184328 | tf_op jit(solution)/shard_map/ppermute | solution.py:24
  45.1 1.3 %collective-permute-start.16 = (bf16[240,128]{1,0:T(8,128)(2,1)S(1)}, bf16[240,128]{1,0:T(8,128)(2,1)S(1)}, u32[]{:S(2)}, u32[]{:S(2)}) collective-permute-start(bf16[240,128]{1,0:T(8,128)(2,1)S(1)} %get-tuple-element.50), channel_id=1, source_target_pairs={{0,3},{1,2},{2,1},{3,0},{4,7},{5,6},{6,5},{7,4},{8,11},{9,10},{10,... | collective-permute-start | bytes 184328 | tf_op jit(solution)/shard_map/ppermute | solution.py:24
  46.7 2.5 %collective-permute-done.15.refs_0_ = bf16[240,128]{1,0:T(8,128)(2,1)S(1)} collective-permute-done((bf16[240,128]{1,0:T(8,128)(2,1)S(1)}, bf16[240,128]{1,0:T(8,128)(2,1)S(1)}, u32[]{:S(2)}, u32[]{:S(2)}) %collective-permute-start.15) | collective-permute-done | bytes 61472 | tf_op jit(solution)/shard_map/ppermute | solution.py:24
  49.2 2.1 %collective-permute-done.16.refs_1_ = bf16[240,128]{1,0:T(8,128)(2,1)S(1)} collective-permute-done((bf16[240,128]{1,0:T(8,128)(2,1)S(1)}, bf16[240,128]{1,0:T(8,128)(2,1)S(1)}, u32[]{:S(2)}, u32[]{:S(2)}) %collective-permute-start.16) | collective-permute-done | bytes 61472 | tf_op jit(solution)/shard_map/ppermute | solution.py:24
  51.8 1.1 %collective-permute-done.18 = bf16[4,3,32,128]{3,2,1,0:T(8,128)(2,1)S(1)} collective-permute-done((bf16[4,3,32,128]{3,2,1,0:T(8,128)(2,1)S(1)}, bf16[4,3,32,128]{3,2,1,0:T(8,128)(2,1)S(1)}, u32[]{:S(2)}, u32[]{:S(2)}) %collective-permute-start.18) | collective-permute-done | bytes 98336 | tf_op jit(solution)/shard_map/ppermute | solution.py:24
  53.0 1.6 %collective-permute-start.21 = (bf16[2,3,32,128]{3,2,1,0:T(8,128)(2,1)S(1)}, bf16[2,3,32,128]{3,2,1,0:T(8,128)(2,1)S(1)}, u32[]{:S(2)}, u32[]{:S(2)}) collective-permute-start(bf16[2,3,32,128]{3,2,1,0:T(8,128)(2,1)S(1)} %get-tuple-element.59), channel_id=1, source_target_pairs={{0,16},{4,20},{8,24},{12,28},{16,0},{20,4},{24,8},{28,12},{1,17},{... | collective-permute-start | bytes 147464 | tf_op jit(solution)/shard_map/ppermute | solution.py:24
  54.5 1.6 %collective-permute-start.19 = (bf16[2,3,32,128]{3,2,1,0:T(8,128)(2,1)S(1)}, bf16[2,3,32,128]{3,2,1,0:T(8,128)(2,1)S(1)}, u32[]{:S(2)}, u32[]{:S(2)}) collective-permute-start(bf16[2,3,32,128]{3,2,1,0:T(8,128)(2,1)S(1)} %get-tuple-element.60), channel_id=1, source_target_pairs={{0,24},{4,28},{8,16},{12,20},{16,8},{20,12},{24,0},{28,4},{1,25},{... | collective-permute-start | bytes 147464 | tf_op jit(solution)/shard_map/ppermute | solution.py:24
  56.5 0.6 collective-permute-done.21.refs_2_
  57.1 2.7 %collective-permute-done.19.refs_0_ = bf16[2,3,32,128]{3,2,1,0:T(8,128)(2,1)S(1)} collective-permute-done((bf16[2,3,32,128]{3,2,1,0:T(8,128)(2,1)S(1)}, bf16[2,3,32,128]{3,2,1,0:T(8,128)(2,1)S(1)}, u32[]{:S(2)}, u32[]{:S(2)}) %collective-permute-start.19) | collective-permute-done | bytes 49184 | tf_op jit(solution)/shard_map/ppermute | solution.py:24
  60.2 0.8 %shard_map.67 = f32[8,3,32,128]{3,2,1,0:T(8,128)} custom-call(f32[3,32,128]{2,1,0:T(8,128)S(1)} %bitcast.27, bf16[3,32,128]{2,1,0:T(8,128)(2,1)S(1)} %slice_bitcast_fusion.1.beside_ref, bf16[2,3,32,128]{3,2,1,0:T(8,128)(2,1)S(1)} %collective-permute-done.19.refs_0_, bf16[2,3,32,128]{3,2,1,0:T(8,128)(2,1)S(1)} %collective-permute-done.20.refs_1_, ...), custom_call_target="tpu_custom_call" | custom-call | tf_op jit(solution)/shard_map/pallas_call | solution.py:407
  (45 shorter events, 5.3 us)
Async XLA Ops:
  2.3 15.2 %collective-permute-start.3 = (bf16[128,2048]{1,0:T(8,128)(2,1)}, bf16[128,2048]{1,0:T(8,128)(2,1)}, u32[]{:S(2)}, u32[]{:S(2)}) collective-permute-start(bf16[128,2048]{1,0:T(8,128)(2,1)} %get-tuple-element.57), channel_id=1, source_target_pairs={{0,16},{4,20},{8,24},{12,28},{16,0},{20,4},{24,8},{28,12},{1,17},{... | collective-permute-start | bytes 1572872 | tf_op jit(solution)/shard_map/ppermute | solution.py:24
  5.3 15.2 %collective-permute-start.2 = (bf16[128,2048]{1,0:T(8,128)(2,1)}, bf16[128,2048]{1,0:T(8,128)(2,1)}, u32[]{:S(2)}, u32[]{:S(2)}) collective-permute-start(bf16[128,2048]{1,0:T(8,128)(2,1)} %get-tuple-element.58), channel_id=1, source_target_pairs={{0,8},{4,12},{8,0},{12,4},{16,24},{20,28},{24,16},{28,20},{1,9},{5... | collective-permute-start | bytes 1572872 | tf_op jit(solution)/shard_map/ppermute | solution.py:24
  6.8 2.7 %copy-start.1 = (s32[14,1]{0,1:T(1,128)S(1)}, s32[14,1]{0,1:T(1,128)}, u32[]{:S(2)}) copy-start(s32[14,1]{0,1:T(1,128)} %param.8) | copy-start | bytes 172
  6.8 2.9 %copy-start.2 = (s32[14,2]{0,1:T(2,128)S(1)}, s32[14,2]{0,1:T(2,128)}, u32[]{:S(2)}) copy-start(s32[14,2]{0,1:T(2,128)} %param.7) | copy-start | bytes 340
  9.3 3.6 %copy-start = (s32[14,1]{0,1:T(1,128)S(1)}, s32[14,1]{0,1:T(1,128)}, u32[]{:S(2)}) copy-start(s32[14,1]{0,1:T(1,128)} %param.9) | copy-start | bytes 172
  9.3 2.0 %collective-permute-start = (bf16[128,2048]{1,0:T(8,128)(2,1)S(1)}, bf16[128,2048]{1,0:T(8,128)(2,1)S(1)}, u32[]{:S(2)}, u32[]{:S(2)}) collective-permute-start(bf16[128,2048]{1,0:T(8,128)(2,1)S(1)} %get-tuple-element.33.refs_0_.refs_1_.refs_2_), channel_id=1, source_target_pairs={{0,4},{4,0},{8,12},{12,8},{16,20},{20,16},{24,28},{28,24},{1,5},{5... | collective-permute-start | bytes 1572872 | tf_op jit(solution)/shard_map/ppermute | solution.py:24
  12.9 16.9 %collective-permute-start.1 = (bf16[128,2048]{1,0:T(8,128)(2,1)S(1)}, bf16[128,2048]{1,0:T(8,128)(2,1)S(1)}, u32[]{:S(2)}, u32[]{:S(2)}) collective-permute-start(bf16[128,2048]{1,0:T(8,128)(2,1)S(1)} %get-tuple-element.34), channel_id=1, source_target_pairs={{0,24},{4,28},{8,16},{12,20},{16,8},{20,12},{24,0},{28,4},{1,25},{... | collective-permute-start | bytes 1572872 | tf_op jit(solution)/shard_map/ppermute | solution.py:24
  22.9 1.7 %collective-permute-start.4 = (bf16[256,512]{1,0:T(8,128)(2,1)S(1)}, bf16[256,512]{1,0:T(8,128)(2,1)S(1)}, u32[]{:S(2)}, u32[]{:S(2)}) collective-permute-start(bf16[256,512]{1,0:T(8,128)(2,1)S(1)} %get-tuple-element.36.refs_2_.refs_3_), channel_id=1, source_target_pairs={{0,4},{4,0},{8,12},{12,8},{16,20},{20,16},{24,28},{28,24},{1,5},{5... | collective-permute-start | bytes 786440 | tf_op jit(solution)/shard_map/ppermute | solution.py:24
  23.0 1.9 %collective-permute-start.5 = (bf16[256,512]{1,0:T(8,128)(2,1)S(1)}, bf16[256,512]{1,0:T(8,128)(2,1)S(1)}, u32[]{:S(2)}, u32[]{:S(2)}) collective-permute-start(bf16[256,512]{1,0:T(8,128)(2,1)S(1)} %get-tuple-element.37.refs_3_.refs_4_), channel_id=1, source_target_pairs={{0,4},{4,0},{8,12},{12,8},{16,20},{20,16},{24,28},{28,24},{1,5},{5... | collective-permute-start | bytes 786440 | tf_op jit(solution)/shard_map/ppermute | solution.py:24
  23.5 1.8 %collective-permute-start.6 = (bf16[256,512]{1,0:T(8,128)(2,1)S(1)}, bf16[256,512]{1,0:T(8,128)(2,1)S(1)}, u32[]{:S(2)}, u32[]{:S(2)}) collective-permute-start(bf16[256,512]{1,0:T(8,128)(2,1)S(1)} %get-tuple-element.38.refs_4_.refs_5_), channel_id=1, source_target_pairs={{0,4},{4,0},{8,12},{12,8},{16,20},{20,16},{24,28},{28,24},{1,5},{5... | collective-permute-start | bytes 786440 | tf_op jit(solution)/shard_map/ppermute | solution.py:24
  23.6 2.1 %collective-permute-start.7 = (bf16[256,512]{1,0:T(8,128)(2,1)S(1)}, bf16[256,512]{1,0:T(8,128)(2,1)S(1)}, u32[]{:S(2)}, u32[]{:S(2)}) collective-permute-start(bf16[256,512]{1,0:T(8,128)(2,1)S(1)} %get-tuple-element.39.refs_5_.refs_6_), channel_id=1, source_target_pairs={{0,4},{4,0},{8,12},{12,8},{16,20},{20,16},{24,28},{28,24},{1,5},{5... | collective-permute-start | bytes 786440 | tf_op jit(solution)/shard_map/ppermute | solution.py:24
  27.4 9.9 %collective-permute-start.9 = (bf16[128,640]{1,0:T(8,128)(2,1)S(1)}, bf16[128,640]{1,0:T(8,128)(2,1)S(1)}, u32[]{:S(2)}, u32[]{:S(2)}) collective-permute-start(bf16[128,640]{1,0:T(8,128)(2,1)S(1)} %get-tuple-element.43), channel_id=1, source_target_pairs={{0,8},{4,12},{8,0},{12,4},{16,24},{20,28},{24,16},{28,20},{1,9},{5... | collective-permute-start | bytes 491528 | tf_op jit(solution)/shard_map/ppermute | solution.py:24
  28.9 9.9 %collective-permute-start.10 = (bf16[128,640]{1,0:T(8,128)(2,1)S(1)}, bf16[128,640]{1,0:T(8,128)(2,1)S(1)}, u32[]{:S(2)}, u32[]{:S(2)}) collective-permute-start(bf16[128,640]{1,0:T(8,128)(2,1)S(1)} %get-tuple-element.44), channel_id=1, source_target_pairs={{0,16},{4,20},{8,24},{12,28},{16,0},{20,4},{24,8},{28,12},{1,17},{... | collective-permute-start | bytes 491528 | tf_op jit(solution)/shard_map/ppermute | solution.py:24
  30.6 4.0 %collective-permute-start.8 = (bf16[128,2048]{1,0:T(8,128)(2,1)S(1)}, bf16[128,2048]{1,0:T(8,128)(2,1)S(1)}, u32[]{:S(2)}, u32[]{:S(2)}) collective-permute-start(bf16[128,2048]{1,0:T(8,128)(2,1)S(1)} %shard_map.60.refs_0_), channel_id=1, source_target_pairs={{0,4},{4,0},{8,12},{12,8},{16,20},{20,16},{24,28},{28,24},{1,5},{5... | collective-permute-start | bytes 1572872 | tf_op jit(solution)/shard_map/ppermute | solution.py:24
  31.8 8.7 %collective-permute-start.11 = (bf16[128,768]{1,0:T(8,128)(2,1)S(1)}, bf16[128,768]{1,0:T(8,128)(2,1)S(1)}, u32[]{:S(2)}, u32[]{:S(2)}) collective-permute-start(bf16[128,768]{1,0:T(8,128)(2,1)S(1)} %get-tuple-element.45), channel_id=1, source_target_pairs={{0,24},{4,28},{8,16},{12,20},{16,8},{20,12},{24,0},{28,4},{1,25},{... | collective-permute-start | bytes 589832 | tf_op jit(solution)/shard_map/ppermute | solution.py:24
  35.3 5.8 %collective-permute-start.12 = (bf16[128,128]{1,0:T(8,128)(2,1)S(1)}, bf16[128,128]{1,0:T(8,128)(2,1)S(1)}, u32[]{:S(2)}, u32[]{:S(2)}) collective-permute-start(bf16[128,128]{1,0:T(8,128)(2,1)S(1)} %get-tuple-element.46), channel_id=1, source_target_pairs={{0,24},{4,28},{8,16},{12,20},{16,8},{20,12},{24,0},{28,4},{1,25},{... | collective-permute-start | bytes 98312 | tf_op jit(solution)/shard_map/ppermute | solution.py:24
  36.1 6.3 %collective-permute-start.13 = (bf16[128,256]{1,0:T(8,128)(2,1)S(1)}, bf16[128,256]{1,0:T(8,128)(2,1)S(1)}, u32[]{:S(2)}, u32[]{:S(2)}) collective-permute-start(bf16[128,256]{1,0:T(8,128)(2,1)S(1)} %get-tuple-element.47), channel_id=1, source_target_pairs={{0,8},{4,12},{8,0},{12,4},{16,24},{20,28},{24,16},{28,20},{1,9},{5... | collective-permute-start | bytes 196616 | tf_op jit(solution)/shard_map/ppermute | solution.py:24
  37.2 5.2 %collective-permute-start.14 = (bf16[128,256]{1,0:T(8,128)(2,1)S(1)}, bf16[128,256]{1,0:T(8,128)(2,1)S(1)}, u32[]{:S(2)}, u32[]{:S(2)}) collective-permute-start(bf16[128,256]{1,0:T(8,128)(2,1)S(1)} %get-tuple-element.48), channel_id=1, source_target_pairs={{0,16},{4,20},{8,24},{12,28},{16,0},{20,4},{24,8},{28,12},{1,17},{... | collective-permute-start | bytes 196616 | tf_op jit(solution)/shard_map/ppermute | solution.py:24
  42.5 6.7 %collective-permute-start.15 = (bf16[240,128]{1,0:T(8,128)(2,1)S(1)}, bf16[240,128]{1,0:T(8,128)(2,1)S(1)}, u32[]{:S(2)}, u32[]{:S(2)}) collective-permute-start(bf16[240,128]{1,0:T(8,128)(2,1)S(1)} %get-tuple-element.49), channel_id=1, source_target_pairs={{0,2},{1,3},{2,0},{3,1},{4,6},{5,7},{6,4},{7,5},{8,10},{9,11},{10,... | collective-permute-start | bytes 184328 | tf_op jit(solution)/shard_map/ppermute | solution.py:24
  45.1 6.2 %collective-permute-start.16 = (bf16[240,128]{1,0:T(8,128)(2,1)S(1)}, bf16[240,128]{1,0:T(8,128)(2,1)S(1)}, u32[]{:S(2)}, u32[]{:S(2)}) collective-permute-start(bf16[240,128]{1,0:T(8,128)(2,1)S(1)} %get-tuple-element.50), channel_id=1, source_target_pairs={{0,3},{1,2},{2,1},{3,0},{4,7},{5,6},{6,5},{7,4},{8,11},{9,10},{10,... | collective-permute-start | bytes 184328 | tf_op jit(solution)/shard_map/ppermute | solution.py:24
  46.5 4.9 %collective-permute-start.17 = (bf16[240,128]{1,0:T(8,128)(2,1)S(1)}, bf16[240,128]{1,0:T(8,128)(2,1)S(1)}, u32[]{:S(2)}, u32[]{:S(2)}) collective-permute-start(bf16[240,128]{1,0:T(8,128)(2,1)S(1)} %get-tuple-element.51), channel_id=1, source_target_pairs={{0,1},{1,0},{2,3},{3,2},{4,5},{5,4},{6,7},{7,6},{8,9},{9,8},{10,11... | collective-permute-start | bytes 184328 | tf_op jit(solution)/shard_map/ppermute | solution.py:24
  51.6 1.4 %collective-permute-start.18 = (bf16[4,3,32,128]{3,2,1,0:T(8,128)(2,1)S(1)}, bf16[4,3,32,128]{3,2,1,0:T(8,128)(2,1)S(1)}, u32[]{:S(2)}, u32[]{:S(2)}) collective-permute-start(bf16[4,3,32,128]{3,2,1,0:T(8,128)(2,1)S(1)} %shard_map.66), channel_id=1, source_target_pairs={{0,4},{4,0},{8,12},{12,8},{16,20},{20,16},{24,28},{28,24},{1,5},{5... | collective-permute-start | bytes 294920 | tf_op jit(solution)/shard_map/ppermute | solution.py:24
  53.0 4.2 %collective-permute-start.21 = (bf16[2,3,32,128]{3,2,1,0:T(8,128)(2,1)S(1)}, bf16[2,3,32,128]{3,2,1,0:T(8,128)(2,1)S(1)}, u32[]{:S(2)}, u32[]{:S(2)}) collective-permute-start(bf16[2,3,32,128]{3,2,1,0:T(8,128)(2,1)S(1)} %get-tuple-element.59), channel_id=1, source_target_pairs={{0,16},{4,20},{8,24},{12,28},{16,0},{20,4},{24,8},{28,12},{1,17},{... | collective-permute-start | bytes 147464 | tf_op jit(solution)/shard_map/ppermute | solution.py:24
  54.5 5.2 %collective-permute-start.19 = (bf16[2,3,32,128]{3,2,1,0:T(8,128)(2,1)S(1)}, bf16[2,3,32,128]{3,2,1,0:T(8,128)(2,1)S(1)}, u32[]{:S(2)}, u32[]{:S(2)}) collective-permute-start(bf16[2,3,32,128]{3,2,1,0:T(8,128)(2,1)S(1)} %get-tuple-element.60), channel_id=1, source_target_pairs={{0,24},{4,28},{8,16},{12,20},{16,8},{20,12},{24,0},{28,4},{1,25},{... | collective-permute-start | bytes 147464 | tf_op jit(solution)/shard_map/ppermute | solution.py:24
  56.1 4.1 %collective-permute-start.20 = (bf16[2,3,32,128]{3,2,1,0:T(8,128)(2,1)S(1)}, bf16[2,3,32,128]{3,2,1,0:T(8,128)(2,1)S(1)}, u32[]{:S(2)}, u32[]{:S(2)}) collective-permute-start(bf16[2,3,32,128]{3,2,1,0:T(8,128)(2,1)S(1)} %get-tuple-element.61), channel_id=1, source_target_pairs={{0,8},{4,12},{8,0},{12,4},{16,24},{20,28},{24,16},{28,20},{1,9},{5... | collective-permute-start | bytes 147464 | tf_op jit(solution)/shard_map/ppermute | solution.py:24

commit v9 on v8

--- a/solution.py
+++ b/solution.py
@@ -453,12 +453,12 @@
     weights = jnp.sum(taken * own_mask[None, :], axis=1).astype(jnp.float32)
     weights = jnp.pad(weights[None], ((0, 15), (0, TILE - weights.shape[0])))
 
-    others = fit(arrived, metric, 4)
+    others = fit(arrived, metric, 4, (), (blocks, weights))
     others_beside = beside(others)
     begun = early(own, own_beside, others, others_beside)
     came_early = [swapped(begun[chip], "blk", CORES * chip) for chip in range(1, final)]
 
-    last_fitted = fit([last], metric, 1, (), (blocks, weights, begun[0]))
+    last_fitted = fit([last], metric, 1, (), (begun[0],))
     last_beside = beside(last_fitted)
     last_slab, straight = middle(last_fitted, own, own_beside, others, others_beside)
     *slabs, corner, side = late(last_fitted, last_beside, own, others, straight)

time: 61.2 us -> 61.2 us (level)
  transfers between devices with their start and end apart: 22 -> 22, of which waited for: 17 -> 18; matrix products, arithmetic and copies ran while one was open for 1% -> 1% of each run, Pallas kernels for 19% -> 19%
where the time goes in v9:
time: 61.2 us; the launch traced here: 60.9 us
  waiting for transfers between devices  23.3 us (38%)
  starting transfers between devices  22 us (36%)
  Pallas kernels  12.7 us (21%)
  local copies, waits for them, and re-layouts  2.33 us (4%)
    ppermute x22, waiting for transfers between devices, swapped(): lax.ppermute(value, axis, [(source, source ^ distance) for source in rang...  23.3 us
    ppermute x22, starting transfers between devices, swapped(): lax.ppermute(value, axis, [(source, source ^ distance) for source in rang...  22 us
    pallas_call x2, Pallas kernels, fit(): kernel_call(functools.partial(fit_kernel, len(panels), pieces), [VMEM] *...  3.22 us
    pallas_call x1, Pallas kernels, first_fit(): kernel_call(first_fit_kernel, [SMEM, HBM, HBM], [kept(metric.shape, metri...  2.56 us
    dynamic_slice x1, local copies, waits for them, and re-layouts, per_device(): lax.dynamic_slice(raw_panels[0], (jnp.int32(0), starts[chip]), (rows, wid...  2.3 us
    pallas_call x1, Pallas kernels, early(): kernel_call(functools.partial(early_kernel, counts), [VMEM] * sum(counts[...  1.73 us
    pallas_call x1, Pallas kernels, cut(): kernel_call(functools.partial(cut_kernel, count), [SMEM, HBM] + [ANY] * l...  1.57 us
  transfers between devices with their start and end apart: 22, of which 18 were waited for; matrix products, arithmetic and copies ran while one was open for 1% of the time, Pallas kernels for 19%

profile of v9, /device:TPU:0, one launch (start us, length us, event | category | flops | bytes accessed | tf_op | source)
XLA Modules:
  0.0 60.9 jit_solution(5732814080239841835)
XLA Ops:
  0.0 2.3 %dynamic-slice_bitcast_fusion = (bf16[128,2048]{1,0:T(8,128)(2,1)}, bf16[128,2048]{1,0:T(8,128)(2,1)}) fusion(bf16[1,128,8192]{2,1,0:T(8,128)(2,1)} %param.5, s32[]{:T(128)S(6)} %select_n.16, s32[]{:T(128)S(6)} %select_n.15), kind=kLoop, calls=%fused_computation | loop fusion | bytes 2097160 | tf_op jit(solution)/shard_map/dynamic_slice | solution.py:434
  2.3 3.0 %collective-permute-start.3 = (bf16[128,2048]{1,0:T(8,128)(2,1)}, bf16[128,2048]{1,0:T(8,128)(2,1)}, u32[]{:S(2)}, u32[]{:S(2)}) collective-permute-start(bf16[128,2048]{1,0:T(8,128)(2,1)} %get-tuple-element.57), channel_id=1, source_target_pairs={{0,16},{4,20},{8,24},{12,28},{16,0},{20,4},{24,8},{28,12},{1,17},{... | collective-permute-start | bytes 1572872 | tf_op jit(solution)/shard_map/ppermute | solution.py:24
  5.3 1.5 %collective-permute-start.2 = (bf16[128,2048]{1,0:T(8,128)(2,1)}, bf16[128,2048]{1,0:T(8,128)(2,1)}, u32[]{:S(2)}, u32[]{:S(2)}) collective-permute-start(bf16[128,2048]{1,0:T(8,128)(2,1)} %get-tuple-element.58), channel_id=1, source_target_pairs={{0,8},{4,12},{8,0},{12,4},{16,24},{20,28},{24,16},{28,20},{1,9},{5... | collective-permute-start | bytes 1572872 | tf_op jit(solution)/shard_map/ppermute | solution.py:24
  6.8 2.6 %shard_map.56 = (bf16[1024,1024]{1,0:T(8,128)(2,1)S(1)}, bf16[128,2048]{1,0:T(8,128)(2,1)S(1)}) custom-call(s32[1]{0:T(128)} %bitcast.6.starts_ref, bf16[128,8192]{1,0:T(8,128)(2,1)} %bitcast.28, bf16[1024,1024]{1,0:T(8,128)(2,1)} %metric_ref.1), custom_call_target="tpu_custom_call" | custom-call | tf_op jit(solution)/shard_map/pallas_call | solution.py:164
  9.8 1.5 %collective-permute-done.refs_0_.refs_1_.refs_2_ = bf16[128,2048]{1,0:T(8,128)(2,1)S(1)} collective-permute-done((bf16[128,2048]{1,0:T(8,128)(2,1)S(1)}, bf16[128,2048]{1,0:T(8,128)(2,1)S(1)}, u32[]{:S(2)}, u32[]{:S(2)}) %collective-permute-start) | collective-permute-done | bytes 524320 | tf_op jit(solution)/shard_map/ppermute | solution.py:24
  11.3 1.6 %shard_map.57 = (bf16[128,2048]{1,0:T(8,128)(2,1)S(1)}, s32[1]{0:T(128)}) custom-call(s32[1]{0:T(128)} %bitcast.4.starts_ref, bf16[128,8192]{1,0:T(8,128)(2,1)} %bitcast.29, bf16[128,2048]{1,0:T(8,128)(2,1)S(1)} %collective-permute-done.refs_0_.refs_1_.refs_2_), custom_call_target="tpu_custom_call" | custom-call | tf_op jit(solution)/shard_map/pallas_call | solution.py:142
  13.0 0.6 shard_map.55.refs_3_.block_ref
  13.6 3.9 %collective-permute-done.3.refs_1_ = bf16[128,2048]{1,0:T(8,128)(2,1)} collective-permute-done((bf16[128,2048]{1,0:T(8,128)(2,1)}, bf16[128,2048]{1,0:T(8,128)(2,1)}, u32[]{:S(2)}, u32[]{:S(2)}) %collective-permute-start.3) | collective-permute-done | bytes 524320 | tf_op jit(solution)/shard_map/ppermute | solution.py:24
  17.5 2.9 %collective-permute-done.2.refs_0_ = bf16[128,2048]{1,0:T(8,128)(2,1)} collective-permute-done((bf16[128,2048]{1,0:T(8,128)(2,1)}, bf16[128,2048]{1,0:T(8,128)(2,1)}, u32[]{:S(2)}, u32[]{:S(2)}) %collective-permute-start.2) | collective-permute-done | bytes 524320 | tf_op jit(solution)/shard_map/ppermute | solution.py:24
  20.4 2.5 %shard_map.58 = (bf16[256,512]{1,0:T(8,128)(2,1)S(1)}, bf16[256,512]{1,0:T(8,128)(2,1)S(1)}, bf16[256,512]{1,0:T(8,128)(2,1)S(1)}, bf16[256,512]{1,0:T(8,128)(2,1)S(1)}) custom-call(bf16[128,2048]{1,0:T(8,128)(2,1)} %collective-permute-done.2.refs_0_, bf16[128,2048]{1,0:T(8,128)(2,1)} %collective-permute-done.3.refs_1_, ...), custom_call_target="tpu_custom_call" | custom-call | tf_op jit(solution)/shard_map/pallas_call | solution.py:105
  25.6 1.7 %shard_map.59 = (f32[128,640]{1,0:T(8,128)S(1)}, bf16[128,640]{1,0:T(8,128)(2,1)S(1)}, bf16[128,640]{1,0:T(8,128)(2,1)S(1)}) custom-call(bf16[128,2048]{1,0:T(8,128)(2,1)S(1)} %get-tuple-element.33.refs_0_.refs_1_.refs_2_, bf16[128,2048]{1,0:T(8,128)(2,1)S(1)} %collective-permute-done.refs_0_.refs_1_.refs_2_, ...), custom_call_target="tpu_custom_call" | custom-call | tf_op jit(solution)/shard_map/pallas_call | solution.py:222
  27.4 1.6 %collective-permute-start.9 = (bf16[128,640]{1,0:T(8,128)(2,1)S(1)}, bf16[128,640]{1,0:T(8,128)(2,1)S(1)}, u32[]{:S(2)}, u32[]{:S(2)}) collective-permute-start(bf16[128,640]{1,0:T(8,128)(2,1)S(1)} %get-tuple-element.43), channel_id=1, source_target_pairs={{0,8},{4,12},{8,0},{12,4},{16,24},{20,28},{24,16},{28,20},{1,9},{5... | collective-permute-start | bytes 491528 | tf_op jit(solution)/shard_map/ppermute | solution.py:24
  29.8 0.7 %shard_map.60.refs_0_ = bf16[128,2048]{1,0:T(8,128)(2,1)S(1)} custom-call(bf16[128,2048]{1,0:T(8,128)(2,1)S(1)} %collective-permute-done.1.refs_0_, bf16[1024,1024]{1,0:T(8,128)(2,1)S(1)} %get-tuple-element.35.refs_2_.refs_1_, f32[128,640]{1,0:T(8,128)S(1)} %get-tuple-element.40.refs_2_), custom_call_target="tpu_custom_call" | custom-call | tf_op jit(solution)/shard_map/pallas_call | solution.py:105
  30.6 1.1 %shard_map.61 = (bf16[128,768]{1,0:T(8,128)(2,1)S(1)}, f32[128,384]{1,0:T(8,128)S(1)}) custom-call(bf16[128,2048]{1,0:T(8,128)(2,1)S(1)} %shard_map.60.refs_0_, bf16[128,2048]{1,0:T(8,128)(2,1)S(1)} %get-tuple-element.33.refs_0_.refs_1_.refs_2_, bf16[128,2048]{1,0:T(8,128)(2,1)S(1)} %collective-permute-done.refs_0_.refs_1_.refs_2_, ...), custom_call_target="tpu_custom_call" | custom-call | flops 16000000000 | bytes 1048576 | tf_op jit(solution)/shard_map/pallas_call | solution.py:250
  31.8 2.8 %collective-permute-start.11 = (bf16[128,768]{1,0:T(8,128)(2,1)S(1)}, bf16[128,768]{1,0:T(8,128)(2,1)S(1)}, u32[]{:S(2)}, u32[]{:S(2)}) collective-permute-start(bf16[128,768]{1,0:T(8,128)(2,1)S(1)} %get-tuple-element.45), channel_id=1, source_target_pairs={{0,24},{4,28},{8,16},{12,20},{16,8},{20,12},{24,0},{28,4},{1,25},{... | collective-permute-start | bytes 589832 | tf_op jit(solution)/shard_map/ppermute | solution.py:24
  34.6 0.7 %shard_map.62 = (bf16[128,256]{1,0:T(8,128)(2,1)S(1)}, bf16[128,256]{1,0:T(8,128)(2,1)S(1)}, bf16[128,128]{1,0:T(8,128)(2,1)S(1)}, f32[128,128]{1,0:T(8,128)S(1)}) custom-call(bf16[128,2048]{1,0:T(8,128)(2,1)S(1)} %shard_map.60.refs_0_, bf16[128,2048]{1,0:T(8,128)(2,1)S(1)} %collective-permute-done.8.refs_1_, ...), custom_call_target="tpu_custom_call" | custom-call | flops 5000000000 | bytes 1048576 | tf_op jit(solution)/shard_map/pallas_call | solution.py:278
  35.3 0.8 %collective-permute-start.12 = (bf16[128,128]{1,0:T(8,128)(2,1)S(1)}, bf16[128,128]{1,0:T(8,128)(2,1)S(1)}, u32[]{:S(2)}, u32[]{:S(2)}) collective-permute-start(bf16[128,128]{1,0:T(8,128)(2,1)S(1)} %get-tuple-element.46), channel_id=1, source_target_pairs={{0,24},{4,28},{8,16},{12,20},{16,8},{20,12},{24,0},{28,4},{1,25},{... | collective-permute-start | bytes 98312 | tf_op jit(solution)/shard_map/ppermute | solution.py:24
  36.1 1.2 %collective-permute-start.13 = (bf16[128,256]{1,0:T(8,128)(2,1)S(1)}, bf16[128,256]{1,0:T(8,128)(2,1)S(1)}, u32[]{:S(2)}, u32[]{:S(2)}) collective-permute-start(bf16[128,256]{1,0:T(8,128)(2,1)S(1)} %get-tuple-element.47), channel_id=1, source_target_pairs={{0,8},{4,12},{8,0},{12,4},{16,24},{20,28},{24,16},{28,20},{1,9},{5... | collective-permute-start | bytes 196616 | tf_op jit(solution)/shard_map/ppermute | solution.py:24
  37.2 1.6 %collective-permute-start.14 = (bf16[128,256]{1,0:T(8,128)(2,1)S(1)}, bf16[128,256]{1,0:T(8,128)(2,1)S(1)}, u32[]{:S(2)}, u32[]{:S(2)}) collective-permute-start(bf16[128,256]{1,0:T(8,128)(2,1)S(1)} %get-tuple-element.48), channel_id=1, source_target_pairs={{0,16},{4,20},{8,24},{12,28},{16,0},{20,4},{24,8},{28,12},{1,17},{... | collective-permute-start | bytes 196616 | tf_op jit(solution)/shard_map/ppermute | solution.py:24
  38.9 1.5 %collective-permute-done.11.refs_0_ = bf16[128,768]{1,0:T(8,128)(2,1)S(1)} collective-permute-done((bf16[128,768]{1,0:T(8,128)(2,1)S(1)}, bf16[128,768]{1,0:T(8,128)(2,1)S(1)}, u32[]{:S(2)}, u32[]{:S(2)}) %collective-permute-start.11) | collective-permute-done | bytes 196640 | tf_op jit(solution)/shard_map/ppermute | solution.py:24
  40.5 0.6 collective-permute-done.12.refs_1_
  41.1 1.3 %collective-permute-done.13.refs_2_ = bf16[128,256]{1,0:T(8,128)(2,1)S(1)} collective-permute-done((bf16[128,256]{1,0:T(8,128)(2,1)S(1)}, bf16[128,256]{1,0:T(8,128)(2,1)S(1)}, u32[]{:S(2)}, u32[]{:S(2)}) %collective-permute-start.13) | collective-permute-done | bytes 65568 | tf_op jit(solution)/shard_map/ppermute | solution.py:24
  42.5 2.7 %collective-permute-start.15 = (bf16[240,128]{1,0:T(8,128)(2,1)S(1)}, bf16[240,128]{1,0:T(8,128)(2,1)S(1)}, u32[]{:S(2)}, u32[]{:S(2)}) collective-permute-start(bf16[240,128]{1,0:T(8,128)(2,1)S(1)} %get-tuple-element.49), channel_id=1, source_target_pairs={{0,2},{1,3},{2,0},{3,1},{4,6},{5,7},{6,4},{7,5},{8,10},{9,11},{10,... | collective-permute-start | bytes 184328 | tf_op jit(solution)/shard_map/ppermute | solution.py:24
  45.1 1.3 %collective-permute-start.16 = (bf16[240,128]{1,0:T(8,128)(2,1)S(1)}, bf16[240,128]{1,0:T(8,128)(2,1)S(1)}, u32[]{:S(2)}, u32[]{:S(2)}) collective-permute-start(bf16[240,128]{1,0:T(8,128)(2,1)S(1)} %get-tuple-element.50), channel_id=1, source_target_pairs={{0,3},{1,2},{2,1},{3,0},{4,7},{5,6},{6,5},{7,4},{8,11},{9,10},{10,... | collective-permute-start | bytes 184328 | tf_op jit(solution)/shard_map/ppermute | solution.py:24
  46.7 2.5 %collective-permute-done.15.refs_0_ = bf16[240,128]{1,0:T(8,128)(2,1)S(1)} collective-permute-done((bf16[240,128]{1,0:T(8,128)(2,1)S(1)}, bf16[240,128]{1,0:T(8,128)(2,1)S(1)}, u32[]{:S(2)}, u32[]{:S(2)}) %collective-permute-start.15) | collective-permute-done | bytes 61472 | tf_op jit(solution)/shard_map/ppermute | solution.py:24
  49.2 2.1 %collective-permute-done.16.refs_1_ = bf16[240,128]{1,0:T(8,128)(2,1)S(1)} collective-permute-done((bf16[240,128]{1,0:T(8,128)(2,1)S(1)}, bf16[240,128]{1,0:T(8,128)(2,1)S(1)}, u32[]{:S(2)}, u32[]{:S(2)}) %collective-permute-start.16) | collective-permute-done | bytes 61472 | tf_op jit(solution)/shard_map/ppermute | solution.py:24
  51.8 1.1 %collective-permute-done.18 = bf16[4,3,32,128]{3,2,1,0:T(8,128)(2,1)S(1)} collective-permute-done((bf16[4,3,32,128]{3,2,1,0:T(8,128)(2,1)S(1)}, bf16[4,3,32,128]{3,2,1,0:T(8,128)(2,1)S(1)}, u32[]{:S(2)}, u32[]{:S(2)}) %collective-permute-start.18) | collective-permute-done | bytes 98336 | tf_op jit(solution)/shard_map/ppermute | solution.py:24
  53.0 1.6 %collective-permute-start.21 = (bf16[2,3,32,128]{3,2,1,0:T(8,128)(2,1)S(1)}, bf16[2,3,32,128]{3,2,1,0:T(8,128)(2,1)S(1)}, u32[]{:S(2)}, u32[]{:S(2)}) collective-permute-start(bf16[2,3,32,128]{3,2,1,0:T(8,128)(2,1)S(1)} %get-tuple-element.59), channel_id=1, source_target_pairs={{0,16},{4,20},{8,24},{12,28},{16,0},{20,4},{24,8},{28,12},{1,17},{... | collective-permute-start | bytes 147464 | tf_op jit(solution)/shard_map/ppermute | solution.py:24
  54.5 1.6 %collective-permute-start.19 = (bf16[2,3,32,128]{3,2,1,0:T(8,128)(2,1)S(1)}, bf16[2,3,32,128]{3,2,1,0:T(8,128)(2,1)S(1)}, u32[]{:S(2)}, u32[]{:S(2)}) collective-permute-start(bf16[2,3,32,128]{3,2,1,0:T(8,128)(2,1)S(1)} %get-tuple-element.60), channel_id=1, source_target_pairs={{0,24},{4,28},{8,16},{12,20},{16,8},{20,12},{24,0},{28,4},{1,25},{... | collective-permute-start | bytes 147464 | tf_op jit(solution)/shard_map/ppermute | solution.py:24
  56.5 0.6 collective-permute-done.21.refs_2_
  57.1 2.6 %collective-permute-done.19.refs_0_ = bf16[2,3,32,128]{3,2,1,0:T(8,128)(2,1)S(1)} collective-permute-done((bf16[2,3,32,128]{3,2,1,0:T(8,128)(2,1)S(1)}, bf16[2,3,32,128]{3,2,1,0:T(8,128)(2,1)S(1)}, u32[]{:S(2)}, u32[]{:S(2)}) %collective-permute-start.19) | collective-permute-done | bytes 49184 | tf_op jit(solution)/shard_map/ppermute | solution.py:24
  60.2 0.8 %shard_map.67 = f32[8,3,32,128]{3,2,1,0:T(8,128)} custom-call(f32[3,32,128]{2,1,0:T(8,128)S(1)} %bitcast.27, bf16[3,32,128]{2,1,0:T(8,128)(2,1)S(1)} %slice_bitcast_fusion.1.beside_ref, bf16[2,3,32,128]{3,2,1,0:T(8,128)(2,1)S(1)} %collective-permute-done.19.refs_0_, bf16[2,3,32,128]{3,2,1,0:T(8,128)(2,1)S(1)} %collective-permute-done.20.refs_1_, ...), custom_call_target="tpu_custom_call" | custom-call | tf_op jit(solution)/shard_map/pallas_call | solution.py:407
  (45 shorter events, 5.9 us)
Async XLA Ops:
  2.3 15.2 %collective-permute-start.3 = (bf16[128,2048]{1,0:T(8,128)(2,1)}, bf16[128,2048]{1,0:T(8,128)(2,1)}, u32[]{:S(2)}, u32[]{:S(2)}) collective-permute-start(bf16[128,2048]{1,0:T(8,128)(2,1)} %get-tuple-element.57), channel_id=1, source_target_pairs={{0,16},{4,20},{8,24},{12,28},{16,0},{20,4},{24,8},{28,12},{1,17},{... | collective-permute-start | bytes 1572872 | tf_op jit(solution)/shard_map/ppermute | solution.py:24
  5.3 15.2 %collective-permute-start.2 = (bf16[128,2048]{1,0:T(8,128)(2,1)}, bf16[128,2048]{1,0:T(8,128)(2,1)}, u32[]{:S(2)}, u32[]{:S(2)}) collective-permute-start(bf16[128,2048]{1,0:T(8,128)(2,1)} %get-tuple-element.58), channel_id=1, source_target_pairs={{0,8},{4,12},{8,0},{12,4},{16,24},{20,28},{24,16},{28,20},{1,9},{5... | collective-permute-start | bytes 1572872 | tf_op jit(solution)/shard_map/ppermute | solution.py:24
  6.8 2.7 %copy-start.1 = (s32[14,1]{0,1:T(1,128)S(1)}, s32[14,1]{0,1:T(1,128)}, u32[]{:S(2)}) copy-start(s32[14,1]{0,1:T(1,128)} %param.8) | copy-start | bytes 172
  6.8 2.9 %copy-start.2 = (s32[14,2]{0,1:T(2,128)S(1)}, s32[14,2]{0,1:T(2,128)}, u32[]{:S(2)}) copy-start(s32[14,2]{0,1:T(2,128)} %param.7) | copy-start | bytes 340
  6.8 2.9 %copy-start = (s32[14,1]{0,1:T(1,128)S(1)}, s32[14,1]{0,1:T(1,128)}, u32[]{:S(2)}) copy-start(s32[14,1]{0,1:T(1,128)} %param.9) | copy-start | bytes 172
  9.3 2.0 %collective-permute-start = (bf16[128,2048]{1,0:T(8,128)(2,1)S(1)}, bf16[128,2048]{1,0:T(8,128)(2,1)S(1)}, u32[]{:S(2)}, u32[]{:S(2)}) collective-permute-start(bf16[128,2048]{1,0:T(8,128)(2,1)S(1)} %get-tuple-element.33.refs_0_.refs_1_.refs_2_), channel_id=1, source_target_pairs={{0,4},{4,0},{8,12},{12,8},{16,20},{20,16},{24,28},{28,24},{1,5},{5... | collective-permute-start | bytes 1572872 | tf_op jit(solution)/shard_map/ppermute | solution.py:24
  12.9 16.9 %collective-permute-start.1 = (bf16[128,2048]{1,0:T(8,128)(2,1)S(1)}, bf16[128,2048]{1,0:T(8,128)(2,1)S(1)}, u32[]{:S(2)}, u32[]{:S(2)}) collective-permute-start(bf16[128,2048]{1,0:T(8,128)(2,1)S(1)} %get-tuple-element.34), channel_id=1, source_target_pairs={{0,24},{4,28},{8,16},{12,20},{16,8},{20,12},{24,0},{28,4},{1,25},{... | collective-permute-start | bytes 1572872 | tf_op jit(solution)/shard_map/ppermute | solution.py:24
  22.9 1.6 %collective-permute-start.4 = (bf16[256,512]{1,0:T(8,128)(2,1)S(1)}, bf16[256,512]{1,0:T(8,128)(2,1)S(1)}, u32[]{:S(2)}, u32[]{:S(2)}) collective-permute-start(bf16[256,512]{1,0:T(8,128)(2,1)S(1)} %get-tuple-element.36.refs_2_.refs_3_), channel_id=1, source_target_pairs={{0,4},{4,0},{8,12},{12,8},{16,20},{20,16},{24,28},{28,24},{1,5},{5... | collective-permute-start | bytes 786440 | tf_op jit(solution)/shard_map/ppermute | solution.py:24
  23.0 1.9 %collective-permute-start.5 = (bf16[256,512]{1,0:T(8,128)(2,1)S(1)}, bf16[256,512]{1,0:T(8,128)(2,1)S(1)}, u32[]{:S(2)}, u32[]{:S(2)}) collective-permute-start(bf16[256,512]{1,0:T(8,128)(2,1)S(1)} %get-tuple-element.37.refs_3_.refs_4_), channel_id=1, source_target_pairs={{0,4},{4,0},{8,12},{12,8},{16,20},{20,16},{24,28},{28,24},{1,5},{5... | collective-permute-start | bytes 786440 | tf_op jit(solution)/shard_map/ppermute | solution.py:24
  23.5 1.8 %collective-permute-start.6 = (bf16[256,512]{1,0:T(8,128)(2,1)S(1)}, bf16[256,512]{1,0:T(8,128)(2,1)S(1)}, u32[]{:S(2)}, u32[]{:S(2)}) collective-permute-start(bf16[256,512]{1,0:T(8,128)(2,1)S(1)} %get-tuple-element.38.refs_4_.refs_5_), channel_id=1, source_target_pairs={{0,4},{4,0},{8,12},{12,8},{16,20},{20,16},{24,28},{28,24},{1,5},{5... | collective-permute-start | bytes 786440 | tf_op jit(solution)/shard_map/ppermute | solution.py:24
  23.6 2.1 %collective-permute-start.7 = (bf16[256,512]{1,0:T(8,128)(2,1)S(1)}, bf16[256,512]{1,0:T(8,128)(2,1)S(1)}, u32[]{:S(2)}, u32[]{:S(2)}) collective-permute-start(bf16[256,512]{1,0:T(8,128)(2,1)S(1)} %get-tuple-element.39.refs_5_.refs_6_), channel_id=1, source_target_pairs={{0,4},{4,0},{8,12},{12,8},{16,20},{20,16},{24,28},{28,24},{1,5},{5... | collective-permute-start | bytes 786440 | tf_op jit(solution)/shard_map/ppermute | solution.py:24
  27.4 9.9 %collective-permute-start.9 = (bf16[128,640]{1,0:T(8,128)(2,1)S(1)}, bf16[128,640]{1,0:T(8,128)(2,1)S(1)}, u32[]{:S(2)}, u32[]{:S(2)}) collective-permute-start(bf16[128,640]{1,0:T(8,128)(2,1)S(1)} %get-tuple-element.43), channel_id=1, source_target_pairs={{0,8},{4,12},{8,0},{12,4},{16,24},{20,28},{24,16},{28,20},{1,9},{5... | collective-permute-start | bytes 491528 | tf_op jit(solution)/shard_map/ppermute | solution.py:24
  28.9 9.9 %collective-permute-start.10 = (bf16[128,640]{1,0:T(8,128)(2,1)S(1)}, bf16[128,640]{1,0:T(8,128)(2,1)S(1)}, u32[]{:S(2)}, u32[]{:S(2)}) collective-permute-start(bf16[128,640]{1,0:T(8,128)(2,1)S(1)} %get-tuple-element.44), channel_id=1, source_target_pairs={{0,16},{4,20},{8,24},{12,28},{16,0},{20,4},{24,8},{28,12},{1,17},{... | collective-permute-start | bytes 491528 | tf_op jit(solution)/shard_map/ppermute | solution.py:24
  30.6 4.0 %collective-permute-start.8 = (bf16[128,2048]{1,0:T(8,128)(2,1)S(1)}, bf16[128,2048]{1,0:T(8,128)(2,1)S(1)}, u32[]{:S(2)}, u32[]{:S(2)}) collective-permute-start(bf16[128,2048]{1,0:T(8,128)(2,1)S(1)} %shard_map.60.refs_0_), channel_id=1, source_target_pairs={{0,4},{4,0},{8,12},{12,8},{16,20},{20,16},{24,28},{28,24},{1,5},{5... | collective-permute-start | bytes 1572872 | tf_op jit(solution)/shard_map/ppermute | solution.py:24
  31.8 8.7 %collective-permute-start.11 = (bf16[128,768]{1,0:T(8,128)(2,1)S(1)}, bf16[128,768]{1,0:T(8,128)(2,1)S(1)}, u32[]{:S(2)}, u32[]{:S(2)}) collective-permute-start(bf16[128,768]{1,0:T(8,128)(2,1)S(1)} %get-tuple-element.45), channel_id=1, source_target_pairs={{0,24},{4,28},{8,16},{12,20},{16,8},{20,12},{24,0},{28,4},{1,25},{... | collective-permute-start | bytes 589832 | tf_op jit(solution)/shard_map/ppermute | solution.py:24
  35.3 5.8 %collective-permute-start.12 = (bf16[128,128]{1,0:T(8,128)(2,1)S(1)}, bf16[128,128]{1,0:T(8,128)(2,1)S(1)}, u32[]{:S(2)}, u32[]{:S(2)}) collective-permute-start(bf16[128,128]{1,0:T(8,128)(2,1)S(1)} %get-tuple-element.46), channel_id=1, source_target_pairs={{0,24},{4,28},{8,16},{12,20},{16,8},{20,12},{24,0},{28,4},{1,25},{... | collective-permute-start | bytes 98312 | tf_op jit(solution)/shard_map/ppermute | solution.py:24
  36.1 6.3 %collective-permute-start.13 = (bf16[128,256]{1,0:T(8,128)(2,1)S(1)}, bf16[128,256]{1,0:T(8,128)(2,1)S(1)}, u32[]{:S(2)}, u32[]{:S(2)}) collective-permute-start(bf16[128,256]{1,0:T(8,128)(2,1)S(1)} %get-tuple-element.47), channel_id=1, source_target_pairs={{0,8},{4,12},{8,0},{12,4},{16,24},{20,28},{24,16},{28,20},{1,9},{5... | collective-permute-start | bytes 196616 | tf_op jit(solution)/shard_map/ppermute | solution.py:24
  37.2 5.2 %collective-permute-start.14 = (bf16[128,256]{1,0:T(8,128)(2,1)S(1)}, bf16[128,256]{1,0:T(8,128)(2,1)S(1)}, u32[]{:S(2)}, u32[]{:S(2)}) collective-permute-start(bf16[128,256]{1,0:T(8,128)(2,1)S(1)} %get-tuple-element.48), channel_id=1, source_target_pairs={{0,16},{4,20},{8,24},{12,28},{16,0},{20,4},{24,8},{28,12},{1,17},{... | collective-permute-start | bytes 196616 | tf_op jit(solution)/shard_map/ppermute | solution.py:24
  42.5 6.7 %collective-permute-start.15 = (bf16[240,128]{1,0:T(8,128)(2,1)S(1)}, bf16[240,128]{1,0:T(8,128)(2,1)S(1)}, u32[]{:S(2)}, u32[]{:S(2)}) collective-permute-start(bf16[240,128]{1,0:T(8,128)(2,1)S(1)} %get-tuple-element.49), channel_id=1, source_target_pairs={{0,2},{1,3},{2,0},{3,1},{4,6},{5,7},{6,4},{7,5},{8,10},{9,11},{10,... | collective-permute-start | bytes 184328 | tf_op jit(solution)/shard_map/ppermute | solution.py:24
  45.1 6.2 %collective-permute-start.16 = (bf16[240,128]{1,0:T(8,128)(2,1)S(1)}, bf16[240,128]{1,0:T(8,128)(2,1)S(1)}, u32[]{:S(2)}, u32[]{:S(2)}) collective-permute-start(bf16[240,128]{1,0:T(8,128)(2,1)S(1)} %get-tuple-element.50), channel_id=1, source_target_pairs={{0,3},{1,2},{2,1},{3,0},{4,7},{5,6},{6,5},{7,4},{8,11},{9,10},{10,... | collective-permute-start | bytes 184328 | tf_op jit(solution)/shard_map/ppermute | solution.py:24
  46.5 4.9 %collective-permute-start.17 = (bf16[240,128]{1,0:T(8,128)(2,1)S(1)}, bf16[240,128]{1,0:T(8,128)(2,1)S(1)}, u32[]{:S(2)}, u32[]{:S(2)}) collective-permute-start(bf16[240,128]{1,0:T(8,128)(2,1)S(1)} %get-tuple-element.51), channel_id=1, source_target_pairs={{0,1},{1,0},{2,3},{3,2},{4,5},{5,4},{6,7},{7,6},{8,9},{9,8},{10,11... | collective-permute-start | bytes 184328 | tf_op jit(solution)/shard_map/ppermute | solution.py:24
  51.6 1.4 %collective-permute-start.18 = (bf16[4,3,32,128]{3,2,1,0:T(8,128)(2,1)S(1)}, bf16[4,3,32,128]{3,2,1,0:T(8,128)(2,1)S(1)}, u32[]{:S(2)}, u32[]{:S(2)}) collective-permute-start(bf16[4,3,32,128]{3,2,1,0:T(8,128)(2,1)S(1)} %shard_map.66), channel_id=1, source_target_pairs={{0,4},{4,0},{8,12},{12,8},{16,20},{20,16},{24,28},{28,24},{1,5},{5... | collective-permute-start | bytes 294920 | tf_op jit(solution)/shard_map/ppermute | solution.py:24
  53.0 4.2 %collective-permute-start.21 = (bf16[2,3,32,128]{3,2,1,0:T(8,128)(2,1)S(1)}, bf16[2,3,32,128]{3,2,1,0:T(8,128)(2,1)S(1)}, u32[]{:S(2)}, u32[]{:S(2)}) collective-permute-start(bf16[2,3,32,128]{3,2,1,0:T(8,128)(2,1)S(1)} %get-tuple-element.59), channel_id=1, source_target_pairs={{0,16},{4,20},{8,24},{12,28},{16,0},{20,4},{24,8},{28,12},{1,17},{... | collective-permute-start | bytes 147464 | tf_op jit(solution)/shard_map/ppermute | solution.py:24
  54.5 5.2 %collective-permute-start.19 = (bf16[2,3,32,128]{3,2,1,0:T(8,128)(2,1)S(1)}, bf16[2,3,32,128]{3,2,1,0:T(8,128)(2,1)S(1)}, u32[]{:S(2)}, u32[]{:S(2)}) collective-permute-start(bf16[2,3,32,128]{3,2,1,0:T(8,128)(2,1)S(1)} %get-tuple-element.60), channel_id=1, source_target_pairs={{0,24},{4,28},{8,16},{12,20},{16,8},{20,12},{24,0},{28,4},{1,25},{... | collective-permute-start | bytes 147464 | tf_op jit(solution)/shard_map/ppermute | solution.py:24
  56.1 4.1 %collective-permute-start.20 = (bf16[2,3,32,128]{3,2,1,0:T(8,128)(2,1)S(1)}, bf16[2,3,32,128]{3,2,1,0:T(8,128)(2,1)S(1)}, u32[]{:S(2)}, u32[]{:S(2)}) collective-permute-start(bf16[2,3,32,128]{3,2,1,0:T(8,128)(2,1)S(1)} %get-tuple-element.61), channel_id=1, source_target_pairs={{0,8},{4,12},{8,0},{12,4},{16,24},{20,28},{24,16},{28,20},{1,9},{5... | collective-permute-start | bytes 147464 | tf_op jit(solution)/shard_map/ppermute | solution.py:24
